TPU v7x, 512 devices: a whole 4x8x8 slice. The times are simulated.
512 devices in a mesh: grp: 16 (over y, x_lo), seq: 32 (over x_hi, z, core).
Axes of the slice: x: 4 (x_hi: 2, x_lo: 2; x = x_hi * 2 + x_lo), y: 8, z: 8, core: 2. Of those that a mesh axis runs over, the one named last changes fastest.
Arguments:
- queries: bfloat16 [512, 2, 64, 128], P(('grp', 'seq')), may hold values from -40 to 40
- root_keys: bfloat16 [16384, 8, 128], P(('grp', 'seq')), may hold values from -12 to 12
- root_values: bfloat16 [16384, 8, 128], P(('grp', 'seq')), may hold values from -4 to 4
- branch_keys: bfloat16 [16, 8192, 8, 128], P('grp', 'seq'), may hold values from -12 to 12
- branch_values: bfloat16 [16, 8192, 8, 128], P('grp', 'seq'), may hold values from -4 to 4
- suffix_keys: bfloat16 [512, 512, 8, 128], P(('grp', 'seq')), may hold values from -12 to 12
- suffix_values: bfloat16 [512, 512, 8, 128], P(('grp', 'seq')), may hold values from -4 to 4
- new_keys: bfloat16 [512, 2, 8, 128], P(('grp', 'seq')), may hold values from -12 to 12
- new_values: bfloat16 [512, 2, 8, 128], P(('grp', 'seq')), may hold values from -4 to 4
- branch_of: int32 [512], replicated, may hold values from 0 to 15, as said below
- owner: int32 [16], replicated, may hold values from 0 to 15, as said below
- suffix_len: int32 [512], P(('grp', 'seq')), may hold values from 1 to 512, 131072 in all
Outputs:
- attended: bfloat16 [512, 2, 64, 128], P(('grp', 'seq'))
Inputs may be any that keep to these rules, and one draw needn't show every extreme that they name: `branch_of`: among the 16 requests g * 32 + s of one s, at most 2 read the same branch; some branch is read by exactly 2 of them for every s. Every branch is read by some request. `owner`: each group holds a different branch. `suffix_len`: some request uses all 512 positions.
All inputs are finite; a program needn't handle non-finite values. No bound on the sum of `suffix_len` on one device may be relied on, other than what follows from the above.
Results may differ from a plain program's by a relative error of at most 0.0025.
Values may be sent and summed in bfloat16 or wider, within the bound.
No kernel may reach another device: no remote copies, remote signals or barrier semaphores. Data moves between devices by JAX's collectives and lax.ppermute only.
A program may use at most 128 MiB of HBM per device.

v0:
```python
import math

import jax
import jax.numpy as jnp
from jax import lax
from jax.sharding import PartitionSpec as P

CAP = 2


def split_heads(rows, kv_heads):
    return rows.reshape(
        rows.shape[0], rows.shape[1], kv_heads, rows.shape[2] // kv_heads, rows.shape[3]
    )


def head_scores(query_rows, key_rows):
    raw = jnp.einsum("rsjgd,ljd->rsjgl", query_rows, key_rows, preferred_element_type=jnp.float32)
    return raw * (1.0 / math.sqrt(key_rows.shape[-1]))


def weighted_sum(scores, highest, value_rows):
    weights = jnp.exp(scores - highest[..., None])
    rounded = weights.astype(jnp.bfloat16)
    numerator = jnp.einsum(
        "rsjgl,ljd->rsjgd", rounded, value_rows, preferred_element_type=jnp.float32
    )
    return (numerator, jnp.sum(weights, axis=-1))


def combine_pieces(pieces):
    overall = pieces[0][0]
    for entry in pieces[1:]:
        overall = jnp.maximum(overall, entry[0])
    numerator = jnp.zeros(pieces[0][1].shape, jnp.float32)
    denominator = jnp.zeros(pieces[0][2].shape, jnp.float32)
    for entry in pieces:
        factor = jnp.exp(entry[0] - overall)
        numerator = numerator + factor[..., None] * entry[1]
        denominator = denominator + factor * entry[2]
    return (numerator / denominator[..., None]).astype(jnp.bfloat16)


def shards(
    queries,
    root_keys,
    root_values,
    branch_keys,
    branch_values,
    suffix_keys,
    suffix_values,
    new_keys,
    new_values,
    branch_of,
    owner,
    suffix_len,
):
    step_count = queries.shape[1]
    kv_heads = root_keys.shape[1]
    grp_count = lax.axis_size("grp")
    seq_count = lax.axis_size("seq")
    grp_place = lax.axis_index("grp")
    seq_place = lax.axis_index("seq")
    peers = lax.all_gather(queries, "grp", axis=0, tiled=True)
    root_rows = (
        lax.all_gather(root_keys, "seq", axis=0, tiled=True),
        lax.all_gather(root_values, "seq", axis=0, tiled=True),
    )
    scores = head_scores(split_heads(peers, kv_heads), root_rows[0])
    highest = lax.pmax(jnp.max(scores, axis=-1), "grp")
    numerator, denominator = weighted_sum(scores, highest, root_rows[1])
    root_num, root_den = (
        lax.psum_scatter(numerator, "grp", scatter_dimension=0, tiled=True),
        lax.psum_scatter(denominator, "grp", scatter_dimension=0, tiled=True),
    )
    root_high = lax.dynamic_slice_in_dim(highest, grp_place, 1, 0)
    branch_count = owner.shape[0]
    matches = branch_of[:, None] == jnp.arange(branch_count)[None, :]
    slot_of = jnp.sum(jnp.where(matches, owner[None, :], 0), axis=1)
    slot_grid = slot_of.reshape(grp_count, seq_count)
    slot_here = lax.dynamic_slice_in_dim(slot_grid, seq_place, 1, 1)[:, 0]
    reading = slot_here == grp_place
    reader_rank = jnp.cumsum(reading.astype(jnp.int32)) - 1
    selector = (reading[None, :] & (reader_rank[None, :] == jnp.arange(CAP)[:, None])).astype(
        jnp.bfloat16
    )
    packed = jnp.einsum(
        "kg,gshd->kshd", selector, peers, preferred_element_type=jnp.float32
    ).astype(jnp.bfloat16)
    reader_rows = lax.all_gather(packed, "seq", axis=0, tiled=True)
    scores = head_scores(split_heads(reader_rows, kv_heads), branch_keys[0])
    block_high = jnp.max(scores, axis=-1)
    numerator, denominator = weighted_sum(scores, block_high, branch_values[0])
    highest = lax.pmax(block_high.astype(jnp.bfloat16), "seq").astype(block_high.dtype)
    factor = jnp.exp(block_high - highest)
    numerator = (numerator * factor[..., None]).reshape((seq_count, CAP) + numerator.shape[1:])
    denominator = (denominator * factor).reshape((seq_count, CAP) + denominator.shape[1:])
    numerator, denominator = (
        lax.all_to_all(numerator, "seq", split_axis=0, concat_axis=0, tiled=True),
        lax.all_to_all(denominator, "seq", split_axis=0, concat_axis=0, tiled=True),
    )
    numerator = jnp.sum(numerator, axis=0)
    denominator = jnp.sum(denominator, axis=0)
    slot_high = lax.dynamic_slice_in_dim(
        highest.reshape((seq_count, CAP) + highest.shape[1:]), seq_place, 1, 0
    )[0]
    returned = (
        lax.all_gather(numerator, "grp", axis=0, tiled=True),
        lax.all_gather(denominator, "grp", axis=0, tiled=True),
        lax.all_gather(slot_high, "grp", axis=0, tiled=True),
    )
    group_ids = jnp.arange(grp_count)
    my_slot = jnp.sum(jnp.where(group_ids == grp_place, slot_here, 0))
    my_rank = jnp.sum(((slot_here == my_slot) & (group_ids < grp_place)).astype(jnp.int32))
    slot_index = my_slot * CAP + my_rank
    branch_num = lax.dynamic_slice_in_dim(returned[0], slot_index, 1, 0)
    branch_den = lax.dynamic_slice_in_dim(returned[1], slot_index, 1, 0)
    branch_high = lax.dynamic_slice_in_dim(returned[2], slot_index, 1, 0)
    local_keys = jnp.concatenate([suffix_keys[0], new_keys[0]], axis=0)
    local_values = jnp.concatenate([suffix_values[0], new_values[0]], axis=0)
    suffix_cap = suffix_keys.shape[1]
    positions = jnp.arange(suffix_cap + step_count)
    step_ids = jnp.arange(step_count)
    visible = jnp.where(
        positions[None, :] < suffix_cap,
        positions[None, :] < suffix_len[0],
        positions[None, :] - suffix_cap <= step_ids[:, None],
    )
    scores = head_scores(split_heads(queries, kv_heads), local_keys)
    scores = jnp.where(visible[None, :, None, None, :], scores, -jnp.inf)
    local_high = jnp.max(scores, axis=-1)
    local_num, local_den = weighted_sum(scores, local_high, local_values)
    attended = combine_pieces(
        [
            (root_high, root_num, root_den),
            (branch_high, branch_num, branch_den),
            (local_high, local_num, local_den),
        ]
    )
    return attended.reshape(queries.shape)


def solution(mesh):
    in_specs = (
        P(("grp", "seq"), None, None, None),
        P(("grp", "seq"), None, None),
        P(("grp", "seq"), None, None),
        P("grp", "seq", None, None),
        P("grp", "seq", None, None),
        P(("grp", "seq"), None, None, None),
        P(("grp", "seq"), None, None, None),
        P(("grp", "seq"), None, None, None),
        P(("grp", "seq"), None, None, None),
        P(),
        P(),
        P(("grp", "seq")),
    )
    out_specs = P(("grp", "seq"), None, None, None)
    return jax.shard_map(shards, mesh=mesh, in_specs=in_specs, out_specs=out_specs, check_vma=False)
```

profile of v0, /device:TPU:6, one launch (start us, length us, event | category | flops | bytes accessed | tf_op | source)
XLA Modules:
  0.0 648.3 jit_solution(13221636188394441599)
XLA Ops:
  6.5 0.8 select_reduce_fusion
  7.4 0.1 reshape.150
  7.5 0.2 dynamic-slice_reduce_fusion
  7.6 0.1 compare_convert_fusion
  7.8 0.1 add_reduce_fusion
  7.9 34.5 %all_gather.22 = bf16[16,2,64,128]{3,2,1,0:T(8,128)(2,1)S(1)} all-gather(bf16[1,2,64,128]{3,2,1,0:T(8,128)(2,1)} %param.12), channel_id=1, replica_groups=mesh['grp'=16,'seq'=32] {'grp'}, dimensions={0}, use_global_device_ids=true | all-gather | bytes 557056 | tf_op jit(solution)/shard_map/all_gather | solution.py:64
  42.4 0.4 convolution_convert_fusion
  42.8 0.6 copy.251
  43.4 0.0 all-gather.8.cloned.1.call-update
  43.5 0.0 all-gather.6.cloned.1.call-start
  43.5 1.5 copy.247
  45.0 0.0 all-gather.6.cloned.1.call-update
  45.0 87.4 %all-gather.8.cloned.1.call-done = bf16[64,2,64,128]{3,2,1,0:T(8,128)(2,1)} async-done(((bf16[2,2,64,128]{3,2,1,0:T(8,128)(2,1)}), bf16[64,2,64,128]{3,2,1,0:T(8,128)(2,1)}) %all-gather.8.cloned.1.call-update) | async-done | bytes 2097168 | tf_op jit(solution)/shard_map/all_gather | solution.py:90
  132.4 3.2 bitcast_reduce_fusion
  135.6 3.2 copy-done.1
  138.8 14.8 %fusion.4 = f32[64,2,8,8]{3,1,0,2:T(2,128)S(1)} fusion(f32[8,64,2,8,256]{4,3,2,1,0:T(8,128)S(1)} %get-tuple-element.15, f32[64,2,8,8]{3,1,0,2:T(2,128)S(1)} %get-tuple-element.14), kind=kLoop, calls=%fused_computation.8 | loop fusion | flops 6283264 | bytes 8454144 | tf_op jit(solution)/shard_map/reduce_sum | solution.py:28
  153.7 0.2 copy.254
  153.9 0.2 copy.279
  154.1 131.9 %pmax.15 = bf16[64,2,8,8]{0,3,2,1:T(8,128)(2,1)S(1)} all-reduce(bf16[64,2,8,8]{0,3,2,1:T(8,128)(2,1)S(1)} %convert_element_type.31), channel_id=1, replica_groups=mesh['grp'=16,'seq'=32] {'seq'}, use_global_device_ids=true, to_apply=%region_5.6 | all-reduce | flops 8192 | bytes 32768 | tf_op jit(solution)/shard_map/pmax | solution.py:94
  286.0 0.3 copy.270
  286.2 5.4 bitcast_multiply_fusion
  291.6 2.6 copy.271
  294.2 6.0 all-to-all-start
  300.3 0.0 all-gather.10.cloned.1.call-start
  300.3 0.6 copy.264
  300.9 0.0 all-gather.10.cloned.1.call-update
  301.0 0.0 reduce-scatter.5.cloned.1.call-start
  301.0 0.0 all-gather.6.cloned.1.call-done
  301.1 6.1 bitcast_reduce_fusion.1
  307.2 0.1 copy.249
  307.3 64.7 %pmax.14 = f32[16,2,8,8]{3,2,1,0:T(8,128)S(1)} all-reduce(f32[16,2,8,8]{3,2,1,0:T(8,128)S(1)} %copy.249), channel_id=1, replica_groups=mesh['grp'=16,'seq'=32] {'grp'}, use_global_device_ids=true, to_apply=%region_1.0 | all-reduce | flops 2048 | bytes 16384 | tf_op jit(solution)/shard_map/pmax | solution.py:70
  372.0 0.1 copy.263
  372.1 4.4 fusion.2
  376.5 0.7 copy.278
  377.2 0.0 reduce-scatter.3.cloned.1.call-start
  377.3 40.7 %all-gather.10.cloned.1.call-done = bf16[1024,8,128]{2,0,1:T(8,128)(2,1)} async-done(((bf16[32,8,128]{2,0,1:T(8,128)(2,1)}), bf16[1024,8,128]{2,0,1:T(8,128)(2,1)}) %all-gather.10.cloned.1.call-update) | async-done | bytes 2097168 | tf_op jit(solution)/shard_map/all_gather | solution.py:67
  418.0 5.1 fusion.21
  423.1 1.3 copy.265
  424.5 0.2 all-gather.12.cloned.1.call-start
  424.7 2.6 reduce_sum.77
  427.3 0.6 copy.273
  428.0 0.6 fusion.59
  429.2 1.2 fusion.60
  431.7 1.1 copy.344
  432.9 1.2 copy.343
  434.1 1.8 fusion.67
  435.9 0.7 copy-done.5
  436.6 0.2 fusion.40
  436.8 0.3 copy.255
  437.1 0.3 copy.280
  437.4 0.3 copy.348
  437.6 1.4 reshape.169
  439.0 7.0 %all-to-all-start.1 = ((f32[32,1,256]{2,1,0:T(1,128)}), f32[32,1,256]{2,1,0:T(1,128)S(1)}, u32[]{:S(2)}, u32[]{:S(2)}) async-start(f32[32,1,256]{2,1,0:T(1,128)} %reshape.169), calls=%async_computation.3 | async-start | bytes 65536 | tf_op jit(solution)/shard_map/all_to_all | solution.py:100
  446.0 31.0 %all-gather = f32[1,32,2,8,8]{4,3,2,0,1:T(8,128)S(1)} all-gather(f32[1,2,2,8,8]{4,3,2,0,1:T(8,128)S(1)} %dynamic-slice_bitcast_fusion), channel_id=2, replica_groups=mesh['grp'=16,'seq'=32] {'grp'}, dimensions={1}, use_global_device_ids=true | all-gather | bytes 17408 | tf_op jit(solution)/shard_map/all_gather | solution.py:110
  477.0 0.5 broadcast.102
  477.5 0.7 reduce.6
  478.2 0.8 reshape.170
  479.1 0.2 bitcast_reduce_fusion.2
  479.2 34.1 %all_gather.27 = f32[32,2,8,8]{3,2,1,0:T(8,128)S(1)} all-gather(f32[2,2,8,8]{3,2,1,0:T(8,128)S(1)} %copy.283), channel_id=1, replica_groups=mesh['grp'=16,'seq'=32] {'grp'}, dimensions={0}, use_global_device_ids=true | all-gather | bytes 17408 | tf_op jit(solution)/shard_map/all_gather | solution.py:109
  513.3 0.7 fusion.51
  514.1 47.7 %reduce-scatter.3.cloned.1.call-done = f32[1,2,8,8,128]{4,3,2,1,0:T(8,128)} async-done(((f32[16,2,8,8,128]{4,3,2,1,0:T(8,128)}), f32[1,2,8,8,128]{4,3,2,1,0:T(8,128)}) %reduce-scatter.3.cloned.1.call-update) | async-done | bytes 65552 | tf_op jit(solution)/shard_map/reduce_scatter | solution.py:73
  561.8 77.6 %all-gather.12.cloned.1.call-done = f32[32,2,8,8,128]{4,3,2,1,0:T(8,128)} async-done(((f32[2,2,8,8,128]{4,3,2,1,0:T(8,128)}), f32[32,2,8,8,128]{4,3,2,1,0:T(8,128)}) %all-gather.12.cloned.1.call-update) | async-done | bytes 2097168 | tf_op jit(solution)/shard_map/all_gather | solution.py:108
  639.4 1.3 fusion.31
  640.8 0.6 copy.345
  (43 shorter events, 0.3 us)
Async XLA Ops:
  6.5 125.8 %copy-start = (bf16[1,256,8,128]{3,2,1,0:T(8,128)(2,1)S(1)}, bf16[1,256,8,128]{3,2,1,0:T(8,128)(2,1)}, u32[]{:S(2)}) copy-start(bf16[1,256,8,128]{3,2,1,0:T(8,128)(2,1)} %param.15) | copy-start | bytes 1572868
  6.5 125.8 %all-gather.8.cloned.1.call-start = ((), (), s32[]{:S(2)}) async-start(), calls=%async_computation.5 | async-start | bytes 2162688 | tf_op jit(solution)/shard_map/all_gather | solution.py:90
  43.5 257.6 %all-gather.6.cloned.1.call-start = ((), (), s32[]{:S(2)}) async-start(), calls=%async_computation.4 | async-start | bytes 2162688 | tf_op jit(solution)/shard_map/all_gather | solution.py:66
  135.6 3.2 copy-start.1
  138.8 147.4 %copy-start.10 = (bf16[1,256,8,128]{3,2,1,0:T(8,128)(2,1)S(1)}, bf16[1,256,8,128]{3,2,1,0:T(8,128)(2,1)}, u32[]{:S(2)}) copy-start(bf16[1,256,8,128]{3,2,1,0:T(8,128)(2,1)} %param.16) | copy-start | bytes 1572868
  294.2 6.1 copy-start.6
  294.2 130.4 %all-to-all-start = ((f32[32,2,2,8,8,128]{5,4,2,1,3,0:T(8,128)}), f32[32,2,2,8,8,128]{5,4,2,1,3,0:T(8,128)}, u32[]{:S(2)}, u32[]{:S(2)}) async-start(f32[32,2,2,8,8,128]{5,4,2,1,3,0:T(8,128)} %copy.271), calls=%async_computation.1 | async-start | bytes 8388608 | tf_op jit(solution)/shard_map/all_to_all | solution.py:99
  300.3 117.7 %all-gather.10.cloned.1.call-start = ((), (), s32[]{:S(2)}) async-start(), calls=%async_computation.6 | async-start | bytes 2162688 | tf_op jit(solution)/shard_map/all_gather | solution.py:67
  301.0 212.3 %reduce-scatter.5.cloned.1.call-start = ((), (), s32[]{:S(2)}) async-start(), calls=%async_computation.9 | async-start | bytes 139264 | tf_op jit(solution)/shard_map/reduce_scatter | solution.py:74
  377.2 184.6 %reduce-scatter.3.cloned.1.call-start = ((), (), s32[]{:S(2)}) async-start(), calls=%async_computation.7 | async-start | bytes 1114112 | tf_op jit(solution)/shard_map/reduce_scatter | solution.py:73
  423.1 8.6 %copy-start.2 = (bf16[1,512,8,128]{3,2,1,0:T(8,128)(2,1)S(1)}, bf16[1,512,8,128]{3,2,1,0:T(8,128)(2,1)}, u32[]{:S(2)}) copy-start(bf16[1,512,8,128]{3,2,1,0:T(8,128)(2,1)} %param.17) | copy-start | bytes 3145732
  424.4 8.4 %copy-start.8 = (bf16[1,2,8,128]{3,2,1,0:T(8,128)(2,1)S(1)}, bf16[1,2,8,128]{3,2,1,0:T(8,128)(2,1)}, u32[]{:S(2)}) copy-start(bf16[1,2,8,128]{3,2,1,0:T(8,128)(2,1)} %param.19) | copy-start | bytes 12292
  424.4 8.4 %copy-start.3 = (bf16[1,512,8,128]{3,2,1,0:T(8,128)(2,1)S(1)}, bf16[1,512,8,128]{3,2,1,0:T(8,128)(2,1)}, u32[]{:S(2)}) copy-start(bf16[1,512,8,128]{3,2,1,0:T(8,128)(2,1)} %param.18) | copy-start | bytes 3145732
  424.4 9.6 %copy-start.9 = (bf16[1,2,8,128]{3,2,1,0:T(8,128)(2,1)S(1)}, bf16[1,2,8,128]{3,2,1,0:T(8,128)(2,1)}, u32[]{:S(2)}) copy-start(bf16[1,2,8,128]{3,2,1,0:T(8,128)(2,1)} %param.20) | copy-start | bytes 12292
  424.4 9.6 %copy-start.7 = (bf16[1,2,64,128]{3,2,1,0:T(8,128)(2,1)S(1)}, bf16[1,2,64,128]{3,2,1,0:T(8,128)(2,1)}, u32[]{:S(2)}) copy-start(bf16[1,2,64,128]{3,2,1,0:T(8,128)(2,1)} %param.12) | copy-start | bytes 98308
  424.5 215.0 %all-gather.12.cloned.1.call-start = ((), (), s32[]{:S(2)}) async-start(), calls=%async_computation.8 | async-start | bytes 2228224 | tf_op jit(solution)/shard_map/all_gather | solution.py:108
  434.0 205.4 %copy-start.4 = (bf16[1,512,8,128]{3,1,2,0:T(8,128)(2,1)S(1)}, bf16[1,512,8,128]{3,1,2,0:T(8,128)(2,1)}, u32[]{:S(2)}) copy-start(bf16[1,512,8,128]{3,1,2,0:T(8,128)(2,1)} %copy.343) | copy-start | bytes 3145732
  435.9 0.7 copy-start.5
  439.0 38.0 %all-to-all-start.1 = ((f32[32,1,256]{2,1,0:T(1,128)}), f32[32,1,256]{2,1,0:T(1,128)S(1)}, u32[]{:S(2)}, u32[]{:S(2)}) async-start(f32[32,1,256]{2,1,0:T(1,128)} %reshape.169), calls=%async_computation.3 | async-start | bytes 65536 | tf_op jit(solution)/shard_map/all_to_all | solution.py:100
Sparse Core Ops, SparseCore 0:
  43.6 88.7 all-gather.7
  135.5 79.4 all-gather.5
  304.2 113.7 all-gather.9
  420.6 65.2 reduce-scatter.4
  488.8 72.9 reduce-scatter.2
  563.8 75.6 all-gather.11
where the time goes:
time: 650 us; the launch traced here: 648 us
  blocking collectives  296 us (46%)
  waiting for transfers between devices  254 us (39%)
  other arithmetic  26.6 us (4%)
  matrix products  23.4 us (4%)
  local copies, waits for them, and re-layouts  19.6 us (3%)
  between operations  15.6 us (2%)
  starting transfers between devices  13.4 us (2%)
    pmax x1, blocking collectives, shards(): lax.pmax(block_high.astype(jnp.bfloat16), 'seq').astype(block_high.dtype)  132 us
    all_gather x1, waiting for transfers between devices, shards(): reader_rows = lax.all_gather(packed, 'seq', axis=0, tiled=True)  87.4 us
    all_gather x1, waiting for transfers between devices, shards(): lax.all_gather(numerator, 'grp', axis=0, tiled=True)  77.6 us
    pmax x1, blocking collectives, shards(): highest = lax.pmax(jnp.max(scores, axis=-1), 'grp')  64.7 us
    reduce_scatter x1, waiting for transfers between devices, shards(): lax.psum_scatter(numerator, 'grp', scatter_dimension=0, tiled=True)  47.7 us
    all_gather x1, waiting for transfers between devices, shards(): lax.all_gather(root_values, 'seq', axis=0, tiled=True)  40.7 us
    all_gather x1, blocking collectives, shards(): peers = lax.all_gather(queries, 'grp', axis=0, tiled=True)  34.5 us
    all_gather x1, blocking collectives, shards(): lax.all_gather(denominator, 'grp', axis=0, tiled=True)  34.1 us
  transfers between devices with their start and end apart: 8, of which 4 were waited for; matrix products, arithmetic and copies ran while one was open for 9% of the time, Pallas kernels for 0%

commit v1 on v0

v1 whole, which is shorter than its diff:
```python
import functools
import math

import jax
import jax.numpy as jnp
from jax import lax
from jax.experimental import pallas as pl
from jax.experimental.pallas import tpu as pltpu
from jax.sharding import Mesh, PartitionSpec as P

CAP = 2
PAD = 8
LOW = -1e30
VMEM_LIMIT = 48 * 1024 * 1024
NT = (((1,), (1,)), ((), ()))


def scores_of(rows, keys):
    raw = lax.dot_general(rows, keys, NT, preferred_element_type=jnp.float32)
    return raw * (1.0 / math.sqrt(keys.shape[-1]))


def times_values(weights, values):
    return jnp.dot(weights.astype(jnp.bfloat16), values, preferred_element_type=jnp.float32)


def put_lse(out_ref, lead, lse, per_head, head):
    lanes = out_ref.shape[-1]
    lse = jnp.broadcast_to(lse, (lse.shape[0], lanes))
    row = lax.broadcasted_iota(jnp.int32, lse.shape, 0)
    col = lax.broadcasted_iota(jnp.int32, lse.shape, 1)
    lse = jnp.where(col == head * per_head + row % per_head, lse, 0.0)
    flat = jnp.sum(lse.reshape(-1, per_head, lanes), axis=1, keepdims=True)
    out_ref[lead, lanes:, :] += jnp.broadcast_to(flat, (flat.shape[0], PAD, lanes))


def split_lse(lse):
    coarse = jnp.round(lse * 0.25) * 4.0
    rest = lse - coarse
    middle = jnp.round(rest * 512.0) * (1.0 / 512.0)
    return coarse, middle, rest - middle


def split_tail(out_ref, lead):
    lanes = out_ref.shape[-1]
    lse = out_ref[lead, lanes:, :]
    coarse, middle, fine = split_lse(lse)
    row = lax.broadcasted_iota(jnp.int32, lse.shape, lse.ndim - 2)
    out_ref[lead, lanes:, :] = jnp.where(
        row == 0, coarse, jnp.where(row == 1, middle, jnp.where(row == 2, fine, 0.0))
    )


def join_lse(tail):
    return tail[..., 0, :] + tail[..., 1, :] + tail[..., 2, :]


def local_kernel(heads, len_ref, q_ref, k_ref, v_ref, nk_ref, nv_ref, out_ref):
    rows = q_ref.shape[0]
    per_head = rows // heads
    q = q_ref[...]
    far = scores_of(q, k_ref[...])
    row = lax.broadcasted_iota(jnp.int32, far.shape, 0)
    col = lax.broadcasted_iota(jnp.int32, far.shape, 1)
    seen = (col % heads == row // per_head) & (col < len_ref[0] * heads)
    far = jnp.where(seen, far, LOW)
    near = scores_of(q, nk_ref[...])
    row = lax.broadcasted_iota(jnp.int32, near.shape, 0)
    col = lax.broadcasted_iota(jnp.int32, near.shape, 1)
    steps = near.shape[1] // heads
    step = (row % per_head) // (per_head // steps)
    seen = (col % heads == row // per_head) & (col // heads <= step)
    near = jnp.where(seen, near, LOW)
    high = jnp.maximum(
        jnp.max(far, axis=1, keepdims=True), jnp.max(near, axis=1, keepdims=True)
    )
    far = jnp.exp(far - high)
    near = jnp.exp(near - high)
    den = jnp.sum(far, axis=1, keepdims=True) + jnp.sum(near, axis=1, keepdims=True)
    num = times_values(far, v_ref[...]) + times_values(near, nv_ref[...])
    out_ref[:rows, :] = num / den
    lse = jnp.broadcast_to(high + jnp.log(den), (rows, rows))
    row = lax.broadcasted_iota(jnp.int32, (rows, rows), 0)
    col = lax.broadcasted_iota(jnp.int32, (rows, rows), 1)
    flat = jnp.sum(jnp.where(row == col, lse, 0.0), axis=0, keepdims=True)
    out_ref[rows:, :] = jnp.broadcast_to(flat, (PAD, rows))


def select_kernel(idx_ref, peer_ref, out_ref):
    out_ref[...] = jnp.broadcast_to(peer_ref[...][None], out_ref.shape)


def branch_kernel(q_ref, own_ref, twin_ref, out_ref):
    head = pl.program_id(0)
    slots, per_head, dim = q_ref.shape
    lanes = out_ref.shape[-1]

    @pl.when(head == 0)
    def _():
        out_ref[:, lanes:, :] = jnp.zeros((slots, PAD, lanes), jnp.float32)

    step = min(16, slots)
    for start in range(0, slots, step):
        lead = slice(start, start + step)
        rows = step * per_head
        q = q_ref[lead].reshape(rows, dim)
        found = []
        for ref in (own_ref, twin_ref):
            scores = scores_of(q, ref[0, 0])
            high = jnp.max(scores, axis=1, keepdims=True)
            weights = jnp.exp(scores - high)
            den = jnp.sum(weights, axis=1, keepdims=True)
            found.append((high, den, times_values(weights, ref[1, 0])))
        (high_a, den_a, num_a), (high_b, den_b, num_b) = found
        high = jnp.maximum(high_a, high_b)
        factor_a = jnp.exp(high_a - high)
        factor_b = jnp.exp(high_b - high)
        den = factor_a * den_a + factor_b * den_b
        num = num_a * (factor_a / den) + num_b * (factor_b / den)
        place = pl.ds(pl.multiple_of(head * per_head, per_head), per_head)
        out_ref[lead, place, :] = num.reshape(step, per_head, dim)
        put_lse(out_ref, lead, high + jnp.log(den), per_head, head)

    @pl.when(head == pl.num_programs(0) - 1)
    def _():
        split_tail(out_ref, slice(0, slots))


def root_kernel(count, *refs):
    q_refs, block_refs, out_refs = refs[:2], refs[2 : 2 + count], refs[2 + count :]
    head = pl.program_id(0)
    requests, per_head, dim = q_refs[0].shape
    rows = requests * per_head
    half = block_refs[0].shape[2] // 2
    keys = jnp.concatenate([r[i, 0, :half, :] for r in block_refs for i in range(2)], axis=0)
    values = jnp.concatenate([r[i, 0, half:, :] for r in block_refs for i in range(2)], axis=0)
    for q_ref, out_ref in zip(q_refs, out_refs):
        lanes = out_ref.shape[-1]

        @pl.when(head == 0)
        def _():
            out_ref[:, lanes:, :] = jnp.zeros((requests, PAD, lanes), jnp.float32)

        scores = scores_of(q_ref[...].reshape(rows, dim), keys)
        high = jnp.max(scores, axis=1, keepdims=True)
        weights = jnp.exp(scores - high)
        den = jnp.sum(weights, axis=1, keepdims=True)
        num = times_values(weights, values) / den
        place = pl.ds(pl.multiple_of(head * per_head, per_head), per_head)
        out_ref[:, place, :] = num.reshape(requests, per_head, dim)
        put_lse(out_ref, slice(0, requests), high + jnp.log(den), per_head, head)


def columns(table):
    lanes = table.shape[1]
    rest = jnp.zeros((lanes - table.shape[0], lanes), jnp.float32)
    return jnp.concatenate([table, rest], axis=0).T


def merge_kernel(idx_ref, part_ref, own_ref, twin_ref, out_ref):
    sources, cap, _, lanes = part_ref.shape
    groups = own_ref.shape[0]
    lse_a = own_ref[:, lanes, :]
    lse_b = twin_ref[:, lanes, :]
    high = jnp.maximum(lse_a, lse_b)
    factor_a = jnp.exp(lse_a - high)
    factor_b = jnp.exp(lse_b - high)
    total = factor_a + factor_b
    table = columns(jnp.concatenate([factor_a / total, factor_b / total], axis=0))
    pieces = split_lse(high + jnp.log(total))
    row = lax.broadcasted_iota(jnp.int32, (PAD, lanes), 0)
    for r in range(groups):
        out_ref[r, :lanes, :] = (
            own_ref[r, :lanes, :] * table[:, r : r + 1]
            + twin_ref[r, :lanes, :] * table[:, groups + r : groups + r + 1]
        )
        a, b, c = (jnp.broadcast_to(p[r : r + 1], (PAD, lanes)) for p in pieces)
        out_ref[r, lanes:, :] = jnp.where(
            row == 0, a, jnp.where(row == 1, b, jnp.where(row == 2, c, 0.0))
        )
    for k in range(cap):
        reader = idx_ref[k]

        @pl.when(reader >= 0)
        def _():
            lse = join_lse(part_ref[:, k, lanes:, :])
            near = join_lse(out_ref[reader, lanes:, :])[None]
            high = jnp.maximum(jnp.max(lse, axis=0, keepdims=True), near)
            factor = jnp.exp(lse - high)
            near = jnp.exp(near - high)
            total = jnp.sum(factor, axis=0, keepdims=True) + near
            table = columns(jnp.concatenate([factor / total, near / total], axis=0))
            out = out_ref[reader, :lanes, :] * table[:, sources : sources + 1]
            for source in range(sources):
                out = out + part_ref[source, k, :lanes, :] * table[:, source : source + 1]
            out_ref[reader, :lanes, :] = out
            a, b, c = (jnp.broadcast_to(p, (PAD, lanes)) for p in split_lse(high + jnp.log(total)))
            out_ref[reader, lanes:, :] = jnp.where(
                row == 0, a, jnp.where(row == 1, b, jnp.where(row == 2, c, 0.0))
            )


def final_kernel(part_ref, local_ref, out_ref):
    groups, _, lanes = part_ref.shape
    lse = join_lse(part_ref[:, lanes:, :])
    near = local_ref[lanes : lanes + 1, :]
    high = jnp.maximum(jnp.max(lse, axis=0, keepdims=True), near)
    factor = jnp.exp(lse - high)
    near = jnp.exp(near - high)
    total = jnp.sum(factor, axis=0, keepdims=True) + near
    table = columns(jnp.concatenate([factor / total, near / total], axis=0))
    out = local_ref[:lanes, :] * table[:, groups : groups + 1]
    for source in range(groups):
        out = out + part_ref[source, :lanes, :] * table[:, source : source + 1]
    out_ref[...] = out.astype(out_ref.dtype)


def params():
    return pltpu.CompilerParams(vmem_limit_bytes=VMEM_LIMIT)


def vmem():
    return pl.BlockSpec(memory_space=pltpu.VMEM)


def smem():
    return pl.BlockSpec(memory_space=pltpu.SMEM)


def exchange(blocks, axis):
    return lax.all_to_all(blocks, axis, split_axis=0, concat_axis=0, tiled=True)


def to_all(block, axis):
    return exchange(jnp.broadcast_to(block[None], (lax.axis_size(axis),) + block.shape), axis)


def shards(
    queries,
    root_keys,
    root_values,
    branch_keys,
    branch_values,
    suffix_keys,
    suffix_values,
    new_keys,
    new_values,
    branch_of,
    owner,
    suffix_len,
):
    steps, q_heads, dim = queries.shape[1:]
    heads = root_keys.shape[1]
    group = q_heads // heads
    per_head = steps * group
    rows = heads * per_head
    grp = lax.axis_size("grp")
    sq = lax.axis_size("sq")
    core = lax.axis_size("core")
    grp_place = lax.axis_index("grp")
    seq_place = lax.axis_index("sq") * core + lax.axis_index("core")
    swap = [(0, 1), (1, 0)]

    q_rows = queries[0].reshape(steps, heads, group, dim).transpose(1, 0, 2, 3)
    q_rows = q_rows.reshape(rows, dim)
    peers = to_all(q_rows, "grp")

    matches = branch_of[:, None] == jnp.arange(owner.shape[0])[None, :]
    slot_of = jnp.sum(jnp.where(matches, owner[None, :], 0), axis=1)
    slot_here = lax.dynamic_slice_in_dim(slot_of.reshape(grp, sq * core), seq_place, 1, 1)[:, 0]
    reading = slot_here == grp_place
    group_ids = jnp.arange(grp)
    before = jnp.sum((reading[None, :] & (group_ids[None, :] < group_ids[:, None])), axis=1)
    chosen = reading[None, :] & (before[None, :] == jnp.arange(CAP)[:, None])
    readers = jnp.max(jnp.where(chosen, group_ids[None, :], -1), axis=1).astype(jnp.int32)

    def gather_readers(peers):
        packed = pl.pallas_call(
            select_kernel,
            out_shape=jax.ShapeDtypeStruct((sq, CAP, rows, dim), jnp.bfloat16),
            grid_spec=pltpu.PrefetchScalarGridSpec(
                num_scalar_prefetch=1,
                grid=(CAP,),
                in_specs=[
                    pl.BlockSpec((1, rows, dim), lambda k, idx: (jnp.maximum(idx[k], 0), 0, 0))
                ],
                out_specs=pl.BlockSpec((sq, 1, rows, dim), lambda k, idx: (0, k, 0, 0)),
            ),
            compiler_params=params(),
            name="pick_readers",
        )(readers, peers)
        return exchange(packed, "sq")

    branch_own = jnp.stack([branch_keys[0], branch_values[0]]).transpose(0, 2, 1, 3)
    branch_twin = lax.ppermute(branch_own, "core", swap)
    root_block = jnp.concatenate([root_keys, root_values], axis=0).transpose(1, 0, 2)
    ring = sq // 2
    flip = [(i, (i + ring) % sq) for i in range(sq)]
    up = [(i, i // ring * ring + (i + 1) % ring) for i in range(sq)]
    down = [(b, a) for a, b in up]
    pair = jnp.stack([root_block, lax.ppermute(root_block, "sq", flip)])
    root_blocks = [pair]
    ahead = behind = pair
    for hop in range(ring // 2):
        ahead = lax.ppermute(ahead, "sq", up)
        root_blocks.append(ahead)
        if hop < ring // 2 - 1:
            behind = lax.ppermute(behind, "sq", down)
            root_blocks.append(behind)
        if hop == 0:
            peers, ahead, behind = lax.optimization_barrier((peers, ahead, behind))
            slots = gather_readers(peers)
        if hop == 1:
            slots, ahead, behind = lax.optimization_barrier((slots, ahead, behind))
    peers_twin = lax.ppermute(peers, "core", swap)

    flat = suffix_keys.shape[1] * heads
    local = pl.pallas_call(
        functools.partial(local_kernel, heads),
        out_shape=jax.ShapeDtypeStruct((rows + PAD, dim), jnp.float32),
        in_specs=[smem()] + [vmem()] * 5,
        out_specs=vmem(),
        compiler_params=params(),
        cost_estimate=pl.CostEstimate(
            flops=4 * rows * flat * dim, bytes_accessed=4 * flat * dim, transcendentals=rows * flat
        ),
        name="local_attention",
    )(
        suffix_len,
        q_rows,
        suffix_keys.reshape(flat, dim),
        suffix_values.reshape(flat, dim),
        new_keys.reshape(steps * heads, dim),
        new_values.reshape(steps * heads, dim),
    )

    slots = slots.reshape(sq * CAP, rows, dim)
    block = (2, 1) + branch_own.shape[2:]
    area = sq * CAP * rows * branch_own.shape[2] * core
    parts = pl.pallas_call(
        branch_kernel,
        grid=(heads,),
        out_shape=jax.ShapeDtypeStruct((sq * CAP, rows + PAD, dim), jnp.float32),
        in_specs=[
            pl.BlockSpec((sq * CAP, per_head, dim), lambda j: (0, j, 0)),
            pl.BlockSpec(block, lambda j: (0, j, 0, 0)),
            pl.BlockSpec(block, lambda j: (0, j, 0, 0)),
        ],
        out_specs=pl.BlockSpec((sq * CAP, rows + PAD, dim), lambda j: (0, 0, 0)),
        compiler_params=params(),
        cost_estimate=pl.CostEstimate(
            flops=4 * area * dim, bytes_accessed=4 * 1024 * 1024, transcendentals=area
        ),
        name="branch_attention",
    )(slots, branch_own, branch_twin)
    parts = parts.astype(jnp.float16).reshape(sq, CAP, rows + PAD, dim)
    parts = exchange(parts, "sq").astype(jnp.float32)

    count = len(root_blocks)
    area = 2 * grp * rows * root_keys.shape[0] * sq
    whole = jax.ShapeDtypeStruct((grp, rows + PAD, dim), jnp.float32)
    root_own, root_twin = pl.pallas_call(
        functools.partial(root_kernel, count),
        grid=(heads,),
        out_shape=(whole, whole),
        in_specs=[pl.BlockSpec((grp, per_head, dim), lambda j: (0, j, 0))] * 2
        + [pl.BlockSpec((2, 1) + pair.shape[2:], lambda j: (0, j, 0, 0))] * count,
        out_specs=(pl.BlockSpec(whole.shape, lambda j: (0, 0, 0)),) * 2,
        compiler_params=params(),
        cost_estimate=pl.CostEstimate(
            flops=4 * area * dim, bytes_accessed=5 * 1024 * 1024, transcendentals=area
        ),
        name="root_attention",
    )(peers, peers_twin, *root_blocks)
    root_twin = lax.ppermute(root_twin, "core", swap)

    merged = pl.pallas_call(
        merge_kernel,
        out_shape=whole,
        in_specs=[smem()] + [vmem()] * 3,
        out_specs=vmem(),
        compiler_params=params(),
        name="merge_parts",
    )(readers, parts, root_own, root_twin)
    back = exchange(merged.astype(jnp.float16), "grp").astype(jnp.float32)
    mine = pl.pallas_call(
        final_kernel,
        out_shape=jax.ShapeDtypeStruct((rows, dim), jnp.bfloat16),
        in_specs=[vmem()] * 2,
        out_specs=vmem(),
        compiler_params=params(),
        name="final_merge",
    )(back, local)
    mine = mine.reshape(heads, steps, group, dim).transpose(1, 0, 2, 3)
    return mine.reshape(queries.shape)


def solution(mesh):
    grp, seq = mesh.devices.shape
    fine = Mesh(mesh.devices.reshape(grp, seq // 2, 2), ("grp", "sq", "core"))
    both = ("grp", "sq", "core")
    in_specs = (
        P(both, None, None, None),
        P(both, None, None),
        P(both, None, None),
        P("grp", ("sq", "core"), None, None),
        P("grp", ("sq", "core"), None, None),
        P(both, None, None, None),
        P(both, None, None, None),
        P(both, None, None, None),
        P(both, None, None, None),
        P(),
        P(),
        P(both),
    )
    out_specs = P(both, None, None, None)
    return jax.shard_map(shards, mesh=fine, in_specs=in_specs, out_specs=out_specs, check_vma=False)
```

time: 650 us -> 181 us (0.28)
  blocking collectives: 296 us -> 0 us
  waiting for transfers between devices: 254 us -> 74.8 us
  starting transfers between devices: 13.4 us -> 71.2 us
  Pallas kernels: 0 us -> 25.2 us
  matrix products: 23.4 us -> 0 us
  other arithmetic: 26.6 us -> 4.14 us
  local copies, waits for them, and re-layouts: 19.6 us -> 3.32 us
  between operations: 15.6 us -> 0.97 us
    all_gather x4 -> x0, waiting for transfers between devices: 206 us -> none  [the longest x1 87.4 us: shards(): reader_rows = lax.all_gather(packed, 'seq', axis=0, tiled=True)]
    pmax x2 -> x0, blocking collectives: 197 us -> none  [the longest x1 132 us: shards(): lax.pmax(block_high.astype(jnp.bfloat16), 'seq').astype(block_high.dtype)]
    all_gather x3 -> x0, blocking collectives: 99.6 us -> none  [the longest x1 34.5 us: shards(): peers = lax.all_gather(queries, 'grp', axis=0, tiled=True)]
    ppermute x0 -> x11, waiting for transfers between devices: none -> 58.9 us  [the longest x4 50.5 us: shards(): ahead = lax.ppermute(ahead, 'sq', up)]
    reduce_scatter x2 -> x0, waiting for transfers between devices: 47.7 us -> none  [the longest x1 47.7 us: shards(): lax.psum_scatter(numerator, 'grp', scatter_dimension=0, tiled=True)]
    ppermute x0 -> x11, starting transfers between devices: none -> 38.2 us  [the longest x3 16 us: shards(): behind = lax.ppermute(behind, 'sq', down)]
    pallas_call x0 -> x6, Pallas kernels: none -> 25.2 us  [the longest x1 10.3 us: shards(): pl.pallas_call(functools.partial(root_kernel, count), grid=(heads,), out_...]
    reduce_sum x7 -> x1, other arithmetic: 24 us -> 0.12 us  [shards(): jnp.sum(reading[None, :] & (group_ids[None, :] < group_ids[:, None]), axi...]
  transfers between devices with their start and end apart: 8 -> 15, of which waited for: 4 -> 8; matrix products, arithmetic and copies ran while one was open for 9% -> 1% of each run, Pallas kernels for 0% -> 7%
where the time goes in v1:
time: 181 us; the launch traced here: 180 us
  waiting for transfers between devices  74.8 us (41%)
  starting transfers between devices  71.2 us (39%)
  Pallas kernels  25.2 us (14%)
  other arithmetic  4.14 us (2%)
  local copies, waits for them, and re-layouts  3.32 us (2%)
    ppermute x4, waiting for transfers between devices, shards(): ahead = lax.ppermute(ahead, 'sq', up)  50.5 us
    all_to_all x4, starting transfers between devices, exchange(): return lax.all_to_all(blocks, axis, split_axis=0, concat_axis=0, tiled=True)  33 us
    ppermute x3, starting transfers between devices, shards(): behind = lax.ppermute(behind, 'sq', down)  16 us
    all_to_all x4, waiting for transfers between devices, exchange(): return lax.all_to_all(blocks, axis, split_axis=0, concat_axis=0, tiled=True)  15.9 us
    ppermute x4, starting transfers between devices, shards(): ahead = lax.ppermute(ahead, 'sq', up)  12.5 us
    pallas_call x1, Pallas kernels, shards(): pl.pallas_call(functools.partial(root_kernel, count), grid=(heads,), out_...  10.3 us
    pallas_call x1, Pallas kernels, shards(): pl.pallas_call(branch_kernel, grid=(heads,), out_shape=jax.ShapeDtypeStru...  8.72 us
    ppermute x1, waiting for transfers between devices, shards(): pair = jnp.stack([root_block, lax.ppermute(root_block, 'sq', flip)])  5.44 us
  transfers between devices with their start and end apart: 15, of which 8 were waited for; matrix products, arithmetic and copies ran while one was open for 1% of the time, Pallas kernels for 7%

profile of v1, /device:TPU:6, one launch (start us, length us, event | category | flops | bytes accessed | tf_op | source)
XLA Modules:
  0.0 179.7 jit_solution(11035146090741398797)
XLA Ops:
  0.0 0.8 copy.31
  0.8 0.9 broadcast_in_dim.46
  1.7 8.6 %all-to-all-start = ((bf16[16,128,128]{2,1,0:T(8,128)(2,1)}), bf16[16,128,128]{2,1,0:T(8,128)(2,1)S(1)}, u32[]{:S(2)}, u32[]{:S(2)}) async-start(bf16[16,128,128]{2,1,0:T(8,128)(2,1)} %broadcast_in_dim.46), calls=%async_computation | async-start | bytes 1048576 | tf_op jit(solution)/shard_map/all_to_all | solution.py:231
  10.3 0.0 copy-done.8
  10.3 0.0 copy-done.9
  10.3 4.0 %collective-permute-start = (bf16[8,64,128]{2,1,0:T(8,128)(2,1)S(1)}, bf16[8,64,128]{2,1,0:T(8,128)(2,1)S(1)}, u32[]{:S(2)}, u32[]{:S(2)}) collective-permute-start(bf16[8,64,128]{2,1,0:T(8,128)(2,1)S(1)} %bitcast.30), channel_id=1, source_target_pairs={{0,16},{2,18},{4,20},{6,22},{8,24},{10,26},{12,28},{14,30},{16,0},... | collective-permute-start | bytes 393224 | tf_op jit(solution)/shard_map/ppermute | solution.py:301
  14.4 5.4 %collective-permute-done = bf16[8,64,128]{2,1,0:T(8,128)(2,1)S(1)} collective-permute-done((bf16[8,64,128]{2,1,0:T(8,128)(2,1)S(1)}, bf16[8,64,128]{2,1,0:T(8,128)(2,1)S(1)}, u32[]{:S(2)}, u32[]{:S(2)}) %collective-permute-start) | collective-permute-done | bytes 131104 | tf_op jit(solution)/shard_map/ppermute | solution.py:301
  19.8 3.9 %collective-permute-start.1 = (bf16[2,8,64,128]{3,2,1,0:T(8,128)(2,1)S(1)}, bf16[2,8,64,128]{3,2,1,0:T(8,128)(2,1)S(1)}, u32[]{:S(2)}, u32[]{:S(2)}) collective-permute-start(bf16[2,8,64,128]{3,2,1,0:T(8,128)(2,1)S(1)} %pad_maximum_fusion.refs_2_), channel_id=1, source_target_pairs={{0,2},{2,4},{4,6},{6,8},{8,10},{10,12},{12,14},{14,0},{16,18},{18,... | collective-permute-start | bytes 786440 | tf_op jit(solution)/shard_map/ppermute | solution.py:305
  23.7 8.6 %collective-permute-start.2 = (bf16[2,8,64,128]{3,2,1,0:T(8,128)(2,1)S(1)}, bf16[2,8,64,128]{3,2,1,0:T(8,128)(2,1)S(1)}, u32[]{:S(2)}, u32[]{:S(2)}) collective-permute-start(bf16[2,8,64,128]{3,2,1,0:T(8,128)(2,1)S(1)} %pad_maximum_fusion.refs_2_), channel_id=1, source_target_pairs={{2,0},{4,2},{6,4},{8,6},{10,8},{12,10},{14,12},{0,14},{18,16},{20,... | collective-permute-start | bytes 786440 | tf_op jit(solution)/shard_map/ppermute | solution.py:308
  32.3 0.0 copy-done.10
  32.3 0.0 copy-done.11
  32.3 0.1 select_reduce_fusion
  32.4 0.1 reshape.39
  32.5 0.2 fusion
  32.7 0.1 convert_reduce_fusion
  32.8 0.1 fusion.2.idx_ref
  32.9 1.8 collective-permute-done.1.refs_3_
  34.7 1.5 collective-permute-done.2.refs_4_
  36.2 0.0 all-to-all-done.peer_ref.refs_0_
  36.2 1.7 pick_readers.1
  37.8 8.6 %all-to-all-start.1 = ((bf16[16,2,128,128]{3,2,1,0:T(8,128)(2,1)}), bf16[16,2,128,128]{3,2,1,0:T(8,128)(2,1)S(1)}, u32[]{:S(2)}, u32[]{:S(2)}) async-start(bf16[16,2,128,128]{3,2,1,0:T(8,128)(2,1)} %pick_readers.1), calls=%async_computation.1 | async-start | bytes 2097152 | tf_op jit(solution)/shard_map/all_to_all | solution.py:231
  46.5 0.0 copy-done.6
  46.5 0.1 copy.34
  46.5 0.0 copy-done.7
  46.5 0.1 copy.35
  46.6 0.1 maximum_bitcast_fusion.own_ref
  46.7 1.9 %collective-permute-start.5 = (bf16[2,8,256,128]{3,2,1,0:T(8,128)(2,1)S(1)}, bf16[2,8,256,128]{3,2,1,0:T(8,128)(2,1)}, u32[]{:S(2)}, u32[]{:S(2)}) collective-permute-start(bf16[2,8,256,128]{3,2,1,0:T(8,128)(2,1)S(1)} %maximum_bitcast_fusion.own_ref), channel_id=1, source_target_pairs={{0,1},{1,0},{2,3},{3,2},{4,5},{5,4},{6,7},{7,6},{8,9},{9,8},{10,11... | collective-permute-start | bytes 3145736 | tf_op jit(solution)/shard_map/ppermute | solution.py:295
  48.7 3.4 %collective-permute-start.3 = (bf16[2,8,64,128]{3,2,1,0:T(8,128)(2,1)S(1)}, bf16[2,8,64,128]{3,2,1,0:T(8,128)(2,1)S(1)}, u32[]{:S(2)}, u32[]{:S(2)}) collective-permute-start(bf16[2,8,64,128]{3,2,1,0:T(8,128)(2,1)S(1)} %collective-permute-done.1.refs_3_), channel_id=1, source_target_pairs={{0,2},{2,4},{4,6},{6,8},{8,10},{10,12},{12,14},{14,0},{16,18},{18,... | collective-permute-start | bytes 786440 | tf_op jit(solution)/shard_map/ppermute | solution.py:305
  52.0 3.7 %collective-permute-start.4 = (bf16[2,8,64,128]{3,2,1,0:T(8,128)(2,1)S(1)}, bf16[2,8,64,128]{3,2,1,0:T(8,128)(2,1)}, u32[]{:S(2)}, u32[]{:S(2)}) collective-permute-start(bf16[2,8,64,128]{3,2,1,0:T(8,128)(2,1)S(1)} %collective-permute-done.2.refs_4_), channel_id=1, source_target_pairs={{2,0},{4,2},{6,4},{8,6},{10,8},{12,10},{14,12},{0,14},{18,16},{20,... | collective-permute-start | bytes 786440 | tf_op jit(solution)/shard_map/ppermute | solution.py:308
  55.7 18.4 %collective-permute-done.3.refs_5_ = bf16[2,8,64,128]{3,2,1,0:T(8,128)(2,1)S(1)} collective-permute-done((bf16[2,8,64,128]{3,2,1,0:T(8,128)(2,1)S(1)}, bf16[2,8,64,128]{3,2,1,0:T(8,128)(2,1)S(1)}, u32[]{:S(2)}, u32[]{:S(2)}) %collective-permute-start.3) | collective-permute-done | bytes 262176 | tf_op jit(solution)/shard_map/ppermute | solution.py:305
  74.1 0.7 copy-done.4
  74.8 0.0 collective-permute-done.4.refs_6_
  74.8 0.0 all-to-all-done.1
  74.8 0.0 collective-permute-done.5.twin_ref
  74.8 8.7 %branch_attention.1 = f32[32,136,128]{2,1,0:T(8,128)S(1)} custom-call(bf16[32,128,128]{2,1,0:T(8,128)(2,1)S(1)} %bitcast.22, bf16[2,8,256,128]{3,2,1,0:T(8,128)(2,1)S(1)} %maximum_bitcast_fusion.own_ref, bf16[2,8,256,128]{3,2,1,0:T(8,128)(2,1)} %collective-permute-done.5.twin_ref), custom_call_target="tpu_custom_call" | custom-call | flops 1073741824 | bytes 4194304 | tf_op jit(solution)/shard_map/branch_attention/pallas_call | solution.py:340
  83.6 1.1 convert_element_type.16
  84.7 7.6 %all-to-all-start.2 = ((f16[16,2,136,128]{3,2,1,0:T(8,128)(2,1)}), f16[16,2,136,128]{3,2,1,0:T(8,128)(2,1)}, u32[]{:S(2)}, u32[]{:S(2)}) async-start(f16[16,2,136,128]{3,2,1,0:T(8,128)(2,1)} %bitcast.8), calls=%async_computation.2 | async-start | bytes 2228224 | tf_op jit(solution)/shard_map/all_to_all | solution.py:231
  92.4 1.9 %collective-permute-start.6 = (bf16[16,128,128]{2,1,0:T(8,128)(2,1)S(1)}, bf16[16,128,128]{2,1,0:T(8,128)(2,1)S(1)}, u32[]{:S(2)}, u32[]{:S(2)}) collective-permute-start(bf16[16,128,128]{2,1,0:T(8,128)(2,1)S(1)} %all-to-all-done.peer_ref.refs_0_), channel_id=1, source_target_pairs={{0,1},{1,0},{2,3},{3,2},{4,5},{5,4},{6,7},{7,6},{8,9},{9,8},{10,11... | collective-permute-start | bytes 1572872 | tf_op jit(solution)/shard_map/ppermute | solution.py:315
  94.3 0.0 copy-done.5
  94.3 3.4 %collective-permute-start.7 = (bf16[2,8,64,128]{3,2,1,0:T(8,128)(2,1)S(1)}, bf16[2,8,64,128]{3,2,1,0:T(8,128)(2,1)S(1)}, u32[]{:S(2)}, u32[]{:S(2)}) collective-permute-start(bf16[2,8,64,128]{3,2,1,0:T(8,128)(2,1)S(1)} %copy-done.5), channel_id=1, source_target_pairs={{0,2},{2,4},{4,6},{6,8},{8,10},{10,12},{12,14},{14,0},{16,18},{18,... | collective-permute-start | bytes 786440 | tf_op jit(solution)/shard_map/ppermute | solution.py:305
  97.7 3.7 %collective-permute-start.8 = (bf16[2,8,64,128]{3,2,1,0:T(8,128)(2,1)}, bf16[2,8,64,128]{3,2,1,0:T(8,128)(2,1)S(1)}, u32[]{:S(2)}, u32[]{:S(2)}) collective-permute-start(bf16[2,8,64,128]{3,2,1,0:T(8,128)(2,1)} %collective-permute-done.4.refs_6_), channel_id=1, source_target_pairs={{2,0},{4,2},{6,4},{8,6},{10,8},{12,10},{14,12},{0,14},{18,16},{20,... | collective-permute-start | bytes 786440 | tf_op jit(solution)/shard_map/ppermute | solution.py:308
  101.3 22.4 %collective-permute-done.7.refs_7_ = bf16[2,8,64,128]{3,2,1,0:T(8,128)(2,1)S(1)} collective-permute-done((bf16[2,8,64,128]{3,2,1,0:T(8,128)(2,1)S(1)}, bf16[2,8,64,128]{3,2,1,0:T(8,128)(2,1)S(1)}, u32[]{:S(2)}, u32[]{:S(2)}) %collective-permute-start.7) | collective-permute-done | bytes 262176 | tf_op jit(solution)/shard_map/ppermute | solution.py:305
  123.7 1.9 %collective-permute-start.9 = (bf16[2,8,64,128]{3,2,1,0:T(8,128)(2,1)S(1)}, bf16[2,8,64,128]{3,2,1,0:T(8,128)(2,1)S(1)}, u32[]{:S(2)}, u32[]{:S(2)}) collective-permute-start(bf16[2,8,64,128]{3,2,1,0:T(8,128)(2,1)S(1)} %collective-permute-done.7.refs_7_), channel_id=1, source_target_pairs={{0,2},{2,4},{4,6},{6,8},{8,10},{10,12},{12,14},{14,0},{16,18},{18,... | collective-permute-start | bytes 786440 | tf_op jit(solution)/shard_map/ppermute | solution.py:305
  125.7 0.0 collective-permute-done.6.refs_1_
  125.7 0.0 collective-permute-done.8.refs_8_
  125.7 7.9 %collective-permute-done.9.refs_9_ = bf16[2,8,64,128]{3,2,1,0:T(8,128)(2,1)S(1)} collective-permute-done((bf16[2,8,64,128]{3,2,1,0:T(8,128)(2,1)S(1)}, bf16[2,8,64,128]{3,2,1,0:T(8,128)(2,1)S(1)}, u32[]{:S(2)}, u32[]{:S(2)}) %collective-permute-start.9) | collective-permute-done | bytes 262176 | tf_op jit(solution)/shard_map/ppermute | solution.py:305
  133.6 10.3 %root_attention.1 = (f32[16,136,128]{2,1,0:T(8,128)S(1)}, f32[16,136,128]{2,1,0:T(8,128)}) custom-call(bf16[16,128,128]{2,1,0:T(8,128)(2,1)S(1)} %all-to-all-done.peer_ref.refs_0_, bf16[16,128,128]{2,1,0:T(8,128)(2,1)S(1)} %collective-permute-done.6.refs_1_, bf16[2,8,64,128]{3,2,1,0:T(8,128)(2,1)S(1)} %pad_maximum_fusion.refs_2_, ...), custom_call_target="tpu_custom_call" | custom-call | flops 1073741824 | bytes 5242880 | tf_op jit(solution)/shard_map/root_attention/pallas_call | solution.py:362
  143.8 1.9 %collective-permute-start.10 = (f32[16,136,128]{2,1,0:T(8,128)}, f32[16,136,128]{2,1,0:T(8,128)S(1)}, u32[]{:S(2)}, u32[]{:S(2)}) collective-permute-start(f32[16,136,128]{2,1,0:T(8,128)} %get-tuple-element.20), channel_id=1, source_target_pairs={{0,1},{1,0},{2,3},{3,2},{4,5},{5,4},{6,7},{7,6},{8,9},{9,8},{10,11... | collective-permute-start | bytes 3342344 | tf_op jit(solution)/shard_map/ppermute | solution.py:375
  145.8 0.0 all-to-all-done.2
  145.8 1.4 convert_element_type.17.part_ref
  147.2 1.5 collective-permute-done.10.twin_ref
  148.7 2.5 %merge_parts.1 = f32[16,136,128]{2,1,0:T(8,128)S(1)} custom-call(s32[2]{0:T(128)S(1)} %fusion.2.idx_ref, f32[16,2,136,128]{3,2,1,0:T(8,128)S(1)} %convert_element_type.17.part_ref, f32[16,136,128]{2,1,0:T(8,128)S(1)} %get-tuple-element.19.own_ref, f32[16,136,128]{2,1,0:T(8,128)S(1)} %collective-permute-done.10.twin_ref), custom_call_target="tpu_custom_call" | custom-call | tf_op jit(solution)/shard_map/merge_parts/pallas_call | solution.py:377
  151.2 0.0 copy-start
  151.3 0.0 copy-start.1
  151.3 0.0 copy-start.2
  151.3 0.0 copy-start.3
  151.3 0.9 convert_element_type.18
  152.2 8.2 %all-to-all-start.3 = ((f16[16,136,128]{2,1,0:T(8,128)(2,1)}), f16[16,136,128]{2,1,0:T(8,128)(2,1)S(1)}, u32[]{:S(2)}, u32[]{:S(2)}) async-start(f16[16,136,128]{2,1,0:T(8,128)(2,1)} %convert_element_type.18), calls=%async_computation.3 | async-start | bytes 1114112 | tf_op jit(solution)/shard_map/all_to_all | solution.py:231
  161.0 0.0 copy-done
  161.1 1.4 local_attention.1.local_ref
  162.5 15.9 %all-to-all-done.3 = f16[16,136,128]{2,1,0:T(8,128)(2,1)S(1)} async-done(((f16[16,136,128]{2,1,0:T(8,128)(2,1)}), f16[16,136,128]{2,1,0:T(8,128)(2,1)S(1)}, u32[]{:S(2)}, u32[]{:S(2)}) %all-to-all-start.3) | async-done | bytes 557088 | tf_op jit(solution)/shard_map/all_to_all | solution.py:231
  178.4 0.1 convert_element_type.19.part_ref
  178.5 0.6 final_merge.1
  179.1 0.6 copy.40
  (14 shorter events, 0.1 us)
Async XLA Ops:
  0.0 10.3 %copy-start.8 = (bf16[32,8,128]{2,1,0:T(8,128)(2,1)S(1)}, bf16[32,8,128]{2,1,0:T(8,128)(2,1)}, u32[]{:S(2)}) copy-start(bf16[32,8,128]{2,1,0:T(8,128)(2,1)} %param.13) | copy-start | bytes 196612
  0.0 10.3 %copy-start.9 = (bf16[32,8,128]{2,1,0:T(8,128)(2,1)S(1)}, bf16[32,8,128]{2,1,0:T(8,128)(2,1)}, u32[]{:S(2)}) copy-start(bf16[32,8,128]{2,1,0:T(8,128)(2,1)} %param.14) | copy-start | bytes 196612
  0.8 31.5 %copy-start.10 = (s32[512]{0:T(512)S(1)}, s32[512]{0:T(512)}, u32[]{:S(2)}) copy-start(s32[512]{0:T(512)} %param.21) | copy-start | bytes 6148
  0.8 31.5 %copy-start.11 = (s32[16]{0:T(128)S(1)}, s32[16]{0:T(128)}, u32[]{:S(2)}) copy-start(s32[16]{0:T(128)} %param.22) | copy-start | bytes 196
  1.7 34.5 %all-to-all-start = ((bf16[16,128,128]{2,1,0:T(8,128)(2,1)}), bf16[16,128,128]{2,1,0:T(8,128)(2,1)S(1)}, u32[]{:S(2)}, u32[]{:S(2)}) async-start(bf16[16,128,128]{2,1,0:T(8,128)(2,1)} %broadcast_in_dim.46), calls=%async_computation | async-start | bytes 1048576 | tf_op jit(solution)/shard_map/all_to_all | solution.py:231
  10.3 9.5 %collective-permute-start = (bf16[8,64,128]{2,1,0:T(8,128)(2,1)S(1)}, bf16[8,64,128]{2,1,0:T(8,128)(2,1)S(1)}, u32[]{:S(2)}, u32[]{:S(2)}) collective-permute-start(bf16[8,64,128]{2,1,0:T(8,128)(2,1)S(1)} %bitcast.30), channel_id=1, source_target_pairs={{0,16},{2,18},{4,20},{6,22},{8,24},{10,26},{12,28},{14,30},{16,0},... | collective-permute-start | bytes 393224 | tf_op jit(solution)/shard_map/ppermute | solution.py:301
  19.8 14.9 %collective-permute-start.1 = (bf16[2,8,64,128]{3,2,1,0:T(8,128)(2,1)S(1)}, bf16[2,8,64,128]{3,2,1,0:T(8,128)(2,1)S(1)}, u32[]{:S(2)}, u32[]{:S(2)}) collective-permute-start(bf16[2,8,64,128]{3,2,1,0:T(8,128)(2,1)S(1)} %pad_maximum_fusion.refs_2_), channel_id=1, source_target_pairs={{0,2},{2,4},{4,6},{6,8},{8,10},{10,12},{12,14},{14,0},{16,18},{18,... | collective-permute-start | bytes 786440 | tf_op jit(solution)/shard_map/ppermute | solution.py:305
  23.7 12.5 %collective-permute-start.2 = (bf16[2,8,64,128]{3,2,1,0:T(8,128)(2,1)S(1)}, bf16[2,8,64,128]{3,2,1,0:T(8,128)(2,1)S(1)}, u32[]{:S(2)}, u32[]{:S(2)}) collective-permute-start(bf16[2,8,64,128]{3,2,1,0:T(8,128)(2,1)S(1)} %pad_maximum_fusion.refs_2_), channel_id=1, source_target_pairs={{2,0},{4,2},{6,4},{8,6},{10,8},{12,10},{14,12},{0,14},{18,16},{20,... | collective-permute-start | bytes 786440 | tf_op jit(solution)/shard_map/ppermute | solution.py:308
  37.8 8.6 %copy-start.6 = (bf16[1,256,8,128]{3,2,1,0:T(8,128)(2,1)S(1)}, bf16[1,256,8,128]{3,2,1,0:T(8,128)(2,1)}, u32[]{:S(2)}) copy-start(bf16[1,256,8,128]{3,2,1,0:T(8,128)(2,1)} %param.15) | copy-start | bytes 1572868
  37.8 8.7 %copy-start.7 = (bf16[1,256,8,128]{3,2,1,0:T(8,128)(2,1)S(1)}, bf16[1,256,8,128]{3,2,1,0:T(8,128)(2,1)}, u32[]{:S(2)}) copy-start(bf16[1,256,8,128]{3,2,1,0:T(8,128)(2,1)} %param.16) | copy-start | bytes 1572868
  37.8 37.0 %all-to-all-start.1 = ((bf16[16,2,128,128]{3,2,1,0:T(8,128)(2,1)}), bf16[16,2,128,128]{3,2,1,0:T(8,128)(2,1)S(1)}, u32[]{:S(2)}, u32[]{:S(2)}) async-start(bf16[16,2,128,128]{3,2,1,0:T(8,128)(2,1)} %pick_readers.1), calls=%async_computation.1 | async-start | bytes 2097152 | tf_op jit(solution)/shard_map/all_to_all | solution.py:231
  46.7 28.1 %collective-permute-start.5 = (bf16[2,8,256,128]{3,2,1,0:T(8,128)(2,1)S(1)}, bf16[2,8,256,128]{3,2,1,0:T(8,128)(2,1)}, u32[]{:S(2)}, u32[]{:S(2)}) collective-permute-start(bf16[2,8,256,128]{3,2,1,0:T(8,128)(2,1)S(1)} %maximum_bitcast_fusion.own_ref), channel_id=1, source_target_pairs={{0,1},{1,0},{2,3},{3,2},{4,5},{5,4},{6,7},{7,6},{8,9},{9,8},{10,11... | collective-permute-start | bytes 3145736 | tf_op jit(solution)/shard_map/ppermute | solution.py:295
  48.7 25.5 %collective-permute-start.3 = (bf16[2,8,64,128]{3,2,1,0:T(8,128)(2,1)S(1)}, bf16[2,8,64,128]{3,2,1,0:T(8,128)(2,1)S(1)}, u32[]{:S(2)}, u32[]{:S(2)}) collective-permute-start(bf16[2,8,64,128]{3,2,1,0:T(8,128)(2,1)S(1)} %collective-permute-done.1.refs_3_), channel_id=1, source_target_pairs={{0,2},{2,4},{4,6},{6,8},{8,10},{10,12},{12,14},{14,0},{16,18},{18,... | collective-permute-start | bytes 786440 | tf_op jit(solution)/shard_map/ppermute | solution.py:305
  52.0 22.8 %collective-permute-start.4 = (bf16[2,8,64,128]{3,2,1,0:T(8,128)(2,1)S(1)}, bf16[2,8,64,128]{3,2,1,0:T(8,128)(2,1)}, u32[]{:S(2)}, u32[]{:S(2)}) collective-permute-start(bf16[2,8,64,128]{3,2,1,0:T(8,128)(2,1)S(1)} %collective-permute-done.2.refs_4_), channel_id=1, source_target_pairs={{2,0},{4,2},{6,4},{8,6},{10,8},{12,10},{14,12},{0,14},{18,16},{20,... | collective-permute-start | bytes 786440 | tf_op jit(solution)/shard_map/ppermute | solution.py:308
  74.1 0.7 copy-start.4
  84.7 9.6 %copy-start.5 = (bf16[2,8,64,128]{3,2,1,0:T(8,128)(2,1)S(1)}, bf16[2,8,64,128]{3,2,1,0:T(8,128)(2,1)}, u32[]{:S(2)}) copy-start(bf16[2,8,64,128]{3,2,1,0:T(8,128)(2,1)} %copy-done.4) | copy-start | bytes 786436
  84.7 61.1 %all-to-all-start.2 = ((f16[16,2,136,128]{3,2,1,0:T(8,128)(2,1)}), f16[16,2,136,128]{3,2,1,0:T(8,128)(2,1)}, u32[]{:S(2)}, u32[]{:S(2)}) async-start(f16[16,2,136,128]{3,2,1,0:T(8,128)(2,1)} %bitcast.8), calls=%async_computation.2 | async-start | bytes 2228224 | tf_op jit(solution)/shard_map/all_to_all | solution.py:231
  92.4 33.3 %collective-permute-start.6 = (bf16[16,128,128]{2,1,0:T(8,128)(2,1)S(1)}, bf16[16,128,128]{2,1,0:T(8,128)(2,1)S(1)}, u32[]{:S(2)}, u32[]{:S(2)}) collective-permute-start(bf16[16,128,128]{2,1,0:T(8,128)(2,1)S(1)} %all-to-all-done.peer_ref.refs_0_), channel_id=1, source_target_pairs={{0,1},{1,0},{2,3},{3,2},{4,5},{5,4},{6,7},{7,6},{8,9},{9,8},{10,11... | collective-permute-start | bytes 1572872 | tf_op jit(solution)/shard_map/ppermute | solution.py:315
  94.3 29.5 %collective-permute-start.7 = (bf16[2,8,64,128]{3,2,1,0:T(8,128)(2,1)S(1)}, bf16[2,8,64,128]{3,2,1,0:T(8,128)(2,1)S(1)}, u32[]{:S(2)}, u32[]{:S(2)}) collective-permute-start(bf16[2,8,64,128]{3,2,1,0:T(8,128)(2,1)S(1)} %copy-done.5), channel_id=1, source_target_pairs={{0,2},{2,4},{4,6},{6,8},{8,10},{10,12},{12,14},{14,0},{16,18},{18,... | collective-permute-start | bytes 786440 | tf_op jit(solution)/shard_map/ppermute | solution.py:305
  97.7 28.0 %collective-permute-start.8 = (bf16[2,8,64,128]{3,2,1,0:T(8,128)(2,1)}, bf16[2,8,64,128]{3,2,1,0:T(8,128)(2,1)S(1)}, u32[]{:S(2)}, u32[]{:S(2)}) collective-permute-start(bf16[2,8,64,128]{3,2,1,0:T(8,128)(2,1)} %collective-permute-done.4.refs_6_), channel_id=1, source_target_pairs={{2,0},{4,2},{6,4},{8,6},{10,8},{12,10},{14,12},{0,14},{18,16},{20,... | collective-permute-start | bytes 786440 | tf_op jit(solution)/shard_map/ppermute | solution.py:308
  123.7 9.8 %collective-permute-start.9 = (bf16[2,8,64,128]{3,2,1,0:T(8,128)(2,1)S(1)}, bf16[2,8,64,128]{3,2,1,0:T(8,128)(2,1)S(1)}, u32[]{:S(2)}, u32[]{:S(2)}) collective-permute-start(bf16[2,8,64,128]{3,2,1,0:T(8,128)(2,1)S(1)} %collective-permute-done.7.refs_7_), channel_id=1, source_target_pairs={{0,2},{2,4},{4,6},{6,8},{8,10},{10,12},{12,14},{14,0},{16,18},{18,... | collective-permute-start | bytes 786440 | tf_op jit(solution)/shard_map/ppermute | solution.py:305
  143.8 4.8 %collective-permute-start.10 = (f32[16,136,128]{2,1,0:T(8,128)}, f32[16,136,128]{2,1,0:T(8,128)S(1)}, u32[]{:S(2)}, u32[]{:S(2)}) collective-permute-start(f32[16,136,128]{2,1,0:T(8,128)} %get-tuple-element.20), channel_id=1, source_target_pairs={{0,1},{1,0},{2,3},{3,2},{4,5},{5,4},{6,7},{7,6},{8,9},{9,8},{10,11... | collective-permute-start | bytes 3342344 | tf_op jit(solution)/shard_map/ppermute | solution.py:375
  151.2 9.8 %copy-start = (bf16[1,512,8,128]{3,2,1,0:T(8,128)(2,1)S(1)}, bf16[1,512,8,128]{3,2,1,0:T(8,128)(2,1)}, u32[]{:S(2)}) copy-start(bf16[1,512,8,128]{3,2,1,0:T(8,128)(2,1)} %param.17) | copy-start | bytes 3145732
  151.3 9.8 %copy-start.1 = (bf16[1,512,8,128]{3,2,1,0:T(8,128)(2,1)S(1)}, bf16[1,512,8,128]{3,2,1,0:T(8,128)(2,1)}, u32[]{:S(2)}) copy-start(bf16[1,512,8,128]{3,2,1,0:T(8,128)(2,1)} %param.18) | copy-start | bytes 3145732
  151.3 9.8 %copy-start.2 = (bf16[1,2,8,128]{3,2,1,0:T(8,128)(2,1)S(1)}, bf16[1,2,8,128]{3,2,1,0:T(8,128)(2,1)}, u32[]{:S(2)}) copy-start(bf16[1,2,8,128]{3,2,1,0:T(8,128)(2,1)} %param.19) | copy-start | bytes 12292
  151.3 9.8 %copy-start.3 = (bf16[1,2,8,128]{3,2,1,0:T(8,128)(2,1)S(1)}, bf16[1,2,8,128]{3,2,1,0:T(8,128)(2,1)}, u32[]{:S(2)}) copy-start(bf16[1,2,8,128]{3,2,1,0:T(8,128)(2,1)} %param.20) | copy-start | bytes 12292
  152.2 26.2 %all-to-all-start.3 = ((f16[16,136,128]{2,1,0:T(8,128)(2,1)}), f16[16,136,128]{2,1,0:T(8,128)(2,1)S(1)}, u32[]{:S(2)}, u32[]{:S(2)}) async-start(f16[16,136,128]{2,1,0:T(8,128)(2,1)} %convert_element_type.18), calls=%async_computation.3 | async-start | bytes 1114112 | tf_op jit(solution)/shard_map/all_to_all | solution.py:231

commit v2 on v1

v2 whole, which is shorter than its diff:
```python
import functools
import math

import jax
import jax.numpy as jnp
from jax import lax
from jax.experimental import pallas as pl
from jax.experimental.pallas import tpu as pltpu
from jax.sharding import Mesh, PartitionSpec as P

CAP = 2
PAD = 8
LOW = -1e30
EMPHASIS = 30
VMEM_LIMIT = 20 * 1024 * 1024
NT = (((1,), (1,)), ((), ()))


def scores_of(rows, keys):
    raw = lax.dot_general(rows, keys, NT, preferred_element_type=jnp.float32)
    return raw * (1.0 / math.sqrt(keys.shape[-1]))


def times_values(weights, values):
    return jnp.dot(weights.astype(jnp.bfloat16), values, preferred_element_type=jnp.float32)


def head_lse(lse, head, per_head, lanes):
    lse = jnp.broadcast_to(lse, (lse.shape[0], lanes))
    row = lax.broadcasted_iota(jnp.int32, lse.shape, 0)
    col = lax.broadcasted_iota(jnp.int32, lse.shape, 1)
    lse = jnp.where(col == head * per_head + row % per_head, lse, 0.0)
    return jnp.sum(lse.reshape(-1, per_head, lanes), axis=1, keepdims=True)


def tail_rows(pieces):
    shape = pieces[0].shape[:-2] + (PAD, pieces[0].shape[-1])
    row = lax.broadcasted_iota(jnp.int32, shape, len(shape) - 2)
    out = jnp.zeros(shape, jnp.float32)
    for place, piece in enumerate(pieces):
        out = jnp.where(row == place, jnp.broadcast_to(piece, shape), out)
    return out


def split_lse(lse):
    coarse = jnp.round(lse * 0.25) * 4.0
    rest = lse - coarse
    middle = jnp.round(rest * 512.0) * (1.0 / 512.0)
    return coarse, middle, rest - middle


def join_lse(tail):
    return tail[..., 0, :] + tail[..., 1, :] + tail[..., 2, :]


def local_kernel(heads, len_ref, q_ref, k_ref, v_ref, nk_ref, nv_ref, out_ref):
    rows = q_ref.shape[0]
    per_head = rows // heads
    q = q_ref[...]
    far = scores_of(q, k_ref[...])
    row = lax.broadcasted_iota(jnp.int32, far.shape, 0)
    col = lax.broadcasted_iota(jnp.int32, far.shape, 1)
    seen = (col % heads == row // per_head) & (col < len_ref[0] * heads)
    far = jnp.where(seen, far, LOW)
    near = scores_of(q, nk_ref[...])
    row = lax.broadcasted_iota(jnp.int32, near.shape, 0)
    col = lax.broadcasted_iota(jnp.int32, near.shape, 1)
    steps = near.shape[1] // heads
    step = (row % per_head) // (per_head // steps)
    seen = (col % heads == row // per_head) & (col // heads <= step)
    near = jnp.where(seen, near, LOW)
    high = jnp.maximum(
        jnp.max(far, axis=1, keepdims=True), jnp.max(near, axis=1, keepdims=True)
    )
    far = jnp.exp(far - high)
    near = jnp.exp(near - high)
    den = jnp.sum(far, axis=1, keepdims=True) + jnp.sum(near, axis=1, keepdims=True)
    num = times_values(far, v_ref[...]) + times_values(near, nv_ref[...])
    out_ref[:rows, :] = num / den
    lse = jnp.broadcast_to(high + jnp.log(den), (rows, rows))
    row = lax.broadcasted_iota(jnp.int32, (rows, rows), 0)
    col = lax.broadcasted_iota(jnp.int32, (rows, rows), 1)
    flat = jnp.sum(jnp.where(row == col, lse, 0.0), axis=0, keepdims=True)
    out_ref[rows:, :] = jnp.broadcast_to(flat, (PAD, rows))


def select_kernel(idx_ref, peer_ref, out_ref):
    out_ref[...] = jnp.broadcast_to(peer_ref[...][None], out_ref.shape)


def branch_kernel(q_ref, *refs):
    out_ref = refs[-1]
    blocks = list(zip(refs[:-1:2], refs[1:-1:2]))
    slots, lanes, dim = q_ref.shape
    heads = refs[0].shape[0]
    per_head = lanes // heads
    tail = jnp.zeros((slots, 1, lanes), jnp.float32)
    for head in range(heads):
        place = slice(head * per_head, (head + 1) * per_head)
        q = q_ref[:, place, :].reshape(slots * per_head, dim)
        found = []
        for k_ref, v_ref in blocks:
            scores = scores_of(q, k_ref[head])
            high = jnp.max(scores, axis=1, keepdims=True)
            weights = jnp.exp(scores - high)
            den = jnp.sum(weights, axis=1, keepdims=True)
            found.append((high, den, times_values(weights, v_ref[head])))
        high = functools.reduce(jnp.maximum, [f[0] for f in found])
        factors = [jnp.exp(f[0] - high) for f in found]
        den = sum(factor * f[1] for factor, f in zip(factors, found))
        num = sum(f[2] * (factor / den) for factor, f in zip(factors, found))
        out_ref[:, place, :] = num.reshape(slots, per_head, dim)
        tail = tail + head_lse(high + jnp.log(den), head, per_head, lanes)
    out_ref[:, lanes:, :] = tail_rows(split_lse(tail))


def root_kernel(q_ref, own_ref, twin_ref, out_ref):
    requests, lanes, dim = q_ref.shape
    count, heads = own_ref.shape[:2]
    per_head = lanes // heads
    half = own_ref.shape[2] // 2
    tail = jnp.zeros((requests, 1, lanes), jnp.float32)
    for head in range(heads):
        place = slice(head * per_head, (head + 1) * per_head)
        q = q_ref[:, place, :].reshape(requests * per_head, dim)
        blocks = [r[:, head, :, :] for r in (own_ref, twin_ref)]
        keys = [block[:, :half, :].reshape(count * half, dim) for block in blocks]
        values = [block[:, half:, :].reshape(count * half, dim) for block in blocks]
        scores = [scores_of(q, k) for k in keys]
        high = functools.reduce(
            jnp.maximum, [jnp.max(s, axis=1, keepdims=True) for s in scores]
        )
        weights = [jnp.exp(s - high) for s in scores]
        den = sum(jnp.sum(w, axis=1, keepdims=True) for w in weights)
        num = sum(times_values(w, v) for w, v in zip(weights, values)) / den
        out_ref[:, place, :] = num.reshape(requests, per_head, dim)
        tail = tail + head_lse(high + jnp.log(den), head, per_head, lanes)
    out_ref[:, lanes:, :] = tail_rows(split_lse(tail))


def columns(table):
    lanes = table.shape[1]
    rest = jnp.zeros((lanes - table.shape[0], lanes), jnp.float32)
    return jnp.concatenate([table, rest], axis=0).T


def merge_kernel(idx_ref, part_ref, root_ref, out_ref):
    sources, cap, _, lanes = part_ref.shape
    out_ref[...] = root_ref[...]
    for k in range(cap):
        reader = idx_ref[k]

        @pl.when(reader >= 0)
        def _():
            lse = join_lse(part_ref[:, k, lanes:, :])
            near = join_lse(out_ref[reader, lanes:, :])[None]
            high = jnp.maximum(jnp.max(lse, axis=0, keepdims=True), near)
            factor = jnp.exp(lse - high)
            near = jnp.exp(near - high)
            total = jnp.sum(factor, axis=0, keepdims=True) + near
            table = columns(jnp.concatenate([factor / total, near / total], axis=0))
            out = out_ref[reader, :lanes, :] * table[:, sources : sources + 1]
            for source in range(sources):
                out = out + part_ref[source, k, :lanes, :] * table[:, source : source + 1]
            out_ref[reader, :lanes, :] = out
            out_ref[reader, lanes:, :] = tail_rows(split_lse(high + jnp.log(total)))


def final_kernel(part_ref, local_ref, out_ref):
    groups, _, lanes = part_ref.shape
    lse = join_lse(part_ref[:, lanes:, :])
    near = local_ref[lanes : lanes + 1, :]
    high = jnp.maximum(jnp.max(lse, axis=0, keepdims=True), near)
    factor = jnp.exp(lse - high)
    near = jnp.exp(near - high)
    total = jnp.sum(factor, axis=0, keepdims=True) + near
    table = columns(jnp.concatenate([factor / total, near / total], axis=0))
    out = local_ref[:lanes, :] * table[:, groups : groups + 1]
    for source in range(groups):
        out = out + part_ref[source, :lanes, :] * table[:, source : source + 1]
    out_ref[...] = out.astype(out_ref.dtype)


def params():
    return pltpu.CompilerParams(vmem_limit_bytes=VMEM_LIMIT)


def estimate(area, dim):
    return pl.CostEstimate(
        flops=EMPHASIS * 4 * area * dim, bytes_accessed=6 * 1024 * 1024, transcendentals=area
    )


def vmem():
    return pl.BlockSpec(memory_space=pltpu.VMEM)


def smem():
    return pl.BlockSpec(memory_space=pltpu.SMEM)


def exchange(blocks, axis):
    return lax.all_to_all(blocks, axis, split_axis=0, concat_axis=0, tiled=True)


def to_all(block, axis):
    return exchange(jnp.broadcast_to(block[None], (lax.axis_size(axis),) + block.shape), axis)


def shards(
    queries,
    root_keys,
    root_values,
    branch_keys,
    branch_values,
    suffix_keys,
    suffix_values,
    new_keys,
    new_values,
    branch_of,
    owner,
    suffix_len,
):
    steps, q_heads, dim = queries.shape[1:]
    heads = root_keys.shape[1]
    group = q_heads // heads
    per_head = steps * group
    rows = heads * per_head
    grp = lax.axis_size("grp")
    ring = lax.axis_size("z")
    core = lax.axis_size("core")
    spots = lax.axis_size("xhi") * ring * core
    grp_place = lax.axis_index("grp")
    seq_place = (lax.axis_index("xhi") * ring + lax.axis_index("z")) * core + lax.axis_index("core")
    swap = [(0, 1), (1, 0)]

    q_rows = queries[0].reshape(steps, heads, group, dim).transpose(1, 0, 2, 3)
    q_rows = q_rows.reshape(rows, dim)
    peers = to_all(q_rows, "grp")

    matches = branch_of[:, None] == jnp.arange(owner.shape[0])[None, :]
    slot_of = jnp.sum(jnp.where(matches, owner[None, :], 0), axis=1)
    slot_here = lax.dynamic_slice_in_dim(slot_of.reshape(grp, spots), seq_place, 1, 1)[:, 0]
    reading = slot_here == grp_place
    group_ids = jnp.arange(grp)
    before = jnp.sum((reading[None, :] & (group_ids[None, :] < group_ids[:, None])), axis=1)
    chosen = reading[None, :] & (before[None, :] == jnp.arange(CAP)[:, None])
    readers = jnp.max(jnp.where(chosen, group_ids[None, :], -1), axis=1).astype(jnp.int32)

    area = ring * CAP * rows * branch_keys.shape[1] * 4

    def gather_readers(peers):
        packed = pl.pallas_call(
            select_kernel,
            out_shape=jax.ShapeDtypeStruct((ring, CAP, rows, dim), jnp.bfloat16),
            grid_spec=pltpu.PrefetchScalarGridSpec(
                num_scalar_prefetch=1,
                grid=(CAP,),
                in_specs=[
                    pl.BlockSpec((1, rows, dim), lambda k, idx: (jnp.maximum(idx[k], 0), 0, 0))
                ],
                out_specs=pl.BlockSpec((ring, 1, rows, dim), lambda k, idx: (0, k, 0, 0)),
            ),
            compiler_params=params(),
            cost_estimate=estimate(area, dim),
            name="pick_readers",
        )(readers, peers)
        return exchange(packed, "z")

    keys_own = branch_keys[0].transpose(1, 0, 2)
    values_own = branch_values[0].transpose(1, 0, 2)
    root_block = jnp.concatenate([root_keys, root_values], axis=0).transpose(1, 0, 2)
    root_far = lax.ppermute(root_block, "xhi", swap)
    root_far, keys_own, values_own = lax.optimization_barrier((root_far, keys_own, values_own))
    root_blocks = lax.all_gather(jnp.stack([root_block, root_far]), "z", axis=0, tiled=True)
    keys_far = lax.ppermute(keys_own, "xhi", swap)
    values_far = lax.ppermute(values_own, "xhi", swap)
    slots = gather_readers(peers)
    branch_blocks = [
        keys_own,
        values_own,
        lax.ppermute(keys_own, "core", swap),
        lax.ppermute(values_own, "core", swap),
        keys_far,
        values_far,
        lax.ppermute(keys_far, "core", swap),
        lax.ppermute(values_far, "core", swap),
    ]

    flat = suffix_keys.shape[1] * heads
    local = pl.pallas_call(
        functools.partial(local_kernel, heads),
        out_shape=jax.ShapeDtypeStruct((rows + PAD, dim), jnp.float32),
        in_specs=[smem()] + [vmem()] * 5,
        out_specs=vmem(),
        compiler_params=params(),
        cost_estimate=pl.CostEstimate(
            flops=4 * rows * flat * dim, bytes_accessed=4 * flat * dim, transcendentals=rows * flat
        ),
        name="local_attention",
    )(
        suffix_len,
        q_rows,
        suffix_keys.reshape(flat, dim),
        suffix_values.reshape(flat, dim),
        new_keys.reshape(steps * heads, dim),
        new_values.reshape(steps * heads, dim),
    )

    slots = slots.reshape(ring * CAP, rows, dim)
    area = ring * CAP * rows * keys_own.shape[1] * 4
    parts = pl.pallas_call(
        branch_kernel,
        out_shape=jax.ShapeDtypeStruct((ring * CAP, rows + PAD, dim), jnp.float32),
        in_specs=[vmem()] * (1 + len(branch_blocks)),
        out_specs=vmem(),
        compiler_params=params(),
        cost_estimate=estimate(area, dim),
        name="branch_attention",
    )(slots, *branch_blocks)
    parts = parts.astype(jnp.float16).reshape(ring, CAP, rows + PAD, dim)
    root_blocks, peers, _ = lax.optimization_barrier((root_blocks, peers, parts))
    root_twin = lax.ppermute(root_blocks, "core", swap)
    parts = exchange(parts, "z")

    area = grp * rows * root_keys.shape[0] * 4 * ring
    whole = jax.ShapeDtypeStruct((grp, rows + PAD, dim), jnp.float32)
    root = pl.pallas_call(
        root_kernel,
        out_shape=whole,
        in_specs=[vmem()] * 3,
        out_specs=vmem(),
        compiler_params=params(),
        cost_estimate=estimate(area, dim),
        name="root_attention",
    )(peers, root_blocks, root_twin)

    parts, root = lax.optimization_barrier((parts, root))
    parts = parts.astype(jnp.float32)
    merged = pl.pallas_call(
        merge_kernel,
        out_shape=whole,
        in_specs=[smem()] + [vmem()] * 2,
        out_specs=vmem(),
        compiler_params=params(),
        name="merge_parts",
    )(readers, parts, root)
    back = exchange(merged.astype(jnp.float16), "grp").astype(jnp.float32)
    mine = pl.pallas_call(
        final_kernel,
        out_shape=jax.ShapeDtypeStruct((rows, dim), jnp.bfloat16),
        in_specs=[vmem()] * 2,
        out_specs=vmem(),
        compiler_params=params(),
        name="final_merge",
    )(back, local)
    mine = mine.reshape(heads, steps, group, dim).transpose(1, 0, 2, 3)
    return mine.reshape(queries.shape)


def solution(mesh):
    grp, seq = mesh.devices.shape
    fine = Mesh(mesh.devices.reshape(grp, 2, seq // 4, 2), ("grp", "xhi", "z", "core"))
    seq = ("xhi", "z", "core")
    both = ("grp",) + seq
    in_specs = (
        P(both, None, None, None),
        P(both, None, None),
        P(both, None, None),
        P("grp", seq, None, None),
        P("grp", seq, None, None),
        P(both, None, None, None),
        P(both, None, None, None),
        P(both, None, None, None),
        P(both, None, None, None),
        P(),
        P(),
        P(both),
    )
    out_specs = P(both, None, None, None)
    return jax.shard_map(shards, mesh=fine, in_specs=in_specs, out_specs=out_specs, check_vma=False)
```

time: 181 us -> 160 us (0.88)
  starting transfers between devices: 71.2 us -> 52.3 us
  waiting for transfers between devices: 74.8 us -> 59.6 us
  between operations: 0.97 us -> 14.3 us
  local copies, waits for them, and re-layouts: 3.32 us -> 14.6 us
  Pallas kernels: 25.2 us -> 14.1 us
    ppermute x11 -> x8, waiting for transfers between devices: 58.9 us -> 6.91 us  [the longest x1 4.61 us: shards(): root_far = lax.ppermute(root_block, 'xhi', swap)]
    all_gather x0 -> x1, waiting for transfers between devices: none -> 27.1 us  [shards(): lax.all_gather(jnp.stack([root_block, root_far]), 'z', axis=0, tiled=True)]
    ppermute x11 -> x8, starting transfers between devices: 38.2 us -> 21.4 us  [the longest x1 4.01 us: shards(): root_far = lax.ppermute(root_block, 'xhi', swap)]
    unnamed x27 -> x43, local copies, waits for them, and re-layouts: 0.9 us -> 11.9 us
    pallas_call x3, Pallas kernels: 20.7 us -> 10.5 us  [the longest x1 4.78 us: shards(): pl.pallas_call(branch_kernel, out_shape=jax.ShapeDtypeStruct((ring * CAP,...]
    all_to_all x4, waiting for transfers between devices: 15.9 us -> 25.6 us  [exchange(): return lax.all_to_all(blocks, axis, split_axis=0, concat_axis=0, tiled=True)]
    all_to_all x4, starting transfers between devices: 33 us -> 30.8 us  [exchange(): return lax.all_to_all(blocks, axis, split_axis=0, concat_axis=0, tiled=True)]
  transfers between devices with their start and end apart: 15 -> 13, of which waited for: 8 -> 7; matrix products, arithmetic and copies ran while one was open for 1% -> 2% of each run, Pallas kernels for 7% -> 8%
where the time goes in v2:
time: 160 us; the launch traced here: 158 us
  waiting for transfers between devices  59.6 us (37%)
  starting transfers between devices  52.3 us (33%)
  local copies, waits for them, and re-layouts  14.6 us (9%)
  between operations  14.3 us (9%)
  Pallas kernels  14.1 us (9%)
  other arithmetic  3.2 us (2%)
    all_to_all x4, starting transfers between devices, exchange(): return lax.all_to_all(blocks, axis, split_axis=0, concat_axis=0, tiled=True)  30.8 us
    all_gather x1, waiting for transfers between devices, shards(): lax.all_gather(jnp.stack([root_block, root_far]), 'z', axis=0, tiled=True)  27.1 us
    all_to_all x4, waiting for transfers between devices, exchange(): return lax.all_to_all(blocks, axis, split_axis=0, concat_axis=0, tiled=True)  25.6 us
    unnamed x43, local copies, waits for them, and re-layouts  11.9 us
    pallas_call x1, Pallas kernels, shards(): pl.pallas_call(branch_kernel, out_shape=jax.ShapeDtypeStruct((ring * CAP,...  4.78 us
    ppermute x1, waiting for transfers between devices, shards(): root_far = lax.ppermute(root_block, 'xhi', swap)  4.61 us
    pallas_call x1, Pallas kernels, shards(): pl.pallas_call(root_kernel, out_shape=whole, in_specs=[vmem()] * 3, out_s...  4.3 us
    ppermute x1, starting transfers between devices, shards(): root_far = lax.ppermute(root_block, 'xhi', swap)  4.01 us
  transfers between devices with their start and end apart: 13, of which 7 were waited for; matrix products, arithmetic and copies ran while one was open for 2% of the time, Pallas kernels for 8%

profile of v2, /device:TPU:6, one launch (start us, length us, event | category | flops | bytes accessed | tf_op | source)
XLA Modules:
  0.0 158.1 jit_solution(14990216924793047674)
XLA Ops:
  6.6 0.9 copy.37
  7.4 0.9 broadcast_in_dim.46
  8.3 8.6 %all-to-all-start = ((bf16[16,128,128]{2,1,0:T(8,128)(2,1)}), bf16[16,128,128]{2,1,0:T(8,128)(2,1)S(1)}, u32[]{:S(2)}, u32[]{:S(2)}) async-start(bf16[16,128,128]{2,1,0:T(8,128)(2,1)} %broadcast_in_dim.46), calls=%async_computation | async-start | bytes 1048576 | tf_op jit(solution)/shard_map/all_to_all | solution.py:203
  17.0 4.0 %collective-permute-start = (bf16[8,64,128]{2,1,0:T(8,128)(2,1)S(1)}, bf16[8,64,128]{2,1,0:T(8,128)(2,1)S(1)}, u32[]{:S(2)}, u32[]{:S(2)}) collective-permute-start(bf16[8,64,128]{2,1,0:T(8,128)(2,1)S(1)} %bitcast.36), channel_id=1, source_target_pairs={{0,16},{16,0},{1,17},{17,1},{2,18},{18,2},{3,19},{19,3},{4,20},{20... | collective-permute-start | bytes 393224 | tf_op jit(solution)/shard_map/ppermute | solution.py:273
  21.0 0.0 copy-done.19
  21.0 0.0 copy-done.20
  21.0 0.1 select_reduce_fusion
  21.1 0.1 reshape.39
  21.2 0.2 fusion
  21.4 0.2 copy_bitcast_fusion
  21.6 0.1 convert_reduce_fusion
  21.7 0.1 fusion.2.idx_ref
  21.8 4.6 %collective-permute-done = bf16[8,64,128]{2,1,0:T(8,128)(2,1)S(1)} collective-permute-done((bf16[8,64,128]{2,1,0:T(8,128)(2,1)S(1)}, bf16[8,64,128]{2,1,0:T(8,128)(2,1)S(1)}, u32[]{:S(2)}, u32[]{:S(2)}) %collective-permute-start) | collective-permute-done | bytes 131104 | tf_op jit(solution)/shard_map/ppermute | solution.py:273
  26.4 3.6 %collective-permute-start.3 = (bf16[8,256,128]{2,1,0:T(8,128)(2,1)S(1)}, bf16[8,256,128]{2,1,0:T(8,128)(2,1)S(1)}, u32[]{:S(2)}, u32[]{:S(2)}) collective-permute-start(bf16[8,256,128]{2,1,0:T(8,128)(2,1)S(1)} %get-tuple-element.12.refs_0_), channel_id=1, source_target_pairs={{0,16},{16,0},{1,17},{17,1},{2,18},{18,2},{3,19},{19,3},{4,20},{20... | collective-permute-start | bytes 1572872 | tf_op jit(solution)/shard_map/ppermute | solution.py:276
  30.0 3.8 %collective-permute-start.4 = (bf16[8,256,128]{2,1,0:T(8,128)(2,1)S(1)}, bf16[8,256,128]{2,1,0:T(8,128)(2,1)S(1)}, u32[]{:S(2)}, u32[]{:S(2)}) collective-permute-start(bf16[8,256,128]{2,1,0:T(8,128)(2,1)S(1)} %get-tuple-element.13.refs_1_), channel_id=1, source_target_pairs={{0,16},{16,0},{1,17},{17,1},{2,18},{18,2},{3,19},{19,3},{4,20},{20... | collective-permute-start | bytes 1572872 | tf_op jit(solution)/shard_map/ppermute | solution.py:277
  33.8 0.0 all-to-all-done.peer_ref.q_ref
  33.8 1.4 pick_readers.1
  35.2 9.9 %all-to-all-start.1 = ((bf16[8,2,128,128]{3,2,1,0:T(8,128)(2,1)}), bf16[8,2,128,128]{3,2,1,0:T(8,128)(2,1)S(1)}, u32[]{:S(2)}, u32[]{:S(2)}) async-start(bf16[8,2,128,128]{3,2,1,0:T(8,128)(2,1)} %pick_readers.1), calls=%async_computation.1 | async-start | bytes 1048576 | tf_op jit(solution)/shard_map/all_to_all | solution.py:203
  45.1 0.0 all-gather.2.cloned.1.call-start
  45.2 0.7 pad_maximum_fusion
  45.9 0.0 all-gather.2.cloned.1.call-update
  45.9 1.9 %collective-permute-start.1 = (bf16[8,256,128]{2,1,0:T(8,128)(2,1)S(1)}, bf16[8,256,128]{2,1,0:T(8,128)(2,1)S(1)}, u32[]{:S(2)}, u32[]{:S(2)}) collective-permute-start(bf16[8,256,128]{2,1,0:T(8,128)(2,1)S(1)} %get-tuple-element.12.refs_0_), channel_id=1, source_target_pairs={{0,1},{1,0},{2,3},{3,2},{4,5},{5,4},{6,7},{7,6},{8,9},{9,8},{10,11... | collective-permute-start | bytes 1572872 | tf_op jit(solution)/shard_map/ppermute | solution.py:282
  47.8 2.4 %collective-permute-start.2 = (bf16[8,256,128]{2,1,0:T(8,128)(2,1)S(1)}, bf16[8,256,128]{2,1,0:T(8,128)(2,1)S(1)}, u32[]{:S(2)}, u32[]{:S(2)}) collective-permute-start(bf16[8,256,128]{2,1,0:T(8,128)(2,1)S(1)} %get-tuple-element.13.refs_1_), channel_id=1, source_target_pairs={{0,1},{1,0},{2,3},{3,2},{4,5},{5,4},{6,7},{7,6},{8,9},{9,8},{10,11... | collective-permute-start | bytes 1572872 | tf_op jit(solution)/shard_map/ppermute | solution.py:283
  50.3 0.0 collective-permute-done.3.refs_4_
  50.3 1.9 %collective-permute-start.5 = (bf16[8,256,128]{2,1,0:T(8,128)(2,1)S(1)}, bf16[8,256,128]{2,1,0:T(8,128)(2,1)S(1)}, u32[]{:S(2)}, u32[]{:S(2)}) collective-permute-start(bf16[8,256,128]{2,1,0:T(8,128)(2,1)S(1)} %collective-permute-done.3.refs_4_), channel_id=1, source_target_pairs={{0,1},{1,0},{2,3},{3,2},{4,5},{5,4},{6,7},{7,6},{8,9},{9,8},{10,11... | collective-permute-start | bytes 1572872 | tf_op jit(solution)/shard_map/ppermute | solution.py:286
  52.2 2.1 %collective-permute-done.4.refs_5_ = bf16[8,256,128]{2,1,0:T(8,128)(2,1)S(1)} collective-permute-done((bf16[8,256,128]{2,1,0:T(8,128)(2,1)S(1)}, bf16[8,256,128]{2,1,0:T(8,128)(2,1)S(1)}, u32[]{:S(2)}, u32[]{:S(2)}) %collective-permute-start.4) | collective-permute-done | bytes 524320 | tf_op jit(solution)/shard_map/ppermute | solution.py:277
  54.3 1.9 %collective-permute-start.6 = (bf16[8,256,128]{2,1,0:T(8,128)(2,1)S(1)}, bf16[8,256,128]{2,1,0:T(8,128)(2,1)S(1)}, u32[]{:S(2)}, u32[]{:S(2)}) collective-permute-start(bf16[8,256,128]{2,1,0:T(8,128)(2,1)S(1)} %collective-permute-done.4.refs_5_), channel_id=1, source_target_pairs={{0,1},{1,0},{2,3},{3,2},{4,5},{5,4},{6,7},{7,6},{8,9},{9,8},{10,11... | collective-permute-start | bytes 1572872 | tf_op jit(solution)/shard_map/ppermute | solution.py:287
  56.2 0.0 collective-permute-done.1.refs_2_
  56.2 0.8 copy-done.7
  57.0 0.0 collective-permute-done.2.refs_3_
  57.0 0.8 copy-done.9
  57.8 0.0 collective-permute-done.5.refs_6_
  57.8 0.8 copy-done.11
  58.6 0.0 collective-permute-done.6.refs_7_
  58.6 0.8 copy-done.13
  59.4 0.6 all-to-all-done.1
  60.0 1.0 copy-done.8
  61.1 1.0 copy-done.10
  62.1 1.0 copy-done.12
  63.2 1.0 copy-done.14
  64.2 4.8 %branch_attention.1 = f32[16,136,128]{2,1,0:T(8,128)S(1)} custom-call(bf16[16,128,128]{2,1,0:T(8,128)(2,1)S(1)} %bitcast.30, bf16[8,256,128]{2,1,0:T(8,128)(2,1)S(1)} %get-tuple-element.12.refs_0_, bf16[8,256,128]{2,1,0:T(8,128)(2,1)S(1)} %get-tuple-element.13.refs_1_, bf16[8,256,128]{2,1,0:T(8,128)(2,1)S(1)} %copy-done.8, ...), custom_call_target="tpu_custom_call" | custom-call | flops 32212254720 | bytes 6291456 | tf_op jit(solution)/shard_map/branch_attention/pallas_call | solution.py:312
  69.0 0.9 convert_element_type.16
  69.9 27.1 %all-gather.2.cloned.1.call-done.own_ref = bf16[16,8,64,128]{3,2,1,0:T(8,128)(2,1)} async-done(((bf16[2,8,64,128]{3,2,1,0:T(8,128)(2,1)}), bf16[16,8,64,128]{3,2,1,0:T(8,128)(2,1)}) %all-gather.2.cloned.1.call-update) | async-done | bytes 2097168 | tf_op jit(solution)/shard_map/all_gather | solution.py:275
  97.0 1.9 %collective-permute-start.7 = (bf16[16,8,64,128]{3,2,1,0:T(8,128)(2,1)}, bf16[16,8,64,128]{3,2,1,0:T(8,128)(2,1)S(1)}, u32[]{:S(2)}, u32[]{:S(2)}) collective-permute-start(bf16[16,8,64,128]{3,2,1,0:T(8,128)(2,1)} %all-gather.2.cloned.1.call-done.own_ref), channel_id=1, source_target_pairs={{0,1},{1,0},{2,3},{3,2},{4,5},{5,4},{6,7},{7,6},{8,9},{9,8},{10,11... | collective-permute-start | bytes 6291464 | tf_op jit(solution)/shard_map/ppermute | solution.py:323
  98.9 4.2 %all-to-all-start.2 = ((f16[8,2,136,128]{3,2,1,0:T(8,128)(2,1)}), f16[8,2,136,128]{3,2,1,0:T(8,128)(2,1)S(1)}, u32[]{:S(2)}, u32[]{:S(2)}) async-start(f16[8,2,136,128]{3,2,1,0:T(8,128)(2,1)} %bitcast.9), calls=%async_computation.2 | async-start | bytes 1114112 | tf_op jit(solution)/shard_map/all_to_all | solution.py:203
  103.1 0.2 collective-permute-done.7.twin_ref
  103.3 1.3 copy-done.5
  104.6 1.6 %copy-done.4 = bf16[16,8,64,128]{3,2,1,0:T(8,128)(2,1)S(1)} copy-done((bf16[16,8,64,128]{3,2,1,0:T(8,128)(2,1)S(1)}, bf16[16,8,64,128]{3,2,1,0:T(8,128)(2,1)}, u32[]{:S(2)}) %copy-start.4) | copy-done | bytes 2097176
  106.2 1.6 %copy-done.6 = bf16[16,8,64,128]{3,2,1,0:T(8,128)(2,1)S(1)} copy-done((bf16[16,8,64,128]{3,2,1,0:T(8,128)(2,1)S(1)}, bf16[16,8,64,128]{3,2,1,0:T(8,128)(2,1)}, u32[]{:S(2)}) %copy-start.6) | copy-done | bytes 2097176
  107.8 4.3 %root_attention.1.root_ref = f32[16,136,128]{2,1,0:T(8,128)S(1)} custom-call(bf16[16,128,128]{2,1,0:T(8,128)(2,1)S(1)} %all-to-all-done.peer_ref.q_ref, bf16[16,8,64,128]{3,2,1,0:T(8,128)(2,1)S(1)} %copy-done.4, bf16[16,8,64,128]{3,2,1,0:T(8,128)(2,1)S(1)} %copy-done.6), custom_call_target="tpu_custom_call" | custom-call | flops 32212254720 | bytes 6291456 | tf_op jit(solution)/shard_map/root_attention/pallas_call | solution.py:328
  112.1 9.9 %all-to-all-done.2 = f16[8,2,136,128]{3,2,1,0:T(8,128)(2,1)S(1)} async-done(((f16[8,2,136,128]{3,2,1,0:T(8,128)(2,1)}), f16[8,2,136,128]{3,2,1,0:T(8,128)(2,1)S(1)}, u32[]{:S(2)}, u32[]{:S(2)}) %all-to-all-start.2) | async-done | bytes 557088 | tf_op jit(solution)/shard_map/all_to_all | solution.py:203
  122.0 0.1 convert_element_type.17.part_ref
  122.1 1.6 merge_parts.1
  123.6 0.0 copy-start
  123.6 0.0 copy-start.1
  123.7 0.0 copy-start.2
  123.7 0.0 copy-start.3
  123.7 0.9 convert_element_type.18
  124.6 8.2 %all-to-all-start.3 = ((f16[16,136,128]{2,1,0:T(8,128)(2,1)}), f16[16,136,128]{2,1,0:T(8,128)(2,1)S(1)}, u32[]{:S(2)}, u32[]{:S(2)}) async-start(f16[16,136,128]{2,1,0:T(8,128)(2,1)} %convert_element_type.18), calls=%async_computation.3 | async-start | bytes 1114112 | tf_op jit(solution)/shard_map/all_to_all | solution.py:203
  133.5 1.5 local_attention.1.local_ref
  134.9 15.0 %all-to-all-done.3 = f16[16,136,128]{2,1,0:T(8,128)(2,1)S(1)} async-done(((f16[16,136,128]{2,1,0:T(8,128)(2,1)}), f16[16,136,128]{2,1,0:T(8,128)(2,1)S(1)}, u32[]{:S(2)}, u32[]{:S(2)}) %all-to-all-start.3) | async-done | bytes 557088 | tf_op jit(solution)/shard_map/all_to_all | solution.py:203
  150.0 0.1 convert_element_type.19.part_ref
  150.1 0.5 final_merge.1
  150.6 0.6 copy.48
  (27 shorter events, 0.1 us)
Async XLA Ops:
  6.5 10.4 %copy-start.17 = (bf16[32,8,128]{2,1,0:T(8,128)(2,1)S(1)}, bf16[32,8,128]{2,1,0:T(8,128)(2,1)}, u32[]{:S(2)}) copy-start(bf16[32,8,128]{2,1,0:T(8,128)(2,1)} %param.13) | copy-start | bytes 196612
  6.5 10.4 %copy-start.18 = (bf16[32,8,128]{2,1,0:T(8,128)(2,1)S(1)}, bf16[32,8,128]{2,1,0:T(8,128)(2,1)}, u32[]{:S(2)}) copy-start(bf16[32,8,128]{2,1,0:T(8,128)(2,1)} %param.14) | copy-start | bytes 196612
  6.5 14.5 %copy-start.19 = (s32[512]{0:T(512)S(1)}, s32[512]{0:T(512)}, u32[]{:S(2)}) copy-start(s32[512]{0:T(512)} %param.21) | copy-start | bytes 6148
  6.5 14.5 %copy-start.20 = (s32[16]{0:T(128)S(1)}, s32[16]{0:T(128)}, u32[]{:S(2)}) copy-start(s32[16]{0:T(128)} %param.22) | copy-start | bytes 196
  6.5 14.8 %copy-start.16 = (bf16[1,256,8,128]{3,2,1,0:T(8,128)(2,1)S(1)}, bf16[1,256,8,128]{3,2,1,0:T(8,128)(2,1)}, u32[]{:S(2)}) copy-start(bf16[1,256,8,128]{3,2,1,0:T(8,128)(2,1)} %param.15) | copy-start | bytes 1572868
  6.5 14.8 %copy-start.15 = (bf16[1,256,8,128]{3,2,1,0:T(8,128)(2,1)S(1)}, bf16[1,256,8,128]{3,2,1,0:T(8,128)(2,1)}, u32[]{:S(2)}) copy-start(bf16[1,256,8,128]{3,2,1,0:T(8,128)(2,1)} %param.16) | copy-start | bytes 1572868
  8.3 25.4 %all-to-all-start = ((bf16[16,128,128]{2,1,0:T(8,128)(2,1)}), bf16[16,128,128]{2,1,0:T(8,128)(2,1)S(1)}, u32[]{:S(2)}, u32[]{:S(2)}) async-start(bf16[16,128,128]{2,1,0:T(8,128)(2,1)} %broadcast_in_dim.46), calls=%async_computation | async-start | bytes 1048576 | tf_op jit(solution)/shard_map/all_to_all | solution.py:203
  17.0 9.5 %collective-permute-start = (bf16[8,64,128]{2,1,0:T(8,128)(2,1)S(1)}, bf16[8,64,128]{2,1,0:T(8,128)(2,1)S(1)}, u32[]{:S(2)}, u32[]{:S(2)}) collective-permute-start(bf16[8,64,128]{2,1,0:T(8,128)(2,1)S(1)} %bitcast.36), channel_id=1, source_target_pairs={{0,16},{16,0},{1,17},{17,1},{2,18},{18,2},{3,19},{19,3},{4,20},{20... | collective-permute-start | bytes 393224 | tf_op jit(solution)/shard_map/ppermute | solution.py:273
  26.4 23.8 %collective-permute-start.3 = (bf16[8,256,128]{2,1,0:T(8,128)(2,1)S(1)}, bf16[8,256,128]{2,1,0:T(8,128)(2,1)S(1)}, u32[]{:S(2)}, u32[]{:S(2)}) collective-permute-start(bf16[8,256,128]{2,1,0:T(8,128)(2,1)S(1)} %get-tuple-element.12.refs_0_), channel_id=1, source_target_pairs={{0,16},{16,0},{1,17},{17,1},{2,18},{18,2},{3,19},{19,3},{4,20},{20... | collective-permute-start | bytes 1572872 | tf_op jit(solution)/shard_map/ppermute | solution.py:276
  30.0 24.3 %collective-permute-start.4 = (bf16[8,256,128]{2,1,0:T(8,128)(2,1)S(1)}, bf16[8,256,128]{2,1,0:T(8,128)(2,1)S(1)}, u32[]{:S(2)}, u32[]{:S(2)}) collective-permute-start(bf16[8,256,128]{2,1,0:T(8,128)(2,1)S(1)} %get-tuple-element.13.refs_1_), channel_id=1, source_target_pairs={{0,16},{16,0},{1,17},{17,1},{2,18},{18,2},{3,19},{19,3},{4,20},{20... | collective-permute-start | bytes 1572872 | tf_op jit(solution)/shard_map/ppermute | solution.py:277
  35.2 24.8 %all-to-all-start.1 = ((bf16[8,2,128,128]{3,2,1,0:T(8,128)(2,1)}), bf16[8,2,128,128]{3,2,1,0:T(8,128)(2,1)S(1)}, u32[]{:S(2)}, u32[]{:S(2)}) async-start(bf16[8,2,128,128]{3,2,1,0:T(8,128)(2,1)} %pick_readers.1), calls=%async_computation.1 | async-start | bytes 1048576 | tf_op jit(solution)/shard_map/all_to_all | solution.py:203
  45.1 51.9 %all-gather.2.cloned.1.call-start = ((), (), s32[]{:S(2)}) async-start(), calls=%async_computation.4 | async-start | bytes 2359296 | tf_op jit(solution)/shard_map/all_gather | solution.py:275
  45.9 10.3 %collective-permute-start.1 = (bf16[8,256,128]{2,1,0:T(8,128)(2,1)S(1)}, bf16[8,256,128]{2,1,0:T(8,128)(2,1)S(1)}, u32[]{:S(2)}, u32[]{:S(2)}) collective-permute-start(bf16[8,256,128]{2,1,0:T(8,128)(2,1)S(1)} %get-tuple-element.12.refs_0_), channel_id=1, source_target_pairs={{0,1},{1,0},{2,3},{3,2},{4,5},{5,4},{6,7},{7,6},{8,9},{9,8},{10,11... | collective-permute-start | bytes 1572872 | tf_op jit(solution)/shard_map/ppermute | solution.py:282
  47.8 9.2 %collective-permute-start.2 = (bf16[8,256,128]{2,1,0:T(8,128)(2,1)S(1)}, bf16[8,256,128]{2,1,0:T(8,128)(2,1)S(1)}, u32[]{:S(2)}, u32[]{:S(2)}) collective-permute-start(bf16[8,256,128]{2,1,0:T(8,128)(2,1)S(1)} %get-tuple-element.13.refs_1_), channel_id=1, source_target_pairs={{0,1},{1,0},{2,3},{3,2},{4,5},{5,4},{6,7},{7,6},{8,9},{9,8},{10,11... | collective-permute-start | bytes 1572872 | tf_op jit(solution)/shard_map/ppermute | solution.py:283
  50.3 7.6 %collective-permute-start.5 = (bf16[8,256,128]{2,1,0:T(8,128)(2,1)S(1)}, bf16[8,256,128]{2,1,0:T(8,128)(2,1)S(1)}, u32[]{:S(2)}, u32[]{:S(2)}) collective-permute-start(bf16[8,256,128]{2,1,0:T(8,128)(2,1)S(1)} %collective-permute-done.3.refs_4_), channel_id=1, source_target_pairs={{0,1},{1,0},{2,3},{3,2},{4,5},{5,4},{6,7},{7,6},{8,9},{9,8},{10,11... | collective-permute-start | bytes 1572872 | tf_op jit(solution)/shard_map/ppermute | solution.py:286
  54.3 4.3 %collective-permute-start.6 = (bf16[8,256,128]{2,1,0:T(8,128)(2,1)S(1)}, bf16[8,256,128]{2,1,0:T(8,128)(2,1)S(1)}, u32[]{:S(2)}, u32[]{:S(2)}) collective-permute-start(bf16[8,256,128]{2,1,0:T(8,128)(2,1)S(1)} %collective-permute-done.4.refs_5_), channel_id=1, source_target_pairs={{0,1},{1,0},{2,3},{3,2},{4,5},{5,4},{6,7},{7,6},{8,9},{9,8},{10,11... | collective-permute-start | bytes 1572872 | tf_op jit(solution)/shard_map/ppermute | solution.py:287
  56.2 0.8 copy-start.7
  57.0 0.8 copy-start.9
  57.8 0.8 copy-start.11
  58.6 0.8 copy-start.13
  60.0 1.0 copy-start.8
  61.1 1.0 copy-start.10
  62.1 1.0 copy-start.12
  63.2 1.0 copy-start.14
  97.0 6.3 %collective-permute-start.7 = (bf16[16,8,64,128]{3,2,1,0:T(8,128)(2,1)}, bf16[16,8,64,128]{3,2,1,0:T(8,128)(2,1)S(1)}, u32[]{:S(2)}, u32[]{:S(2)}) collective-permute-start(bf16[16,8,64,128]{3,2,1,0:T(8,128)(2,1)} %all-gather.2.cloned.1.call-done.own_ref), channel_id=1, source_target_pairs={{0,1},{1,0},{2,3},{3,2},{4,5},{5,4},{6,7},{7,6},{8,9},{9,8},{10,11... | collective-permute-start | bytes 6291464 | tf_op jit(solution)/shard_map/ppermute | solution.py:323
  98.9 23.1 %all-to-all-start.2 = ((f16[8,2,136,128]{3,2,1,0:T(8,128)(2,1)}), f16[8,2,136,128]{3,2,1,0:T(8,128)(2,1)S(1)}, u32[]{:S(2)}, u32[]{:S(2)}) async-start(f16[8,2,136,128]{3,2,1,0:T(8,128)(2,1)} %bitcast.9), calls=%async_computation.2 | async-start | bytes 1114112 | tf_op jit(solution)/shard_map/all_to_all | solution.py:203
  103.3 1.3 copy-start.5
  104.6 1.6 %copy-start.4 = (bf16[16,8,64,128]{3,2,1,0:T(8,128)(2,1)S(1)}, bf16[16,8,64,128]{3,2,1,0:T(8,128)(2,1)}, u32[]{:S(2)}) copy-start(bf16[16,8,64,128]{3,2,1,0:T(8,128)(2,1)} %all-gather.2.cloned.1.call-done.own_ref) | copy-start | bytes 6291460
  106.2 1.6 %copy-start.6 = (bf16[16,8,64,128]{3,2,1,0:T(8,128)(2,1)S(1)}, bf16[16,8,64,128]{3,2,1,0:T(8,128)(2,1)}, u32[]{:S(2)}) copy-start(bf16[16,8,64,128]{3,2,1,0:T(8,128)(2,1)} %copy-done.5) | copy-start | bytes 6291460
  123.6 9.8 %copy-start = (bf16[1,512,8,128]{3,2,1,0:T(8,128)(2,1)S(1)}, bf16[1,512,8,128]{3,2,1,0:T(8,128)(2,1)}, u32[]{:S(2)}) copy-start(bf16[1,512,8,128]{3,2,1,0:T(8,128)(2,1)} %param.17) | copy-start | bytes 3145732
  123.6 9.8 %copy-start.1 = (bf16[1,512,8,128]{3,2,1,0:T(8,128)(2,1)S(1)}, bf16[1,512,8,128]{3,2,1,0:T(8,128)(2,1)}, u32[]{:S(2)}) copy-start(bf16[1,512,8,128]{3,2,1,0:T(8,128)(2,1)} %param.18) | copy-start | bytes 3145732
  123.7 9.8 %copy-start.2 = (bf16[1,2,8,128]{3,2,1,0:T(8,128)(2,1)S(1)}, bf16[1,2,8,128]{3,2,1,0:T(8,128)(2,1)}, u32[]{:S(2)}) copy-start(bf16[1,2,8,128]{3,2,1,0:T(8,128)(2,1)} %param.19) | copy-start | bytes 12292
  123.7 9.8 %copy-start.3 = (bf16[1,2,8,128]{3,2,1,0:T(8,128)(2,1)S(1)}, bf16[1,2,8,128]{3,2,1,0:T(8,128)(2,1)}, u32[]{:S(2)}) copy-start(bf16[1,2,8,128]{3,2,1,0:T(8,128)(2,1)} %param.20) | copy-start | bytes 12292
  124.6 25.4 %all-to-all-start.3 = ((f16[16,136,128]{2,1,0:T(8,128)(2,1)}), f16[16,136,128]{2,1,0:T(8,128)(2,1)S(1)}, u32[]{:S(2)}, u32[]{:S(2)}) async-start(f16[16,136,128]{2,1,0:T(8,128)(2,1)} %convert_element_type.18), calls=%async_computation.3 | async-start | bytes 1114112 | tf_op jit(solution)/shard_map/all_to_all | solution.py:203
Sparse Core Ops, SparseCore 0:
  48.0 48.9 all-gather.1

commit v3 on v2

--- a/solution.py
+++ b/solution.py
@@ -12,7 +12,6 @@
 PAD = 8
 LOW = -1e30
 EMPHASIS = 30
-VMEM_LIMIT = 20 * 1024 * 1024
 NT = (((1,), (1,)), ((), ()))
 
 
@@ -88,23 +87,34 @@
     out_ref[...] = jnp.broadcast_to(peer_ref[...][None], out_ref.shape)
 
 
-def branch_kernel(q_ref, *refs):
-    out_ref = refs[-1]
-    blocks = list(zip(refs[:-1:2], refs[1:-1:2]))
+def branch_kernel(count, q_ref, *refs):
+    sources, out_ref, held, sems = refs[:count], refs[count], refs[count + 1], refs[count + 2]
     slots, lanes, dim = q_ref.shape
-    heads = refs[0].shape[0]
+    heads = sources[0].shape[0]
     per_head = lanes // heads
+
+    def copies(head):
+        return [
+            pltpu.make_async_copy(ref.at[head], held.at[place, head], sems.at[place, head])
+            for place, ref in enumerate(sources)
+        ]
+
+    for head in range(heads):
+        for copy in copies(head):
+            copy.start()
     tail = jnp.zeros((slots, 1, lanes), jnp.float32)
     for head in range(heads):
+        for copy in copies(head):
+            copy.wait()
         place = slice(head * per_head, (head + 1) * per_head)
         q = q_ref[:, place, :].reshape(slots * per_head, dim)
         found = []
-        for k_ref, v_ref in blocks:
-            scores = scores_of(q, k_ref[head])
+        for block in range(0, count, 2):
+            scores = scores_of(q, held[block, head])
             high = jnp.max(scores, axis=1, keepdims=True)
             weights = jnp.exp(scores - high)
             den = jnp.sum(weights, axis=1, keepdims=True)
-            found.append((high, den, times_values(weights, v_ref[head])))
+            found.append((high, den, times_values(weights, held[block + 1, head])))
         high = functools.reduce(jnp.maximum, [f[0] for f in found])
         factors = [jnp.exp(f[0] - high) for f in found]
         den = sum(factor * f[1] for factor, f in zip(factors, found))
@@ -114,28 +124,37 @@
     out_ref[:, lanes:, :] = tail_rows(split_lse(tail))
 
 
-def root_kernel(q_ref, own_ref, twin_ref, out_ref):
+def root_kernel(count, q_ref, q_twin_ref, *refs):
+    sources, out_refs = refs[:count], refs[count : count + 2]
+    held, sems = refs[count + 2 :]
+    copies = [
+        pltpu.make_async_copy(ref, held.at[place], sems.at[place])
+        for place, ref in enumerate(sources)
+    ]
+    for copy in copies:
+        copy.start()
+    for copy in copies:
+        copy.wait()
     requests, lanes, dim = q_ref.shape
-    count, heads = own_ref.shape[:2]
+    pairs, heads, half = held.shape[1], held.shape[2], held.shape[3] // 2
     per_head = lanes // heads
-    half = own_ref.shape[2] // 2
-    tail = jnp.zeros((requests, 1, lanes), jnp.float32)
+    span = count * pairs * half
+    tails = [jnp.zeros((requests, 1, lanes), jnp.float32) for _ in out_refs]
     for head in range(heads):
         place = slice(head * per_head, (head + 1) * per_head)
-        q = q_ref[:, place, :].reshape(requests * per_head, dim)
-        blocks = [r[:, head, :, :] for r in (own_ref, twin_ref)]
-        keys = [block[:, :half, :].reshape(count * half, dim) for block in blocks]
-        values = [block[:, half:, :].reshape(count * half, dim) for block in blocks]
-        scores = [scores_of(q, k) for k in keys]
-        high = functools.reduce(
-            jnp.maximum, [jnp.max(s, axis=1, keepdims=True) for s in scores]
-        )
-        weights = [jnp.exp(s - high) for s in scores]
-        den = sum(jnp.sum(w, axis=1, keepdims=True) for w in weights)
-        num = sum(times_values(w, v) for w, v in zip(weights, values)) / den
-        out_ref[:, place, :] = num.reshape(requests, per_head, dim)
-        tail = tail + head_lse(high + jnp.log(den), head, per_head, lanes)
-    out_ref[:, lanes:, :] = tail_rows(split_lse(tail))
+        keys = held[:, :, head, :half, :].reshape(span, dim)
+        values = held[:, :, head, half:, :].reshape(span, dim)
+        for which, (rows_ref, out_ref) in enumerate(zip((q_ref, q_twin_ref), out_refs)):
+            q = rows_ref[:, place, :].reshape(requests * per_head, dim)
+            scores = scores_of(q, keys)
+            high = jnp.max(scores, axis=1, keepdims=True)
+            weights = jnp.exp(scores - high)
+            den = jnp.sum(weights, axis=1, keepdims=True)
+            num = times_values(weights, values) / den
+            out_ref[:, place, :] = num.reshape(requests, per_head, dim)
+            tails[which] = tails[which] + head_lse(high + jnp.log(den), head, per_head, lanes)
+    for out_ref, tail in zip(out_refs, tails):
+        out_ref[:, lanes:, :] = tail_rows(split_lse(tail))
 
 
 def columns(table):
@@ -144,9 +163,23 @@
     return jnp.concatenate([table, rest], axis=0).T
 
 
-def merge_kernel(idx_ref, part_ref, root_ref, out_ref):
+def merge_kernel(idx_ref, part_ref, own_ref, twin_ref, out_ref):
     sources, cap, _, lanes = part_ref.shape
-    out_ref[...] = root_ref[...]
+    groups = own_ref.shape[0]
+    lse_a = join_lse(own_ref[:, lanes:, :])
+    lse_b = join_lse(twin_ref[:, lanes:, :])
+    high = jnp.maximum(lse_a, lse_b)
+    factor_a = jnp.exp(lse_a - high)
+    factor_b = jnp.exp(lse_b - high)
+    total = factor_a + factor_b
+    table = columns(jnp.concatenate([factor_a / total, factor_b / total], axis=0))
+    pieces = split_lse(high + jnp.log(total))
+    for r in range(groups):
+        out_ref[r, :lanes, :] = (
+            own_ref[r, :lanes, :] * table[:, r : r + 1]
+            + twin_ref[r, :lanes, :] * table[:, groups + r : groups + r + 1]
+        )
+        out_ref[r, lanes:, :] = tail_rows([piece[r : r + 1] for piece in pieces])
     for k in range(cap):
         reader = idx_ref[k]
 
@@ -181,8 +214,8 @@
     out_ref[...] = out.astype(out_ref.dtype)
 
 
-def params():
-    return pltpu.CompilerParams(vmem_limit_bytes=VMEM_LIMIT)
+def params(megabytes=48):
+    return pltpu.CompilerParams(vmem_limit_bytes=megabytes * 1024 * 1024)
 
 
 def estimate(area, dim):
@@ -193,6 +226,10 @@
 
 def vmem():
     return pl.BlockSpec(memory_space=pltpu.VMEM)
+
+
+def hbm():
+    return pl.BlockSpec(memory_space=pltpu.HBM)
 
 
 def smem():
@@ -271,11 +308,27 @@
     values_own = branch_values[0].transpose(1, 0, 2)
     root_block = jnp.concatenate([root_keys, root_values], axis=0).transpose(1, 0, 2)
     root_far = lax.ppermute(root_block, "xhi", swap)
-    root_far, keys_own, values_own = lax.optimization_barrier((root_far, keys_own, values_own))
-    root_blocks = lax.all_gather(jnp.stack([root_block, root_far]), "z", axis=0, tiled=True)
+    up = [(i, (i + 1) % ring) for i in range(ring)]
+    down = [(b, a) for a, b in up]
+    pair = jnp.stack([root_block, root_far])
+    root_blocks = [pair]
+
+    def hop(ahead, behind):
+        ahead = lax.ppermute(ahead, "z", up)
+        root_blocks.append(ahead)
+        if len(root_blocks) < ring:
+            behind = lax.ppermute(behind, "z", down)
+            root_blocks.append(behind)
+        return ahead, behind
+
+    pair, keys_own, values_own = lax.optimization_barrier((pair, keys_own, values_own))
+    ahead, behind = hop(pair, pair)
     keys_far = lax.ppermute(keys_own, "xhi", swap)
     values_far = lax.ppermute(values_own, "xhi", swap)
+    peers, ahead, behind = lax.optimization_barrier((peers, ahead, behind))
     slots = gather_readers(peers)
+    while len(root_blocks) < ring:
+        ahead, behind = hop(ahead, behind)
     branch_blocks = [
         keys_own,
         values_own,
@@ -286,6 +339,7 @@
         lax.ppermute(keys_far, "core", swap),
         lax.ppermute(values_far, "core", swap),
     ]
+    peers_twin = lax.ppermute(peers, "core", swap)
 
     flat = suffix_keys.shape[1] * heads
     local = pl.pallas_call(
@@ -308,43 +362,50 @@
     )
 
     slots = slots.reshape(ring * CAP, rows, dim)
-    area = ring * CAP * rows * keys_own.shape[1] * 4
+    area = ring * CAP * rows * branch_keys.shape[1] * 4
+    count = len(branch_blocks)
     parts = pl.pallas_call(
-        branch_kernel,
+        functools.partial(branch_kernel, count),
         out_shape=jax.ShapeDtypeStruct((ring * CAP, rows + PAD, dim), jnp.float32),
-        in_specs=[vmem()] * (1 + len(branch_blocks)),
+        in_specs=[vmem()] + [hbm()] * count,
         out_specs=vmem(),
-        compiler_params=params(),
+        scratch_shapes=[
+            pltpu.VMEM((count,) + keys_own.shape, jnp.bfloat16),
+            pltpu.SemaphoreType.DMA((count, heads)),
+        ],
+        compiler_params=params(58),
         cost_estimate=estimate(area, dim),
         name="branch_attention",
     )(slots, *branch_blocks)
     parts = parts.astype(jnp.float16).reshape(ring, CAP, rows + PAD, dim)
-    root_blocks, peers, _ = lax.optimization_barrier((root_blocks, peers, parts))
-    root_twin = lax.ppermute(root_blocks, "core", swap)
+    peers, _ = lax.optimization_barrier((peers, parts))
     parts = exchange(parts, "z")
 
-    area = grp * rows * root_keys.shape[0] * 4 * ring
     whole = jax.ShapeDtypeStruct((grp, rows + PAD, dim), jnp.float32)
-    root = pl.pallas_call(
-        root_kernel,
-        out_shape=whole,
-        in_specs=[vmem()] * 3,
-        out_specs=vmem(),
-        compiler_params=params(),
+    root_own, root_twin = pl.pallas_call(
+        functools.partial(root_kernel, ring),
+        out_shape=(whole, whole),
+        in_specs=[vmem()] * 2 + [hbm()] * ring,
+        out_specs=(vmem(), vmem()),
+        scratch_shapes=[
+            pltpu.VMEM((ring,) + pair.shape, jnp.bfloat16),
+            pltpu.SemaphoreType.DMA((ring,)),
+        ],
+        compiler_params=params(58),
         cost_estimate=estimate(area, dim),
         name="root_attention",
-    )(peers, root_blocks, root_twin)
-
-    parts, root = lax.optimization_barrier((parts, root))
+    )(peers, peers_twin, *root_blocks)
+    root_twin = lax.ppermute(root_twin.astype(jnp.float16), "core", swap).astype(jnp.float32)
+    parts, root_own, root_twin = lax.optimization_barrier((parts, root_own, root_twin))
     parts = parts.astype(jnp.float32)
     merged = pl.pallas_call(
         merge_kernel,
         out_shape=whole,
-        in_specs=[smem()] + [vmem()] * 2,
+        in_specs=[smem()] + [vmem()] * 3,
         out_specs=vmem(),
         compiler_params=params(),
         name="merge_parts",
-    )(readers, parts, root)
+    )(readers, parts, root_own, root_twin)
     back = exchange(merged.astype(jnp.float16), "grp").astype(jnp.float32)
     mine = pl.pallas_call(
         final_kernel,

time: 160 us -> 148 us (0.925)
  waiting for transfers between devices: 59.6 us -> 26.9 us
  starting transfers between devices: 52.3 us -> 81.1 us
  between operations: 14.3 us -> 1.29 us
  Pallas kernels: 14.1 us -> 25.1 us
  local copies, waits for them, and re-layouts: 14.6 us -> 6.53 us
  other arithmetic: 3.2 us -> 5.12 us
    ppermute x1 -> x9, starting transfers between devices: 1.91 us -> 32.8 us  [the longest x3 17.1 us: hop(): behind = lax.ppermute(behind, 'z', down)]
    all_gather x1 -> x0, waiting for transfers between devices: 27.1 us -> none  [shards(): lax.all_gather(jnp.stack([root_block, root_far]), 'z', axis=0, tiled=True)]
    all_to_all x4, waiting for transfers between devices: 25.6 us -> 14.2 us  [exchange(): return lax.all_to_all(blocks, axis, split_axis=0, concat_axis=0, tiled=True)]
    pallas_call x2, Pallas kernels: 9.08 us -> 19.5 us  [the longest x1 9.79 us: shards(): pl.pallas_call(functools.partial(root_kernel, ring), out_shape=(whole, wh...]
    unnamed x43 -> x57, local copies, waits for them, and re-layouts: 11.9 us -> 3.84 us
    ppermute x1 -> x9, waiting for transfers between devices: 0.18 us -> 4.92 us  [the longest x3 2.98 us: hop(): behind = lax.ppermute(behind, 'z', down)]
    all_to_all x4, starting transfers between devices: 30.8 us -> 28.8 us  [exchange(): return lax.all_to_all(blocks, axis, split_axis=0, concat_axis=0, tiled=True)]
  transfers between devices with their start and end apart: 13 -> 20, of which waited for: 7 -> 6; matrix products, arithmetic and copies ran while one was open for 2% -> 3% of each run, Pallas kernels for 8% -> 15%
where the time goes in v3:
time: 148 us; the launch traced here: 146 us
  starting transfers between devices  81.1 us (55%)
  waiting for transfers between devices  26.9 us (18%)
  Pallas kernels  25.1 us (17%)
  local copies, waits for them, and re-layouts  6.53 us (4%)
  other arithmetic  5.12 us (3%)
    all_to_all x4, starting transfers between devices, exchange(): return lax.all_to_all(blocks, axis, split_axis=0, concat_axis=0, tiled=True)  28.8 us
    ppermute x3, starting transfers between devices, hop(): behind = lax.ppermute(behind, 'z', down)  17.1 us
    all_to_all x4, waiting for transfers between devices, exchange(): return lax.all_to_all(blocks, axis, split_axis=0, concat_axis=0, tiled=True)  14.2 us
    ppermute x4, starting transfers between devices, hop(): ahead = lax.ppermute(ahead, 'z', up)  11.9 us
    pallas_call x1, Pallas kernels, shards(): pl.pallas_call(functools.partial(root_kernel, ring), out_shape=(whole, wh...  9.79 us
    pallas_call x1, Pallas kernels, shards(): pl.pallas_call(functools.partial(branch_kernel, count), out_shape=jax.Sha...  9.68 us
    ppermute x1, waiting for transfers between devices, shards(): root_far = lax.ppermute(root_block, 'xhi', swap)  5.21 us
    ppermute x1, starting transfers between devices, shards(): values_far = lax.ppermute(values_own, 'xhi', swap)  4.31 us
  transfers between devices with their start and end apart: 20, of which 6 were waited for; matrix products, arithmetic and copies ran while one was open for 3% of the time, Pallas kernels for 15%

profile of v3, /device:TPU:6, one launch (start us, length us, event | category | flops | bytes accessed | tf_op | source)
XLA Modules:
  0.0 146.1 jit_solution(15190189158301671164)
XLA Ops:
  0.0 0.9 copy.31
  0.9 0.9 broadcast_in_dim.46
  1.8 8.6 %all-to-all-start = ((bf16[16,128,128]{2,1,0:T(8,128)(2,1)}), bf16[16,128,128]{2,1,0:T(8,128)(2,1)S(1)}, u32[]{:S(2)}, u32[]{:S(2)}) async-start(bf16[16,128,128]{2,1,0:T(8,128)(2,1)} %broadcast_in_dim.46), calls=%async_computation | async-start | bytes 1048576 | tf_op jit(solution)/shard_map/all_to_all | solution.py:240
  10.4 0.0 copy-start.14
  10.4 0.0 copy-start.15
  10.5 4.0 %collective-permute-start = (bf16[8,64,128]{2,1,0:T(8,128)(2,1)S(1)}, bf16[8,64,128]{2,1,0:T(8,128)(2,1)S(1)}, u32[]{:S(2)}, u32[]{:S(2)}) collective-permute-start(bf16[8,64,128]{2,1,0:T(8,128)(2,1)S(1)} %bitcast.36), channel_id=1, source_target_pairs={{0,16},{16,0},{1,17},{17,1},{2,18},{18,2},{3,19},{19,3},{4,20},{20... | collective-permute-start | bytes 393224 | tf_op jit(solution)/shard_map/ppermute | solution.py:310
  14.5 0.2 copy_bitcast_fusion
  14.7 5.2 %collective-permute-done = bf16[8,64,128]{2,1,0:T(8,128)(2,1)S(1)} collective-permute-done((bf16[8,64,128]{2,1,0:T(8,128)(2,1)S(1)}, bf16[8,64,128]{2,1,0:T(8,128)(2,1)S(1)}, u32[]{:S(2)}, u32[]{:S(2)}) %collective-permute-start) | collective-permute-done | bytes 131104 | tf_op jit(solution)/shard_map/ppermute | solution.py:310
  20.0 3.9 %collective-permute-start.1 = (bf16[2,8,64,128]{3,2,1,0:T(8,128)(2,1)S(1)}, bf16[2,8,64,128]{3,2,1,0:T(8,128)(2,1)S(1)}, u32[]{:S(2)}, u32[]{:S(2)}) collective-permute-start(bf16[2,8,64,128]{3,2,1,0:T(8,128)(2,1)S(1)} %pad_maximum_fusion.refs_0_), channel_id=1, source_target_pairs={{0,2},{2,4},{4,6},{6,8},{8,10},{10,12},{12,14},{14,0},{1,3},{3,5},... | collective-permute-start | bytes 786440 | tf_op jit(solution)/shard_map/ppermute | solution.py:317
  23.9 8.6 %collective-permute-start.2 = (bf16[2,8,64,128]{3,2,1,0:T(8,128)(2,1)S(1)}, bf16[2,8,64,128]{3,2,1,0:T(8,128)(2,1)S(1)}, u32[]{:S(2)}, u32[]{:S(2)}) collective-permute-start(bf16[2,8,64,128]{3,2,1,0:T(8,128)(2,1)S(1)} %pad_maximum_fusion.refs_0_), channel_id=1, source_target_pairs={{2,0},{4,2},{6,4},{8,6},{10,8},{12,10},{14,12},{0,14},{3,1},{5,3},... | collective-permute-start | bytes 786440 | tf_op jit(solution)/shard_map/ppermute | solution.py:320
  32.5 0.1 select_reduce_fusion
  32.6 0.1 reshape.39
  32.6 0.2 fusion
  32.8 0.1 convert_reduce_fusion
  32.9 0.1 fusion.2.idx_ref
  33.1 3.0 %collective-permute-start.5 = (bf16[8,256,128]{2,1,0:T(8,128)(2,1)S(1)}, bf16[8,256,128]{2,1,0:T(8,128)(2,1)S(1)}, u32[]{:S(2)}, u32[]{:S(2)}) collective-permute-start(bf16[8,256,128]{2,1,0:T(8,128)(2,1)S(1)} %get-tuple-element.19.refs_0_), channel_id=1, source_target_pairs={{0,16},{16,0},{1,17},{17,1},{2,18},{18,2},{3,19},{19,3},{4,20},{20... | collective-permute-start | bytes 1572872 | tf_op jit(solution)/shard_map/ppermute | solution.py:326
  36.1 4.3 %collective-permute-start.6 = (bf16[8,256,128]{2,1,0:T(8,128)(2,1)S(1)}, bf16[8,256,128]{2,1,0:T(8,128)(2,1)}, u32[]{:S(2)}, u32[]{:S(2)}) collective-permute-start(bf16[8,256,128]{2,1,0:T(8,128)(2,1)S(1)} %get-tuple-element.20.refs_1_), channel_id=1, source_target_pairs={{0,16},{16,0},{1,17},{17,1},{2,18},{18,2},{3,19},{19,3},{4,20},{20... | collective-permute-start | bytes 1572872 | tf_op jit(solution)/shard_map/ppermute | solution.py:327
  40.4 0.0 collective-permute-done.1.refs_1_
  40.5 1.4 pick_readers.1
  41.9 4.5 %all-to-all-start.1 = ((bf16[8,2,128,128]{3,2,1,0:T(8,128)(2,1)}), bf16[8,2,128,128]{3,2,1,0:T(8,128)(2,1)S(1)}, u32[]{:S(2)}, u32[]{:S(2)}) async-start(bf16[8,2,128,128]{3,2,1,0:T(8,128)(2,1)} %pick_readers.1), calls=%async_computation.1 | async-start | bytes 1048576 | tf_op jit(solution)/shard_map/all_to_all | solution.py:240
  46.4 1.9 %collective-permute-start.3 = (bf16[8,256,128]{2,1,0:T(8,128)(2,1)S(1)}, bf16[8,256,128]{2,1,0:T(8,128)(2,1)S(1)}, u32[]{:S(2)}, u32[]{:S(2)}) collective-permute-start(bf16[8,256,128]{2,1,0:T(8,128)(2,1)S(1)} %get-tuple-element.19.refs_0_), channel_id=1, source_target_pairs={{0,1},{1,0},{2,3},{3,2},{4,5},{5,4},{6,7},{7,6},{8,9},{9,8},{10,11... | collective-permute-start | bytes 1572872 | tf_op jit(solution)/shard_map/ppermute | solution.py:335
  48.3 2.4 %collective-permute-start.4 = (bf16[8,256,128]{2,1,0:T(8,128)(2,1)S(1)}, bf16[8,256,128]{2,1,0:T(8,128)(2,1)S(1)}, u32[]{:S(2)}, u32[]{:S(2)}) collective-permute-start(bf16[8,256,128]{2,1,0:T(8,128)(2,1)S(1)} %get-tuple-element.20.refs_1_), channel_id=1, source_target_pairs={{0,1},{1,0},{2,3},{3,2},{4,5},{5,4},{6,7},{7,6},{8,9},{9,8},{10,11... | collective-permute-start | bytes 1572872 | tf_op jit(solution)/shard_map/ppermute | solution.py:336
  50.8 3.9 %collective-permute-start.10 = (bf16[2,8,64,128]{3,2,1,0:T(8,128)(2,1)S(1)}, bf16[2,8,64,128]{3,2,1,0:T(8,128)(2,1)S(1)}, u32[]{:S(2)}, u32[]{:S(2)}) collective-permute-start(bf16[2,8,64,128]{3,2,1,0:T(8,128)(2,1)S(1)} %collective-permute-done.1.refs_1_), channel_id=1, source_target_pairs={{0,2},{2,4},{4,6},{6,8},{8,10},{10,12},{12,14},{14,0},{1,3},{3,5},... | collective-permute-start | bytes 786440 | tf_op jit(solution)/shard_map/ppermute | solution.py:317
  54.7 0.0 collective-permute-done.5.refs_4_
  54.7 1.9 %collective-permute-start.7 = (bf16[8,256,128]{2,1,0:T(8,128)(2,1)S(1)}, bf16[8,256,128]{2,1,0:T(8,128)(2,1)S(1)}, u32[]{:S(2)}, u32[]{:S(2)}) collective-permute-start(bf16[8,256,128]{2,1,0:T(8,128)(2,1)S(1)} %collective-permute-done.5.refs_4_), channel_id=1, source_target_pairs={{0,1},{1,0},{2,3},{3,2},{4,5},{5,4},{6,7},{7,6},{8,9},{9,8},{10,11... | collective-permute-start | bytes 1572872 | tf_op jit(solution)/shard_map/ppermute | solution.py:339
  56.6 2.5 %collective-permute-done.6.refs_5_ = bf16[8,256,128]{2,1,0:T(8,128)(2,1)} collective-permute-done((bf16[8,256,128]{2,1,0:T(8,128)(2,1)S(1)}, bf16[8,256,128]{2,1,0:T(8,128)(2,1)}, u32[]{:S(2)}, u32[]{:S(2)}) %collective-permute-start.6) | collective-permute-done | bytes 524320 | tf_op jit(solution)/shard_map/ppermute | solution.py:327
  59.2 1.9 %collective-permute-start.8 = (bf16[8,256,128]{2,1,0:T(8,128)(2,1)}, bf16[8,256,128]{2,1,0:T(8,128)(2,1)}, u32[]{:S(2)}, u32[]{:S(2)}) collective-permute-start(bf16[8,256,128]{2,1,0:T(8,128)(2,1)} %collective-permute-done.6.refs_5_), channel_id=1, source_target_pairs={{0,1},{1,0},{2,3},{3,2},{4,5},{5,4},{6,7},{7,6},{8,9},{9,8},{10,11... | collective-permute-start | bytes 1572872 | tf_op jit(solution)/shard_map/ppermute | solution.py:340
  61.1 3.6 %collective-permute-start.11 = (bf16[2,8,64,128]{3,2,1,0:T(8,128)(2,1)}, bf16[2,8,64,128]{3,2,1,0:T(8,128)(2,1)S(1)}, u32[]{:S(2)}, u32[]{:S(2)}) collective-permute-start(bf16[2,8,64,128]{3,2,1,0:T(8,128)(2,1)} %copy-done.22), channel_id=1, source_target_pairs={{2,0},{4,2},{6,4},{8,6},{10,8},{12,10},{14,12},{0,14},{3,1},{5,3},... | collective-permute-start | bytes 786440 | tf_op jit(solution)/shard_map/ppermute | solution.py:320
  64.8 2.2 %collective-permute-start.12 = (bf16[2,8,64,128]{3,2,1,0:T(8,128)(2,1)S(1)}, bf16[2,8,64,128]{3,2,1,0:T(8,128)(2,1)S(1)}, u32[]{:S(2)}, u32[]{:S(2)}) collective-permute-start(bf16[2,8,64,128]{3,2,1,0:T(8,128)(2,1)S(1)} %collective-permute-done.10.refs_3_), channel_id=1, source_target_pairs={{0,2},{2,4},{4,6},{6,8},{8,10},{10,12},{12,14},{14,0},{1,3},{3,5},... | collective-permute-start | bytes 786440 | tf_op jit(solution)/shard_map/ppermute | solution.py:317
  67.0 0.0 collective-permute-done.4.refs_3_
  67.0 1.9 %collective-permute-start.9 = (bf16[16,128,128]{2,1,0:T(8,128)(2,1)S(1)}, bf16[16,128,128]{2,1,0:T(8,128)(2,1)S(1)}, u32[]{:S(2)}, u32[]{:S(2)}) collective-permute-start(bf16[16,128,128]{2,1,0:T(8,128)(2,1)S(1)} %all-to-all-done.peer_ref.q_ref), channel_id=1, source_target_pairs={{0,1},{1,0},{2,3},{3,2},{4,5},{5,4},{6,7},{7,6},{8,9},{9,8},{10,11... | collective-permute-start | bytes 1572872 | tf_op jit(solution)/shard_map/ppermute | solution.py:342
  69.0 3.0 %collective-permute-done.11.refs_4_ = bf16[2,8,64,128]{3,2,1,0:T(8,128)(2,1)S(1)} collective-permute-done((bf16[2,8,64,128]{3,2,1,0:T(8,128)(2,1)}, bf16[2,8,64,128]{3,2,1,0:T(8,128)(2,1)S(1)}, u32[]{:S(2)}, u32[]{:S(2)}) %collective-permute-start.11) | collective-permute-done | bytes 262176 | tf_op jit(solution)/shard_map/ppermute | solution.py:320
  71.9 4.8 %collective-permute-start.13 = (bf16[2,8,64,128]{3,2,1,0:T(8,128)(2,1)S(1)}, bf16[2,8,64,128]{3,2,1,0:T(8,128)(2,1)S(1)}, u32[]{:S(2)}, u32[]{:S(2)}) collective-permute-start(bf16[2,8,64,128]{3,2,1,0:T(8,128)(2,1)S(1)} %collective-permute-done.11.refs_4_), channel_id=1, source_target_pairs={{2,0},{4,2},{6,4},{8,6},{10,8},{12,10},{14,12},{0,14},{3,1},{5,3},... | collective-permute-start | bytes 786440 | tf_op jit(solution)/shard_map/ppermute | solution.py:320
  76.8 1.9 %collective-permute-start.14 = (bf16[2,8,64,128]{3,2,1,0:T(8,128)(2,1)S(1)}, bf16[2,8,64,128]{3,2,1,0:T(8,128)(2,1)S(1)}, u32[]{:S(2)}, u32[]{:S(2)}) collective-permute-start(bf16[2,8,64,128]{3,2,1,0:T(8,128)(2,1)S(1)} %collective-permute-done.12.refs_5_), channel_id=1, source_target_pairs={{0,2},{2,4},{4,6},{6,8},{8,10},{10,12},{12,14},{14,0},{1,3},{3,5},... | collective-permute-start | bytes 786440 | tf_op jit(solution)/shard_map/ppermute | solution.py:317
  78.7 0.0 collective-permute-done.7.refs_6_
  78.8 0.8 copy-done.19
  79.6 0.8 copy-done.6
  80.4 9.7 %branch_attention.1 = f32[16,136,128]{2,1,0:T(8,128)} custom-call(bf16[16,128,128]{2,1,0:T(8,128)(2,1)} %bitcast.35, bf16[8,256,128]{2,1,0:T(8,128)(2,1)} %copy-done.10, bf16[8,256,128]{2,1,0:T(8,128)(2,1)} %copy-done.9, bf16[8,256,128]{2,1,0:T(8,128)(2,1)} %copy-done.17, bf16[8,256,128]{2,1,0:T(8,128)(2,1)} %copy-done.18, bf16[8,256,128]{2,1,0:T(8,128)(2,1)} %copy-done.16, ...), custom_call_target="tpu_custom_call" | custom-call | flops 32212254720 | bytes 6291456 | tf_op jit(solution)/shard_map/branch_attention/pallas_call | solution.py:367
  90.1 2.1 %convert_element_type.22 = f16[16,136,128]{2,1,0:T(8,128)(2,1)} convert(f32[16,136,128]{2,1,0:T(8,128)} %branch_attention.1) | non-fusion elementwise | flops 278528 | bytes 1671168 | tf_op jit(solution)/shard_map/convert_element_type | solution.py:380
  92.3 4.7 %all-to-all-start.2 = ((f16[8,2,136,128]{3,2,1,0:T(8,128)(2,1)}), f16[8,2,136,128]{3,2,1,0:T(8,128)(2,1)S(1)}, u32[]{:S(2)}, u32[]{:S(2)}) async-start(f16[8,2,136,128]{3,2,1,0:T(8,128)(2,1)} %bitcast.11), calls=%async_computation.2 | async-start | bytes 1114112 | tf_op jit(solution)/shard_map/all_to_all | solution.py:240
  97.0 0.0 collective-permute-done.13.refs_6_
  97.0 0.8 copy-done.20
  97.8 0.1 copy-done.26
  97.9 0.7 copy-done.27
  98.6 9.8 %root_attention.1 = (f32[16,136,128]{2,1,0:T(8,128)}, f32[16,136,128]{2,1,0:T(8,128)}) custom-call(bf16[16,128,128]{2,1,0:T(8,128)(2,1)} %copy-done.3, bf16[16,128,128]{2,1,0:T(8,128)(2,1)} %copy-done.20, bf16[2,8,64,128]{3,2,1,0:T(8,128)(2,1)} %copy-done.11, bf16[2,8,64,128]{3,2,1,0:T(8,128)(2,1)} %copy-done.21, bf16[2,8,64,128]{3,2,1,0:T(8,128)(2,1)} %copy-done.22, ...), custom_call_target="tpu_custom_call" | custom-call | flops 32212254720 | bytes 6291456 | tf_op jit(solution)/shard_map/root_attention/pallas_call | solution.py:385
  108.4 1.3 convert_element_type.23
  109.7 1.9 %collective-permute-start.15 = (f16[16,136,128]{2,1,0:T(8,128)(2,1)S(1)}, f16[16,136,128]{2,1,0:T(8,128)(2,1)S(1)}, u32[]{:S(2)}, u32[]{:S(2)}) collective-permute-start(f16[16,136,128]{2,1,0:T(8,128)(2,1)S(1)} %convert_element_type.23), channel_id=1, source_target_pairs={{0,1},{1,0},{2,3},{3,2},{4,5},{5,4},{6,7},{7,6},{8,9},{9,8},{10,11... | collective-permute-start | bytes 1671176 | tf_op jit(solution)/shard_map/ppermute | solution.py:398
  111.7 1.9 %collective-permute-done.15 = f16[16,136,128]{2,1,0:T(8,128)(2,1)S(1)} collective-permute-done((f16[16,136,128]{2,1,0:T(8,128)(2,1)S(1)}, f16[16,136,128]{2,1,0:T(8,128)(2,1)S(1)}, u32[]{:S(2)}, u32[]{:S(2)}) %collective-permute-start.15) | collective-permute-done | bytes 557088 | tf_op jit(solution)/shard_map/ppermute | solution.py:398
  113.6 0.1 convert_element_type.24.twin_ref
  113.7 0.6 all-to-all-done.2
  114.3 0.1 convert_element_type.25.part_ref
  114.4 0.5 copy-done
  114.9 2.2 %merge_parts.1 = f32[16,136,128]{2,1,0:T(8,128)S(1)} custom-call(s32[2]{0:T(128)S(1)} %fusion.2.idx_ref, f32[8,2,136,128]{3,2,1,0:T(8,128)S(1)} %convert_element_type.25.part_ref, f32[16,136,128]{2,1,0:T(8,128)S(1)} %copy-done, f32[16,136,128]{2,1,0:T(8,128)S(1)} %convert_element_type.24.twin_ref), custom_call_target="tpu_custom_call" | custom-call | tf_op jit(solution)/shard_map/merge_parts/pallas_call | solution.py:401
  117.1 0.0 copy-start.1
  117.1 0.0 copy-start.2
  117.1 0.0 copy-start.4
  117.1 0.0 copy-start.5
  117.1 0.9 convert_element_type.26
  118.0 11.0 %all-to-all-start.3 = ((f16[16,136,128]{2,1,0:T(8,128)(2,1)}), f16[16,136,128]{2,1,0:T(8,128)(2,1)S(1)}, u32[]{:S(2)}, u32[]{:S(2)}) async-start(f16[16,136,128]{2,1,0:T(8,128)(2,1)} %convert_element_type.26), calls=%async_computation.3 | async-start | bytes 1114112 | tf_op jit(solution)/shard_map/all_to_all | solution.py:240
  129.7 1.5 local_attention.1.local_ref
  131.2 13.6 %all-to-all-done.3 = f16[16,136,128]{2,1,0:T(8,128)(2,1)S(1)} async-done(((f16[16,136,128]{2,1,0:T(8,128)(2,1)}), f16[16,136,128]{2,1,0:T(8,128)(2,1)S(1)}, u32[]{:S(2)}, u32[]{:S(2)}) %all-to-all-start.3) | async-done | bytes 557088 | tf_op jit(solution)/shard_map/all_to_all | solution.py:240
  144.8 0.1 convert_element_type.27.part_ref
  144.9 0.5 final_merge.1
  145.4 0.6 copy.42
  (56 shorter events, 0.2 us)
Async XLA Ops:
  0.0 10.4 %copy-start.12 = (bf16[32,8,128]{2,1,0:T(8,128)(2,1)S(1)}, bf16[32,8,128]{2,1,0:T(8,128)(2,1)}, u32[]{:S(2)}) copy-start(bf16[32,8,128]{2,1,0:T(8,128)(2,1)} %param.13) | copy-start | bytes 196612
  0.0 10.4 %copy-start.13 = (bf16[32,8,128]{2,1,0:T(8,128)(2,1)S(1)}, bf16[32,8,128]{2,1,0:T(8,128)(2,1)}, u32[]{:S(2)}) copy-start(bf16[32,8,128]{2,1,0:T(8,128)(2,1)} %param.14) | copy-start | bytes 196612
  0.0 14.5 %copy-start.8 = (bf16[1,256,8,128]{3,2,1,0:T(8,128)(2,1)S(1)}, bf16[1,256,8,128]{3,2,1,0:T(8,128)(2,1)}, u32[]{:S(2)}) copy-start(bf16[1,256,8,128]{3,2,1,0:T(8,128)(2,1)} %param.15) | copy-start | bytes 1572868
  0.0 14.5 %copy-start.7 = (bf16[1,256,8,128]{3,2,1,0:T(8,128)(2,1)S(1)}, bf16[1,256,8,128]{3,2,1,0:T(8,128)(2,1)}, u32[]{:S(2)}) copy-start(bf16[1,256,8,128]{3,2,1,0:T(8,128)(2,1)} %param.16) | copy-start | bytes 1572868
  1.8 38.7 %all-to-all-start = ((bf16[16,128,128]{2,1,0:T(8,128)(2,1)}), bf16[16,128,128]{2,1,0:T(8,128)(2,1)S(1)}, u32[]{:S(2)}, u32[]{:S(2)}) async-start(bf16[16,128,128]{2,1,0:T(8,128)(2,1)} %broadcast_in_dim.46), calls=%async_computation | async-start | bytes 1048576 | tf_op jit(solution)/shard_map/all_to_all | solution.py:240
  10.4 22.0 %copy-start.14 = (s32[512]{0:T(512)S(1)}, s32[512]{0:T(512)}, u32[]{:S(2)}) copy-start(s32[512]{0:T(512)} %param.21) | copy-start | bytes 6148
  10.4 22.0 %copy-start.15 = (s32[16]{0:T(128)S(1)}, s32[16]{0:T(128)}, u32[]{:S(2)}) copy-start(s32[16]{0:T(128)} %param.22) | copy-start | bytes 196
  10.5 9.5 %collective-permute-start = (bf16[8,64,128]{2,1,0:T(8,128)(2,1)S(1)}, bf16[8,64,128]{2,1,0:T(8,128)(2,1)S(1)}, u32[]{:S(2)}, u32[]{:S(2)}) collective-permute-start(bf16[8,64,128]{2,1,0:T(8,128)(2,1)S(1)} %bitcast.36), channel_id=1, source_target_pairs={{0,16},{16,0},{1,17},{17,1},{2,18},{18,2},{3,19},{19,3},{4,20},{20... | collective-permute-start | bytes 393224 | tf_op jit(solution)/shard_map/ppermute | solution.py:310
  14.7 31.7 %copy-start.10 = (bf16[8,256,128]{2,1,0:T(8,128)(2,1)}, bf16[8,256,128]{2,1,0:T(8,128)(2,1)S(1)}, u32[]{:S(2)}) copy-start(bf16[8,256,128]{2,1,0:T(8,128)(2,1)S(1)} %get-tuple-element.19.refs_0_) | copy-start | bytes 1572868
  14.7 33.6 %copy-start.9 = (bf16[8,256,128]{2,1,0:T(8,128)(2,1)}, bf16[8,256,128]{2,1,0:T(8,128)(2,1)S(1)}, u32[]{:S(2)}) copy-start(bf16[8,256,128]{2,1,0:T(8,128)(2,1)S(1)} %get-tuple-element.20.refs_1_) | copy-start | bytes 1572868
  19.9 22.0 %copy-start.11 = (bf16[2,8,64,128]{3,2,1,0:T(8,128)(2,1)}, bf16[2,8,64,128]{3,2,1,0:T(8,128)(2,1)S(1)}, u32[]{:S(2)}) copy-start(bf16[2,8,64,128]{3,2,1,0:T(8,128)(2,1)S(1)} %pad_maximum_fusion.refs_0_) | copy-start | bytes 786436
  20.0 20.5 %collective-permute-start.1 = (bf16[2,8,64,128]{3,2,1,0:T(8,128)(2,1)S(1)}, bf16[2,8,64,128]{3,2,1,0:T(8,128)(2,1)S(1)}, u32[]{:S(2)}, u32[]{:S(2)}) collective-permute-start(bf16[2,8,64,128]{3,2,1,0:T(8,128)(2,1)S(1)} %pad_maximum_fusion.refs_0_), channel_id=1, source_target_pairs={{0,2},{2,4},{4,6},{6,8},{8,10},{10,12},{12,14},{14,0},{1,3},{3,5},... | collective-permute-start | bytes 786440 | tf_op jit(solution)/shard_map/ppermute | solution.py:317
  23.9 16.6 %collective-permute-start.2 = (bf16[2,8,64,128]{3,2,1,0:T(8,128)(2,1)S(1)}, bf16[2,8,64,128]{3,2,1,0:T(8,128)(2,1)S(1)}, u32[]{:S(2)}, u32[]{:S(2)}) collective-permute-start(bf16[2,8,64,128]{3,2,1,0:T(8,128)(2,1)S(1)} %pad_maximum_fusion.refs_0_), channel_id=1, source_target_pairs={{2,0},{4,2},{6,4},{8,6},{10,8},{12,10},{14,12},{0,14},{3,1},{5,3},... | collective-permute-start | bytes 786440 | tf_op jit(solution)/shard_map/ppermute | solution.py:320
  33.1 21.6 %collective-permute-start.5 = (bf16[8,256,128]{2,1,0:T(8,128)(2,1)S(1)}, bf16[8,256,128]{2,1,0:T(8,128)(2,1)S(1)}, u32[]{:S(2)}, u32[]{:S(2)}) collective-permute-start(bf16[8,256,128]{2,1,0:T(8,128)(2,1)S(1)} %get-tuple-element.19.refs_0_), channel_id=1, source_target_pairs={{0,16},{16,0},{1,17},{17,1},{2,18},{18,2},{3,19},{19,3},{4,20},{20... | collective-permute-start | bytes 1572872 | tf_op jit(solution)/shard_map/ppermute | solution.py:326
  36.1 23.1 %collective-permute-start.6 = (bf16[8,256,128]{2,1,0:T(8,128)(2,1)S(1)}, bf16[8,256,128]{2,1,0:T(8,128)(2,1)}, u32[]{:S(2)}, u32[]{:S(2)}) collective-permute-start(bf16[8,256,128]{2,1,0:T(8,128)(2,1)S(1)} %get-tuple-element.20.refs_1_), channel_id=1, source_target_pairs={{0,16},{16,0},{1,17},{17,1},{2,18},{18,2},{3,19},{19,3},{4,20},{20... | collective-permute-start | bytes 1572872 | tf_op jit(solution)/shard_map/ppermute | solution.py:327
  40.4 10.3 %copy-start.21 = (bf16[2,8,64,128]{3,2,1,0:T(8,128)(2,1)}, bf16[2,8,64,128]{3,2,1,0:T(8,128)(2,1)S(1)}, u32[]{:S(2)}) copy-start(bf16[2,8,64,128]{3,2,1,0:T(8,128)(2,1)S(1)} %collective-permute-done.1.refs_1_) | copy-start | bytes 786436
  40.5 1.5 %copy-start.22 = (bf16[2,8,64,128]{3,2,1,0:T(8,128)(2,1)}, bf16[2,8,64,128]{3,2,1,0:T(8,128)(2,1)S(1)}, u32[]{:S(2)}) copy-start(bf16[2,8,64,128]{3,2,1,0:T(8,128)(2,1)S(1)} %collective-permute-done.2.refs_2_) | copy-start | bytes 786436
  40.5 26.5 %copy-start.3 = (bf16[16,128,128]{2,1,0:T(8,128)(2,1)}, bf16[16,128,128]{2,1,0:T(8,128)(2,1)S(1)}, u32[]{:S(2)}) copy-start(bf16[16,128,128]{2,1,0:T(8,128)(2,1)S(1)} %all-to-all-done.peer_ref.q_ref) | copy-start | bytes 1572868
  41.9 37.6 %all-to-all-start.1 = ((bf16[8,2,128,128]{3,2,1,0:T(8,128)(2,1)}), bf16[8,2,128,128]{3,2,1,0:T(8,128)(2,1)S(1)}, u32[]{:S(2)}, u32[]{:S(2)}) async-start(bf16[8,2,128,128]{3,2,1,0:T(8,128)(2,1)} %pick_readers.1), calls=%async_computation.1 | async-start | bytes 1048576 | tf_op jit(solution)/shard_map/all_to_all | solution.py:240
  46.4 14.7 %collective-permute-start.3 = (bf16[8,256,128]{2,1,0:T(8,128)(2,1)S(1)}, bf16[8,256,128]{2,1,0:T(8,128)(2,1)S(1)}, u32[]{:S(2)}, u32[]{:S(2)}) collective-permute-start(bf16[8,256,128]{2,1,0:T(8,128)(2,1)S(1)} %get-tuple-element.19.refs_0_), channel_id=1, source_target_pairs={{0,1},{1,0},{2,3},{3,2},{4,5},{5,4},{6,7},{7,6},{8,9},{9,8},{10,11... | collective-permute-start | bytes 1572872 | tf_op jit(solution)/shard_map/ppermute | solution.py:335
  48.3 18.7 %collective-permute-start.4 = (bf16[8,256,128]{2,1,0:T(8,128)(2,1)S(1)}, bf16[8,256,128]{2,1,0:T(8,128)(2,1)S(1)}, u32[]{:S(2)}, u32[]{:S(2)}) collective-permute-start(bf16[8,256,128]{2,1,0:T(8,128)(2,1)S(1)} %get-tuple-element.20.refs_1_), channel_id=1, source_target_pairs={{0,1},{1,0},{2,3},{3,2},{4,5},{5,4},{6,7},{7,6},{8,9},{9,8},{10,11... | collective-permute-start | bytes 1572872 | tf_op jit(solution)/shard_map/ppermute | solution.py:336
  50.8 14.0 %collective-permute-start.10 = (bf16[2,8,64,128]{3,2,1,0:T(8,128)(2,1)S(1)}, bf16[2,8,64,128]{3,2,1,0:T(8,128)(2,1)S(1)}, u32[]{:S(2)}, u32[]{:S(2)}) collective-permute-start(bf16[2,8,64,128]{3,2,1,0:T(8,128)(2,1)S(1)} %collective-permute-done.1.refs_1_), channel_id=1, source_target_pairs={{0,2},{2,4},{4,6},{6,8},{8,10},{10,12},{12,14},{14,0},{1,3},{3,5},... | collective-permute-start | bytes 786440 | tf_op jit(solution)/shard_map/ppermute | solution.py:317
  54.7 24.9 %copy-start.16 = (bf16[8,256,128]{2,1,0:T(8,128)(2,1)}, bf16[8,256,128]{2,1,0:T(8,128)(2,1)S(1)}, u32[]{:S(2)}) copy-start(bf16[8,256,128]{2,1,0:T(8,128)(2,1)S(1)} %collective-permute-done.5.refs_4_) | copy-start | bytes 1572868
  54.7 24.0 %collective-permute-start.7 = (bf16[8,256,128]{2,1,0:T(8,128)(2,1)S(1)}, bf16[8,256,128]{2,1,0:T(8,128)(2,1)S(1)}, u32[]{:S(2)}, u32[]{:S(2)}) collective-permute-start(bf16[8,256,128]{2,1,0:T(8,128)(2,1)S(1)} %collective-permute-done.5.refs_4_), channel_id=1, source_target_pairs={{0,1},{1,0},{2,3},{3,2},{4,5},{5,4},{6,7},{7,6},{8,9},{9,8},{10,11... | collective-permute-start | bytes 1572872 | tf_op jit(solution)/shard_map/ppermute | solution.py:339
  59.2 20.4 %collective-permute-start.8 = (bf16[8,256,128]{2,1,0:T(8,128)(2,1)}, bf16[8,256,128]{2,1,0:T(8,128)(2,1)}, u32[]{:S(2)}, u32[]{:S(2)}) collective-permute-start(bf16[8,256,128]{2,1,0:T(8,128)(2,1)} %collective-permute-done.6.refs_5_), channel_id=1, source_target_pairs={{0,1},{1,0},{2,3},{3,2},{4,5},{5,4},{6,7},{7,6},{8,9},{9,8},{10,11... | collective-permute-start | bytes 1572872 | tf_op jit(solution)/shard_map/ppermute | solution.py:340
  61.1 17.6 %copy-start.17 = (bf16[8,256,128]{2,1,0:T(8,128)(2,1)}, bf16[8,256,128]{2,1,0:T(8,128)(2,1)S(1)}, u32[]{:S(2)}) copy-start(bf16[8,256,128]{2,1,0:T(8,128)(2,1)S(1)} %collective-permute-done.3.refs_2_) | copy-start | bytes 1572868
  61.1 10.8 %collective-permute-start.11 = (bf16[2,8,64,128]{3,2,1,0:T(8,128)(2,1)}, bf16[2,8,64,128]{3,2,1,0:T(8,128)(2,1)S(1)}, u32[]{:S(2)}, u32[]{:S(2)}) collective-permute-start(bf16[2,8,64,128]{3,2,1,0:T(8,128)(2,1)} %copy-done.22), channel_id=1, source_target_pairs={{2,0},{4,2},{6,4},{8,6},{10,8},{12,10},{14,12},{0,14},{3,1},{5,3},... | collective-permute-start | bytes 786440 | tf_op jit(solution)/shard_map/ppermute | solution.py:320
  64.8 14.0 %copy-start.23 = (bf16[2,8,64,128]{3,2,1,0:T(8,128)(2,1)}, bf16[2,8,64,128]{3,2,1,0:T(8,128)(2,1)S(1)}, u32[]{:S(2)}) copy-start(bf16[2,8,64,128]{3,2,1,0:T(8,128)(2,1)S(1)} %collective-permute-done.10.refs_3_) | copy-start | bytes 786436
  64.8 12.0 %collective-permute-start.12 = (bf16[2,8,64,128]{3,2,1,0:T(8,128)(2,1)S(1)}, bf16[2,8,64,128]{3,2,1,0:T(8,128)(2,1)S(1)}, u32[]{:S(2)}, u32[]{:S(2)}) collective-permute-start(bf16[2,8,64,128]{3,2,1,0:T(8,128)(2,1)S(1)} %collective-permute-done.10.refs_3_), channel_id=1, source_target_pairs={{0,2},{2,4},{4,6},{6,8},{8,10},{10,12},{12,14},{14,0},{1,3},{3,5},... | collective-permute-start | bytes 786440 | tf_op jit(solution)/shard_map/ppermute | solution.py:317
  67.0 11.7 %copy-start.18 = (bf16[8,256,128]{2,1,0:T(8,128)(2,1)}, bf16[8,256,128]{2,1,0:T(8,128)(2,1)S(1)}, u32[]{:S(2)}) copy-start(bf16[8,256,128]{2,1,0:T(8,128)(2,1)S(1)} %collective-permute-done.4.refs_3_) | copy-start | bytes 1572868
  67.0 30.0 %collective-permute-start.9 = (bf16[16,128,128]{2,1,0:T(8,128)(2,1)S(1)}, bf16[16,128,128]{2,1,0:T(8,128)(2,1)S(1)}, u32[]{:S(2)}, u32[]{:S(2)}) collective-permute-start(bf16[16,128,128]{2,1,0:T(8,128)(2,1)S(1)} %all-to-all-done.peer_ref.q_ref), channel_id=1, source_target_pairs={{0,1},{1,0},{2,3},{3,2},{4,5},{5,4},{6,7},{7,6},{8,9},{9,8},{10,11... | collective-permute-start | bytes 1572872 | tf_op jit(solution)/shard_map/ppermute | solution.py:342
  71.9 18.2 %copy-start.24 = (bf16[2,8,64,128]{3,2,1,0:T(8,128)(2,1)}, bf16[2,8,64,128]{3,2,1,0:T(8,128)(2,1)S(1)}, u32[]{:S(2)}) copy-start(bf16[2,8,64,128]{3,2,1,0:T(8,128)(2,1)S(1)} %collective-permute-done.11.refs_4_) | copy-start | bytes 786436
  71.9 25.1 %collective-permute-start.13 = (bf16[2,8,64,128]{3,2,1,0:T(8,128)(2,1)S(1)}, bf16[2,8,64,128]{3,2,1,0:T(8,128)(2,1)S(1)}, u32[]{:S(2)}, u32[]{:S(2)}) collective-permute-start(bf16[2,8,64,128]{3,2,1,0:T(8,128)(2,1)S(1)} %collective-permute-done.11.refs_4_), channel_id=1, source_target_pairs={{2,0},{4,2},{6,4},{8,6},{10,8},{12,10},{14,12},{0,14},{3,1},{5,3},... | collective-permute-start | bytes 786440 | tf_op jit(solution)/shard_map/ppermute | solution.py:320
  76.8 13.3 %copy-start.25 = (bf16[2,8,64,128]{3,2,1,0:T(8,128)(2,1)}, bf16[2,8,64,128]{3,2,1,0:T(8,128)(2,1)S(1)}, u32[]{:S(2)}) copy-start(bf16[2,8,64,128]{3,2,1,0:T(8,128)(2,1)S(1)} %collective-permute-done.12.refs_5_) | copy-start | bytes 786436
  76.8 20.2 %collective-permute-start.14 = (bf16[2,8,64,128]{3,2,1,0:T(8,128)(2,1)S(1)}, bf16[2,8,64,128]{3,2,1,0:T(8,128)(2,1)S(1)}, u32[]{:S(2)}, u32[]{:S(2)}) collective-permute-start(bf16[2,8,64,128]{3,2,1,0:T(8,128)(2,1)S(1)} %collective-permute-done.12.refs_5_), channel_id=1, source_target_pairs={{0,2},{2,4},{4,6},{6,8},{8,10},{10,12},{12,14},{14,0},{1,3},{3,5},... | collective-permute-start | bytes 786440 | tf_op jit(solution)/shard_map/ppermute | solution.py:317
  78.8 0.8 copy-start.19
  79.6 0.8 copy-start.6
  92.3 22.0 %all-to-all-start.2 = ((f16[8,2,136,128]{3,2,1,0:T(8,128)(2,1)}), f16[8,2,136,128]{3,2,1,0:T(8,128)(2,1)S(1)}, u32[]{:S(2)}, u32[]{:S(2)}) async-start(f16[8,2,136,128]{3,2,1,0:T(8,128)(2,1)} %bitcast.11), calls=%async_computation.2 | async-start | bytes 1114112 | tf_op jit(solution)/shard_map/all_to_all | solution.py:240
  97.0 0.8 copy-start.20
  97.0 0.9 copy-start.26
  97.9 0.7 copy-start.27
  109.7 3.9 %collective-permute-start.15 = (f16[16,136,128]{2,1,0:T(8,128)(2,1)S(1)}, f16[16,136,128]{2,1,0:T(8,128)(2,1)S(1)}, u32[]{:S(2)}, u32[]{:S(2)}) collective-permute-start(f16[16,136,128]{2,1,0:T(8,128)(2,1)S(1)} %convert_element_type.23), channel_id=1, source_target_pairs={{0,1},{1,0},{2,3},{3,2},{4,5},{5,4},{6,7},{7,6},{8,9},{9,8},{10,11... | collective-permute-start | bytes 1671176 | tf_op jit(solution)/shard_map/ppermute | solution.py:398
  113.7 1.2 copy-start
  117.1 12.6 %copy-start.1 = (bf16[1,512,8,128]{3,2,1,0:T(8,128)(2,1)S(1)}, bf16[1,512,8,128]{3,2,1,0:T(8,128)(2,1)}, u32[]{:S(2)}) copy-start(bf16[1,512,8,128]{3,2,1,0:T(8,128)(2,1)} %param.17) | copy-start | bytes 3145732
  117.1 12.6 %copy-start.2 = (bf16[1,512,8,128]{3,2,1,0:T(8,128)(2,1)S(1)}, bf16[1,512,8,128]{3,2,1,0:T(8,128)(2,1)}, u32[]{:S(2)}) copy-start(bf16[1,512,8,128]{3,2,1,0:T(8,128)(2,1)} %param.18) | copy-start | bytes 3145732
  117.1 12.6 %copy-start.4 = (bf16[1,2,8,128]{3,2,1,0:T(8,128)(2,1)S(1)}, bf16[1,2,8,128]{3,2,1,0:T(8,128)(2,1)}, u32[]{:S(2)}) copy-start(bf16[1,2,8,128]{3,2,1,0:T(8,128)(2,1)} %param.19) | copy-start | bytes 12292
  117.1 12.6 %copy-start.5 = (bf16[1,2,8,128]{3,2,1,0:T(8,128)(2,1)S(1)}, bf16[1,2,8,128]{3,2,1,0:T(8,128)(2,1)}, u32[]{:S(2)}) copy-start(bf16[1,2,8,128]{3,2,1,0:T(8,128)(2,1)} %param.20) | copy-start | bytes 12292
  118.0 26.8 %all-to-all-start.3 = ((f16[16,136,128]{2,1,0:T(8,128)(2,1)}), f16[16,136,128]{2,1,0:T(8,128)(2,1)S(1)}, u32[]{:S(2)}, u32[]{:S(2)}) async-start(f16[16,136,128]{2,1,0:T(8,128)(2,1)} %convert_element_type.26), calls=%async_computation.3 | async-start | bytes 1114112 | tf_op jit(solution)/shard_map/all_to_all | solution.py:240

commit v4 on v3

--- a/solution.py
+++ b/solution.py
@@ -11,6 +11,7 @@
 CAP = 2
 PAD = 8
 LOW = -1e30
+PARTS = 4
 EMPHASIS = 30
 NT = (((1,), (1,)), ((), ()))
 
@@ -87,27 +88,89 @@
     out_ref[...] = jnp.broadcast_to(peer_ref[...][None], out_ref.shape)
 
 
+def staged(heads, per_head, queries, results, q_sems, out_sems, feeds, feed_sem):
+    parts = out_sems.shape[1] - 1
+    group = heads // parts
+    reads = [
+        [
+            pltpu.make_async_copy(source(part), target(part), feed_sem(place, part))
+            for place, (source, target) in enumerate(feeds)
+        ]
+        for part in range(parts)
+    ]
+    q_copies = [
+        pltpu.make_async_copy(ref, held, q_sems.at[place])
+        for place, (ref, held) in enumerate(queries)
+    ]
+    for copy in q_copies:
+        copy.start()
+    for copies in reads:
+        for copy in copies:
+            copy.start()
+    for copy in q_copies:
+        copy.wait()
+    span = group * per_head
+    pieces = [pl.ds(part * span, span) for part in range(parts)]
+    pieces.append(pl.ds(heads * per_head, PAD))
+    writes = [
+        [
+            pltpu.make_async_copy(
+                held.at[:, piece, :], ref.at[:, piece, :], out_sems.at[place, part]
+            )
+            for place, (ref, held) in enumerate(results)
+        ]
+        for part, piece in enumerate(pieces)
+    ]
+
+    def enter(head):
+        if head % group == 0:
+            for copy in reads[head // group]:
+                copy.wait()
+
+    def leave(head):
+        if (head + 1) % group == 0:
+            for copy in writes[head // group]:
+                copy.start()
+
+    def finish():
+        for copy in writes[-1]:
+            copy.start()
+        for copies in writes:
+            for copy in copies:
+                copy.wait()
+
+    return enter, leave, finish
+
+
 def branch_kernel(count, q_ref, *refs):
-    sources, out_ref, held, sems = refs[:count], refs[count], refs[count + 1], refs[count + 2]
+    sources, out_ref = refs[:count], refs[count]
+    held, q_held, out_held, sems, q_sems, out_sems = refs[count + 1 :]
     slots, lanes, dim = q_ref.shape
     heads = sources[0].shape[0]
     per_head = lanes // heads
-
-    def copies(head):
-        return [
-            pltpu.make_async_copy(ref.at[head], held.at[place, head], sems.at[place, head])
-            for place, ref in enumerate(sources)
-        ]
-
-    for head in range(heads):
-        for copy in copies(head):
-            copy.start()
+    group = heads // sems.shape[1]
+
+    def feed(place, ref):
+        def some(part):
+            return pl.ds(part * group, group)
+
+        return lambda part: ref.at[some(part)], lambda part: held.at[place, some(part)]
+
+    enter, leave, finish = staged(
+        heads,
+        per_head,
+        [(q_ref, q_held.at[0])],
+        [(out_ref, out_held.at[0])],
+        q_sems,
+        out_sems,
+        [feed(place, ref) for place, ref in enumerate(sources)],
+        lambda place, part: sems.at[place, part],
+    )
     tail = jnp.zeros((slots, 1, lanes), jnp.float32)
     for head in range(heads):
-        for copy in copies(head):
-            copy.wait()
+        enter(head)
         place = slice(head * per_head, (head + 1) * per_head)
-        q = q_ref[:, place, :].reshape(slots * per_head, dim)
+        q = q_held[0, :, place, :].reshape(slots * per_head, dim)
         found = []
         for block in range(0, count, 2):
             scores = scores_of(q, held[block, head])
@@ -119,42 +182,57 @@
         factors = [jnp.exp(f[0] - high) for f in found]
         den = sum(factor * f[1] for factor, f in zip(factors, found))
         num = sum(f[2] * (factor / den) for factor, f in zip(factors, found))
-        out_ref[:, place, :] = num.reshape(slots, per_head, dim)
+        out_held[0, :, place, :] = num.reshape(slots, per_head, dim)
         tail = tail + head_lse(high + jnp.log(den), head, per_head, lanes)
-    out_ref[:, lanes:, :] = tail_rows(split_lse(tail))
-
-
-def root_kernel(count, q_ref, q_twin_ref, *refs):
+        leave(head)
+    out_held[0, :, lanes:, :] = tail_rows(split_lse(tail))
+    finish()
+
+
+def root_kernel(count, q_ref, q_far_ref, *refs):
     sources, out_refs = refs[:count], refs[count : count + 2]
-    held, sems = refs[count + 2 :]
-    copies = [
-        pltpu.make_async_copy(ref, held.at[place], sems.at[place])
-        for place, ref in enumerate(sources)
-    ]
-    for copy in copies:
-        copy.start()
-    for copy in copies:
-        copy.wait()
+    held, q_held, out_held, sems, q_sems, out_sems = refs[count + 2 :]
     requests, lanes, dim = q_ref.shape
-    pairs, heads, half = held.shape[1], held.shape[2], held.shape[3] // 2
+    blocks, heads, half = held.shape[1], held.shape[2], held.shape[3] // 2
     per_head = lanes // heads
-    span = count * pairs * half
+    group = heads // sems.shape[1]
+    span = count * blocks * half
+
+    def feed(place, ref):
+        def some(part):
+            return pl.ds(part * group, group)
+
+        return lambda part: ref.at[:, some(part)], lambda part: held.at[place, :, some(part)]
+
+    enter, leave, finish = staged(
+        heads,
+        per_head,
+        [(ref, q_held.at[i]) for i, ref in enumerate((q_ref, q_far_ref))],
+        [(ref, out_held.at[i]) for i, ref in enumerate(out_refs)],
+        q_sems,
+        out_sems,
+        [feed(place, ref) for place, ref in enumerate(sources)],
+        lambda place, part: sems.at[place, part],
+    )
     tails = [jnp.zeros((requests, 1, lanes), jnp.float32) for _ in out_refs]
     for head in range(heads):
+        enter(head)
         place = slice(head * per_head, (head + 1) * per_head)
         keys = held[:, :, head, :half, :].reshape(span, dim)
         values = held[:, :, head, half:, :].reshape(span, dim)
-        for which, (rows_ref, out_ref) in enumerate(zip((q_ref, q_twin_ref), out_refs)):
-            q = rows_ref[:, place, :].reshape(requests * per_head, dim)
+        for i in range(len(tails)):
+            q = q_held[i, :, place, :].reshape(requests * per_head, dim)
             scores = scores_of(q, keys)
             high = jnp.max(scores, axis=1, keepdims=True)
             weights = jnp.exp(scores - high)
             den = jnp.sum(weights, axis=1, keepdims=True)
             num = times_values(weights, values) / den
-            out_ref[:, place, :] = num.reshape(requests, per_head, dim)
-            tails[which] = tails[which] + head_lse(high + jnp.log(den), head, per_head, lanes)
-    for out_ref, tail in zip(out_refs, tails):
-        out_ref[:, lanes:, :] = tail_rows(split_lse(tail))
+            out_held[i, :, place, :] = num.reshape(requests, per_head, dim)
+            tails[i] = tails[i] + head_lse(high + jnp.log(den), head, per_head, lanes)
+        leave(head)
+    for i, tail in enumerate(tails):
+        out_held[i, :, lanes:, :] = tail_rows(split_lse(tail))
+    finish()
 
 
 def columns(table):
@@ -163,11 +241,11 @@
     return jnp.concatenate([table, rest], axis=0).T
 
 
-def merge_kernel(idx_ref, part_ref, own_ref, twin_ref, out_ref):
+def merge_kernel(idx_ref, part_ref, own_ref, far_ref, out_ref):
     sources, cap, _, lanes = part_ref.shape
     groups = own_ref.shape[0]
     lse_a = join_lse(own_ref[:, lanes:, :])
-    lse_b = join_lse(twin_ref[:, lanes:, :])
+    lse_b = join_lse(far_ref[:, lanes:, :])
     high = jnp.maximum(lse_a, lse_b)
     factor_a = jnp.exp(lse_a - high)
     factor_b = jnp.exp(lse_b - high)
@@ -177,7 +255,7 @@
     for r in range(groups):
         out_ref[r, :lanes, :] = (
             own_ref[r, :lanes, :] * table[:, r : r + 1]
-            + twin_ref[r, :lanes, :] * table[:, groups + r : groups + r + 1]
+            + far_ref[r, :lanes, :] * table[:, groups + r : groups + r + 1]
         )
         out_ref[r, lanes:, :] = tail_rows([piece[r : r + 1] for piece in pieces])
     for k in range(cap):
@@ -218,9 +296,9 @@
     return pltpu.CompilerParams(vmem_limit_bytes=megabytes * 1024 * 1024)
 
 
-def estimate(area, dim):
+def estimate(area, dim, emphasis=1):
     return pl.CostEstimate(
-        flops=EMPHASIS * 4 * area * dim, bytes_accessed=6 * 1024 * 1024, transcendentals=area
+        flops=emphasis * 4 * area * dim, bytes_accessed=6 * 1024 * 1024, transcendentals=area
     )
 
 
@@ -228,12 +306,23 @@
     return pl.BlockSpec(memory_space=pltpu.VMEM)
 
 
-def hbm():
-    return pl.BlockSpec(memory_space=pltpu.HBM)
+def anywhere():
+    return pl.BlockSpec(memory_space=pl.ANY)
 
 
 def smem():
     return pl.BlockSpec(memory_space=pltpu.SMEM)
+
+
+def scratch(count, block, q, sets):
+    return [
+        pltpu.VMEM((count,) + block.shape, jnp.bfloat16),
+        pltpu.VMEM((sets,) + q.shape, jnp.bfloat16),
+        pltpu.VMEM((sets, q.shape[0], q.shape[1] + PAD, q.shape[2]), jnp.float32),
+        pltpu.SemaphoreType.DMA((count, PARTS)),
+        pltpu.SemaphoreType.DMA((sets,)),
+        pltpu.SemaphoreType.DMA((sets, PARTS + 1)),
+    ]
 
 
 def exchange(blocks, axis):
@@ -299,7 +388,7 @@
                 out_specs=pl.BlockSpec((ring, 1, rows, dim), lambda k, idx: (0, k, 0, 0)),
             ),
             compiler_params=params(),
-            cost_estimate=estimate(area, dim),
+            cost_estimate=estimate(area, dim, EMPHASIS),
             name="pick_readers",
         )(readers, peers)
         return exchange(packed, "z")
@@ -307,28 +396,12 @@
     keys_own = branch_keys[0].transpose(1, 0, 2)
     values_own = branch_values[0].transpose(1, 0, 2)
     root_block = jnp.concatenate([root_keys, root_values], axis=0).transpose(1, 0, 2)
-    root_far = lax.ppermute(root_block, "xhi", swap)
-    up = [(i, (i + 1) % ring) for i in range(ring)]
-    down = [(b, a) for a, b in up]
-    pair = jnp.stack([root_block, root_far])
-    root_blocks = [pair]
-
-    def hop(ahead, behind):
-        ahead = lax.ppermute(ahead, "z", up)
-        root_blocks.append(ahead)
-        if len(root_blocks) < ring:
-            behind = lax.ppermute(behind, "z", down)
-            root_blocks.append(behind)
-        return ahead, behind
-
-    pair, keys_own, values_own = lax.optimization_barrier((pair, keys_own, values_own))
-    ahead, behind = hop(pair, pair)
+    root_block = lax.optimization_barrier(root_block)
+    root_own = lax.all_gather(root_block, "z")
+    peers_far = lax.ppermute(peers, "xhi", swap)
     keys_far = lax.ppermute(keys_own, "xhi", swap)
     values_far = lax.ppermute(values_own, "xhi", swap)
-    peers, ahead, behind = lax.optimization_barrier((peers, ahead, behind))
     slots = gather_readers(peers)
-    while len(root_blocks) < ring:
-        ahead, behind = hop(ahead, behind)
     branch_blocks = [
         keys_own,
         values_own,
@@ -339,8 +412,6 @@
         lax.ppermute(keys_far, "core", swap),
         lax.ppermute(values_far, "core", swap),
     ]
-    peers_twin = lax.ppermute(peers, "core", swap)
-
     flat = suffix_keys.shape[1] * heads
     local = pl.pallas_call(
         functools.partial(local_kernel, heads),
@@ -367,36 +438,32 @@
     parts = pl.pallas_call(
         functools.partial(branch_kernel, count),
         out_shape=jax.ShapeDtypeStruct((ring * CAP, rows + PAD, dim), jnp.float32),
-        in_specs=[vmem()] + [hbm()] * count,
-        out_specs=vmem(),
-        scratch_shapes=[
-            pltpu.VMEM((count,) + keys_own.shape, jnp.bfloat16),
-            pltpu.SemaphoreType.DMA((count, heads)),
-        ],
-        compiler_params=params(58),
+        in_specs=[anywhere()] * (1 + count),
+        out_specs=anywhere(),
+        scratch_shapes=scratch(count, keys_own, slots, 1),
+        compiler_params=params(54),
         cost_estimate=estimate(area, dim),
         name="branch_attention",
     )(slots, *branch_blocks)
     parts = parts.astype(jnp.float16).reshape(ring, CAP, rows + PAD, dim)
-    peers, _ = lax.optimization_barrier((peers, parts))
+    peers, peers_far, root_own, _ = lax.optimization_barrier((peers, peers_far, root_own, parts))
+    root_blocks = [root_own, lax.ppermute(root_own, "core", swap)]
     parts = exchange(parts, "z")
 
     whole = jax.ShapeDtypeStruct((grp, rows + PAD, dim), jnp.float32)
-    root_own, root_twin = pl.pallas_call(
-        functools.partial(root_kernel, ring),
+    count = len(root_blocks)
+    root, root_far = pl.pallas_call(
+        functools.partial(root_kernel, count),
         out_shape=(whole, whole),
-        in_specs=[vmem()] * 2 + [hbm()] * ring,
-        out_specs=(vmem(), vmem()),
-        scratch_shapes=[
-            pltpu.VMEM((ring,) + pair.shape, jnp.bfloat16),
-            pltpu.SemaphoreType.DMA((ring,)),
-        ],
-        compiler_params=params(58),
+        in_specs=[anywhere()] * (2 + count),
+        out_specs=(anywhere(), anywhere()),
+        scratch_shapes=scratch(count, root_own, peers, 2),
+        compiler_params=params(),
         cost_estimate=estimate(area, dim),
         name="root_attention",
-    )(peers, peers_twin, *root_blocks)
-    root_twin = lax.ppermute(root_twin.astype(jnp.float16), "core", swap).astype(jnp.float32)
-    parts, root_own, root_twin = lax.optimization_barrier((parts, root_own, root_twin))
+    )(peers, peers_far, *root_blocks)
+    root_far = lax.ppermute(root_far.astype(jnp.float16), "xhi", swap).astype(jnp.float32)
+    parts, root, root_far = lax.optimization_barrier((parts, root, root_far))
     parts = parts.astype(jnp.float32)
     merged = pl.pallas_call(
         merge_kernel,
@@ -405,7 +472,7 @@
         out_specs=vmem(),
         compiler_params=params(),
         name="merge_parts",
-    )(readers, parts, root_own, root_twin)
+    )(readers, parts, root, root_far)
     back = exchange(merged.astype(jnp.float16), "grp").astype(jnp.float32)
     mine = pl.pallas_call(
         final_kernel,

time: 148 us -> 162 us (1.095)
  waiting for transfers between devices: 26.9 us -> 56.9 us
  starting transfers between devices: 81.1 us -> 55.8 us
  between operations: 1.29 us -> 14.5 us
  Pallas kernels: 25.1 us -> 20.8 us
    ppermute x10 -> x3, starting transfers between devices: 36.8 us -> 8.57 us  [the longest x1 3.34 us: shards(): lax.ppermute(root_far.astype(jnp.float16), 'xhi', swap).astype(jnp.float32)]
    all_gather x0 -> x1, waiting for transfers between devices: none -> 22 us  [shards(): root_own = lax.all_gather(root_block, 'z')]
    all_to_all x4, waiting for transfers between devices: 14.2 us -> 20 us  [exchange(): return lax.all_to_all(blocks, axis, split_axis=0, concat_axis=0, tiled=True)]
    ppermute x10 -> x3, waiting for transfers between devices: 10.1 us -> 14.8 us  [the longest x1 14.8 us: shards(): lax.ppermute(root_far.astype(jnp.float16), 'xhi', swap).astype(jnp.float32)]
    pallas_call x1, Pallas kernels: 9.79 us -> 6.63 us  [shards(): pl.pallas_call(functools.partial(root_kernel, count), out_shape=(whole, w...]
    ppermute x1, waiting for transfers between devices: 2.54 us -> 0.01 us  [shards(): values_far = lax.ppermute(values_own, 'xhi', swap)]
    all_to_all x4, starting transfers between devices: 28.8 us -> 31.2 us  [exchange(): return lax.all_to_all(blocks, axis, split_axis=0, concat_axis=0, tiled=True)]
    all_gather x0 -> x1, local copies, waits for them, and re-layouts: none -> 1.9 us  [shards(): root_own = lax.all_gather(root_block, 'z')]
  transfers between devices with their start and end apart: 20 -> 14, of which waited for: 6 -> 4; matrix products, arithmetic and copies ran while one was open for 3% -> 3% of each run, Pallas kernels for 15% -> 11%
where the time goes in v4:
time: 162 us; the launch traced here: 160 us
  waiting for transfers between devices  56.9 us (35%)
  starting transfers between devices  55.8 us (34%)
  Pallas kernels  20.8 us (13%)
  between operations  14.5 us (9%)
  local copies, waits for them, and re-layouts  6.68 us (4%)
  other arithmetic  5.56 us (3%)
    all_to_all x4, starting transfers between devices, exchange(): return lax.all_to_all(blocks, axis, split_axis=0, concat_axis=0, tiled=True)  31.2 us
    all_gather x1, waiting for transfers between devices, shards(): root_own = lax.all_gather(root_block, 'z')  22 us
    all_to_all x4, waiting for transfers between devices, exchange(): return lax.all_to_all(blocks, axis, split_axis=0, concat_axis=0, tiled=True)  20 us
    ppermute x1, waiting for transfers between devices, shards(): lax.ppermute(root_far.astype(jnp.float16), 'xhi', swap).astype(jnp.float32)  14.8 us
    pallas_call x1, Pallas kernels, shards(): pl.pallas_call(functools.partial(branch_kernel, count), out_shape=jax.Sha...  8.55 us
    pallas_call x1, Pallas kernels, shards(): pl.pallas_call(functools.partial(root_kernel, count), out_shape=(whole, w...  6.63 us
    ppermute x1, starting transfers between devices, shards(): keys_far = lax.ppermute(keys_own, 'xhi', swap)  4.01 us
    ppermute x1, starting transfers between devices, shards(): lax.ppermute(root_far.astype(jnp.float16), 'xhi', swap).astype(jnp.float32)  3.34 us
  transfers between devices with their start and end apart: 14, of which 4 were waited for; matrix products, arithmetic and copies ran while one was open for 3% of the time, Pallas kernels for 11%

profile of v4, /device:TPU:6, one launch (start us, length us, event | category | flops | bytes accessed | tf_op | source)
XLA Modules:
  0.0 160.1 jit_solution(6085961333948501967)
XLA Ops:
  6.5 0.8 copy.28
  7.4 0.9 broadcast_in_dim.46
  8.2 8.7 %all-to-all-start = ((bf16[16,128,128]{2,1,0:T(8,128)(2,1)}), bf16[16,128,128]{2,1,0:T(8,128)(2,1)S(1)}, u32[]{:S(2)}, u32[]{:S(2)}) async-start(bf16[16,128,128]{2,1,0:T(8,128)(2,1)} %broadcast_in_dim.46), calls=%async_computation | async-start | bytes 1048576 | tf_op jit(solution)/shard_map/all_to_all | solution.py:329
  17.0 0.0 copy-start.11
  17.0 0.0 copy-start.12
  17.0 0.0 copy-start.13
  17.0 0.0 all-gather.3.cloned.1.call-start
  17.0 0.0 copy-done.8
  17.1 0.1 copy.37
  17.1 4.0 %collective-permute-start.2 = (bf16[8,256,128]{2,1,0:T(8,128)(2,1)S(1)}, bf16[8,256,128]{2,1,0:T(8,128)(2,1)}, u32[]{:S(2)}, u32[]{:S(2)}) collective-permute-start(bf16[8,256,128]{2,1,0:T(8,128)(2,1)S(1)} %bitcast.39), channel_id=1, source_target_pairs={{0,16},{16,0},{1,17},{17,1},{2,18},{18,2},{3,19},{19,3},{4,20},{20... | collective-permute-start | bytes 1572872 | tf_op jit(solution)/shard_map/ppermute | solution.py:402
  21.2 0.1 copy.36
  21.3 3.3 %collective-permute-start.3 = (bf16[8,256,128]{2,1,0:T(8,128)(2,1)S(1)}, bf16[8,256,128]{2,1,0:T(8,128)(2,1)}, u32[]{:S(2)}, u32[]{:S(2)}) collective-permute-start(bf16[8,256,128]{2,1,0:T(8,128)(2,1)S(1)} %bitcast.42), channel_id=1, source_target_pairs={{0,16},{16,0},{1,17},{17,1},{2,18},{18,2},{3,19},{19,3},{4,20},{20... | collective-permute-start | bytes 1572872 | tf_op jit(solution)/shard_map/ppermute | solution.py:403
  24.6 0.7 maximum_bitcast_fusion
  25.3 0.0 all-gather.3.cloned.1.call-update
  25.3 0.1 select_reduce_fusion
  25.4 0.1 reshape.39
  25.5 0.2 fusion
  25.7 0.1 convert_reduce_fusion
  25.8 0.1 fusion.2.idx_ref
  25.9 6.3 %all-to-all-done.peer_ref.q_ref = bf16[16,128,128]{2,1,0:T(8,128)(2,1)S(1)} async-done(((bf16[16,128,128]{2,1,0:T(8,128)(2,1)}), bf16[16,128,128]{2,1,0:T(8,128)(2,1)S(1)}, u32[]{:S(2)}, u32[]{:S(2)}) %all-to-all-start) | async-done | bytes 524320 | tf_op jit(solution)/shard_map/all_to_all | solution.py:329
  32.3 1.4 pick_readers.1
  33.7 10.3 %all-to-all-start.1 = ((bf16[8,2,128,128]{3,2,1,0:T(8,128)(2,1)}), bf16[8,2,128,128]{3,2,1,0:T(8,128)(2,1)}, u32[]{:S(2)}, u32[]{:S(2)}) async-start(bf16[8,2,128,128]{3,2,1,0:T(8,128)(2,1)} %pick_readers.1), calls=%async_computation.1 | async-start | bytes 1048576 | tf_op jit(solution)/shard_map/all_to_all | solution.py:329
  44.0 1.9 %collective-permute-start = (bf16[8,256,128]{2,1,0:T(8,128)(2,1)S(1)}, bf16[8,256,128]{2,1,0:T(8,128)(2,1)}, u32[]{:S(2)}, u32[]{:S(2)}) collective-permute-start(bf16[8,256,128]{2,1,0:T(8,128)(2,1)S(1)} %bitcast.40), channel_id=1, source_target_pairs={{0,1},{1,0},{2,3},{3,2},{4,5},{5,4},{6,7},{7,6},{8,9},{9,8},{10,11... | collective-permute-start | bytes 1572872 | tf_op jit(solution)/shard_map/ppermute | solution.py:408
  46.0 2.4 %collective-permute-start.1 = (bf16[8,256,128]{2,1,0:T(8,128)(2,1)S(1)}, bf16[8,256,128]{2,1,0:T(8,128)(2,1)}, u32[]{:S(2)}, u32[]{:S(2)}) collective-permute-start(bf16[8,256,128]{2,1,0:T(8,128)(2,1)S(1)} %bitcast.43), channel_id=1, source_target_pairs={{0,1},{1,0},{2,3},{3,2},{4,5},{5,4},{6,7},{7,6},{8,9},{9,8},{10,11... | collective-permute-start | bytes 1572872 | tf_op jit(solution)/shard_map/ppermute | solution.py:409
  48.4 0.0 collective-permute-done.2.refs_4_
  48.4 1.9 %collective-permute-start.4 = (bf16[8,256,128]{2,1,0:T(8,128)(2,1)}, bf16[8,256,128]{2,1,0:T(8,128)(2,1)}, u32[]{:S(2)}, u32[]{:S(2)}) collective-permute-start(bf16[8,256,128]{2,1,0:T(8,128)(2,1)} %collective-permute-done.2.refs_4_), channel_id=1, source_target_pairs={{0,1},{1,0},{2,3},{3,2},{4,5},{5,4},{6,7},{7,6},{8,9},{9,8},{10,11... | collective-permute-start | bytes 1572872 | tf_op jit(solution)/shard_map/ppermute | solution.py:412
  50.3 0.0 collective-permute-done.3.refs_5_
  50.3 2.4 %collective-permute-start.5 = (bf16[8,256,128]{2,1,0:T(8,128)(2,1)}, bf16[8,256,128]{2,1,0:T(8,128)(2,1)}, u32[]{:S(2)}, u32[]{:S(2)}) collective-permute-start(bf16[8,256,128]{2,1,0:T(8,128)(2,1)} %collective-permute-done.3.refs_5_), channel_id=1, source_target_pairs={{0,1},{1,0},{2,3},{3,2},{4,5},{5,4},{6,7},{7,6},{8,9},{9,8},{10,11... | collective-permute-start | bytes 1572872 | tf_op jit(solution)/shard_map/ppermute | solution.py:413
  52.7 3.3 %collective-permute-start.6 = (bf16[16,128,128]{2,1,0:T(8,128)(2,1)S(1)}, bf16[16,128,128]{2,1,0:T(8,128)(2,1)S(1)}, u32[]{:S(2)}, u32[]{:S(2)}) collective-permute-start(bf16[16,128,128]{2,1,0:T(8,128)(2,1)S(1)} %all-to-all-done.peer_ref.q_ref), channel_id=1, source_target_pairs={{0,16},{16,0},{1,17},{17,1},{2,18},{18,2},{3,19},{19,3},{4,20},{20... | collective-permute-start | bytes 1572872 | tf_op jit(solution)/shard_map/ppermute | solution.py:401
  56.1 22.0 %all-gather.3.cloned.1.call-done = bf16[64,64,128]{2,0,1:T(8,128)(2,1)} async-done(((bf16[8,64,128]{2,0,1:T(8,128)(2,1)}), bf16[64,64,128]{2,0,1:T(8,128)(2,1)}) %all-gather.3.cloned.1.call-update) | async-done | bytes 1048592 | tf_op jit(solution)/shard_map/all_gather | solution.py:400
  78.1 1.9 %copy.31 = bf16[64,64,128]{2,1,0:T(8,128)(2,1)S(1)} copy(bf16[64,64,128]{2,0,1:T(8,128)(2,1)} %all-gather.3.cloned.1.call-done) | data formatting | bytes 2097152 | tf_op jit(solution)/shard_map/all_gather | solution.py:400
  80.0 0.0 collective-permute-done.refs_2_
  80.0 0.0 collective-permute-done.1.refs_3_
  80.0 0.0 collective-permute-done.4.refs_6_
  80.0 0.0 collective-permute-done.5.refs_7_
  80.1 0.0 all-to-all-done.1
  80.1 8.5 %branch_attention.1 = f32[16,136,128]{2,1,0:T(8,128)} custom-call(bf16[16,128,128]{2,1,0:T(8,128)(2,1)} %bitcast.3.q_ref, bf16[8,256,128]{2,1,0:T(8,128)(2,1)} %bitcast.41, bf16[8,256,128]{2,1,0:T(8,128)(2,1)} %bitcast.44, bf16[8,256,128]{2,1,0:T(8,128)(2,1)} %collective-permute-done.refs_2_, bf16[8,256,128]{2,1,0:T(8,128)(2,1)} %collective-permute-done.1.refs_3_, ...), custom_call_target="tpu_custom_call" | custom-call | flops 1073741824 | bytes 6291456 | tf_op jit(solution)/shard_map/branch_attention/pallas_call | solution.py:438
  88.6 2.1 %convert_element_type.22 = f16[16,136,128]{2,1,0:T(8,128)(2,1)} convert(f32[16,136,128]{2,1,0:T(8,128)} %branch_attention.1) | non-fusion elementwise | flops 278528 | bytes 1671168 | tf_op jit(solution)/shard_map/convert_element_type | solution.py:448
  90.8 0.0 collective-permute-done.6.q_far_ref
  90.8 1.9 %collective-permute-start.7 = (bf16[8,8,64,128]{3,2,1,0:T(8,128)(2,1)S(1)}, bf16[8,8,64,128]{3,2,1,0:T(8,128)(2,1)S(1)}, u32[]{:S(2)}, u32[]{:S(2)}) collective-permute-start(bf16[8,8,64,128]{3,2,1,0:T(8,128)(2,1)S(1)} %bitcast.31), channel_id=1, source_target_pairs={{0,1},{1,0},{2,3},{3,2},{4,5},{5,4},{6,7},{7,6},{8,9},{9,8},{10,11... | collective-permute-start | bytes 3145736 | tf_op jit(solution)/shard_map/ppermute | solution.py:450
  92.7 5.2 %all-to-all-start.2 = ((f16[8,2,136,128]{3,2,1,0:T(8,128)(2,1)}), f16[8,2,136,128]{3,2,1,0:T(8,128)(2,1)}, u32[]{:S(2)}, u32[]{:S(2)}) async-start(f16[8,2,136,128]{3,2,1,0:T(8,128)(2,1)} %bitcast.38), calls=%async_computation.2 | async-start | bytes 1114112 | tf_op jit(solution)/shard_map/all_to_all | solution.py:329
  97.8 0.0 collective-permute-done.7.refs_1_
  97.8 0.0 copy-start.4
  97.9 0.9 copy-done.4
  98.8 1.2 copy-done.5
  100.0 6.6 %root_attention.1 = (f32[16,136,128]{2,1,0:T(8,128)S(1)}, f32[16,136,128]{2,1,0:T(8,128)S(1)}) custom-call(bf16[16,128,128]{2,1,0:T(8,128)(2,1)S(1)} %all-to-all-done.peer_ref.q_ref, bf16[16,128,128]{2,1,0:T(8,128)(2,1)S(1)} %collective-permute-done.6.q_far_ref, bf16[8,8,64,128]{3,2,1,0:T(8,128)(2,1)S(1)} %bitcast.32, bf16[8,8,64,128]{3,2,1,0:T(8,128)(2,1)S(1)} %copy-done.5), custom_call_target="tpu_custom_call" | custom-call | flops 1073741824 | bytes 6291456 | tf_op jit(solution)/shard_map/root_attention/pallas_call | solution.py:455
  106.7 0.1 convert_element_type.23
  106.7 3.3 %collective-permute-start.8 = (f16[16,136,128]{2,1,0:T(8,128)(2,1)S(1)}, f16[16,136,128]{2,1,0:T(8,128)(2,1)S(1)}, u32[]{:S(2)}, u32[]{:S(2)}) collective-permute-start(f16[16,136,128]{2,1,0:T(8,128)(2,1)S(1)} %convert_element_type.23), channel_id=1, source_target_pairs={{0,16},{16,0},{1,17},{17,1},{2,18},{18,2},{3,19},{19,3},{4,20},{20... | collective-permute-start | bytes 1671176 | tf_op jit(solution)/shard_map/ppermute | solution.py:465
  110.1 14.8 %collective-permute-done.8 = f16[16,136,128]{2,1,0:T(8,128)(2,1)S(1)} collective-permute-done((f16[16,136,128]{2,1,0:T(8,128)(2,1)S(1)}, f16[16,136,128]{2,1,0:T(8,128)(2,1)S(1)}, u32[]{:S(2)}, u32[]{:S(2)}) %collective-permute-start.8) | collective-permute-done | bytes 557088 | tf_op jit(solution)/shard_map/ppermute | solution.py:465
  124.9 0.1 convert_element_type.24.far_ref
  125.0 0.0 all-to-all-done.2
  125.0 1.1 convert_element_type.25.part_ref
  126.1 2.2 %merge_parts.1 = f32[16,136,128]{2,1,0:T(8,128)S(1)} custom-call(s32[2]{0:T(128)S(1)} %fusion.2.idx_ref, f32[8,2,136,128]{3,2,1,0:T(8,128)S(1)} %convert_element_type.25.part_ref, f32[16,136,128]{2,1,0:T(8,128)S(1)} %get-tuple-element.19.own_ref, f32[16,136,128]{2,1,0:T(8,128)S(1)} %convert_element_type.24.far_ref), custom_call_target="tpu_custom_call" | custom-call | tf_op jit(solution)/shard_map/merge_parts/pallas_call | solution.py:468
  128.3 0.0 copy-start
  128.3 0.0 copy-start.1
  128.3 0.0 copy-start.2
  128.3 0.0 copy-start.3
  128.3 0.9 convert_element_type.26
  129.2 7.0 %all-to-all-start.3 = ((f16[16,136,128]{2,1,0:T(8,128)(2,1)}), f16[16,136,128]{2,1,0:T(8,128)(2,1)S(1)}, u32[]{:S(2)}, u32[]{:S(2)}) async-start(f16[16,136,128]{2,1,0:T(8,128)(2,1)} %convert_element_type.26), calls=%async_computation.3 | async-start | bytes 1114112 | tf_op jit(solution)/shard_map/all_to_all | solution.py:329
  136.9 1.5 local_attention.1.local_ref
  138.4 13.6 %all-to-all-done.3 = f16[16,136,128]{2,1,0:T(8,128)(2,1)S(1)} async-done(((f16[16,136,128]{2,1,0:T(8,128)(2,1)}), f16[16,136,128]{2,1,0:T(8,128)(2,1)S(1)}, u32[]{:S(2)}, u32[]{:S(2)}) %all-to-all-start.3) | async-done | bytes 557088 | tf_op jit(solution)/shard_map/all_to_all | solution.py:329
  152.0 0.1 convert_element_type.27.part_ref
  152.1 0.5 final_merge.1
  152.7 0.6 copy.38
  (17 shorter events, 0.0 us)
Async XLA Ops:
  6.5 10.5 %copy-start.8 = (bf16[1,256,8,128]{3,2,1,0:T(8,128)(2,1)S(1)}, bf16[1,256,8,128]{3,2,1,0:T(8,128)(2,1)}, u32[]{:S(2)}) copy-start(bf16[1,256,8,128]{3,2,1,0:T(8,128)(2,1)} %param.15) | copy-start | bytes 1572868
  8.2 12.9 %copy-start.9 = (bf16[1,256,8,128]{3,2,1,0:T(8,128)(2,1)S(1)}, bf16[1,256,8,128]{3,2,1,0:T(8,128)(2,1)}, u32[]{:S(2)}) copy-start(bf16[1,256,8,128]{3,2,1,0:T(8,128)(2,1)} %param.16) | copy-start | bytes 1572868
  8.2 24.0 %all-to-all-start = ((bf16[16,128,128]{2,1,0:T(8,128)(2,1)}), bf16[16,128,128]{2,1,0:T(8,128)(2,1)S(1)}, u32[]{:S(2)}, u32[]{:S(2)}) async-start(bf16[16,128,128]{2,1,0:T(8,128)(2,1)} %broadcast_in_dim.46), calls=%async_computation | async-start | bytes 1048576 | tf_op jit(solution)/shard_map/all_to_all | solution.py:329
  17.0 7.7 %copy-start.10 = (bf16[32,8,128]{2,1,0:T(8,128)(2,1)S(1)}, bf16[32,8,128]{2,1,0:T(8,128)(2,1)}, u32[]{:S(2)}) copy-start(bf16[32,8,128]{2,1,0:T(8,128)(2,1)} %param.14) | copy-start | bytes 196612
  17.0 7.7 %copy-start.11 = (bf16[32,8,128]{2,1,0:T(8,128)(2,1)S(1)}, bf16[32,8,128]{2,1,0:T(8,128)(2,1)}, u32[]{:S(2)}) copy-start(bf16[32,8,128]{2,1,0:T(8,128)(2,1)} %param.13) | copy-start | bytes 196612
  17.0 8.4 %copy-start.12 = (s32[512]{0:T(512)S(1)}, s32[512]{0:T(512)}, u32[]{:S(2)}) copy-start(s32[512]{0:T(512)} %param.21) | copy-start | bytes 6148
  17.0 8.4 %copy-start.13 = (s32[16]{0:T(128)S(1)}, s32[16]{0:T(128)}, u32[]{:S(2)}) copy-start(s32[16]{0:T(128)} %param.22) | copy-start | bytes 196
  17.0 61.1 %all-gather.3.cloned.1.call-start = ((), (), s32[]{:S(2)}) async-start(), calls=%async_computation.4 | async-start | bytes 1179648 | tf_op jit(solution)/shard_map/all_gather | solution.py:400
  17.1 26.9 %copy-start.6 = (bf16[1,256,8,128]{3,1,2,0:T(8,128)(2,1)}, bf16[1,256,8,128]{3,1,2,0:T(8,128)(2,1)S(1)}, u32[]{:S(2)}) copy-start(bf16[1,256,8,128]{3,1,2,0:T(8,128)(2,1)S(1)} %copy.37) | copy-start | bytes 1572868
  17.1 31.2 %collective-permute-start.2 = (bf16[8,256,128]{2,1,0:T(8,128)(2,1)S(1)}, bf16[8,256,128]{2,1,0:T(8,128)(2,1)}, u32[]{:S(2)}, u32[]{:S(2)}) collective-permute-start(bf16[8,256,128]{2,1,0:T(8,128)(2,1)S(1)} %bitcast.39), channel_id=1, source_target_pairs={{0,16},{16,0},{1,17},{17,1},{2,18},{18,2},{3,19},{19,3},{4,20},{20... | collective-permute-start | bytes 1572872 | tf_op jit(solution)/shard_map/ppermute | solution.py:402
  21.2 24.7 %copy-start.7 = (bf16[1,256,8,128]{3,1,2,0:T(8,128)(2,1)}, bf16[1,256,8,128]{3,1,2,0:T(8,128)(2,1)S(1)}, u32[]{:S(2)}) copy-start(bf16[1,256,8,128]{3,1,2,0:T(8,128)(2,1)S(1)} %copy.36) | copy-start | bytes 1572868
  21.3 29.1 %collective-permute-start.3 = (bf16[8,256,128]{2,1,0:T(8,128)(2,1)S(1)}, bf16[8,256,128]{2,1,0:T(8,128)(2,1)}, u32[]{:S(2)}, u32[]{:S(2)}) collective-permute-start(bf16[8,256,128]{2,1,0:T(8,128)(2,1)S(1)} %bitcast.42), channel_id=1, source_target_pairs={{0,16},{16,0},{1,17},{17,1},{2,18},{18,2},{3,19},{19,3},{4,20},{20... | collective-permute-start | bytes 1572872 | tf_op jit(solution)/shard_map/ppermute | solution.py:403
  33.7 46.4 %all-to-all-start.1 = ((bf16[8,2,128,128]{3,2,1,0:T(8,128)(2,1)}), bf16[8,2,128,128]{3,2,1,0:T(8,128)(2,1)}, u32[]{:S(2)}, u32[]{:S(2)}) async-start(bf16[8,2,128,128]{3,2,1,0:T(8,128)(2,1)} %pick_readers.1), calls=%async_computation.1 | async-start | bytes 1048576 | tf_op jit(solution)/shard_map/all_to_all | solution.py:329
  44.0 36.0 %collective-permute-start = (bf16[8,256,128]{2,1,0:T(8,128)(2,1)S(1)}, bf16[8,256,128]{2,1,0:T(8,128)(2,1)}, u32[]{:S(2)}, u32[]{:S(2)}) collective-permute-start(bf16[8,256,128]{2,1,0:T(8,128)(2,1)S(1)} %bitcast.40), channel_id=1, source_target_pairs={{0,1},{1,0},{2,3},{3,2},{4,5},{5,4},{6,7},{7,6},{8,9},{9,8},{10,11... | collective-permute-start | bytes 1572872 | tf_op jit(solution)/shard_map/ppermute | solution.py:408
  46.0 34.1 %collective-permute-start.1 = (bf16[8,256,128]{2,1,0:T(8,128)(2,1)S(1)}, bf16[8,256,128]{2,1,0:T(8,128)(2,1)}, u32[]{:S(2)}, u32[]{:S(2)}) collective-permute-start(bf16[8,256,128]{2,1,0:T(8,128)(2,1)S(1)} %bitcast.43), channel_id=1, source_target_pairs={{0,1},{1,0},{2,3},{3,2},{4,5},{5,4},{6,7},{7,6},{8,9},{9,8},{10,11... | collective-permute-start | bytes 1572872 | tf_op jit(solution)/shard_map/ppermute | solution.py:409
  48.4 31.7 %collective-permute-start.4 = (bf16[8,256,128]{2,1,0:T(8,128)(2,1)}, bf16[8,256,128]{2,1,0:T(8,128)(2,1)}, u32[]{:S(2)}, u32[]{:S(2)}) collective-permute-start(bf16[8,256,128]{2,1,0:T(8,128)(2,1)} %collective-permute-done.2.refs_4_), channel_id=1, source_target_pairs={{0,1},{1,0},{2,3},{3,2},{4,5},{5,4},{6,7},{7,6},{8,9},{9,8},{10,11... | collective-permute-start | bytes 1572872 | tf_op jit(solution)/shard_map/ppermute | solution.py:412
  50.3 29.7 %collective-permute-start.5 = (bf16[8,256,128]{2,1,0:T(8,128)(2,1)}, bf16[8,256,128]{2,1,0:T(8,128)(2,1)}, u32[]{:S(2)}, u32[]{:S(2)}) collective-permute-start(bf16[8,256,128]{2,1,0:T(8,128)(2,1)} %collective-permute-done.3.refs_5_), channel_id=1, source_target_pairs={{0,1},{1,0},{2,3},{3,2},{4,5},{5,4},{6,7},{7,6},{8,9},{9,8},{10,11... | collective-permute-start | bytes 1572872 | tf_op jit(solution)/shard_map/ppermute | solution.py:413
  52.7 38.0 %collective-permute-start.6 = (bf16[16,128,128]{2,1,0:T(8,128)(2,1)S(1)}, bf16[16,128,128]{2,1,0:T(8,128)(2,1)S(1)}, u32[]{:S(2)}, u32[]{:S(2)}) collective-permute-start(bf16[16,128,128]{2,1,0:T(8,128)(2,1)S(1)} %all-to-all-done.peer_ref.q_ref), channel_id=1, source_target_pairs={{0,16},{16,0},{1,17},{17,1},{2,18},{18,2},{3,19},{19,3},{4,20},{20... | collective-permute-start | bytes 1572872 | tf_op jit(solution)/shard_map/ppermute | solution.py:401
  90.8 7.1 %collective-permute-start.7 = (bf16[8,8,64,128]{3,2,1,0:T(8,128)(2,1)S(1)}, bf16[8,8,64,128]{3,2,1,0:T(8,128)(2,1)S(1)}, u32[]{:S(2)}, u32[]{:S(2)}) collective-permute-start(bf16[8,8,64,128]{3,2,1,0:T(8,128)(2,1)S(1)} %bitcast.31), channel_id=1, source_target_pairs={{0,1},{1,0},{2,3},{3,2},{4,5},{5,4},{6,7},{7,6},{8,9},{9,8},{10,11... | collective-permute-start | bytes 3145736 | tf_op jit(solution)/shard_map/ppermute | solution.py:450
  92.7 32.3 %all-to-all-start.2 = ((f16[8,2,136,128]{3,2,1,0:T(8,128)(2,1)}), f16[8,2,136,128]{3,2,1,0:T(8,128)(2,1)}, u32[]{:S(2)}, u32[]{:S(2)}) async-start(f16[8,2,136,128]{3,2,1,0:T(8,128)(2,1)} %bitcast.38), calls=%async_computation.2 | async-start | bytes 1114112 | tf_op jit(solution)/shard_map/all_to_all | solution.py:329
  97.8 0.9 copy-start.4
  98.8 1.2 copy-start.5
  106.7 18.1 %collective-permute-start.8 = (f16[16,136,128]{2,1,0:T(8,128)(2,1)S(1)}, f16[16,136,128]{2,1,0:T(8,128)(2,1)S(1)}, u32[]{:S(2)}, u32[]{:S(2)}) collective-permute-start(f16[16,136,128]{2,1,0:T(8,128)(2,1)S(1)} %convert_element_type.23), channel_id=1, source_target_pairs={{0,16},{16,0},{1,17},{17,1},{2,18},{18,2},{3,19},{19,3},{4,20},{20... | collective-permute-start | bytes 1671176 | tf_op jit(solution)/shard_map/ppermute | solution.py:465
  128.3 8.6 %copy-start = (bf16[1,512,8,128]{3,2,1,0:T(8,128)(2,1)S(1)}, bf16[1,512,8,128]{3,2,1,0:T(8,128)(2,1)}, u32[]{:S(2)}) copy-start(bf16[1,512,8,128]{3,2,1,0:T(8,128)(2,1)} %param.17) | copy-start | bytes 3145732
  128.3 8.6 %copy-start.1 = (bf16[1,512,8,128]{3,2,1,0:T(8,128)(2,1)S(1)}, bf16[1,512,8,128]{3,2,1,0:T(8,128)(2,1)}, u32[]{:S(2)}) copy-start(bf16[1,512,8,128]{3,2,1,0:T(8,128)(2,1)} %param.18) | copy-start | bytes 3145732
  128.3 8.6 %copy-start.2 = (bf16[1,2,8,128]{3,2,1,0:T(8,128)(2,1)S(1)}, bf16[1,2,8,128]{3,2,1,0:T(8,128)(2,1)}, u32[]{:S(2)}) copy-start(bf16[1,2,8,128]{3,2,1,0:T(8,128)(2,1)} %param.19) | copy-start | bytes 12292
  128.3 8.6 %copy-start.3 = (bf16[1,2,8,128]{3,2,1,0:T(8,128)(2,1)S(1)}, bf16[1,2,8,128]{3,2,1,0:T(8,128)(2,1)}, u32[]{:S(2)}) copy-start(bf16[1,2,8,128]{3,2,1,0:T(8,128)(2,1)} %param.20) | copy-start | bytes 12292
  129.2 22.8 %all-to-all-start.3 = ((f16[16,136,128]{2,1,0:T(8,128)(2,1)}), f16[16,136,128]{2,1,0:T(8,128)(2,1)S(1)}, u32[]{:S(2)}, u32[]{:S(2)}) async-start(f16[16,136,128]{2,1,0:T(8,128)(2,1)} %convert_element_type.26), calls=%async_computation.3 | async-start | bytes 1114112 | tf_op jit(solution)/shard_map/all_to_all | solution.py:329
Sparse Core Ops, SparseCore 0:
  25.4 52.6 all-gather.2

commit v5 on v4

--- a/solution.py
+++ b/solution.py
@@ -12,7 +12,7 @@
 PAD = 8
 LOW = -1e30
 PARTS = 4
-EMPHASIS = 30
+EMPHASIS = 18
 NT = (((1,), (1,)), ((), ()))
 
 
@@ -88,8 +88,8 @@
     out_ref[...] = jnp.broadcast_to(peer_ref[...][None], out_ref.shape)
 
 
-def staged(heads, per_head, queries, results, q_sems, out_sems, feeds, feed_sem):
-    parts = out_sems.shape[1] - 1
+def staged(heads, per_head, q_ref, out_ref, q_held, out_held, q_sem, out_sems, feeds, feed_sem):
+    parts = out_sems.shape[0] - 1
     group = heads // parts
     reads = [
         [
@@ -98,29 +98,27 @@
         ]
         for part in range(parts)
     ]
-    q_copies = [
-        pltpu.make_async_copy(ref, held, q_sems.at[place])
-        for place, (ref, held) in enumerate(queries)
-    ]
-    for copy in q_copies:
-        copy.start()
+    q_copy = pltpu.make_async_copy(q_ref, q_held, q_sem)
+    q_copy.start()
     for copies in reads:
         for copy in copies:
             copy.start()
-    for copy in q_copies:
-        copy.wait()
+    q_copy.wait()
     span = group * per_head
-    pieces = [pl.ds(part * span, span) for part in range(parts)]
-    pieces.append(pl.ds(heads * per_head, PAD))
     writes = [
-        [
-            pltpu.make_async_copy(
-                held.at[:, piece, :], ref.at[:, piece, :], out_sems.at[place, part]
-            )
-            for place, (ref, held) in enumerate(results)
-        ]
-        for part, piece in enumerate(pieces)
+        pltpu.make_async_copy(
+            out_held.at[:, pl.ds(part * span, span), :],
+            out_ref.at[:, pl.ds(part * span, span), :],
+            out_sems.at[part],
+        )
+        for part in range(parts)
     ]
+    tail = pl.ds(heads * per_head, PAD)
+    writes.append(
+        pltpu.make_async_copy(
+            out_held.at[:, tail, :], out_ref.at[:, tail, :], out_sems.at[parts]
+        )
+    )
 
     def enter(head):
         if head % group == 0:
@@ -129,22 +127,19 @@
 
     def leave(head):
         if (head + 1) % group == 0:
-            for copy in writes[head // group]:
-                copy.start()
+            writes[head // group].start()
 
     def finish():
-        for copy in writes[-1]:
-            copy.start()
-        for copies in writes:
-            for copy in copies:
-                copy.wait()
+        writes[-1].start()
+        for copy in writes:
+            copy.wait()
 
     return enter, leave, finish
 
 
 def branch_kernel(count, q_ref, *refs):
     sources, out_ref = refs[:count], refs[count]
-    held, q_held, out_held, sems, q_sems, out_sems = refs[count + 1 :]
+    held, q_held, out_held, sems, q_sem, out_sems = refs[count + 1 :]
     slots, lanes, dim = q_ref.shape
     heads = sources[0].shape[0]
     per_head = lanes // heads
@@ -159,9 +154,11 @@
     enter, leave, finish = staged(
         heads,
         per_head,
-        [(q_ref, q_held.at[0])],
-        [(out_ref, out_held.at[0])],
-        q_sems,
+        q_ref,
+        out_ref,
+        q_held,
+        out_held,
+        q_sem,
         out_sems,
         [feed(place, ref) for place, ref in enumerate(sources)],
         lambda place, part: sems.at[place, part],
@@ -170,7 +167,7 @@
     for head in range(heads):
         enter(head)
         place = slice(head * per_head, (head + 1) * per_head)
-        q = q_held[0, :, place, :].reshape(slots * per_head, dim)
+        q = q_held[:, place, :].reshape(slots * per_head, dim)
         found = []
         for block in range(0, count, 2):
             scores = scores_of(q, held[block, head])
@@ -182,21 +179,21 @@
         factors = [jnp.exp(f[0] - high) for f in found]
         den = sum(factor * f[1] for factor, f in zip(factors, found))
         num = sum(f[2] * (factor / den) for factor, f in zip(factors, found))
-        out_held[0, :, place, :] = num.reshape(slots, per_head, dim)
+        out_held[:, place, :] = num.reshape(slots, per_head, dim)
         tail = tail + head_lse(high + jnp.log(den), head, per_head, lanes)
         leave(head)
-    out_held[0, :, lanes:, :] = tail_rows(split_lse(tail))
+    out_held[:, lanes:, :] = tail_rows(split_lse(tail))
     finish()
 
 
-def root_kernel(count, q_ref, q_far_ref, *refs):
-    sources, out_refs = refs[:count], refs[count : count + 2]
-    held, q_held, out_held, sems, q_sems, out_sems = refs[count + 2 :]
+def root_kernel(count, q_ref, *refs):
+    sources, out_ref = refs[:count], refs[count]
+    held, q_held, out_held, sems, q_sem, out_sems = refs[count + 1 :]
     requests, lanes, dim = q_ref.shape
     blocks, heads, half = held.shape[1], held.shape[2], held.shape[3] // 2
     per_head = lanes // heads
     group = heads // sems.shape[1]
-    span = count * blocks * half
+    span = blocks * half
 
     def feed(place, ref):
         def some(part):
@@ -207,31 +204,34 @@
     enter, leave, finish = staged(
         heads,
         per_head,
-        [(ref, q_held.at[i]) for i, ref in enumerate((q_ref, q_far_ref))],
-        [(ref, out_held.at[i]) for i, ref in enumerate(out_refs)],
-        q_sems,
+        q_ref,
+        out_ref,
+        q_held,
+        out_held,
+        q_sem,
         out_sems,
         [feed(place, ref) for place, ref in enumerate(sources)],
         lambda place, part: sems.at[place, part],
     )
-    tails = [jnp.zeros((requests, 1, lanes), jnp.float32) for _ in out_refs]
+    tail = jnp.zeros((requests, 1, lanes), jnp.float32)
     for head in range(heads):
         enter(head)
         place = slice(head * per_head, (head + 1) * per_head)
-        keys = held[:, :, head, :half, :].reshape(span, dim)
-        values = held[:, :, head, half:, :].reshape(span, dim)
-        for i in range(len(tails)):
-            q = q_held[i, :, place, :].reshape(requests * per_head, dim)
-            scores = scores_of(q, keys)
-            high = jnp.max(scores, axis=1, keepdims=True)
-            weights = jnp.exp(scores - high)
-            den = jnp.sum(weights, axis=1, keepdims=True)
-            num = times_values(weights, values) / den
-            out_held[i, :, place, :] = num.reshape(requests, per_head, dim)
-            tails[i] = tails[i] + head_lse(high + jnp.log(den), head, per_head, lanes)
+        q = q_held[:, place, :].reshape(requests * per_head, dim)
+        scores = [scores_of(q, held[i, :, head, :half, :].reshape(span, dim)) for i in range(count)]
+        high = functools.reduce(
+            jnp.maximum, [jnp.max(s, axis=1, keepdims=True) for s in scores]
+        )
+        weights = [jnp.exp(s - high) for s in scores]
+        den = sum(jnp.sum(w, axis=1, keepdims=True) for w in weights)
+        num = sum(
+            times_values(w, held[i, :, head, half:, :].reshape(span, dim))
+            for i, w in enumerate(weights)
+        )
+        out_held[:, place, :] = (num / den).reshape(requests, per_head, dim)
+        tail = tail + head_lse(high + jnp.log(den), head, per_head, lanes)
         leave(head)
-    for i, tail in enumerate(tails):
-        out_held[i, :, lanes:, :] = tail_rows(split_lse(tail))
+    out_held[:, lanes:, :] = tail_rows(split_lse(tail))
     finish()
 
 
@@ -241,23 +241,9 @@
     return jnp.concatenate([table, rest], axis=0).T
 
 
-def merge_kernel(idx_ref, part_ref, own_ref, far_ref, out_ref):
+def merge_kernel(idx_ref, part_ref, root_ref, out_ref):
     sources, cap, _, lanes = part_ref.shape
-    groups = own_ref.shape[0]
-    lse_a = join_lse(own_ref[:, lanes:, :])
-    lse_b = join_lse(far_ref[:, lanes:, :])
-    high = jnp.maximum(lse_a, lse_b)
-    factor_a = jnp.exp(lse_a - high)
-    factor_b = jnp.exp(lse_b - high)
-    total = factor_a + factor_b
-    table = columns(jnp.concatenate([factor_a / total, factor_b / total], axis=0))
-    pieces = split_lse(high + jnp.log(total))
-    for r in range(groups):
-        out_ref[r, :lanes, :] = (
-            own_ref[r, :lanes, :] * table[:, r : r + 1]
-            + far_ref[r, :lanes, :] * table[:, groups + r : groups + r + 1]
-        )
-        out_ref[r, lanes:, :] = tail_rows([piece[r : r + 1] for piece in pieces])
+    out_ref[...] = root_ref[...]
     for k in range(cap):
         reader = idx_ref[k]
 
@@ -314,14 +300,14 @@
     return pl.BlockSpec(memory_space=pltpu.SMEM)
 
 
-def scratch(count, block, q, sets):
+def scratch(count, block, q):
     return [
         pltpu.VMEM((count,) + block.shape, jnp.bfloat16),
-        pltpu.VMEM((sets,) + q.shape, jnp.bfloat16),
-        pltpu.VMEM((sets, q.shape[0], q.shape[1] + PAD, q.shape[2]), jnp.float32),
+        pltpu.VMEM(q.shape, jnp.bfloat16),
+        pltpu.VMEM((q.shape[0], q.shape[1] + PAD, q.shape[2]), jnp.float32),
         pltpu.SemaphoreType.DMA((count, PARTS)),
-        pltpu.SemaphoreType.DMA((sets,)),
-        pltpu.SemaphoreType.DMA((sets, PARTS + 1)),
+        pltpu.SemaphoreType.DMA(()),
+        pltpu.SemaphoreType.DMA((PARTS + 1,)),
     ]
 
 
@@ -393,12 +379,13 @@
         )(readers, peers)
         return exchange(packed, "z")
 
-    keys_own = branch_keys[0].transpose(1, 0, 2)
-    values_own = branch_values[0].transpose(1, 0, 2)
     root_block = jnp.concatenate([root_keys, root_values], axis=0).transpose(1, 0, 2)
-    root_block = lax.optimization_barrier(root_block)
-    root_own = lax.all_gather(root_block, "z")
-    peers_far = lax.ppermute(peers, "xhi", swap)
+    pair = jnp.stack([root_block, lax.ppermute(root_block, "xhi", swap)])
+    pair, keys_own, values_own = lax.optimization_barrier((pair, branch_keys[0], branch_values[0]))
+    root_own = lax.all_gather(pair, "z", axis=0, tiled=True)
+    keys_own = keys_own.transpose(1, 0, 2)
+    values_own = values_own.transpose(1, 0, 2)
+    peers, _ = lax.optimization_barrier((peers, pair))
     keys_far = lax.ppermute(keys_own, "xhi", swap)
     values_far = lax.ppermute(values_own, "xhi", swap)
     slots = gather_readers(peers)
@@ -440,39 +427,38 @@
         out_shape=jax.ShapeDtypeStruct((ring * CAP, rows + PAD, dim), jnp.float32),
         in_specs=[anywhere()] * (1 + count),
         out_specs=anywhere(),
-        scratch_shapes=scratch(count, keys_own, slots, 1),
+        scratch_shapes=scratch(count, keys_own, slots),
         compiler_params=params(54),
         cost_estimate=estimate(area, dim),
         name="branch_attention",
     )(slots, *branch_blocks)
     parts = parts.astype(jnp.float16).reshape(ring, CAP, rows + PAD, dim)
-    peers, peers_far, root_own, _ = lax.optimization_barrier((peers, peers_far, root_own, parts))
+    peers, root_own, _ = lax.optimization_barrier((peers, root_own, parts))
     root_blocks = [root_own, lax.ppermute(root_own, "core", swap)]
     parts = exchange(parts, "z")
 
     whole = jax.ShapeDtypeStruct((grp, rows + PAD, dim), jnp.float32)
     count = len(root_blocks)
-    root, root_far = pl.pallas_call(
+    root = pl.pallas_call(
         functools.partial(root_kernel, count),
-        out_shape=(whole, whole),
-        in_specs=[anywhere()] * (2 + count),
-        out_specs=(anywhere(), anywhere()),
-        scratch_shapes=scratch(count, root_own, peers, 2),
+        out_shape=whole,
+        in_specs=[anywhere()] * (1 + count),
+        out_specs=anywhere(),
+        scratch_shapes=scratch(count, root_own, peers),
         compiler_params=params(),
         cost_estimate=estimate(area, dim),
         name="root_attention",
-    )(peers, peers_far, *root_blocks)
-    root_far = lax.ppermute(root_far.astype(jnp.float16), "xhi", swap).astype(jnp.float32)
-    parts, root, root_far = lax.optimization_barrier((parts, root, root_far))
+    )(peers, *root_blocks)
+    parts, root = lax.optimization_barrier((parts, root))
     parts = parts.astype(jnp.float32)
     merged = pl.pallas_call(
         merge_kernel,
         out_shape=whole,
-        in_specs=[smem()] + [vmem()] * 3,
+        in_specs=[smem()] + [vmem()] * 2,
         out_specs=vmem(),
         compiler_params=params(),
         name="merge_parts",
-    )(readers, parts, root, root_far)
+    )(readers, parts, root)
     back = exchange(merged.astype(jnp.float16), "grp").astype(jnp.float32)
     mine = pl.pallas_call(
         final_kernel,

time: 162 us -> 144 us (0.89)
  waiting for transfers between devices: 56.9 us -> 41.1 us
  local copies, waits for them, and re-layouts: 6.68 us -> 11.5 us
  starting transfers between devices: 55.8 us -> 52.9 us
  Pallas kernels: 20.8 us -> 18 us
    all_gather x1, waiting for transfers between devices: 22 us -> 0.01 us  [shards(): root_own = lax.all_gather(pair, 'z', axis=0, tiled=True)]
    all_to_all x4, waiting for transfers between devices: 20 us -> 40 us  [exchange(): return lax.all_to_all(blocks, axis, split_axis=0, concat_axis=0, tiled=True)]
    ppermute x2 -> x1, waiting for transfers between devices: 14.8 us -> 0.01 us  [shards(): pair = jnp.stack([root_block, lax.ppermute(root_block, 'xhi', swap)])]
    unnamed x30 -> x39, local copies, waits for them, and re-layouts: 2.37 us -> 8.08 us
    ppermute x2 -> x1, starting transfers between devices: 6.66 us -> 3.31 us  [shards(): pair = jnp.stack([root_block, lax.ppermute(root_block, 'xhi', swap)])]
    all_gather x1 -> x0, local copies, waits for them, and re-layouts: 1.9 us -> none  [shards(): root_own = lax.all_gather(root_block, 'z')]
  transfers between devices with their start and end apart: 14 -> 13, of which waited for: 4 -> 7; matrix products, arithmetic and copies ran while one was open for 3% -> 4% of each run, Pallas kernels for 11% -> 12%
where the time goes in v5:
time: 144 us; the launch traced here: 142 us
  starting transfers between devices  52.9 us (37%)
  waiting for transfers between devices  41.1 us (29%)
  Pallas kernels  18 us (12%)
  between operations  14.4 us (10%)
  local copies, waits for them, and re-layouts  11.5 us (8%)
  other arithmetic  4.5 us (3%)
    all_to_all x4, waiting for transfers between devices, exchange(): return lax.all_to_all(blocks, axis, split_axis=0, concat_axis=0, tiled=True)  40 us
    all_to_all x4, starting transfers between devices, exchange(): return lax.all_to_all(blocks, axis, split_axis=0, concat_axis=0, tiled=True)  32 us
    pallas_call x1, Pallas kernels, shards(): pl.pallas_call(functools.partial(branch_kernel, count), out_shape=jax.Sha...  8.59 us
    unnamed x39, local copies, waits for them, and re-layouts  8.08 us
    pallas_call x1, Pallas kernels, shards(): pl.pallas_call(functools.partial(root_kernel, count), out_shape=whole, in...  5.36 us
    ppermute x1, starting transfers between devices, shards(): keys_far = lax.ppermute(keys_own, 'xhi', swap)  3.95 us
    ppermute x1, starting transfers between devices, shards(): values_far = lax.ppermute(values_own, 'xhi', swap)  3.4 us
    ppermute x1, starting transfers between devices, shards(): pair = jnp.stack([root_block, lax.ppermute(root_block, 'xhi', swap)])  3.31 us
  transfers between devices with their start and end apart: 13, of which 7 were waited for; matrix products, arithmetic and copies ran while one was open for 4% of the time, Pallas kernels for 12%

profile of v5, /device:TPU:6, one launch (start us, length us, event | category | flops | bytes accessed | tf_op | source)
XLA Modules:
  0.0 142.4 jit_solution(7271836854425841059)
XLA Ops:
  6.5 0.9 copy_dynamic-update-slice_fusion.1
  7.5 0.9 copy_dynamic-update-slice_fusion
  8.3 3.3 %collective-permute-start = (bf16[8,64,128]{2,1,0:T(8,128)(2,1)S(1)}, bf16[8,64,128]{2,1,0:T(8,128)(2,1)S(1)}, u32[]{:S(2)}, u32[]{:S(2)}) collective-permute-start(bf16[8,64,128]{2,1,0:T(8,128)(2,1)S(1)} %bitcast.40), channel_id=1, source_target_pairs={{0,16},{16,0},{1,17},{17,1},{2,18},{18,2},{3,19},{19,3},{4,20},{20... | collective-permute-start | bytes 393224 | tf_op jit(solution)/shard_map/ppermute | solution.py:383
  11.7 0.8 copy.37
  12.4 0.9 broadcast_in_dim.46
  13.3 8.7 %all-to-all-start = ((bf16[16,128,128]{2,1,0:T(8,128)(2,1)}), bf16[16,128,128]{2,1,0:T(8,128)(2,1)S(1)}, u32[]{:S(2)}, u32[]{:S(2)}) async-start(bf16[16,128,128]{2,1,0:T(8,128)(2,1)} %broadcast_in_dim.46), calls=%async_computation | async-start | bytes 1048576 | tf_op jit(solution)/shard_map/all_to_all | solution.py:315
  22.0 0.0 copy-start.18
  22.0 0.0 all-gather.2.cloned.1.call-start
  22.1 0.2 copy_bitcast_fusion
  22.3 0.0 copy-start.9
  22.3 0.0 copy-start.8
  22.3 0.0 collective-permute-done
  22.3 0.8 pad_maximum_fusion
  23.1 0.0 all-gather.2.cloned.1.call-update
  23.2 0.1 select_reduce_fusion
  23.2 0.1 reshape.39
  23.3 0.2 fusion
  23.5 0.1 convert_reduce_fusion
  23.6 0.1 fusion.2.idx_ref
  23.8 3.9 %collective-permute-start.3 = (bf16[8,256,128]{2,1,0:T(8,128)(2,1)S(1)}, bf16[8,256,128]{2,1,0:T(8,128)(2,1)S(1)}, u32[]{:S(2)}, u32[]{:S(2)}) collective-permute-start(bf16[8,256,128]{2,1,0:T(8,128)(2,1)S(1)} %bitcast.37), channel_id=1, source_target_pairs={{0,16},{16,0},{1,17},{17,1},{2,18},{18,2},{3,19},{19,3},{4,20},{20... | collective-permute-start | bytes 1572872 | tf_op jit(solution)/shard_map/ppermute | solution.py:389
  27.7 3.4 %collective-permute-start.4 = (bf16[8,256,128]{2,1,0:T(8,128)(2,1)S(1)}, bf16[8,256,128]{2,1,0:T(8,128)(2,1)S(1)}, u32[]{:S(2)}, u32[]{:S(2)}) collective-permute-start(bf16[8,256,128]{2,1,0:T(8,128)(2,1)S(1)} %bitcast.34), channel_id=1, source_target_pairs={{0,16},{16,0},{1,17},{17,1},{2,18},{18,2},{3,19},{19,3},{4,20},{20... | collective-permute-start | bytes 1572872 | tf_op jit(solution)/shard_map/ppermute | solution.py:390
  31.1 6.1 %all-to-all-done.peer_ref.q_ref = bf16[16,128,128]{2,1,0:T(8,128)(2,1)S(1)} async-done(((bf16[16,128,128]{2,1,0:T(8,128)(2,1)}), bf16[16,128,128]{2,1,0:T(8,128)(2,1)S(1)}, u32[]{:S(2)}, u32[]{:S(2)}) %all-to-all-start) | async-done | bytes 524320 | tf_op jit(solution)/shard_map/all_to_all | solution.py:315
  37.2 1.4 pick_readers.1
  38.6 10.3 %all-to-all-start.1 = ((bf16[8,2,128,128]{3,2,1,0:T(8,128)(2,1)}), bf16[8,2,128,128]{3,2,1,0:T(8,128)(2,1)S(1)}, u32[]{:S(2)}, u32[]{:S(2)}) async-start(bf16[8,2,128,128]{3,2,1,0:T(8,128)(2,1)} %pick_readers.1), calls=%async_computation.1 | async-start | bytes 1048576 | tf_op jit(solution)/shard_map/all_to_all | solution.py:315
  48.9 1.9 %collective-permute-start.1 = (bf16[8,256,128]{2,1,0:T(8,128)(2,1)S(1)}, bf16[8,256,128]{2,1,0:T(8,128)(2,1)S(1)}, u32[]{:S(2)}, u32[]{:S(2)}) collective-permute-start(bf16[8,256,128]{2,1,0:T(8,128)(2,1)S(1)} %bitcast.38), channel_id=1, source_target_pairs={{0,1},{1,0},{2,3},{3,2},{4,5},{5,4},{6,7},{7,6},{8,9},{9,8},{10,11... | collective-permute-start | bytes 1572872 | tf_op jit(solution)/shard_map/ppermute | solution.py:395
  50.9 0.0 copy-done.8
  50.9 2.4 %collective-permute-start.2 = (bf16[8,256,128]{2,1,0:T(8,128)(2,1)S(1)}, bf16[8,256,128]{2,1,0:T(8,128)(2,1)S(1)}, u32[]{:S(2)}, u32[]{:S(2)}) collective-permute-start(bf16[8,256,128]{2,1,0:T(8,128)(2,1)S(1)} %bitcast.35), channel_id=1, source_target_pairs={{0,1},{1,0},{2,3},{3,2},{4,5},{5,4},{6,7},{7,6},{8,9},{9,8},{10,11... | collective-permute-start | bytes 1572872 | tf_op jit(solution)/shard_map/ppermute | solution.py:396
  53.3 0.0 collective-permute-done.3.refs_4_
  53.3 0.0 copy-start.10
  53.3 1.9 %collective-permute-start.5 = (bf16[8,256,128]{2,1,0:T(8,128)(2,1)S(1)}, bf16[8,256,128]{2,1,0:T(8,128)(2,1)S(1)}, u32[]{:S(2)}, u32[]{:S(2)}) collective-permute-start(bf16[8,256,128]{2,1,0:T(8,128)(2,1)S(1)} %collective-permute-done.3.refs_4_), channel_id=1, source_target_pairs={{0,1},{1,0},{2,3},{3,2},{4,5},{5,4},{6,7},{7,6},{8,9},{9,8},{10,11... | collective-permute-start | bytes 1572872 | tf_op jit(solution)/shard_map/ppermute | solution.py:399
  55.2 0.4 collective-permute-done.4.refs_5_
  55.7 2.0 %collective-permute-start.6 = (bf16[8,256,128]{2,1,0:T(8,128)(2,1)S(1)}, bf16[8,256,128]{2,1,0:T(8,128)(2,1)}, u32[]{:S(2)}, u32[]{:S(2)}) collective-permute-start(bf16[8,256,128]{2,1,0:T(8,128)(2,1)S(1)} %collective-permute-done.4.refs_5_), channel_id=1, source_target_pairs={{0,1},{1,0},{2,3},{3,2},{4,5},{5,4},{6,7},{7,6},{8,9},{9,8},{10,11... | collective-permute-start | bytes 1572872 | tf_op jit(solution)/shard_map/ppermute | solution.py:400
  57.7 0.0 collective-permute-done.1.refs_2_
  57.7 0.0 collective-permute-done.2.refs_3_
  57.7 0.0 collective-permute-done.5.refs_6_
  57.7 0.8 copy-done.12
  58.5 0.2 copy-done.13
  58.7 0.8 copy-done.14
  59.5 0.1 collective-permute-done.6.refs_7_
  59.6 11.7 %all-to-all-done.1 = bf16[8,2,128,128]{3,2,1,0:T(8,128)(2,1)S(1)} async-done(((bf16[8,2,128,128]{3,2,1,0:T(8,128)(2,1)}), bf16[8,2,128,128]{3,2,1,0:T(8,128)(2,1)S(1)}, u32[]{:S(2)}, u32[]{:S(2)}) %all-to-all-start.1) | async-done | bytes 524320 | tf_op jit(solution)/shard_map/all_to_all | solution.py:315
  71.3 0.8 copy-done.7
  72.1 8.6 %branch_attention.1 = f32[16,136,128]{2,1,0:T(8,128)} custom-call(bf16[16,128,128]{2,1,0:T(8,128)(2,1)} %bitcast.33, bf16[8,256,128]{2,1,0:T(8,128)(2,1)} %bitcast.39, bf16[8,256,128]{2,1,0:T(8,128)(2,1)} %bitcast.36, bf16[8,256,128]{2,1,0:T(8,128)(2,1)} %copy-done.12, bf16[8,256,128]{2,1,0:T(8,128)(2,1)} %copy-done.13, bf16[8,256,128]{2,1,0:T(8,128)(2,1)} %copy-done.10, ...), custom_call_target="tpu_custom_call" | custom-call | flops 1073741824 | bytes 6291456 | tf_op jit(solution)/shard_map/branch_attention/pallas_call | solution.py:425
  80.7 2.1 %convert_element_type.16 = f16[16,136,128]{2,1,0:T(8,128)(2,1)} convert(f32[16,136,128]{2,1,0:T(8,128)} %branch_attention.1) | non-fusion elementwise | flops 278528 | bytes 1671168 | tf_op jit(solution)/shard_map/convert_element_type | solution.py:435
  82.9 1.9 %collective-permute-start.7 = (bf16[16,8,64,128]{3,2,1,0:T(8,128)(2,1)}, bf16[16,8,64,128]{3,2,1,0:T(8,128)(2,1)S(1)}, u32[]{:S(2)}, u32[]{:S(2)}) collective-permute-start(bf16[16,8,64,128]{3,2,1,0:T(8,128)(2,1)} %all-gather.2.cloned.1.call-done.refs_0_), channel_id=1, source_target_pairs={{0,1},{1,0},{2,3},{3,2},{4,5},{5,4},{6,7},{7,6},{8,9},{9,8},{10,11... | collective-permute-start | bytes 6291464 | tf_op jit(solution)/shard_map/ppermute | solution.py:437
  84.8 3.7 %all-to-all-start.2 = ((f16[8,2,136,128]{3,2,1,0:T(8,128)(2,1)}), f16[8,2,136,128]{3,2,1,0:T(8,128)(2,1)S(1)}, u32[]{:S(2)}, u32[]{:S(2)}) async-start(f16[8,2,136,128]{3,2,1,0:T(8,128)(2,1)} %bitcast.11), calls=%async_computation.2 | async-start | bytes 1114112 | tf_op jit(solution)/shard_map/all_to_all | solution.py:315
  88.5 0.6 collective-permute-done.7.refs_1_
  89.1 1.3 copy-done.1
  90.4 1.6 %copy-done = bf16[16,8,64,128]{3,2,1,0:T(8,128)(2,1)S(1)} copy-done((bf16[16,8,64,128]{3,2,1,0:T(8,128)(2,1)S(1)}, bf16[16,8,64,128]{3,2,1,0:T(8,128)(2,1)}, u32[]{:S(2)}) %copy-start) | copy-done | bytes 2097176
  92.0 1.6 %copy-done.2 = bf16[16,8,64,128]{3,2,1,0:T(8,128)(2,1)S(1)} copy-done((bf16[16,8,64,128]{3,2,1,0:T(8,128)(2,1)S(1)}, bf16[16,8,64,128]{3,2,1,0:T(8,128)(2,1)}, u32[]{:S(2)}) %copy-start.2) | copy-done | bytes 2097176
  93.6 5.4 %root_attention.1.root_ref = f32[16,136,128]{2,1,0:T(8,128)S(1)} custom-call(bf16[16,128,128]{2,1,0:T(8,128)(2,1)S(1)} %all-to-all-done.peer_ref.q_ref, bf16[16,8,64,128]{3,2,1,0:T(8,128)(2,1)S(1)} %copy-done, bf16[16,8,64,128]{3,2,1,0:T(8,128)(2,1)S(1)} %copy-done.2), custom_call_target="tpu_custom_call" | custom-call | flops 1073741824 | bytes 6291456 | tf_op jit(solution)/shard_map/root_attention/pallas_call | solution.py:442
  99.0 7.1 %all-to-all-done.2 = f16[8,2,136,128]{3,2,1,0:T(8,128)(2,1)S(1)} async-done(((f16[8,2,136,128]{3,2,1,0:T(8,128)(2,1)}), f16[8,2,136,128]{3,2,1,0:T(8,128)(2,1)S(1)}, u32[]{:S(2)}, u32[]{:S(2)}) %all-to-all-start.2) | async-done | bytes 557088 | tf_op jit(solution)/shard_map/all_to_all | solution.py:315
  106.1 0.1 convert_element_type.17.part_ref
  106.2 0.6 merge_parts.1
  106.8 0.0 copy-start.3
  106.8 0.0 copy-start.4
  106.8 0.0 copy-start.5
  106.9 0.0 copy-start.6
  106.9 0.9 convert_element_type.18
  107.8 9.3 %all-to-all-start.3 = ((f16[16,136,128]{2,1,0:T(8,128)(2,1)}), f16[16,136,128]{2,1,0:T(8,128)(2,1)S(1)}, u32[]{:S(2)}, u32[]{:S(2)}) async-start(f16[16,136,128]{2,1,0:T(8,128)(2,1)} %convert_element_type.18), calls=%async_computation.3 | async-start | bytes 1114112 | tf_op jit(solution)/shard_map/all_to_all | solution.py:315
  117.8 1.5 %local_attention.1.local_ref = f32[136,128]{1,0:T(8,128)S(1)} custom-call(s32[1]{0:T(128)S(6)} %copy.50.len_ref, bf16[128,128]{1,0:T(8,128)(2,1)S(1)} %bitcast.29, bf16[4096,128]{1,0:T(8,128)(2,1)S(1)} %bitcast.26, bf16[4096,128]{1,0:T(8,128)(2,1)S(1)} %bitcast.27, bf16[16,128]{1,0:T(8,128)(2,1)S(1)} %bitcast.31, bf16[16,128]{1,0:T(8,128)(2,1)S(1)} %bitcast.32), custom_call_target="tpu_custom_call" | custom-call | flops 268435456 | bytes 2097152 | tf_op jit(solution)/shard_map/local_attention/pallas_call | solution.py:403
  119.2 15.1 %all-to-all-done.3 = f16[16,136,128]{2,1,0:T(8,128)(2,1)S(1)} async-done(((f16[16,136,128]{2,1,0:T(8,128)(2,1)}), f16[16,136,128]{2,1,0:T(8,128)(2,1)S(1)}, u32[]{:S(2)}, u32[]{:S(2)}) %all-to-all-start.3) | async-done | bytes 557088 | tf_op jit(solution)/shard_map/all_to_all | solution.py:315
  134.3 0.1 convert_element_type.19.part_ref
  134.4 0.5 final_merge.1
  134.9 0.6 copy.48
  (23 shorter events, 0.0 us)
Async XLA Ops:
  6.5 15.5 %copy-start.16 = (bf16[1,256,8,128]{3,2,1,0:T(8,128)(2,1)S(1)}, bf16[1,256,8,128]{3,2,1,0:T(8,128)(2,1)}, u32[]{:S(2)}) copy-start(bf16[1,256,8,128]{3,2,1,0:T(8,128)(2,1)} %param.15) | copy-start | bytes 1572868
  6.5 15.5 %copy-start.15 = (bf16[1,256,8,128]{3,2,1,0:T(8,128)(2,1)S(1)}, bf16[1,256,8,128]{3,2,1,0:T(8,128)(2,1)}, u32[]{:S(2)}) copy-start(bf16[1,256,8,128]{3,2,1,0:T(8,128)(2,1)} %param.16) | copy-start | bytes 1572868
  8.3 14.0 %collective-permute-start = (bf16[8,64,128]{2,1,0:T(8,128)(2,1)S(1)}, bf16[8,64,128]{2,1,0:T(8,128)(2,1)S(1)}, u32[]{:S(2)}, u32[]{:S(2)}) collective-permute-start(bf16[8,64,128]{2,1,0:T(8,128)(2,1)S(1)} %bitcast.40), channel_id=1, source_target_pairs={{0,16},{16,0},{1,17},{17,1},{2,18},{18,2},{3,19},{19,3},{4,20},{20... | collective-permute-start | bytes 393224 | tf_op jit(solution)/shard_map/ppermute | solution.py:383
  13.3 23.9 %all-to-all-start = ((bf16[16,128,128]{2,1,0:T(8,128)(2,1)}), bf16[16,128,128]{2,1,0:T(8,128)(2,1)S(1)}, u32[]{:S(2)}, u32[]{:S(2)}) async-start(bf16[16,128,128]{2,1,0:T(8,128)(2,1)} %broadcast_in_dim.46), calls=%async_computation | async-start | bytes 1048576 | tf_op jit(solution)/shard_map/all_to_all | solution.py:315
  22.0 1.1 copy-start.17
  22.0 1.1 copy-start.18
  22.0 60.9 %all-gather.2.cloned.1.call-start = ((), (), s32[]{:S(2)}) async-start(), calls=%async_computation.4 | async-start | bytes 2359296 | tf_op jit(solution)/shard_map/all_gather | solution.py:385
  22.3 26.6 %copy-start.9 = (bf16[256,8,128]{2,0,1:T(8,128)(2,1)}, bf16[256,8,128]{2,0,1:T(8,128)(2,1)S(1)}, u32[]{:S(2)}) copy-start(bf16[256,8,128]{2,0,1:T(8,128)(2,1)S(1)} %get-tuple-element.15) | copy-start | bytes 1572868
  22.3 28.6 %copy-start.8 = (bf16[256,8,128]{2,0,1:T(8,128)(2,1)}, bf16[256,8,128]{2,0,1:T(8,128)(2,1)S(1)}, u32[]{:S(2)}) copy-start(bf16[256,8,128]{2,0,1:T(8,128)(2,1)S(1)} %get-tuple-element.16) | copy-start | bytes 1572868
  23.8 29.5 %collective-permute-start.3 = (bf16[8,256,128]{2,1,0:T(8,128)(2,1)S(1)}, bf16[8,256,128]{2,1,0:T(8,128)(2,1)S(1)}, u32[]{:S(2)}, u32[]{:S(2)}) collective-permute-start(bf16[8,256,128]{2,1,0:T(8,128)(2,1)S(1)} %bitcast.37), channel_id=1, source_target_pairs={{0,16},{16,0},{1,17},{17,1},{2,18},{18,2},{3,19},{19,3},{4,20},{20... | collective-permute-start | bytes 1572872 | tf_op jit(solution)/shard_map/ppermute | solution.py:389
  27.7 28.0 %collective-permute-start.4 = (bf16[8,256,128]{2,1,0:T(8,128)(2,1)S(1)}, bf16[8,256,128]{2,1,0:T(8,128)(2,1)S(1)}, u32[]{:S(2)}, u32[]{:S(2)}) collective-permute-start(bf16[8,256,128]{2,1,0:T(8,128)(2,1)S(1)} %bitcast.34), channel_id=1, source_target_pairs={{0,16},{16,0},{1,17},{17,1},{2,18},{18,2},{3,19},{19,3},{4,20},{20... | collective-permute-start | bytes 1572872 | tf_op jit(solution)/shard_map/ppermute | solution.py:390
  38.6 32.7 %all-to-all-start.1 = ((bf16[8,2,128,128]{3,2,1,0:T(8,128)(2,1)}), bf16[8,2,128,128]{3,2,1,0:T(8,128)(2,1)S(1)}, u32[]{:S(2)}, u32[]{:S(2)}) async-start(bf16[8,2,128,128]{3,2,1,0:T(8,128)(2,1)} %pick_readers.1), calls=%async_computation.1 | async-start | bytes 1048576 | tf_op jit(solution)/shard_map/all_to_all | solution.py:315
  48.9 8.7 %collective-permute-start.1 = (bf16[8,256,128]{2,1,0:T(8,128)(2,1)S(1)}, bf16[8,256,128]{2,1,0:T(8,128)(2,1)S(1)}, u32[]{:S(2)}, u32[]{:S(2)}) collective-permute-start(bf16[8,256,128]{2,1,0:T(8,128)(2,1)S(1)} %bitcast.38), channel_id=1, source_target_pairs={{0,1},{1,0},{2,3},{3,2},{4,5},{5,4},{6,7},{7,6},{8,9},{9,8},{10,11... | collective-permute-start | bytes 1572872 | tf_op jit(solution)/shard_map/ppermute | solution.py:395
  50.9 6.8 %collective-permute-start.2 = (bf16[8,256,128]{2,1,0:T(8,128)(2,1)S(1)}, bf16[8,256,128]{2,1,0:T(8,128)(2,1)S(1)}, u32[]{:S(2)}, u32[]{:S(2)}) collective-permute-start(bf16[8,256,128]{2,1,0:T(8,128)(2,1)S(1)} %bitcast.35), channel_id=1, source_target_pairs={{0,1},{1,0},{2,3},{3,2},{4,5},{5,4},{6,7},{7,6},{8,9},{9,8},{10,11... | collective-permute-start | bytes 1572872 | tf_op jit(solution)/shard_map/ppermute | solution.py:396
  53.3 18.0 %copy-start.10 = (bf16[8,256,128]{2,1,0:T(8,128)(2,1)}, bf16[8,256,128]{2,1,0:T(8,128)(2,1)S(1)}, u32[]{:S(2)}) copy-start(bf16[8,256,128]{2,1,0:T(8,128)(2,1)S(1)} %collective-permute-done.3.refs_4_) | copy-start | bytes 1572868
  53.3 4.4 %collective-permute-start.5 = (bf16[8,256,128]{2,1,0:T(8,128)(2,1)S(1)}, bf16[8,256,128]{2,1,0:T(8,128)(2,1)S(1)}, u32[]{:S(2)}, u32[]{:S(2)}) collective-permute-start(bf16[8,256,128]{2,1,0:T(8,128)(2,1)S(1)} %collective-permute-done.3.refs_4_), channel_id=1, source_target_pairs={{0,1},{1,0},{2,3},{3,2},{4,5},{5,4},{6,7},{7,6},{8,9},{9,8},{10,11... | collective-permute-start | bytes 1572872 | tf_op jit(solution)/shard_map/ppermute | solution.py:399
  55.7 15.7 %copy-start.11 = (bf16[8,256,128]{2,1,0:T(8,128)(2,1)}, bf16[8,256,128]{2,1,0:T(8,128)(2,1)S(1)}, u32[]{:S(2)}) copy-start(bf16[8,256,128]{2,1,0:T(8,128)(2,1)S(1)} %collective-permute-done.4.refs_5_) | copy-start | bytes 1572868
  55.7 3.9 %collective-permute-start.6 = (bf16[8,256,128]{2,1,0:T(8,128)(2,1)S(1)}, bf16[8,256,128]{2,1,0:T(8,128)(2,1)}, u32[]{:S(2)}, u32[]{:S(2)}) collective-permute-start(bf16[8,256,128]{2,1,0:T(8,128)(2,1)S(1)} %collective-permute-done.4.refs_5_), channel_id=1, source_target_pairs={{0,1},{1,0},{2,3},{3,2},{4,5},{5,4},{6,7},{7,6},{8,9},{9,8},{10,11... | collective-permute-start | bytes 1572872 | tf_op jit(solution)/shard_map/ppermute | solution.py:400
  57.7 0.8 copy-start.12
  57.7 1.0 copy-start.13
  58.7 0.8 copy-start.14
  71.3 0.8 copy-start.7
  82.9 6.3 %collective-permute-start.7 = (bf16[16,8,64,128]{3,2,1,0:T(8,128)(2,1)}, bf16[16,8,64,128]{3,2,1,0:T(8,128)(2,1)S(1)}, u32[]{:S(2)}, u32[]{:S(2)}) collective-permute-start(bf16[16,8,64,128]{3,2,1,0:T(8,128)(2,1)} %all-gather.2.cloned.1.call-done.refs_0_), channel_id=1, source_target_pairs={{0,1},{1,0},{2,3},{3,2},{4,5},{5,4},{6,7},{7,6},{8,9},{9,8},{10,11... | collective-permute-start | bytes 6291464 | tf_op jit(solution)/shard_map/ppermute | solution.py:437
  84.8 21.3 %all-to-all-start.2 = ((f16[8,2,136,128]{3,2,1,0:T(8,128)(2,1)}), f16[8,2,136,128]{3,2,1,0:T(8,128)(2,1)S(1)}, u32[]{:S(2)}, u32[]{:S(2)}) async-start(f16[8,2,136,128]{3,2,1,0:T(8,128)(2,1)} %bitcast.11), calls=%async_computation.2 | async-start | bytes 1114112 | tf_op jit(solution)/shard_map/all_to_all | solution.py:315
  89.1 1.3 copy-start.1
  90.4 1.6 %copy-start = (bf16[16,8,64,128]{3,2,1,0:T(8,128)(2,1)S(1)}, bf16[16,8,64,128]{3,2,1,0:T(8,128)(2,1)}, u32[]{:S(2)}) copy-start(bf16[16,8,64,128]{3,2,1,0:T(8,128)(2,1)} %all-gather.2.cloned.1.call-done.refs_0_) | copy-start | bytes 6291460
  92.0 1.6 %copy-start.2 = (bf16[16,8,64,128]{3,2,1,0:T(8,128)(2,1)S(1)}, bf16[16,8,64,128]{3,2,1,0:T(8,128)(2,1)}, u32[]{:S(2)}) copy-start(bf16[16,8,64,128]{3,2,1,0:T(8,128)(2,1)} %copy-done.1) | copy-start | bytes 6291460
  106.8 10.9 %copy-start.3 = (bf16[1,512,8,128]{3,2,1,0:T(8,128)(2,1)S(1)}, bf16[1,512,8,128]{3,2,1,0:T(8,128)(2,1)}, u32[]{:S(2)}) copy-start(bf16[1,512,8,128]{3,2,1,0:T(8,128)(2,1)} %param.17) | copy-start | bytes 3145732
  106.8 10.9 %copy-start.4 = (bf16[1,512,8,128]{3,2,1,0:T(8,128)(2,1)S(1)}, bf16[1,512,8,128]{3,2,1,0:T(8,128)(2,1)}, u32[]{:S(2)}) copy-start(bf16[1,512,8,128]{3,2,1,0:T(8,128)(2,1)} %param.18) | copy-start | bytes 3145732
  106.8 10.9 %copy-start.5 = (bf16[1,2,8,128]{3,2,1,0:T(8,128)(2,1)S(1)}, bf16[1,2,8,128]{3,2,1,0:T(8,128)(2,1)}, u32[]{:S(2)}) copy-start(bf16[1,2,8,128]{3,2,1,0:T(8,128)(2,1)} %param.19) | copy-start | bytes 12292
  106.9 10.9 %copy-start.6 = (bf16[1,2,8,128]{3,2,1,0:T(8,128)(2,1)S(1)}, bf16[1,2,8,128]{3,2,1,0:T(8,128)(2,1)}, u32[]{:S(2)}) copy-start(bf16[1,2,8,128]{3,2,1,0:T(8,128)(2,1)} %param.20) | copy-start | bytes 12292
  107.8 26.5 %all-to-all-start.3 = ((f16[16,136,128]{2,1,0:T(8,128)(2,1)}), f16[16,136,128]{2,1,0:T(8,128)(2,1)S(1)}, u32[]{:S(2)}, u32[]{:S(2)}) async-start(f16[16,136,128]{2,1,0:T(8,128)(2,1)} %convert_element_type.18), calls=%async_computation.3 | async-start | bytes 1114112 | tf_op jit(solution)/shard_map/all_to_all | solution.py:315
Sparse Core Ops, SparseCore 0:
  24.9 56.8 all-gather.1

commit v6 on v2

--- a/solution.py
+++ b/solution.py
@@ -11,8 +11,9 @@
 CAP = 2
 PAD = 8
 LOW = -1e30
-EMPHASIS = 30
-VMEM_LIMIT = 20 * 1024 * 1024
+PARTS = 4
+SPLITS = 4
+EMPHASIS = 24
 NT = (((1,), (1,)), ((), ()))
 
 
@@ -88,23 +89,37 @@
     out_ref[...] = jnp.broadcast_to(peer_ref[...][None], out_ref.shape)
 
 
-def branch_kernel(q_ref, *refs):
-    out_ref = refs[-1]
-    blocks = list(zip(refs[:-1:2], refs[1:-1:2]))
+def branch_kernel(count, q_ref, *refs):
+    sources, out_ref, held, sems = refs[:count], refs[count], refs[count + 1], refs[count + 2]
     slots, lanes, dim = q_ref.shape
-    heads = refs[0].shape[0]
+    heads = sources[0].shape[0]
     per_head = lanes // heads
+    group = heads // PARTS
+
+    def copies(part):
+        some = pl.ds(part * group, group)
+        return [
+            pltpu.make_async_copy(ref.at[some], held.at[place, some], sems.at[place, part])
+            for place, ref in enumerate(sources)
+        ]
+
+    for part in range(PARTS):
+        for place, copy in enumerate(copies(part)):
+            copy.start(priority=place % 2)
     tail = jnp.zeros((slots, 1, lanes), jnp.float32)
     for head in range(heads):
+        if head % group == 0:
+            for copy in copies(head // group):
+                copy.wait()
         place = slice(head * per_head, (head + 1) * per_head)
         q = q_ref[:, place, :].reshape(slots * per_head, dim)
         found = []
-        for k_ref, v_ref in blocks:
-            scores = scores_of(q, k_ref[head])
+        for block in range(0, count, 2):
+            scores = scores_of(q, held[block, head])
             high = jnp.max(scores, axis=1, keepdims=True)
             weights = jnp.exp(scores - high)
             den = jnp.sum(weights, axis=1, keepdims=True)
-            found.append((high, den, times_values(weights, v_ref[head])))
+            found.append((high, den, times_values(weights, held[block + 1, head])))
         high = functools.reduce(jnp.maximum, [f[0] for f in found])
         factors = [jnp.exp(f[0] - high) for f in found]
         den = sum(factor * f[1] for factor, f in zip(factors, found))
@@ -114,25 +129,39 @@
     out_ref[:, lanes:, :] = tail_rows(split_lse(tail))
 
 
-def root_kernel(q_ref, own_ref, twin_ref, out_ref):
+def root_kernel(count, q_ref, *refs):
+    sources, out_ref, held, sems = refs[:count], refs[count], refs[count + 1], refs[count + 2]
     requests, lanes, dim = q_ref.shape
-    count, heads = own_ref.shape[:2]
+    blocks, heads, half = held.shape[0], held.shape[1], held.shape[2] // 2
     per_head = lanes // heads
-    half = own_ref.shape[2] // 2
+    group = heads // PARTS
+    span = blocks * half
+    offsets = [sum(ref.shape[0] for ref in sources[:place]) for place in range(count)]
+
+    def copies(part):
+        some = pl.ds(part * group, group)
+        return [
+            pltpu.make_async_copy(
+                ref.at[:, some], held.at[pl.ds(offset, ref.shape[0]), some], sems.at[place, part]
+            )
+            for place, (ref, offset) in enumerate(zip(sources, offsets))
+        ]
+
+    for part in range(PARTS):
+        for place, copy in enumerate(copies(part)):
+            copy.start(priority=place % 2)
     tail = jnp.zeros((requests, 1, lanes), jnp.float32)
     for head in range(heads):
+        if head % group == 0:
+            for copy in copies(head // group):
+                copy.wait()
         place = slice(head * per_head, (head + 1) * per_head)
         q = q_ref[:, place, :].reshape(requests * per_head, dim)
-        blocks = [r[:, head, :, :] for r in (own_ref, twin_ref)]
-        keys = [block[:, :half, :].reshape(count * half, dim) for block in blocks]
-        values = [block[:, half:, :].reshape(count * half, dim) for block in blocks]
-        scores = [scores_of(q, k) for k in keys]
-        high = functools.reduce(
-            jnp.maximum, [jnp.max(s, axis=1, keepdims=True) for s in scores]
-        )
-        weights = [jnp.exp(s - high) for s in scores]
-        den = sum(jnp.sum(w, axis=1, keepdims=True) for w in weights)
-        num = sum(times_values(w, v) for w, v in zip(weights, values)) / den
+        scores = scores_of(q, held[:, head, :half, :].reshape(span, dim))
+        high = jnp.max(scores, axis=1, keepdims=True)
+        weights = jnp.exp(scores - high)
+        den = jnp.sum(weights, axis=1, keepdims=True)
+        num = times_values(weights, held[:, head, half:, :].reshape(span, dim)) / den
         out_ref[:, place, :] = num.reshape(requests, per_head, dim)
         tail = tail + head_lse(high + jnp.log(den), head, per_head, lanes)
     out_ref[:, lanes:, :] = tail_rows(split_lse(tail))
@@ -181,13 +210,13 @@
     out_ref[...] = out.astype(out_ref.dtype)
 
 
-def params():
-    return pltpu.CompilerParams(vmem_limit_bytes=VMEM_LIMIT)
-
-
-def estimate(area, dim):
+def params(megabytes=20):
+    return pltpu.CompilerParams(vmem_limit_bytes=megabytes * 1024 * 1024)
+
+
+def estimate(area, dim, emphasis=1):
     return pl.CostEstimate(
-        flops=EMPHASIS * 4 * area * dim, bytes_accessed=6 * 1024 * 1024, transcendentals=area
+        flops=emphasis * 4 * area * dim, bytes_accessed=6 * 1024 * 1024, transcendentals=area
     )
 
 
@@ -195,8 +224,20 @@
     return pl.BlockSpec(memory_space=pltpu.VMEM)
 
 
+def hbm():
+    return pl.BlockSpec(memory_space=pltpu.HBM)
+
+
 def smem():
     return pl.BlockSpec(memory_space=pltpu.SMEM)
+
+
+def scratch(count, shape):
+    return [pltpu.VMEM(shape, jnp.bfloat16), pltpu.SemaphoreType.DMA((count, PARTS))]
+
+
+def in_hbm(blocks):
+    return [pltpu.with_memory_space_constraint(block, pltpu.HBM) for block in blocks]
 
 
 def exchange(blocks, axis):
@@ -262,17 +303,18 @@
                 out_specs=pl.BlockSpec((ring, 1, rows, dim), lambda k, idx: (0, k, 0, 0)),
             ),
             compiler_params=params(),
-            cost_estimate=estimate(area, dim),
+            cost_estimate=estimate(area, dim, EMPHASIS),
             name="pick_readers",
         )(readers, peers)
         return exchange(packed, "z")
 
-    keys_own = branch_keys[0].transpose(1, 0, 2)
-    values_own = branch_values[0].transpose(1, 0, 2)
     root_block = jnp.concatenate([root_keys, root_values], axis=0).transpose(1, 0, 2)
-    root_far = lax.ppermute(root_block, "xhi", swap)
-    root_far, keys_own, values_own = lax.optimization_barrier((root_far, keys_own, values_own))
-    root_blocks = lax.all_gather(jnp.stack([root_block, root_far]), "z", axis=0, tiled=True)
+    pair = jnp.stack([root_block, lax.ppermute(root_block, "xhi", swap)])
+    pair, keys_own, values_own = lax.optimization_barrier((pair, branch_keys[0], branch_values[0]))
+    root_own = lax.all_gather(pair, "z", axis=0, tiled=True)
+    keys_own = keys_own.transpose(1, 0, 2)
+    values_own = values_own.transpose(1, 0, 2)
+    peers, _ = lax.optimization_barrier((peers, pair))
     keys_far = lax.ppermute(keys_own, "xhi", swap)
     values_far = lax.ppermute(values_own, "xhi", swap)
     slots = gather_readers(peers)
@@ -286,7 +328,6 @@
         lax.ppermute(keys_far, "core", swap),
         lax.ppermute(values_far, "core", swap),
     ]
-
     flat = suffix_keys.shape[1] * heads
     local = pl.pallas_call(
         functools.partial(local_kernel, heads),
@@ -308,33 +349,36 @@
     )
 
     slots = slots.reshape(ring * CAP, rows, dim)
-    area = ring * CAP * rows * keys_own.shape[1] * 4
+    area = ring * CAP * rows * branch_keys.shape[1] * 4
+    count = len(branch_blocks)
     parts = pl.pallas_call(
-        branch_kernel,
+        functools.partial(branch_kernel, count),
         out_shape=jax.ShapeDtypeStruct((ring * CAP, rows + PAD, dim), jnp.float32),
-        in_specs=[vmem()] * (1 + len(branch_blocks)),
+        in_specs=[vmem()] + [hbm()] * count,
         out_specs=vmem(),
+        scratch_shapes=scratch(count, (count,) + keys_own.shape),
         compiler_params=params(),
         cost_estimate=estimate(area, dim),
         name="branch_attention",
-    )(slots, *branch_blocks)
+    )(slots, *in_hbm(branch_blocks))
     parts = parts.astype(jnp.float16).reshape(ring, CAP, rows + PAD, dim)
-    root_blocks, peers, _ = lax.optimization_barrier((root_blocks, peers, parts))
-    root_twin = lax.ppermute(root_blocks, "core", swap)
+    peers, root_own, _ = lax.optimization_barrier((peers, root_own, parts))
+    root_blocks = [root_own]
+    root_blocks += [lax.ppermute(some, "core", swap) for some in jnp.split(root_own, SPLITS)]
     parts = exchange(parts, "z")
 
-    area = grp * rows * root_keys.shape[0] * 4 * ring
     whole = jax.ShapeDtypeStruct((grp, rows + PAD, dim), jnp.float32)
+    count = len(root_blocks)
     root = pl.pallas_call(
-        root_kernel,
+        functools.partial(root_kernel, count),
         out_shape=whole,
-        in_specs=[vmem()] * 3,
+        in_specs=[vmem()] + [hbm()] * count,
         out_specs=vmem(),
+        scratch_shapes=scratch(count, (core * root_own.shape[0],) + root_own.shape[1:]),
         compiler_params=params(),
         cost_estimate=estimate(area, dim),
         name="root_attention",
-    )(peers, root_blocks, root_twin)
-
+    )(peers, *in_hbm(root_blocks))
     parts, root = lax.optimization_barrier((parts, root))
     parts = parts.astype(jnp.float32)
     merged = pl.pallas_call(

time: 160 us -> 146 us (0.912)
  waiting for transfers between devices: 59.6 us -> 40.1 us
  local copies, waits for them, and re-layouts: 14.6 us -> 7.03 us
  starting transfers between devices: 52.3 us -> 59.5 us
  Pallas kernels: 14.1 us -> 19 us
    all_gather x1, waiting for transfers between devices: 27.1 us -> 8.66 us  [shards(): root_own = lax.all_gather(pair, 'z', axis=0, tiled=True)]
    unnamed x43, local copies, waits for them, and re-layouts: 11.9 us -> 2.63 us
    ppermute x2 -> x5, starting transfers between devices: 5.91 us -> 12.8 us  [the longest x4 8.83 us: shards(): lax.ppermute(some, 'core', swap)]
    pallas_call x2, Pallas kernels: 9.08 us -> 14.2 us  [the longest x1 7.25 us: shards(): pl.pallas_call(functools.partial(branch_kernel, count), out_shape=jax.Sha...]
    all_to_all x4, waiting for transfers between devices: 25.6 us -> 23.1 us  [exchange(): return lax.all_to_all(blocks, axis, split_axis=0, concat_axis=0, tiled=True)]
    split x0 -> x1, local copies, waits for them, and re-layouts: none -> 1.73 us  [shards(): jnp.split(root_own, SPLITS)]
    ppermute x2 -> x5, waiting for transfers between devices: 4.79 us -> 6.13 us  [the longest x1 4.85 us: shards(): pair = jnp.stack([root_block, lax.ppermute(root_block, 'xhi', swap)])]
  transfers between devices with their start and end apart: 13 -> 16, of which waited for: 7 -> 7; matrix products, arithmetic and copies ran while one was open for 2% -> 3% of each run, Pallas kernels for 8% -> 12%
where the time goes in v6:
time: 146 us; the launch traced here: 143 us
  starting transfers between devices  59.5 us (41%)
  waiting for transfers between devices  40.1 us (27%)
  Pallas kernels  19 us (13%)
  between operations  14.5 us (10%)
  local copies, waits for them, and re-layouts  7.03 us (5%)
  other arithmetic  3.15 us (2%)
    all_to_all x4, starting transfers between devices, exchange(): return lax.all_to_all(blocks, axis, split_axis=0, concat_axis=0, tiled=True)  31.1 us
    all_to_all x4, waiting for transfers between devices, exchange(): return lax.all_to_all(blocks, axis, split_axis=0, concat_axis=0, tiled=True)  23.1 us
    ppermute x4, starting transfers between devices, shards(): lax.ppermute(some, 'core', swap)  8.83 us
    all_gather x1, waiting for transfers between devices, shards(): root_own = lax.all_gather(pair, 'z', axis=0, tiled=True)  8.66 us
    pallas_call x1, Pallas kernels, shards(): pl.pallas_call(functools.partial(branch_kernel, count), out_shape=jax.Sha...  7.25 us
    pallas_call x1, Pallas kernels, shards(): pl.pallas_call(functools.partial(root_kernel, count), out_shape=whole, in...  6.98 us
    ppermute x1, waiting for transfers between devices, shards(): pair = jnp.stack([root_block, lax.ppermute(root_block, 'xhi', swap)])  4.85 us
    ppermute x1, starting transfers between devices, shards(): pair = jnp.stack([root_block, lax.ppermute(root_block, 'xhi', swap)])  4.01 us
  transfers between devices with their start and end apart: 16, of which 7 were waited for; matrix products, arithmetic and copies ran while one was open for 3% of the time, Pallas kernels for 12%

profile of v6, /device:TPU:6, one launch (start us, length us, event | category | flops | bytes accessed | tf_op | source)
XLA Modules:
  0.0 143.3 jit_solution(18363201448855876330)
XLA Ops:
  6.5 0.9 copy.37
  7.4 0.9 broadcast_in_dim.46
  8.3 8.6 %all-to-all-start = ((bf16[16,128,128]{2,1,0:T(8,128)(2,1)}), bf16[16,128,128]{2,1,0:T(8,128)(2,1)S(1)}, u32[]{:S(2)}, u32[]{:S(2)}) async-start(bf16[16,128,128]{2,1,0:T(8,128)(2,1)} %broadcast_in_dim.46), calls=%async_computation | async-start | bytes 1048576 | tf_op jit(solution)/shard_map/all_to_all | solution.py:244
  16.9 0.0 all-gather.2.cloned.1.call-start
  17.0 0.0 copy-start.19
  17.0 0.0 copy-start.20
  17.0 4.0 %collective-permute-start = (bf16[8,64,128]{2,1,0:T(8,128)(2,1)S(1)}, bf16[8,64,128]{2,1,0:T(8,128)(2,1)S(1)}, u32[]{:S(2)}, u32[]{:S(2)}) collective-permute-start(bf16[8,64,128]{2,1,0:T(8,128)(2,1)S(1)} %bitcast.40), channel_id=1, source_target_pairs={{0,16},{16,0},{1,17},{17,1},{2,18},{18,2},{3,19},{19,3},{4,20},{20... | collective-permute-start | bytes 393224 | tf_op jit(solution)/shard_map/ppermute | solution.py:312
  21.0 0.2 copy_bitcast_fusion
  21.3 0.1 select_reduce_fusion
  21.4 0.1 reshape.39
  21.5 0.2 fusion
  21.6 4.8 %collective-permute-done = bf16[8,64,128]{2,1,0:T(8,128)(2,1)S(1)} collective-permute-done((bf16[8,64,128]{2,1,0:T(8,128)(2,1)S(1)}, bf16[8,64,128]{2,1,0:T(8,128)(2,1)S(1)}, u32[]{:S(2)}, u32[]{:S(2)}) %collective-permute-start) | collective-permute-done | bytes 131104 | tf_op jit(solution)/shard_map/ppermute | solution.py:312
  26.5 0.7 pad_maximum_fusion
  27.2 0.0 all-gather.2.cloned.1.call-update
  27.2 0.1 convert_reduce_fusion
  27.4 0.1 fusion.2.idx_ref
  27.5 3.6 %collective-permute-start.3 = (bf16[8,256,128]{2,1,0:T(8,128)(2,1)S(1)}, bf16[8,256,128]{2,1,0:T(8,128)(2,1)S(1)}, u32[]{:S(2)}, u32[]{:S(2)}) collective-permute-start(bf16[8,256,128]{2,1,0:T(8,128)(2,1)S(1)} %bitcast.37), channel_id=1, source_target_pairs={{0,16},{16,0},{1,17},{17,1},{2,18},{18,2},{3,19},{19,3},{4,20},{20... | collective-permute-start | bytes 1572872 | tf_op jit(solution)/shard_map/ppermute | solution.py:318
  31.1 3.8 %collective-permute-start.4 = (bf16[8,256,128]{2,1,0:T(8,128)(2,1)S(1)}, bf16[8,256,128]{2,1,0:T(8,128)(2,1)S(1)}, u32[]{:S(2)}, u32[]{:S(2)}) collective-permute-start(bf16[8,256,128]{2,1,0:T(8,128)(2,1)S(1)} %bitcast.34), channel_id=1, source_target_pairs={{0,16},{16,0},{1,17},{17,1},{2,18},{18,2},{3,19},{19,3},{4,20},{20... | collective-permute-start | bytes 1572872 | tf_op jit(solution)/shard_map/ppermute | solution.py:319
  34.8 0.0 all-to-all-done.peer_ref.q_ref
  34.9 1.4 pick_readers.1
  36.3 9.9 %all-to-all-start.1 = ((bf16[8,2,128,128]{3,2,1,0:T(8,128)(2,1)}), bf16[8,2,128,128]{3,2,1,0:T(8,128)(2,1)S(1)}, u32[]{:S(2)}, u32[]{:S(2)}) async-start(bf16[8,2,128,128]{3,2,1,0:T(8,128)(2,1)} %pick_readers.1), calls=%async_computation.1 | async-start | bytes 1048576 | tf_op jit(solution)/shard_map/all_to_all | solution.py:244
  46.2 1.9 %collective-permute-start.1 = (bf16[8,256,128]{2,1,0:T(8,128)(2,1)S(1)}, bf16[8,256,128]{2,1,0:T(8,128)(2,1)S(1)}, u32[]{:S(2)}, u32[]{:S(2)}) collective-permute-start(bf16[8,256,128]{2,1,0:T(8,128)(2,1)S(1)} %bitcast.38), channel_id=1, source_target_pairs={{0,1},{1,0},{2,3},{3,2},{4,5},{5,4},{6,7},{7,6},{8,9},{9,8},{10,11... | collective-permute-start | bytes 1572872 | tf_op jit(solution)/shard_map/ppermute | solution.py:324
  48.1 2.4 %collective-permute-start.2 = (bf16[8,256,128]{2,1,0:T(8,128)(2,1)S(1)}, bf16[8,256,128]{2,1,0:T(8,128)(2,1)S(1)}, u32[]{:S(2)}, u32[]{:S(2)}) collective-permute-start(bf16[8,256,128]{2,1,0:T(8,128)(2,1)S(1)} %bitcast.35), channel_id=1, source_target_pairs={{0,1},{1,0},{2,3},{3,2},{4,5},{5,4},{6,7},{7,6},{8,9},{9,8},{10,11... | collective-permute-start | bytes 1572872 | tf_op jit(solution)/shard_map/ppermute | solution.py:325
  50.5 0.0 collective-permute-done.3.refs_4_
  50.6 1.9 %collective-permute-start.5 = (bf16[8,256,128]{2,1,0:T(8,128)(2,1)S(1)}, bf16[8,256,128]{2,1,0:T(8,128)(2,1)S(1)}, u32[]{:S(2)}, u32[]{:S(2)}) collective-permute-start(bf16[8,256,128]{2,1,0:T(8,128)(2,1)S(1)} %collective-permute-done.3.refs_4_), channel_id=1, source_target_pairs={{0,1},{1,0},{2,3},{3,2},{4,5},{5,4},{6,7},{7,6},{8,9},{9,8},{10,11... | collective-permute-start | bytes 1572872 | tf_op jit(solution)/shard_map/ppermute | solution.py:328
  52.5 2.0 %collective-permute-done.4.refs_5_ = bf16[8,256,128]{2,1,0:T(8,128)(2,1)S(1)} collective-permute-done((bf16[8,256,128]{2,1,0:T(8,128)(2,1)S(1)}, bf16[8,256,128]{2,1,0:T(8,128)(2,1)S(1)}, u32[]{:S(2)}, u32[]{:S(2)}) %collective-permute-start.4) | collective-permute-done | bytes 524320 | tf_op jit(solution)/shard_map/ppermute | solution.py:319
  54.5 1.9 %collective-permute-start.6 = (bf16[8,256,128]{2,1,0:T(8,128)(2,1)S(1)}, bf16[8,256,128]{2,1,0:T(8,128)(2,1)}, u32[]{:S(2)}, u32[]{:S(2)}) collective-permute-start(bf16[8,256,128]{2,1,0:T(8,128)(2,1)S(1)} %collective-permute-done.4.refs_5_), channel_id=1, source_target_pairs={{0,1},{1,0},{2,3},{3,2},{4,5},{5,4},{6,7},{7,6},{8,9},{9,8},{10,11... | collective-permute-start | bytes 1572872 | tf_op jit(solution)/shard_map/ppermute | solution.py:329
  56.4 0.0 collective-permute-done.1.refs_2_
  56.4 0.0 collective-permute-done.2.refs_3_
  56.4 0.0 collective-permute-done.5.refs_6_
  56.4 0.8 copy-done.8
  57.2 0.2 copy-done.9
  57.4 0.8 copy-done.10
  58.2 0.2 collective-permute-done.6.refs_7_
  58.4 7.5 %all-to-all-done.1 = bf16[8,2,128,128]{3,2,1,0:T(8,128)(2,1)S(1)} async-done(((bf16[8,2,128,128]{3,2,1,0:T(8,128)(2,1)}), bf16[8,2,128,128]{3,2,1,0:T(8,128)(2,1)S(1)}, u32[]{:S(2)}, u32[]{:S(2)}) %all-to-all-start.1) | async-done | bytes 524320 | tf_op jit(solution)/shard_map/all_to_all | solution.py:244
  65.9 7.2 %branch_attention.1 = f32[16,136,128]{2,1,0:T(8,128)S(1)} custom-call(bf16[16,128,128]{2,1,0:T(8,128)(2,1)S(1)} %bitcast.26, bf16[8,256,128]{2,1,0:T(8,128)(2,1)} %bitcast.39, bf16[8,256,128]{2,1,0:T(8,128)(2,1)} %bitcast.36, bf16[8,256,128]{2,1,0:T(8,128)(2,1)} %copy-done.8, bf16[8,256,128]{2,1,0:T(8,128)(2,1)} %copy-done.9, ...), custom_call_target="tpu_custom_call" | custom-call | flops 1073741824 | bytes 6291456 | tf_op jit(solution)/shard_map/branch_attention/pallas_call | solution.py:354
  73.2 0.9 convert_element_type.16
  74.1 3.5 %all-to-all-start.2 = ((f16[8,2,136,128]{3,2,1,0:T(8,128)(2,1)}), f16[8,2,136,128]{3,2,1,0:T(8,128)(2,1)S(1)}, u32[]{:S(2)}, u32[]{:S(2)}) async-start(f16[8,2,136,128]{3,2,1,0:T(8,128)(2,1)} %bitcast.11), calls=%async_computation.2 | async-start | bytes 1114112 | tf_op jit(solution)/shard_map/all_to_all | solution.py:244
  77.6 8.7 %all-gather.2.cloned.1.call-done.refs_0_ = bf16[16,8,64,128]{3,2,1,0:T(8,128)(2,1)} async-done(((bf16[2,8,64,128]{3,2,1,0:T(8,128)(2,1)}), bf16[16,8,64,128]{3,2,1,0:T(8,128)(2,1)}) %all-gather.2.cloned.1.call-update) | async-done | bytes 2097168 | tf_op jit(solution)/shard_map/all_gather | solution.py:314
  86.3 1.7 %fusion.3 = (bf16[4,8,64,128]{3,2,1,0:T(8,128)(2,1)S(1)}, bf16[4,8,64,128]{3,2,1,0:T(8,128)(2,1)S(1)}, bf16[4,8,64,128]{3,2,1,0:T(8,128)(2,1)S(1)}, bf16[4,8,64,128]{3,2,1,0:T(8,128)(2,1)S(1)}) fusion(bf16[16,8,64,128]{3,2,1,0:T(8,128)(2,1)} %all-gather.2.cloned.1.call-done.refs_0_), kind=kLoop, calls=%fused_computation.15 | loop fusion | bytes 4194304 | tf_op jit(solution)/shard_map/split | solution.py:367
  88.0 1.9 %collective-permute-start.10 = (bf16[4,8,64,128]{3,2,1,0:T(8,128)(2,1)S(1)}, bf16[4,8,64,128]{3,2,1,0:T(8,128)(2,1)S(1)}, u32[]{:S(2)}, u32[]{:S(2)}) collective-permute-start(bf16[4,8,64,128]{3,2,1,0:T(8,128)(2,1)S(1)} %get-tuple-element.21), channel_id=1, source_target_pairs={{0,1},{1,0},{2,3},{3,2},{4,5},{5,4},{6,7},{7,6},{8,9},{9,8},{10,11... | collective-permute-start | bytes 1572872 | tf_op jit(solution)/shard_map/ppermute | solution.py:367
  89.9 2.4 %collective-permute-start.7 = (bf16[4,8,64,128]{3,2,1,0:T(8,128)(2,1)S(1)}, bf16[4,8,64,128]{3,2,1,0:T(8,128)(2,1)S(1)}, u32[]{:S(2)}, u32[]{:S(2)}) collective-permute-start(bf16[4,8,64,128]{3,2,1,0:T(8,128)(2,1)S(1)} %get-tuple-element.24), channel_id=1, source_target_pairs={{0,1},{1,0},{2,3},{3,2},{4,5},{5,4},{6,7},{7,6},{8,9},{9,8},{10,11... | collective-permute-start | bytes 1572872 | tf_op jit(solution)/shard_map/ppermute | solution.py:367
  92.4 1.9 %collective-permute-start.8 = (bf16[4,8,64,128]{3,2,1,0:T(8,128)(2,1)S(1)}, bf16[4,8,64,128]{3,2,1,0:T(8,128)(2,1)S(1)}, u32[]{:S(2)}, u32[]{:S(2)}) collective-permute-start(bf16[4,8,64,128]{3,2,1,0:T(8,128)(2,1)S(1)} %get-tuple-element.23), channel_id=1, source_target_pairs={{0,1},{1,0},{2,3},{3,2},{4,5},{5,4},{6,7},{7,6},{8,9},{9,8},{10,11... | collective-permute-start | bytes 1572872 | tf_op jit(solution)/shard_map/ppermute | solution.py:367
  94.3 2.6 %collective-permute-start.9 = (bf16[4,8,64,128]{3,2,1,0:T(8,128)(2,1)S(1)}, bf16[4,8,64,128]{3,2,1,0:T(8,128)(2,1)S(1)}, u32[]{:S(2)}, u32[]{:S(2)}) collective-permute-start(bf16[4,8,64,128]{3,2,1,0:T(8,128)(2,1)S(1)} %get-tuple-element.22), channel_id=1, source_target_pairs={{0,1},{1,0},{2,3},{3,2},{4,5},{5,4},{6,7},{7,6},{8,9},{9,8},{10,11... | collective-permute-start | bytes 1572872 | tf_op jit(solution)/shard_map/ppermute | solution.py:367
  96.9 0.0 collective-permute-done.10.refs_4_
  96.9 0.0 collective-permute-done.7.refs_1_
  96.9 0.0 collective-permute-done.8.refs_2_
  96.9 1.3 collective-permute-done.9.refs_3_
  98.2 0.8 copy-done.14
  99.0 7.0 %root_attention.1.root_ref = f32[16,136,128]{2,1,0:T(8,128)S(1)} custom-call(bf16[16,128,128]{2,1,0:T(8,128)(2,1)S(1)} %all-to-all-done.peer_ref.q_ref, bf16[16,8,64,128]{3,2,1,0:T(8,128)(2,1)} %all-gather.2.cloned.1.call-done.refs_0_, bf16[4,8,64,128]{3,2,1,0:T(8,128)(2,1)} %copy-done.12, bf16[4,8,64,128]{3,2,1,0:T(8,128)(2,1)} %copy-done.13, ...), custom_call_target="tpu_custom_call" | custom-call | flops 1073741824 | bytes 6291456 | tf_op jit(solution)/shard_map/root_attention/pallas_call | solution.py:372
  106.0 0.0 all-to-all-done.2
  106.0 0.1 convert_element_type.17.part_ref
  106.1 1.4 merge_parts.1
  107.5 0.0 copy-start
  107.5 0.0 copy-start.1
  107.5 0.0 copy-start.2
  107.5 0.0 copy-start.3
  107.5 0.9 convert_element_type.18
  108.4 9.1 %all-to-all-start.3 = ((f16[16,136,128]{2,1,0:T(8,128)(2,1)}), f16[16,136,128]{2,1,0:T(8,128)(2,1)S(1)}, u32[]{:S(2)}, u32[]{:S(2)}) async-start(f16[16,136,128]{2,1,0:T(8,128)(2,1)} %convert_element_type.18), calls=%async_computation.3 | async-start | bytes 1114112 | tf_op jit(solution)/shard_map/all_to_all | solution.py:244
  118.2 1.5 %local_attention.1.local_ref = f32[136,128]{1,0:T(8,128)S(1)} custom-call(s32[1]{0:T(128)S(6)} %copy.50.len_ref, bf16[128,128]{1,0:T(8,128)(2,1)S(1)} %bitcast.30, bf16[4096,128]{1,0:T(8,128)(2,1)S(1)} %bitcast.27, bf16[4096,128]{1,0:T(8,128)(2,1)S(1)} %bitcast.28, bf16[16,128]{1,0:T(8,128)(2,1)S(1)} %bitcast.32, bf16[16,128]{1,0:T(8,128)(2,1)S(1)} %bitcast.33), custom_call_target="tpu_custom_call" | custom-call | flops 268435456 | bytes 2097152 | tf_op jit(solution)/shard_map/local_attention/pallas_call | solution.py:332
  119.6 15.5 %all-to-all-done.3 = f16[16,136,128]{2,1,0:T(8,128)(2,1)S(1)} async-done(((f16[16,136,128]{2,1,0:T(8,128)(2,1)}), f16[16,136,128]{2,1,0:T(8,128)(2,1)S(1)}, u32[]{:S(2)}, u32[]{:S(2)}) %all-to-all-start.3) | async-done | bytes 557088 | tf_op jit(solution)/shard_map/all_to_all | solution.py:244
  135.2 0.1 convert_element_type.19.part_ref
  135.2 0.5 final_merge.1
  135.8 0.6 copy.48
  (34 shorter events, 0.1 us)
Async XLA Ops:
  6.5 10.4 %copy-start.17 = (bf16[32,8,128]{2,1,0:T(8,128)(2,1)S(1)}, bf16[32,8,128]{2,1,0:T(8,128)(2,1)}, u32[]{:S(2)}) copy-start(bf16[32,8,128]{2,1,0:T(8,128)(2,1)} %param.13) | copy-start | bytes 196612
  6.5 10.4 %copy-start.18 = (bf16[32,8,128]{2,1,0:T(8,128)(2,1)S(1)}, bf16[32,8,128]{2,1,0:T(8,128)(2,1)}, u32[]{:S(2)}) copy-start(bf16[32,8,128]{2,1,0:T(8,128)(2,1)} %param.14) | copy-start | bytes 196612
  6.5 14.5 %copy-start.16 = (bf16[1,256,8,128]{3,2,1,0:T(8,128)(2,1)S(1)}, bf16[1,256,8,128]{3,2,1,0:T(8,128)(2,1)}, u32[]{:S(2)}) copy-start(bf16[1,256,8,128]{3,2,1,0:T(8,128)(2,1)} %param.15) | copy-start | bytes 1572868
  6.5 14.5 %copy-start.15 = (bf16[1,256,8,128]{3,2,1,0:T(8,128)(2,1)S(1)}, bf16[1,256,8,128]{3,2,1,0:T(8,128)(2,1)}, u32[]{:S(2)}) copy-start(bf16[1,256,8,128]{3,2,1,0:T(8,128)(2,1)} %param.16) | copy-start | bytes 1572868
  8.3 26.5 %all-to-all-start = ((bf16[16,128,128]{2,1,0:T(8,128)(2,1)}), bf16[16,128,128]{2,1,0:T(8,128)(2,1)S(1)}, u32[]{:S(2)}, u32[]{:S(2)}) async-start(bf16[16,128,128]{2,1,0:T(8,128)(2,1)} %broadcast_in_dim.46), calls=%async_computation | async-start | bytes 1048576 | tf_op jit(solution)/shard_map/all_to_all | solution.py:244
  16.9 69.4 %all-gather.2.cloned.1.call-start = ((), (), s32[]{:S(2)}) async-start(), calls=%async_computation.4 | async-start | bytes 2359296 | tf_op jit(solution)/shard_map/all_gather | solution.py:314
  17.0 4.3 %copy-start.19 = (s32[512]{0:T(512)S(1)}, s32[512]{0:T(512)}, u32[]{:S(2)}) copy-start(s32[512]{0:T(512)} %param.21) | copy-start | bytes 6148
  17.0 4.3 %copy-start.20 = (s32[16]{0:T(128)S(1)}, s32[16]{0:T(128)}, u32[]{:S(2)}) copy-start(s32[16]{0:T(128)} %param.22) | copy-start | bytes 196
  17.0 9.5 %collective-permute-start = (bf16[8,64,128]{2,1,0:T(8,128)(2,1)S(1)}, bf16[8,64,128]{2,1,0:T(8,128)(2,1)S(1)}, u32[]{:S(2)}, u32[]{:S(2)}) collective-permute-start(bf16[8,64,128]{2,1,0:T(8,128)(2,1)S(1)} %bitcast.40), channel_id=1, source_target_pairs={{0,16},{16,0},{1,17},{17,1},{2,18},{18,2},{3,19},{19,3},{4,20},{20... | collective-permute-start | bytes 393224 | tf_op jit(solution)/shard_map/ppermute | solution.py:312
  21.2 24.9 %copy-start.5 = (bf16[256,8,128]{2,0,1:T(8,128)(2,1)}, bf16[256,8,128]{2,0,1:T(8,128)(2,1)S(1)}, u32[]{:S(2)}) copy-start(bf16[256,8,128]{2,0,1:T(8,128)(2,1)S(1)} %get-tuple-element.15) | copy-start | bytes 1572868
  21.3 26.9 %copy-start.4 = (bf16[256,8,128]{2,0,1:T(8,128)(2,1)}, bf16[256,8,128]{2,0,1:T(8,128)(2,1)S(1)}, u32[]{:S(2)}) copy-start(bf16[256,8,128]{2,0,1:T(8,128)(2,1)S(1)} %get-tuple-element.16) | copy-start | bytes 1572868
  27.5 23.1 %collective-permute-start.3 = (bf16[8,256,128]{2,1,0:T(8,128)(2,1)S(1)}, bf16[8,256,128]{2,1,0:T(8,128)(2,1)S(1)}, u32[]{:S(2)}, u32[]{:S(2)}) collective-permute-start(bf16[8,256,128]{2,1,0:T(8,128)(2,1)S(1)} %bitcast.37), channel_id=1, source_target_pairs={{0,16},{16,0},{1,17},{17,1},{2,18},{18,2},{3,19},{19,3},{4,20},{20... | collective-permute-start | bytes 1572872 | tf_op jit(solution)/shard_map/ppermute | solution.py:318
  31.1 23.4 %collective-permute-start.4 = (bf16[8,256,128]{2,1,0:T(8,128)(2,1)S(1)}, bf16[8,256,128]{2,1,0:T(8,128)(2,1)S(1)}, u32[]{:S(2)}, u32[]{:S(2)}) collective-permute-start(bf16[8,256,128]{2,1,0:T(8,128)(2,1)S(1)} %bitcast.34), channel_id=1, source_target_pairs={{0,16},{16,0},{1,17},{17,1},{2,18},{18,2},{3,19},{19,3},{4,20},{20... | collective-permute-start | bytes 1572872 | tf_op jit(solution)/shard_map/ppermute | solution.py:319
  36.3 29.6 %all-to-all-start.1 = ((bf16[8,2,128,128]{3,2,1,0:T(8,128)(2,1)}), bf16[8,2,128,128]{3,2,1,0:T(8,128)(2,1)S(1)}, u32[]{:S(2)}, u32[]{:S(2)}) async-start(bf16[8,2,128,128]{3,2,1,0:T(8,128)(2,1)} %pick_readers.1), calls=%async_computation.1 | async-start | bytes 1048576 | tf_op jit(solution)/shard_map/all_to_all | solution.py:244
  46.2 10.2 %collective-permute-start.1 = (bf16[8,256,128]{2,1,0:T(8,128)(2,1)S(1)}, bf16[8,256,128]{2,1,0:T(8,128)(2,1)S(1)}, u32[]{:S(2)}, u32[]{:S(2)}) collective-permute-start(bf16[8,256,128]{2,1,0:T(8,128)(2,1)S(1)} %bitcast.38), channel_id=1, source_target_pairs={{0,1},{1,0},{2,3},{3,2},{4,5},{5,4},{6,7},{7,6},{8,9},{9,8},{10,11... | collective-permute-start | bytes 1572872 | tf_op jit(solution)/shard_map/ppermute | solution.py:324
  48.1 8.3 %collective-permute-start.2 = (bf16[8,256,128]{2,1,0:T(8,128)(2,1)S(1)}, bf16[8,256,128]{2,1,0:T(8,128)(2,1)S(1)}, u32[]{:S(2)}, u32[]{:S(2)}) collective-permute-start(bf16[8,256,128]{2,1,0:T(8,128)(2,1)S(1)} %bitcast.35), channel_id=1, source_target_pairs={{0,1},{1,0},{2,3},{3,2},{4,5},{5,4},{6,7},{7,6},{8,9},{9,8},{10,11... | collective-permute-start | bytes 1572872 | tf_op jit(solution)/shard_map/ppermute | solution.py:325
  50.6 15.4 %copy-start.6 = (bf16[8,256,128]{2,1,0:T(8,128)(2,1)}, bf16[8,256,128]{2,1,0:T(8,128)(2,1)S(1)}, u32[]{:S(2)}) copy-start(bf16[8,256,128]{2,1,0:T(8,128)(2,1)S(1)} %collective-permute-done.3.refs_4_) | copy-start | bytes 1572868
  50.6 5.8 %collective-permute-start.5 = (bf16[8,256,128]{2,1,0:T(8,128)(2,1)S(1)}, bf16[8,256,128]{2,1,0:T(8,128)(2,1)S(1)}, u32[]{:S(2)}, u32[]{:S(2)}) collective-permute-start(bf16[8,256,128]{2,1,0:T(8,128)(2,1)S(1)} %collective-permute-done.3.refs_4_), channel_id=1, source_target_pairs={{0,1},{1,0},{2,3},{3,2},{4,5},{5,4},{6,7},{7,6},{8,9},{9,8},{10,11... | collective-permute-start | bytes 1572872 | tf_op jit(solution)/shard_map/ppermute | solution.py:328
  54.4 11.5 %copy-start.7 = (bf16[8,256,128]{2,1,0:T(8,128)(2,1)}, bf16[8,256,128]{2,1,0:T(8,128)(2,1)S(1)}, u32[]{:S(2)}) copy-start(bf16[8,256,128]{2,1,0:T(8,128)(2,1)S(1)} %collective-permute-done.4.refs_5_) | copy-start | bytes 1572868
  54.5 3.9 %collective-permute-start.6 = (bf16[8,256,128]{2,1,0:T(8,128)(2,1)S(1)}, bf16[8,256,128]{2,1,0:T(8,128)(2,1)}, u32[]{:S(2)}, u32[]{:S(2)}) collective-permute-start(bf16[8,256,128]{2,1,0:T(8,128)(2,1)S(1)} %collective-permute-done.4.refs_5_), channel_id=1, source_target_pairs={{0,1},{1,0},{2,3},{3,2},{4,5},{5,4},{6,7},{7,6},{8,9},{9,8},{10,11... | collective-permute-start | bytes 1572872 | tf_op jit(solution)/shard_map/ppermute | solution.py:329
  56.4 0.8 copy-start.8
  56.4 0.9 copy-start.9
  57.4 0.8 copy-start.10
  74.1 31.9 %all-to-all-start.2 = ((f16[8,2,136,128]{3,2,1,0:T(8,128)(2,1)}), f16[8,2,136,128]{3,2,1,0:T(8,128)(2,1)S(1)}, u32[]{:S(2)}, u32[]{:S(2)}) async-start(f16[8,2,136,128]{3,2,1,0:T(8,128)(2,1)} %bitcast.11), calls=%async_computation.2 | async-start | bytes 1114112 | tf_op jit(solution)/shard_map/all_to_all | solution.py:244
  88.0 8.9 %collective-permute-start.10 = (bf16[4,8,64,128]{3,2,1,0:T(8,128)(2,1)S(1)}, bf16[4,8,64,128]{3,2,1,0:T(8,128)(2,1)S(1)}, u32[]{:S(2)}, u32[]{:S(2)}) collective-permute-start(bf16[4,8,64,128]{3,2,1,0:T(8,128)(2,1)S(1)} %get-tuple-element.21), channel_id=1, source_target_pairs={{0,1},{1,0},{2,3},{3,2},{4,5},{5,4},{6,7},{7,6},{8,9},{9,8},{10,11... | collective-permute-start | bytes 1572872 | tf_op jit(solution)/shard_map/ppermute | solution.py:367
  89.9 7.0 %collective-permute-start.7 = (bf16[4,8,64,128]{3,2,1,0:T(8,128)(2,1)S(1)}, bf16[4,8,64,128]{3,2,1,0:T(8,128)(2,1)S(1)}, u32[]{:S(2)}, u32[]{:S(2)}) collective-permute-start(bf16[4,8,64,128]{3,2,1,0:T(8,128)(2,1)S(1)} %get-tuple-element.24), channel_id=1, source_target_pairs={{0,1},{1,0},{2,3},{3,2},{4,5},{5,4},{6,7},{7,6},{8,9},{9,8},{10,11... | collective-permute-start | bytes 1572872 | tf_op jit(solution)/shard_map/ppermute | solution.py:367
  92.4 4.6 %collective-permute-start.8 = (bf16[4,8,64,128]{3,2,1,0:T(8,128)(2,1)S(1)}, bf16[4,8,64,128]{3,2,1,0:T(8,128)(2,1)S(1)}, u32[]{:S(2)}, u32[]{:S(2)}) collective-permute-start(bf16[4,8,64,128]{3,2,1,0:T(8,128)(2,1)S(1)} %get-tuple-element.23), channel_id=1, source_target_pairs={{0,1},{1,0},{2,3},{3,2},{4,5},{5,4},{6,7},{7,6},{8,9},{9,8},{10,11... | collective-permute-start | bytes 1572872 | tf_op jit(solution)/shard_map/ppermute | solution.py:367
  94.3 3.9 %collective-permute-start.9 = (bf16[4,8,64,128]{3,2,1,0:T(8,128)(2,1)S(1)}, bf16[4,8,64,128]{3,2,1,0:T(8,128)(2,1)S(1)}, u32[]{:S(2)}, u32[]{:S(2)}) collective-permute-start(bf16[4,8,64,128]{3,2,1,0:T(8,128)(2,1)S(1)} %get-tuple-element.22), channel_id=1, source_target_pairs={{0,1},{1,0},{2,3},{3,2},{4,5},{5,4},{6,7},{7,6},{8,9},{9,8},{10,11... | collective-permute-start | bytes 1572872 | tf_op jit(solution)/shard_map/ppermute | solution.py:367
  96.9 1.3 copy-start.11
  96.9 1.3 copy-start.12
  96.9 1.3 copy-start.13
  98.2 0.8 copy-start.14
  107.5 10.7 %copy-start = (bf16[1,512,8,128]{3,2,1,0:T(8,128)(2,1)S(1)}, bf16[1,512,8,128]{3,2,1,0:T(8,128)(2,1)}, u32[]{:S(2)}) copy-start(bf16[1,512,8,128]{3,2,1,0:T(8,128)(2,1)} %param.17) | copy-start | bytes 3145732
  107.5 10.6 %copy-start.1 = (bf16[1,512,8,128]{3,2,1,0:T(8,128)(2,1)S(1)}, bf16[1,512,8,128]{3,2,1,0:T(8,128)(2,1)}, u32[]{:S(2)}) copy-start(bf16[1,512,8,128]{3,2,1,0:T(8,128)(2,1)} %param.18) | copy-start | bytes 3145732
  107.5 10.6 %copy-start.2 = (bf16[1,2,8,128]{3,2,1,0:T(8,128)(2,1)S(1)}, bf16[1,2,8,128]{3,2,1,0:T(8,128)(2,1)}, u32[]{:S(2)}) copy-start(bf16[1,2,8,128]{3,2,1,0:T(8,128)(2,1)} %param.19) | copy-start | bytes 12292
  107.5 10.6 %copy-start.3 = (bf16[1,2,8,128]{3,2,1,0:T(8,128)(2,1)S(1)}, bf16[1,2,8,128]{3,2,1,0:T(8,128)(2,1)}, u32[]{:S(2)}) copy-start(bf16[1,2,8,128]{3,2,1,0:T(8,128)(2,1)} %param.20) | copy-start | bytes 12292
  108.4 26.8 %all-to-all-start.3 = ((f16[16,136,128]{2,1,0:T(8,128)(2,1)}), f16[16,136,128]{2,1,0:T(8,128)(2,1)S(1)}, u32[]{:S(2)}, u32[]{:S(2)}) async-start(f16[16,136,128]{2,1,0:T(8,128)(2,1)} %convert_element_type.18), calls=%async_computation.3 | async-start | bytes 1114112 | tf_op jit(solution)/shard_map/all_to_all | solution.py:244
Sparse Core Ops, SparseCore 0:
  27.4 58.8 all-gather.1

commit v7 on v6

--- a/solution.py
+++ b/solution.py
@@ -12,8 +12,7 @@
 PAD = 8
 LOW = -1e30
 PARTS = 4
-SPLITS = 4
-EMPHASIS = 24
+EMPHASIS = 20
 NT = (((1,), (1,)), ((), ()))
 
 
@@ -129,42 +128,46 @@
     out_ref[:, lanes:, :] = tail_rows(split_lse(tail))
 
 
-def root_kernel(count, q_ref, *refs):
-    sources, out_ref, held, sems = refs[:count], refs[count], refs[count + 1], refs[count + 2]
+def root_kernel(q_ref, q_twin_ref, block_ref, out_ref, out_twin_ref, held, sems):
     requests, lanes, dim = q_ref.shape
     blocks, heads, half = held.shape[0], held.shape[1], held.shape[2] // 2
     per_head = lanes // heads
     group = heads // PARTS
     span = blocks * half
-    offsets = [sum(ref.shape[0] for ref in sources[:place]) for place in range(count)]
 
     def copies(part):
         some = pl.ds(part * group, group)
+        cuts = [pl.ds(i * (blocks // 2), blocks // 2) for i in range(2)]
         return [
             pltpu.make_async_copy(
-                ref.at[:, some], held.at[pl.ds(offset, ref.shape[0]), some], sems.at[place, part]
+                block_ref.at[cut, some], held.at[cut, some], sems.at[place, part]
             )
-            for place, (ref, offset) in enumerate(zip(sources, offsets))
+            for place, cut in enumerate(cuts)
         ]
 
     for part in range(PARTS):
         for place, copy in enumerate(copies(part)):
-            copy.start(priority=place % 2)
-    tail = jnp.zeros((requests, 1, lanes), jnp.float32)
+            copy.start(priority=place)
+    pairs = ((q_ref, out_ref), (q_twin_ref, out_twin_ref))
+    tails = [jnp.zeros((requests, 1, lanes), jnp.float32) for _ in pairs]
     for head in range(heads):
         if head % group == 0:
             for copy in copies(head // group):
                 copy.wait()
         place = slice(head * per_head, (head + 1) * per_head)
-        q = q_ref[:, place, :].reshape(requests * per_head, dim)
-        scores = scores_of(q, held[:, head, :half, :].reshape(span, dim))
-        high = jnp.max(scores, axis=1, keepdims=True)
-        weights = jnp.exp(scores - high)
-        den = jnp.sum(weights, axis=1, keepdims=True)
-        num = times_values(weights, held[:, head, half:, :].reshape(span, dim)) / den
-        out_ref[:, place, :] = num.reshape(requests, per_head, dim)
-        tail = tail + head_lse(high + jnp.log(den), head, per_head, lanes)
-    out_ref[:, lanes:, :] = tail_rows(split_lse(tail))
+        keys = held[:, head, :half, :].reshape(span, dim)
+        values = held[:, head, half:, :].reshape(span, dim)
+        for i, (rows_ref, result_ref) in enumerate(pairs):
+            q = rows_ref[:, place, :].reshape(requests * per_head, dim)
+            scores = scores_of(q, keys)
+            high = jnp.max(scores, axis=1, keepdims=True)
+            weights = jnp.exp(scores - high)
+            den = jnp.sum(weights, axis=1, keepdims=True)
+            num = times_values(weights, values) / den
+            result_ref[:, place, :] = num.reshape(requests, per_head, dim)
+            tails[i] = tails[i] + head_lse(high + jnp.log(den), head, per_head, lanes)
+    for (_, result_ref), tail in zip(pairs, tails):
+        result_ref[:, lanes:, :] = tail_rows(split_lse(tail))
 
 
 def columns(table):
@@ -173,9 +176,23 @@
     return jnp.concatenate([table, rest], axis=0).T
 
 
-def merge_kernel(idx_ref, part_ref, root_ref, out_ref):
+def merge_kernel(idx_ref, part_ref, own_ref, twin_ref, out_ref):
     sources, cap, _, lanes = part_ref.shape
-    out_ref[...] = root_ref[...]
+    groups = own_ref.shape[0]
+    lse_a = join_lse(own_ref[:, lanes:, :])
+    lse_b = join_lse(twin_ref[:, lanes:, :])
+    high = jnp.maximum(lse_a, lse_b)
+    factor_a = jnp.exp(lse_a - high)
+    factor_b = jnp.exp(lse_b - high)
+    total = factor_a + factor_b
+    table = columns(jnp.concatenate([factor_a / total, factor_b / total], axis=0))
+    pieces = split_lse(high + jnp.log(total))
+    for r in range(groups):
+        out_ref[r, :lanes, :] = (
+            own_ref[r, :lanes, :] * table[:, r : r + 1]
+            + twin_ref[r, :lanes, :] * table[:, groups + r : groups + r + 1]
+        )
+        out_ref[r, lanes:, :] = tail_rows([piece[r : r + 1] for piece in pieces])
     for k in range(cap):
         reader = idx_ref[k]
 
@@ -362,33 +379,32 @@
         name="branch_attention",
     )(slots, *in_hbm(branch_blocks))
     parts = parts.astype(jnp.float16).reshape(ring, CAP, rows + PAD, dim)
-    peers, root_own, _ = lax.optimization_barrier((peers, root_own, parts))
-    root_blocks = [root_own]
-    root_blocks += [lax.ppermute(some, "core", swap) for some in jnp.split(root_own, SPLITS)]
+    peers_twin = lax.ppermute(peers, "core", swap)
+    peers, peers_twin, _ = lax.optimization_barrier((peers, peers_twin, parts))
     parts = exchange(parts, "z")
 
     whole = jax.ShapeDtypeStruct((grp, rows + PAD, dim), jnp.float32)
-    count = len(root_blocks)
-    root = pl.pallas_call(
-        functools.partial(root_kernel, count),
-        out_shape=whole,
-        in_specs=[vmem()] + [hbm()] * count,
-        out_specs=vmem(),
-        scratch_shapes=scratch(count, (core * root_own.shape[0],) + root_own.shape[1:]),
+    root, root_twin = pl.pallas_call(
+        root_kernel,
+        out_shape=(whole, whole),
+        in_specs=[vmem()] * 2 + [hbm()],
+        out_specs=(vmem(), vmem()),
+        scratch_shapes=scratch(2, root_own.shape),
         compiler_params=params(),
         cost_estimate=estimate(area, dim),
         name="root_attention",
-    )(peers, *in_hbm(root_blocks))
-    parts, root = lax.optimization_barrier((parts, root))
+    )(peers, peers_twin, *in_hbm([root_own]))
+    root_twin = lax.ppermute(root_twin.astype(jnp.float16), "core", swap).astype(jnp.float32)
+    parts, root, root_twin = lax.optimization_barrier((parts, root, root_twin))
     parts = parts.astype(jnp.float32)
     merged = pl.pallas_call(
         merge_kernel,
         out_shape=whole,
-        in_specs=[smem()] + [vmem()] * 2,
+        in_specs=[smem()] + [vmem()] * 3,
         out_specs=vmem(),
         compiler_params=params(),
         name="merge_parts",
-    )(readers, parts, root)
+    )(readers, parts, root, root_twin)
     back = exchange(merged.astype(jnp.float16), "grp").astype(jnp.float32)
     mine = pl.pallas_call(
         final_kernel,

time: 146 us -> 135 us (0.925); the launches traced: 143 us -> 134 us
  starting transfers between devices: 59.5 us -> 55.1 us
  waiting for transfers between devices: 40.1 us -> 36.2 us
  local copies, waits for them, and re-layouts: 7.03 us -> 4.47 us
    ppermute x4 -> x2, starting transfers between devices: 8.83 us -> 4.33 us  [the longest x1 2.41 us: shards(): peers_twin = lax.ppermute(peers, 'core', swap)]
    all_gather x1, waiting for transfers between devices: 8.66 us -> 6.12 us  [shards(): root_own = lax.all_gather(pair, 'z', axis=0, tiled=True)]
    all_to_all x4, waiting for transfers between devices: 23.1 us -> 20.8 us  [exchange(): return lax.all_to_all(blocks, axis, split_axis=0, concat_axis=0, tiled=True)]
    split x1 -> x0, local copies, waits for them, and re-layouts: 1.73 us -> none  [shards(): jnp.split(root_own, SPLITS)]
  transfers between devices with their start and end apart: 16 -> 14, of which waited for: 7 -> 6; matrix products, arithmetic and copies ran while one was open for 3% -> 2% of each run, Pallas kernels for 12% -> 13%
where the time goes in v7:
time: 135 us; the launch traced here: 134 us
  starting transfers between devices  55.1 us (41%)
  waiting for transfers between devices  36.2 us (27%)
  Pallas kernels  20.2 us (15%)
  between operations  14.4 us (11%)
  local copies, waits for them, and re-layouts  4.47 us (3%)
  other arithmetic  3.33 us (2%)
    all_to_all x4, starting transfers between devices, exchange(): return lax.all_to_all(blocks, axis, split_axis=0, concat_axis=0, tiled=True)  31.3 us
    all_to_all x4, waiting for transfers between devices, exchange(): return lax.all_to_all(blocks, axis, split_axis=0, concat_axis=0, tiled=True)  20.8 us
    pallas_call x1, Pallas kernels, shards(): pl.pallas_call(root_kernel, out_shape=(whole, whole), in_specs=[vmem()] *...  7.38 us
    pallas_call x1, Pallas kernels, shards(): pl.pallas_call(functools.partial(branch_kernel, count), out_shape=jax.Sha...  7.19 us
    all_gather x1, waiting for transfers between devices, shards(): root_own = lax.all_gather(pair, 'z', axis=0, tiled=True)  6.12 us
    ppermute x1, waiting for transfers between devices, shards(): pair = jnp.stack([root_block, lax.ppermute(root_block, 'xhi', swap)])  5.23 us
    ppermute x1, starting transfers between devices, shards(): pair = jnp.stack([root_block, lax.ppermute(root_block, 'xhi', swap)])  4.01 us
    ppermute x1, starting transfers between devices, shards(): values_far = lax.ppermute(values_own, 'xhi', swap)  3.76 us
  transfers between devices with their start and end apart: 14, of which 6 were waited for; matrix products, arithmetic and copies ran while one was open for 2% of the time, Pallas kernels for 13%

profile of v7, /device:TPU:6, one launch (start us, length us, event | category | flops | bytes accessed | tf_op | source)
XLA Modules:
  0.0 133.8 jit_solution(7649128196718582622)
XLA Ops:
  6.5 0.9 copy.37
  7.4 0.9 broadcast_in_dim.46
  8.3 8.6 %all-to-all-start = ((bf16[16,128,128]{2,1,0:T(8,128)(2,1)}), bf16[16,128,128]{2,1,0:T(8,128)(2,1)S(1)}, u32[]{:S(2)}, u32[]{:S(2)}) async-start(bf16[16,128,128]{2,1,0:T(8,128)(2,1)} %broadcast_in_dim.46), calls=%async_computation | async-start | bytes 1048576 | tf_op jit(solution)/shard_map/all_to_all | solution.py:261
  16.9 0.0 all-gather.2.cloned.1.call-start
  16.9 0.0 copy-done.13
  17.0 0.0 copy-start.14
  17.0 0.0 copy-start.15
  17.0 4.0 %collective-permute-start = (bf16[8,64,128]{2,1,0:T(8,128)(2,1)S(1)}, bf16[8,64,128]{2,1,0:T(8,128)(2,1)S(1)}, u32[]{:S(2)}, u32[]{:S(2)}) collective-permute-start(bf16[8,64,128]{2,1,0:T(8,128)(2,1)S(1)} %bitcast.40), channel_id=1, source_target_pairs={{0,16},{16,0},{1,17},{17,1},{2,18},{18,2},{3,19},{19,3},{4,20},{20... | collective-permute-start | bytes 393224 | tf_op jit(solution)/shard_map/ppermute | solution.py:329
  21.0 0.2 copy_bitcast_fusion
  21.2 0.0 copy-start.5
  21.2 0.0 copy-start.4
  21.3 5.2 %collective-permute-done = bf16[8,64,128]{2,1,0:T(8,128)(2,1)S(1)} collective-permute-done((bf16[8,64,128]{2,1,0:T(8,128)(2,1)S(1)}, bf16[8,64,128]{2,1,0:T(8,128)(2,1)S(1)}, u32[]{:S(2)}, u32[]{:S(2)}) %collective-permute-start) | collective-permute-done | bytes 131104 | tf_op jit(solution)/shard_map/ppermute | solution.py:329
  26.5 0.7 pad_maximum_fusion
  27.2 0.0 all-gather.2.cloned.1.call-update
  27.3 0.1 select_reduce_fusion
  27.3 0.1 reshape.39
  27.4 0.2 fusion
  27.6 0.1 convert_reduce_fusion
  27.7 0.1 fusion.2.idx_ref
  27.9 3.6 %collective-permute-start.3 = (bf16[8,256,128]{2,1,0:T(8,128)(2,1)S(1)}, bf16[8,256,128]{2,1,0:T(8,128)(2,1)S(1)}, u32[]{:S(2)}, u32[]{:S(2)}) collective-permute-start(bf16[8,256,128]{2,1,0:T(8,128)(2,1)S(1)} %bitcast.37), channel_id=1, source_target_pairs={{0,16},{16,0},{1,17},{17,1},{2,18},{18,2},{3,19},{19,3},{4,20},{20... | collective-permute-start | bytes 1572872 | tf_op jit(solution)/shard_map/ppermute | solution.py:335
  31.5 3.8 %collective-permute-start.4 = (bf16[8,256,128]{2,1,0:T(8,128)(2,1)S(1)}, bf16[8,256,128]{2,1,0:T(8,128)(2,1)}, u32[]{:S(2)}, u32[]{:S(2)}) collective-permute-start(bf16[8,256,128]{2,1,0:T(8,128)(2,1)S(1)} %bitcast.34), channel_id=1, source_target_pairs={{0,16},{16,0},{1,17},{17,1},{2,18},{18,2},{3,19},{19,3},{4,20},{20... | collective-permute-start | bytes 1572872 | tf_op jit(solution)/shard_map/ppermute | solution.py:336
  35.2 0.0 all-to-all-done.peer_ref.q_ref
  35.2 1.4 %pick_readers.1 = bf16[8,2,128,128]{3,2,1,0:T(8,128)(2,1)} custom-call(s32[2]{0:T(128)S(1)} %fusion.2.idx_ref, bf16[16,128,128]{2,1,0:T(8,128)(2,1)S(1)} %all-to-all-done.peer_ref.q_ref), custom_call_target="tpu_custom_call" | custom-call | flops 21474836480 | bytes 6291456 | tf_op jit(solution)/shard_map/pick_readers/pallas_call | solution.py:311
  36.6 9.9 %all-to-all-start.1 = ((bf16[8,2,128,128]{3,2,1,0:T(8,128)(2,1)}), bf16[8,2,128,128]{3,2,1,0:T(8,128)(2,1)S(1)}, u32[]{:S(2)}, u32[]{:S(2)}) async-start(bf16[8,2,128,128]{3,2,1,0:T(8,128)(2,1)} %pick_readers.1), calls=%async_computation.1 | async-start | bytes 1048576 | tf_op jit(solution)/shard_map/all_to_all | solution.py:261
  46.6 1.9 %collective-permute-start.1 = (bf16[8,256,128]{2,1,0:T(8,128)(2,1)S(1)}, bf16[8,256,128]{2,1,0:T(8,128)(2,1)S(1)}, u32[]{:S(2)}, u32[]{:S(2)}) collective-permute-start(bf16[8,256,128]{2,1,0:T(8,128)(2,1)S(1)} %bitcast.38), channel_id=1, source_target_pairs={{0,1},{1,0},{2,3},{3,2},{4,5},{5,4},{6,7},{7,6},{8,9},{9,8},{10,11... | collective-permute-start | bytes 1572872 | tf_op jit(solution)/shard_map/ppermute | solution.py:341
  48.5 2.4 %collective-permute-start.2 = (bf16[8,256,128]{2,1,0:T(8,128)(2,1)S(1)}, bf16[8,256,128]{2,1,0:T(8,128)(2,1)S(1)}, u32[]{:S(2)}, u32[]{:S(2)}) collective-permute-start(bf16[8,256,128]{2,1,0:T(8,128)(2,1)S(1)} %bitcast.35), channel_id=1, source_target_pairs={{0,1},{1,0},{2,3},{3,2},{4,5},{5,4},{6,7},{7,6},{8,9},{9,8},{10,11... | collective-permute-start | bytes 1572872 | tf_op jit(solution)/shard_map/ppermute | solution.py:342
  50.9 0.0 collective-permute-done.3.refs_4_
  50.9 1.9 %collective-permute-start.5 = (bf16[8,256,128]{2,1,0:T(8,128)(2,1)S(1)}, bf16[8,256,128]{2,1,0:T(8,128)(2,1)S(1)}, u32[]{:S(2)}, u32[]{:S(2)}) collective-permute-start(bf16[8,256,128]{2,1,0:T(8,128)(2,1)S(1)} %collective-permute-done.3.refs_4_), channel_id=1, source_target_pairs={{0,1},{1,0},{2,3},{3,2},{4,5},{5,4},{6,7},{7,6},{8,9},{9,8},{10,11... | collective-permute-start | bytes 1572872 | tf_op jit(solution)/shard_map/ppermute | solution.py:345
  52.9 2.1 %collective-permute-done.4.refs_5_ = bf16[8,256,128]{2,1,0:T(8,128)(2,1)} collective-permute-done((bf16[8,256,128]{2,1,0:T(8,128)(2,1)S(1)}, bf16[8,256,128]{2,1,0:T(8,128)(2,1)}, u32[]{:S(2)}, u32[]{:S(2)}) %collective-permute-start.4) | collective-permute-done | bytes 524320 | tf_op jit(solution)/shard_map/ppermute | solution.py:336
  54.9 1.9 %collective-permute-start.6 = (bf16[8,256,128]{2,1,0:T(8,128)(2,1)}, bf16[8,256,128]{2,1,0:T(8,128)(2,1)}, u32[]{:S(2)}, u32[]{:S(2)}) collective-permute-start(bf16[8,256,128]{2,1,0:T(8,128)(2,1)} %collective-permute-done.4.refs_5_), channel_id=1, source_target_pairs={{0,1},{1,0},{2,3},{3,2},{4,5},{5,4},{6,7},{7,6},{8,9},{9,8},{10,11... | collective-permute-start | bytes 1572872 | tf_op jit(solution)/shard_map/ppermute | solution.py:346
  56.8 2.4 %collective-permute-start.7 = (bf16[16,128,128]{2,1,0:T(8,128)(2,1)S(1)}, bf16[16,128,128]{2,1,0:T(8,128)(2,1)S(1)}, u32[]{:S(2)}, u32[]{:S(2)}) collective-permute-start(bf16[16,128,128]{2,1,0:T(8,128)(2,1)S(1)} %all-to-all-done.peer_ref.q_ref), channel_id=1, source_target_pairs={{0,1},{1,0},{2,3},{3,2},{4,5},{5,4},{6,7},{7,6},{8,9},{9,8},{10,11... | collective-permute-start | bytes 1572872 | tf_op jit(solution)/shard_map/ppermute | solution.py:382
  59.3 0.0 collective-permute-done.1.refs_2_
  59.3 0.0 collective-permute-done.2.refs_3_
  59.3 0.0 copy-start.8
  59.3 0.0 collective-permute-done.5.refs_6_
  59.3 0.7 copy-done.7
  60.1 0.2 copy-done.8
  60.2 0.8 copy-done.9
  61.1 0.0 collective-permute-done.6.refs_7_
  61.1 5.6 %all-to-all-done.1 = bf16[8,2,128,128]{3,2,1,0:T(8,128)(2,1)S(1)} async-done(((bf16[8,2,128,128]{3,2,1,0:T(8,128)(2,1)}), bf16[8,2,128,128]{3,2,1,0:T(8,128)(2,1)S(1)}, u32[]{:S(2)}, u32[]{:S(2)}) %all-to-all-start.1) | async-done | bytes 524320 | tf_op jit(solution)/shard_map/all_to_all | solution.py:261
  66.6 7.2 %branch_attention.1 = f32[16,136,128]{2,1,0:T(8,128)S(1)} custom-call(bf16[16,128,128]{2,1,0:T(8,128)(2,1)S(1)} %bitcast.26, bf16[8,256,128]{2,1,0:T(8,128)(2,1)} %bitcast.39, bf16[8,256,128]{2,1,0:T(8,128)(2,1)} %bitcast.36, bf16[8,256,128]{2,1,0:T(8,128)(2,1)} %copy-done.7, bf16[8,256,128]{2,1,0:T(8,128)(2,1)} %copy-done.8, ...), custom_call_target="tpu_custom_call" | custom-call | flops 1073741824 | bytes 6291456 | tf_op jit(solution)/shard_map/branch_attention/pallas_call | solution.py:371
  73.8 0.9 convert_element_type.22
  74.7 4.2 %all-to-all-start.2 = ((f16[8,2,136,128]{3,2,1,0:T(8,128)(2,1)}), f16[8,2,136,128]{3,2,1,0:T(8,128)(2,1)S(1)}, u32[]{:S(2)}, u32[]{:S(2)}) async-start(f16[8,2,136,128]{3,2,1,0:T(8,128)(2,1)} %bitcast.11), calls=%async_computation.2 | async-start | bytes 1114112 | tf_op jit(solution)/shard_map/all_to_all | solution.py:261
  79.0 0.0 collective-permute-done.7.q_twin_ref
  79.0 6.1 %all-gather.2.cloned.1.call-done.block_ref = bf16[16,8,64,128]{3,2,1,0:T(8,128)(2,1)} async-done(((bf16[2,8,64,128]{3,2,1,0:T(8,128)(2,1)}), bf16[16,8,64,128]{3,2,1,0:T(8,128)(2,1)}) %all-gather.2.cloned.1.call-update) | async-done | bytes 2097168 | tf_op jit(solution)/shard_map/all_gather | solution.py:331
  85.1 7.4 %root_attention.1 = (f32[16,136,128]{2,1,0:T(8,128)S(1)}, f32[16,136,128]{2,1,0:T(8,128)S(1)}) custom-call(bf16[16,128,128]{2,1,0:T(8,128)(2,1)S(1)} %all-to-all-done.peer_ref.q_ref, bf16[16,128,128]{2,1,0:T(8,128)(2,1)S(1)} %collective-permute-done.7.q_twin_ref, bf16[16,8,64,128]{3,2,1,0:T(8,128)(2,1)} %all-gather.2.cloned.1.call-done.block_ref), custom_call_target="tpu_custom_call" | custom-call | flops 1073741824 | bytes 6291456 | tf_op jit(solution)/shard_map/root_attention/pallas_call | solution.py:387
  92.5 0.1 convert_element_type.23
  92.6 1.9 %collective-permute-start.8 = (f16[16,136,128]{2,1,0:T(8,128)(2,1)S(1)}, f16[16,136,128]{2,1,0:T(8,128)(2,1)S(1)}, u32[]{:S(2)}, u32[]{:S(2)}) collective-permute-start(f16[16,136,128]{2,1,0:T(8,128)(2,1)S(1)} %convert_element_type.23), channel_id=1, source_target_pairs={{0,1},{1,0},{2,3},{3,2},{4,5},{5,4},{6,7},{7,6},{8,9},{9,8},{10,11... | collective-permute-start | bytes 1671176 | tf_op jit(solution)/shard_map/ppermute | solution.py:397
  94.5 1.9 %collective-permute-done.8 = f16[16,136,128]{2,1,0:T(8,128)(2,1)S(1)} collective-permute-done((f16[16,136,128]{2,1,0:T(8,128)(2,1)S(1)}, f16[16,136,128]{2,1,0:T(8,128)(2,1)S(1)}, u32[]{:S(2)}, u32[]{:S(2)}) %collective-permute-start.8) | collective-permute-done | bytes 557088 | tf_op jit(solution)/shard_map/ppermute | solution.py:397
  96.4 0.1 convert_element_type.24.twin_ref
  96.5 0.0 all-to-all-done.2
  96.5 0.1 convert_element_type.25.part_ref
  96.6 2.2 %merge_parts.1 = f32[16,136,128]{2,1,0:T(8,128)S(1)} custom-call(s32[2]{0:T(128)S(1)} %fusion.2.idx_ref, f32[8,2,136,128]{3,2,1,0:T(8,128)S(1)} %convert_element_type.25.part_ref, f32[16,136,128]{2,1,0:T(8,128)S(1)} %get-tuple-element.25.own_ref, f32[16,136,128]{2,1,0:T(8,128)S(1)} %convert_element_type.24.twin_ref), custom_call_target="tpu_custom_call" | custom-call | tf_op jit(solution)/shard_map/merge_parts/pallas_call | solution.py:400
  98.8 0.0 copy-start
  98.8 0.0 copy-start.1
  98.8 0.0 copy-start.2
  98.8 0.0 copy-start.3
  98.8 0.9 convert_element_type.26
  99.7 8.5 %all-to-all-start.3 = ((f16[16,136,128]{2,1,0:T(8,128)(2,1)}), f16[16,136,128]{2,1,0:T(8,128)(2,1)S(1)}, u32[]{:S(2)}, u32[]{:S(2)}) async-start(f16[16,136,128]{2,1,0:T(8,128)(2,1)} %convert_element_type.26), calls=%async_computation.3 | async-start | bytes 1114112 | tf_op jit(solution)/shard_map/all_to_all | solution.py:261
  108.9 1.5 %local_attention.1.local_ref = f32[136,128]{1,0:T(8,128)S(1)} custom-call(s32[1]{0:T(128)S(6)} %copy.50.len_ref, bf16[128,128]{1,0:T(8,128)(2,1)S(1)} %bitcast.30, bf16[4096,128]{1,0:T(8,128)(2,1)S(1)} %bitcast.27, bf16[4096,128]{1,0:T(8,128)(2,1)S(1)} %bitcast.28, bf16[16,128]{1,0:T(8,128)(2,1)S(1)} %bitcast.32, bf16[16,128]{1,0:T(8,128)(2,1)S(1)} %bitcast.33), custom_call_target="tpu_custom_call" | custom-call | flops 268435456 | bytes 2097152 | tf_op jit(solution)/shard_map/local_attention/pallas_call | solution.py:349
  110.4 15.2 %all-to-all-done.3 = f16[16,136,128]{2,1,0:T(8,128)(2,1)S(1)} async-done(((f16[16,136,128]{2,1,0:T(8,128)(2,1)}), f16[16,136,128]{2,1,0:T(8,128)(2,1)S(1)}, u32[]{:S(2)}, u32[]{:S(2)}) %all-to-all-start.3) | async-done | bytes 557088 | tf_op jit(solution)/shard_map/all_to_all | solution.py:261
  125.6 0.1 convert_element_type.27.part_ref
  125.7 0.6 final_merge.1
  126.3 0.6 copy.48
  (21 shorter events, 0.1 us)
Async XLA Ops:
  6.5 10.4 %copy-start.12 = (bf16[32,8,128]{2,1,0:T(8,128)(2,1)S(1)}, bf16[32,8,128]{2,1,0:T(8,128)(2,1)}, u32[]{:S(2)}) copy-start(bf16[32,8,128]{2,1,0:T(8,128)(2,1)} %param.13) | copy-start | bytes 196612
  6.5 10.4 %copy-start.13 = (bf16[32,8,128]{2,1,0:T(8,128)(2,1)S(1)}, bf16[32,8,128]{2,1,0:T(8,128)(2,1)}, u32[]{:S(2)}) copy-start(bf16[32,8,128]{2,1,0:T(8,128)(2,1)} %param.14) | copy-start | bytes 196612
  6.5 14.5 %copy-start.11 = (bf16[1,256,8,128]{3,2,1,0:T(8,128)(2,1)S(1)}, bf16[1,256,8,128]{3,2,1,0:T(8,128)(2,1)}, u32[]{:S(2)}) copy-start(bf16[1,256,8,128]{3,2,1,0:T(8,128)(2,1)} %param.15) | copy-start | bytes 1572868
  6.5 14.5 %copy-start.10 = (bf16[1,256,8,128]{3,2,1,0:T(8,128)(2,1)S(1)}, bf16[1,256,8,128]{3,2,1,0:T(8,128)(2,1)}, u32[]{:S(2)}) copy-start(bf16[1,256,8,128]{3,2,1,0:T(8,128)(2,1)} %param.16) | copy-start | bytes 1572868
  8.3 26.9 %all-to-all-start = ((bf16[16,128,128]{2,1,0:T(8,128)(2,1)}), bf16[16,128,128]{2,1,0:T(8,128)(2,1)S(1)}, u32[]{:S(2)}, u32[]{:S(2)}) async-start(bf16[16,128,128]{2,1,0:T(8,128)(2,1)} %broadcast_in_dim.46), calls=%async_computation | async-start | bytes 1048576 | tf_op jit(solution)/shard_map/all_to_all | solution.py:261
  16.9 68.2 %all-gather.2.cloned.1.call-start = ((), (), s32[]{:S(2)}) async-start(), calls=%async_computation.4 | async-start | bytes 2359296 | tf_op jit(solution)/shard_map/all_gather | solution.py:331
  17.0 10.3 %copy-start.14 = (s32[512]{0:T(512)S(1)}, s32[512]{0:T(512)}, u32[]{:S(2)}) copy-start(s32[512]{0:T(512)} %param.21) | copy-start | bytes 6148
  17.0 10.3 %copy-start.15 = (s32[16]{0:T(128)S(1)}, s32[16]{0:T(128)}, u32[]{:S(2)}) copy-start(s32[16]{0:T(128)} %param.22) | copy-start | bytes 196
  17.0 9.5 %collective-permute-start = (bf16[8,64,128]{2,1,0:T(8,128)(2,1)S(1)}, bf16[8,64,128]{2,1,0:T(8,128)(2,1)S(1)}, u32[]{:S(2)}, u32[]{:S(2)}) collective-permute-start(bf16[8,64,128]{2,1,0:T(8,128)(2,1)S(1)} %bitcast.40), channel_id=1, source_target_pairs={{0,16},{16,0},{1,17},{17,1},{2,18},{18,2},{3,19},{19,3},{4,20},{20... | collective-permute-start | bytes 393224 | tf_op jit(solution)/shard_map/ppermute | solution.py:329
  21.2 25.3 %copy-start.5 = (bf16[256,8,128]{2,0,1:T(8,128)(2,1)}, bf16[256,8,128]{2,0,1:T(8,128)(2,1)S(1)}, u32[]{:S(2)}) copy-start(bf16[256,8,128]{2,0,1:T(8,128)(2,1)S(1)} %get-tuple-element.18) | copy-start | bytes 1572868
  21.2 27.3 %copy-start.4 = (bf16[256,8,128]{2,0,1:T(8,128)(2,1)}, bf16[256,8,128]{2,0,1:T(8,128)(2,1)S(1)}, u32[]{:S(2)}) copy-start(bf16[256,8,128]{2,0,1:T(8,128)(2,1)S(1)} %get-tuple-element.19) | copy-start | bytes 1572868
  27.9 23.1 %collective-permute-start.3 = (bf16[8,256,128]{2,1,0:T(8,128)(2,1)S(1)}, bf16[8,256,128]{2,1,0:T(8,128)(2,1)S(1)}, u32[]{:S(2)}, u32[]{:S(2)}) collective-permute-start(bf16[8,256,128]{2,1,0:T(8,128)(2,1)S(1)} %bitcast.37), channel_id=1, source_target_pairs={{0,16},{16,0},{1,17},{17,1},{2,18},{18,2},{3,19},{19,3},{4,20},{20... | collective-permute-start | bytes 1572872 | tf_op jit(solution)/shard_map/ppermute | solution.py:335
  31.5 23.5 %collective-permute-start.4 = (bf16[8,256,128]{2,1,0:T(8,128)(2,1)S(1)}, bf16[8,256,128]{2,1,0:T(8,128)(2,1)}, u32[]{:S(2)}, u32[]{:S(2)}) collective-permute-start(bf16[8,256,128]{2,1,0:T(8,128)(2,1)S(1)} %bitcast.34), channel_id=1, source_target_pairs={{0,16},{16,0},{1,17},{17,1},{2,18},{18,2},{3,19},{19,3},{4,20},{20... | collective-permute-start | bytes 1572872 | tf_op jit(solution)/shard_map/ppermute | solution.py:336
  36.6 30.0 %all-to-all-start.1 = ((bf16[8,2,128,128]{3,2,1,0:T(8,128)(2,1)}), bf16[8,2,128,128]{3,2,1,0:T(8,128)(2,1)S(1)}, u32[]{:S(2)}, u32[]{:S(2)}) async-start(bf16[8,2,128,128]{3,2,1,0:T(8,128)(2,1)} %pick_readers.1), calls=%async_computation.1 | async-start | bytes 1048576 | tf_op jit(solution)/shard_map/all_to_all | solution.py:261
  46.6 12.7 %collective-permute-start.1 = (bf16[8,256,128]{2,1,0:T(8,128)(2,1)S(1)}, bf16[8,256,128]{2,1,0:T(8,128)(2,1)S(1)}, u32[]{:S(2)}, u32[]{:S(2)}) collective-permute-start(bf16[8,256,128]{2,1,0:T(8,128)(2,1)S(1)} %bitcast.38), channel_id=1, source_target_pairs={{0,1},{1,0},{2,3},{3,2},{4,5},{5,4},{6,7},{7,6},{8,9},{9,8},{10,11... | collective-permute-start | bytes 1572872 | tf_op jit(solution)/shard_map/ppermute | solution.py:341
  48.5 10.8 %collective-permute-start.2 = (bf16[8,256,128]{2,1,0:T(8,128)(2,1)S(1)}, bf16[8,256,128]{2,1,0:T(8,128)(2,1)S(1)}, u32[]{:S(2)}, u32[]{:S(2)}) collective-permute-start(bf16[8,256,128]{2,1,0:T(8,128)(2,1)S(1)} %bitcast.35), channel_id=1, source_target_pairs={{0,1},{1,0},{2,3},{3,2},{4,5},{5,4},{6,7},{7,6},{8,9},{9,8},{10,11... | collective-permute-start | bytes 1572872 | tf_op jit(solution)/shard_map/ppermute | solution.py:342
  50.9 15.7 %copy-start.6 = (bf16[8,256,128]{2,1,0:T(8,128)(2,1)}, bf16[8,256,128]{2,1,0:T(8,128)(2,1)S(1)}, u32[]{:S(2)}) copy-start(bf16[8,256,128]{2,1,0:T(8,128)(2,1)S(1)} %collective-permute-done.3.refs_4_) | copy-start | bytes 1572868
  50.9 8.4 %collective-permute-start.5 = (bf16[8,256,128]{2,1,0:T(8,128)(2,1)S(1)}, bf16[8,256,128]{2,1,0:T(8,128)(2,1)S(1)}, u32[]{:S(2)}, u32[]{:S(2)}) collective-permute-start(bf16[8,256,128]{2,1,0:T(8,128)(2,1)S(1)} %collective-permute-done.3.refs_4_), channel_id=1, source_target_pairs={{0,1},{1,0},{2,3},{3,2},{4,5},{5,4},{6,7},{7,6},{8,9},{9,8},{10,11... | collective-permute-start | bytes 1572872 | tf_op jit(solution)/shard_map/ppermute | solution.py:345
  54.9 6.1 %collective-permute-start.6 = (bf16[8,256,128]{2,1,0:T(8,128)(2,1)}, bf16[8,256,128]{2,1,0:T(8,128)(2,1)}, u32[]{:S(2)}, u32[]{:S(2)}) collective-permute-start(bf16[8,256,128]{2,1,0:T(8,128)(2,1)} %collective-permute-done.4.refs_5_), channel_id=1, source_target_pairs={{0,1},{1,0},{2,3},{3,2},{4,5},{5,4},{6,7},{7,6},{8,9},{9,8},{10,11... | collective-permute-start | bytes 1572872 | tf_op jit(solution)/shard_map/ppermute | solution.py:346
  56.8 22.1 %collective-permute-start.7 = (bf16[16,128,128]{2,1,0:T(8,128)(2,1)S(1)}, bf16[16,128,128]{2,1,0:T(8,128)(2,1)S(1)}, u32[]{:S(2)}, u32[]{:S(2)}) collective-permute-start(bf16[16,128,128]{2,1,0:T(8,128)(2,1)S(1)} %all-to-all-done.peer_ref.q_ref), channel_id=1, source_target_pairs={{0,1},{1,0},{2,3},{3,2},{4,5},{5,4},{6,7},{7,6},{8,9},{9,8},{10,11... | collective-permute-start | bytes 1572872 | tf_op jit(solution)/shard_map/ppermute | solution.py:382
  59.3 0.8 copy-start.7
  59.3 1.0 copy-start.8
  60.2 0.8 copy-start.9
  74.7 21.8 %all-to-all-start.2 = ((f16[8,2,136,128]{3,2,1,0:T(8,128)(2,1)}), f16[8,2,136,128]{3,2,1,0:T(8,128)(2,1)S(1)}, u32[]{:S(2)}, u32[]{:S(2)}) async-start(f16[8,2,136,128]{3,2,1,0:T(8,128)(2,1)} %bitcast.11), calls=%async_computation.2 | async-start | bytes 1114112 | tf_op jit(solution)/shard_map/all_to_all | solution.py:261
  92.6 3.9 %collective-permute-start.8 = (f16[16,136,128]{2,1,0:T(8,128)(2,1)S(1)}, f16[16,136,128]{2,1,0:T(8,128)(2,1)S(1)}, u32[]{:S(2)}, u32[]{:S(2)}) collective-permute-start(f16[16,136,128]{2,1,0:T(8,128)(2,1)S(1)} %convert_element_type.23), channel_id=1, source_target_pairs={{0,1},{1,0},{2,3},{3,2},{4,5},{5,4},{6,7},{7,6},{8,9},{9,8},{10,11... | collective-permute-start | bytes 1671176 | tf_op jit(solution)/shard_map/ppermute | solution.py:397
  98.8 10.1 %copy-start = (bf16[1,512,8,128]{3,2,1,0:T(8,128)(2,1)S(1)}, bf16[1,512,8,128]{3,2,1,0:T(8,128)(2,1)}, u32[]{:S(2)}) copy-start(bf16[1,512,8,128]{3,2,1,0:T(8,128)(2,1)} %param.17) | copy-start | bytes 3145732
  98.8 10.1 %copy-start.1 = (bf16[1,512,8,128]{3,2,1,0:T(8,128)(2,1)S(1)}, bf16[1,512,8,128]{3,2,1,0:T(8,128)(2,1)}, u32[]{:S(2)}) copy-start(bf16[1,512,8,128]{3,2,1,0:T(8,128)(2,1)} %param.18) | copy-start | bytes 3145732
  98.8 10.1 %copy-start.2 = (bf16[1,2,8,128]{3,2,1,0:T(8,128)(2,1)S(1)}, bf16[1,2,8,128]{3,2,1,0:T(8,128)(2,1)}, u32[]{:S(2)}) copy-start(bf16[1,2,8,128]{3,2,1,0:T(8,128)(2,1)} %param.19) | copy-start | bytes 12292
  98.8 10.1 %copy-start.3 = (bf16[1,2,8,128]{3,2,1,0:T(8,128)(2,1)S(1)}, bf16[1,2,8,128]{3,2,1,0:T(8,128)(2,1)}, u32[]{:S(2)}) copy-start(bf16[1,2,8,128]{3,2,1,0:T(8,128)(2,1)} %param.20) | copy-start | bytes 12292
  99.7 25.9 %all-to-all-start.3 = ((f16[16,136,128]{2,1,0:T(8,128)(2,1)}), f16[16,136,128]{2,1,0:T(8,128)(2,1)S(1)}, u32[]{:S(2)}, u32[]{:S(2)}) async-start(f16[16,136,128]{2,1,0:T(8,128)(2,1)} %convert_element_type.26), calls=%async_computation.3 | async-start | bytes 1114112 | tf_op jit(solution)/shard_map/all_to_all | solution.py:261
Sparse Core Ops, SparseCore 0:
  27.4 57.6 all-gather.1

commit v8 on v7

--- a/solution.py
+++ b/solution.py
@@ -11,7 +11,7 @@
 CAP = 2
 PAD = 8
 LOW = -1e30
-PARTS = 4
+PARTS = 8
 EMPHASIS = 20
 NT = (((1,), (1,)), ((), ()))
 
@@ -84,6 +84,16 @@
     out_ref[rows:, :] = jnp.broadcast_to(flat, (PAD, rows))
 
 
+def order_kernel(heads, q_ref, copies_ref, rows_ref):
+    steps, q_heads, _ = q_ref.shape
+    group = q_heads // heads
+    q = q_ref[...].astype(jnp.float32)
+    rows = [q[t, j * group : (j + 1) * group] for j in range(heads) for t in range(steps)]
+    rows = jnp.concatenate(rows, axis=0).astype(rows_ref.dtype)
+    rows_ref[...] = rows
+    copies_ref[...] = jnp.broadcast_to(rows[None], copies_ref.shape)
+
+
 def select_kernel(idx_ref, peer_ref, out_ref):
     out_ref[...] = jnp.broadcast_to(peer_ref[...][None], out_ref.shape)
 
@@ -212,7 +222,7 @@
             out_ref[reader, lanes:, :] = tail_rows(split_lse(high + jnp.log(total)))
 
 
-def final_kernel(part_ref, local_ref, out_ref):
+def final_kernel(heads, part_ref, local_ref, out_ref):
     groups, _, lanes = part_ref.shape
     lse = join_lse(part_ref[:, lanes:, :])
     near = local_ref[lanes : lanes + 1, :]
@@ -224,7 +234,12 @@
     out = local_ref[:lanes, :] * table[:, groups : groups + 1]
     for source in range(groups):
         out = out + part_ref[source, :lanes, :] * table[:, source : source + 1]
-    out_ref[...] = out.astype(out_ref.dtype)
+    steps, q_heads, _ = out_ref.shape
+    group = q_heads // heads
+    for t in range(steps):
+        starts = [(j * steps + t) * group for j in range(heads)]
+        rows = jnp.concatenate([out[start : start + group] for start in starts], axis=0)
+        out_ref[t] = rows.astype(out_ref.dtype)
 
 
 def params(megabytes=20):
@@ -259,10 +274,6 @@
 
 def exchange(blocks, axis):
     return lax.all_to_all(blocks, axis, split_axis=0, concat_axis=0, tiled=True)
-
-
-def to_all(block, axis):
-    return exchange(jnp.broadcast_to(block[None], (lax.axis_size(axis),) + block.shape), axis)
 
 
 def shards(
@@ -292,9 +303,18 @@
     seq_place = (lax.axis_index("xhi") * ring + lax.axis_index("z")) * core + lax.axis_index("core")
     swap = [(0, 1), (1, 0)]
 
-    q_rows = queries[0].reshape(steps, heads, group, dim).transpose(1, 0, 2, 3)
-    q_rows = q_rows.reshape(rows, dim)
-    peers = to_all(q_rows, "grp")
+    copies, q_rows = pl.pallas_call(
+        functools.partial(order_kernel, heads),
+        out_shape=(
+            jax.ShapeDtypeStruct((grp, rows, dim), jnp.bfloat16),
+            jax.ShapeDtypeStruct((rows, dim), jnp.bfloat16),
+        ),
+        in_specs=[vmem()],
+        out_specs=(vmem(), vmem()),
+        compiler_params=params(),
+        name="order_queries",
+    )(queries[0])
+    peers = exchange(copies, "grp")
 
     matches = branch_of[:, None] == jnp.arange(owner.shape[0])[None, :]
     slot_of = jnp.sum(jnp.where(matches, owner[None, :], 0), axis=1)
@@ -407,14 +427,13 @@
     )(readers, parts, root, root_twin)
     back = exchange(merged.astype(jnp.float16), "grp").astype(jnp.float32)
     mine = pl.pallas_call(
-        final_kernel,
-        out_shape=jax.ShapeDtypeStruct((rows, dim), jnp.bfloat16),
+        functools.partial(final_kernel, heads),
+        out_shape=jax.ShapeDtypeStruct((steps, q_heads, dim), jnp.bfloat16),
         in_specs=[vmem()] * 2,
         out_specs=vmem(),
         compiler_params=params(),
         name="final_merge",
     )(back, local)
-    mine = mine.reshape(heads, steps, group, dim).transpose(1, 0, 2, 3)
     return mine.reshape(queries.shape)
 
 

time: 135 us -> 137 us (1.015)
  starting transfers between devices: 55.1 us -> 58.1 us
  waiting for transfers between devices: 36.2 us -> 33.7 us
  Pallas kernels: 20.2 us -> 22.4 us
    all_to_all x4, starting transfers between devices: 31.3 us -> 34.2 us  [exchange(): return lax.all_to_all(blocks, axis, split_axis=0, concat_axis=0, tiled=True)]
    unnamed x33, local copies, waits for them, and re-layouts: 1.82 us -> 3.4 us
    all_gather x1, waiting for transfers between devices: 6.12 us -> 4.6 us  [shards(): root_own = lax.all_gather(pair, 'z', axis=0, tiled=True)]
    pallas_call x1 -> x2, Pallas kernels: 0.58 us -> 2.1 us  [the longest x1 1.2 us: shards(): pl.pallas_call(functools.partial(final_kernel, heads), out_shape=jax.Shap...]
  transfers between devices with their start and end apart: 14 -> 14, of which waited for: 6 -> 7; matrix products, arithmetic and copies ran while one was open for 2% -> 3% of each run, Pallas kernels for 13% -> 14%
where the time goes in v8:
time: 137 us; the launch traced here: 136 us
  starting transfers between devices  58.1 us (42%)
  waiting for transfers between devices  33.7 us (25%)
  Pallas kernels  22.4 us (16%)
  between operations  14.4 us (11%)
  local copies, waits for them, and re-layouts  3.69 us (3%)
  other arithmetic  3.35 us (2%)
    all_to_all x4, starting transfers between devices, exchange(): return lax.all_to_all(blocks, axis, split_axis=0, concat_axis=0, tiled=True)  34.2 us
    all_to_all x4, waiting for transfers between devices, exchange(): return lax.all_to_all(blocks, axis, split_axis=0, concat_axis=0, tiled=True)  20 us
    pallas_call x1, Pallas kernels, shards(): pl.pallas_call(functools.partial(branch_kernel, count), out_shape=jax.Sha...  8.23 us
    pallas_call x1, Pallas kernels, shards(): pl.pallas_call(root_kernel, out_shape=(whole, whole), in_specs=[vmem()] *...  7.81 us
    ppermute x1, waiting for transfers between devices, shards(): pair = jnp.stack([root_block, lax.ppermute(root_block, 'xhi', swap)])  5.28 us
    all_gather x1, waiting for transfers between devices, shards(): root_own = lax.all_gather(pair, 'z', axis=0, tiled=True)  4.6 us
    ppermute x1, starting transfers between devices, shards(): keys_far = lax.ppermute(keys_own, 'xhi', swap)  4.06 us
    ppermute x1, starting transfers between devices, shards(): pair = jnp.stack([root_block, lax.ppermute(root_block, 'xhi', swap)])  4.01 us
  transfers between devices with their start and end apart: 14, of which 7 were waited for; matrix products, arithmetic and copies ran while one was open for 3% of the time, Pallas kernels for 14%

profile of v8, /device:TPU:6, one launch (start us, length us, event | category | flops | bytes accessed | tf_op | source)
XLA Modules:
  0.0 135.7 jit_solution(5918263713352548808)
XLA Ops:
  6.5 0.8 copy-done.2
  7.3 0.9 order_queries.1
  8.2 8.6 %all-to-all-start = ((bf16[16,128,128]{2,1,0:T(8,128)(2,1)}), bf16[16,128,128]{2,1,0:T(8,128)(2,1)S(1)}, u32[]{:S(2)}, u32[]{:S(2)}) async-start(bf16[16,128,128]{2,1,0:T(8,128)(2,1)} %get-tuple-element.18), calls=%async_computation | async-start | bytes 1048576 | tf_op jit(solution)/shard_map/all_to_all | solution.py:276
  16.8 0.0 all-gather.2.cloned.1.call-start
  16.8 0.9 copy_dynamic-update-slice_fusion.1
  17.7 0.0 copy-done.13
  17.7 0.0 copy-start.14
  17.7 0.0 copy-start.15
  17.7 4.0 %collective-permute-start = (bf16[8,64,128]{2,1,0:T(8,128)(2,1)S(1)}, bf16[8,64,128]{2,1,0:T(8,128)(2,1)S(1)}, u32[]{:S(2)}, u32[]{:S(2)}) collective-permute-start(bf16[8,64,128]{2,1,0:T(8,128)(2,1)S(1)} %bitcast.30), channel_id=1, source_target_pairs={{0,16},{16,0},{1,17},{17,1},{2,18},{18,2},{3,19},{19,3},{4,20},{20... | collective-permute-start | bytes 393224 | tf_op jit(solution)/shard_map/ppermute | solution.py:349
  21.8 0.2 copy_bitcast_fusion
  22.0 5.3 %collective-permute-done = bf16[8,64,128]{2,1,0:T(8,128)(2,1)S(1)} collective-permute-done((bf16[8,64,128]{2,1,0:T(8,128)(2,1)S(1)}, bf16[8,64,128]{2,1,0:T(8,128)(2,1)S(1)}, u32[]{:S(2)}, u32[]{:S(2)}) %collective-permute-start) | collective-permute-done | bytes 131104 | tf_op jit(solution)/shard_map/ppermute | solution.py:349
  27.3 0.7 pad_maximum_fusion
  28.0 0.0 all-gather.2.cloned.1.call-update
  28.1 0.1 select_reduce_fusion
  28.1 0.1 reshape.34
  28.2 0.2 fusion
  28.4 0.1 convert_reduce_fusion
  28.5 0.1 fusion.2.idx_ref
  28.7 4.1 %collective-permute-start.3 = (bf16[8,256,128]{2,1,0:T(8,128)(2,1)S(1)}, bf16[8,256,128]{2,1,0:T(8,128)(2,1)S(1)}, u32[]{:S(2)}, u32[]{:S(2)}) collective-permute-start(bf16[8,256,128]{2,1,0:T(8,128)(2,1)S(1)} %bitcast.27), channel_id=1, source_target_pairs={{0,16},{16,0},{1,17},{17,1},{2,18},{18,2},{3,19},{19,3},{4,20},{20... | collective-permute-start | bytes 1572872 | tf_op jit(solution)/shard_map/ppermute | solution.py:355
  32.7 3.3 %collective-permute-start.4 = (bf16[8,256,128]{2,1,0:T(8,128)(2,1)S(1)}, bf16[8,256,128]{2,1,0:T(8,128)(2,1)}, u32[]{:S(2)}, u32[]{:S(2)}) collective-permute-start(bf16[8,256,128]{2,1,0:T(8,128)(2,1)S(1)} %bitcast.24), channel_id=1, source_target_pairs={{0,16},{16,0},{1,17},{17,1},{2,18},{18,2},{3,19},{19,3},{4,20},{20... | collective-permute-start | bytes 1572872 | tf_op jit(solution)/shard_map/ppermute | solution.py:356
  36.0 0.0 all-to-all-done.peer_ref.q_ref
  36.0 1.4 %pick_readers.1 = bf16[8,2,128,128]{3,2,1,0:T(8,128)(2,1)} custom-call(s32[2]{0:T(128)S(1)} %fusion.2.idx_ref, bf16[16,128,128]{2,1,0:T(8,128)(2,1)S(1)} %all-to-all-done.peer_ref.q_ref), custom_call_target="tpu_custom_call" | custom-call | flops 21474836480 | bytes 6291456 | tf_op jit(solution)/shard_map/pick_readers/pallas_call | solution.py:331
  37.4 10.4 %all-to-all-start.1 = ((bf16[8,2,128,128]{3,2,1,0:T(8,128)(2,1)}), bf16[8,2,128,128]{3,2,1,0:T(8,128)(2,1)S(1)}, u32[]{:S(2)}, u32[]{:S(2)}) async-start(bf16[8,2,128,128]{3,2,1,0:T(8,128)(2,1)} %pick_readers.1), calls=%async_computation.1 | async-start | bytes 1048576 | tf_op jit(solution)/shard_map/all_to_all | solution.py:276
  47.9 1.9 %collective-permute-start.1 = (bf16[8,256,128]{2,1,0:T(8,128)(2,1)S(1)}, bf16[8,256,128]{2,1,0:T(8,128)(2,1)S(1)}, u32[]{:S(2)}, u32[]{:S(2)}) collective-permute-start(bf16[8,256,128]{2,1,0:T(8,128)(2,1)S(1)} %bitcast.28), channel_id=1, source_target_pairs={{0,1},{1,0},{2,3},{3,2},{4,5},{5,4},{6,7},{7,6},{8,9},{9,8},{10,11... | collective-permute-start | bytes 1572872 | tf_op jit(solution)/shard_map/ppermute | solution.py:361
  49.8 0.0 copy-done.5
  49.8 2.4 %collective-permute-start.2 = (bf16[8,256,128]{2,1,0:T(8,128)(2,1)S(1)}, bf16[8,256,128]{2,1,0:T(8,128)(2,1)S(1)}, u32[]{:S(2)}, u32[]{:S(2)}) collective-permute-start(bf16[8,256,128]{2,1,0:T(8,128)(2,1)S(1)} %bitcast.25), channel_id=1, source_target_pairs={{0,1},{1,0},{2,3},{3,2},{4,5},{5,4},{6,7},{7,6},{8,9},{9,8},{10,11... | collective-permute-start | bytes 1572872 | tf_op jit(solution)/shard_map/ppermute | solution.py:362
  52.2 0.0 collective-permute-done.3.refs_4_
  52.3 0.0 copy-start.7
  52.3 1.9 %collective-permute-start.5 = (bf16[8,256,128]{2,1,0:T(8,128)(2,1)S(1)}, bf16[8,256,128]{2,1,0:T(8,128)(2,1)S(1)}, u32[]{:S(2)}, u32[]{:S(2)}) collective-permute-start(bf16[8,256,128]{2,1,0:T(8,128)(2,1)S(1)} %collective-permute-done.3.refs_4_), channel_id=1, source_target_pairs={{0,1},{1,0},{2,3},{3,2},{4,5},{5,4},{6,7},{7,6},{8,9},{9,8},{10,11... | collective-permute-start | bytes 1572872 | tf_op jit(solution)/shard_map/ppermute | solution.py:365
  54.2 1.8 %collective-permute-done.4.refs_5_ = bf16[8,256,128]{2,1,0:T(8,128)(2,1)} collective-permute-done((bf16[8,256,128]{2,1,0:T(8,128)(2,1)S(1)}, bf16[8,256,128]{2,1,0:T(8,128)(2,1)}, u32[]{:S(2)}, u32[]{:S(2)}) %collective-permute-start.4) | collective-permute-done | bytes 524320 | tf_op jit(solution)/shard_map/ppermute | solution.py:356
  56.0 1.9 %collective-permute-start.6 = (bf16[8,256,128]{2,1,0:T(8,128)(2,1)}, bf16[8,256,128]{2,1,0:T(8,128)(2,1)}, u32[]{:S(2)}, u32[]{:S(2)}) collective-permute-start(bf16[8,256,128]{2,1,0:T(8,128)(2,1)} %collective-permute-done.4.refs_5_), channel_id=1, source_target_pairs={{0,1},{1,0},{2,3},{3,2},{4,5},{5,4},{6,7},{7,6},{8,9},{9,8},{10,11... | collective-permute-start | bytes 1572872 | tf_op jit(solution)/shard_map/ppermute | solution.py:366
  57.9 2.4 %collective-permute-start.7 = (bf16[16,128,128]{2,1,0:T(8,128)(2,1)S(1)}, bf16[16,128,128]{2,1,0:T(8,128)(2,1)S(1)}, u32[]{:S(2)}, u32[]{:S(2)}) collective-permute-start(bf16[16,128,128]{2,1,0:T(8,128)(2,1)S(1)} %all-to-all-done.peer_ref.q_ref), channel_id=1, source_target_pairs={{0,1},{1,0},{2,3},{3,2},{4,5},{5,4},{6,7},{7,6},{8,9},{9,8},{10,11... | collective-permute-start | bytes 1572872 | tf_op jit(solution)/shard_map/ppermute | solution.py:402
  60.4 0.0 collective-permute-done.1.refs_2_
  60.4 0.0 collective-permute-done.2.refs_3_
  60.4 0.0 copy-start.9
  60.4 0.0 collective-permute-done.5.refs_6_
  60.4 0.7 copy-done.8
  61.2 0.2 copy-done.9
  61.3 0.8 copy-done.10
  62.1 0.0 collective-permute-done.6.refs_7_
  62.1 6.0 %all-to-all-done.1 = bf16[8,2,128,128]{3,2,1,0:T(8,128)(2,1)S(1)} async-done(((bf16[8,2,128,128]{3,2,1,0:T(8,128)(2,1)}), bf16[8,2,128,128]{3,2,1,0:T(8,128)(2,1)S(1)}, u32[]{:S(2)}, u32[]{:S(2)}) %all-to-all-start.1) | async-done | bytes 524320 | tf_op jit(solution)/shard_map/all_to_all | solution.py:276
  68.1 8.2 %branch_attention.1 = f32[16,136,128]{2,1,0:T(8,128)S(1)} custom-call(bf16[16,128,128]{2,1,0:T(8,128)(2,1)S(1)} %bitcast.18, bf16[8,256,128]{2,1,0:T(8,128)(2,1)} %bitcast.29, bf16[8,256,128]{2,1,0:T(8,128)(2,1)} %bitcast.26, bf16[8,256,128]{2,1,0:T(8,128)(2,1)} %copy-done.8, bf16[8,256,128]{2,1,0:T(8,128)(2,1)} %copy-done.9, ...), custom_call_target="tpu_custom_call" | custom-call | flops 1073741824 | bytes 6291456 | tf_op jit(solution)/shard_map/branch_attention/pallas_call | solution.py:391
  76.4 0.9 convert_element_type.22
  77.2 3.7 %all-to-all-start.2 = ((f16[8,2,136,128]{3,2,1,0:T(8,128)(2,1)}), f16[8,2,136,128]{3,2,1,0:T(8,128)(2,1)S(1)}, u32[]{:S(2)}, u32[]{:S(2)}) async-start(f16[8,2,136,128]{3,2,1,0:T(8,128)(2,1)} %bitcast.9), calls=%async_computation.2 | async-start | bytes 1114112 | tf_op jit(solution)/shard_map/all_to_all | solution.py:276
  81.0 0.0 collective-permute-done.7.q_twin_ref
  81.0 4.6 %all-gather.2.cloned.1.call-done.block_ref = bf16[16,8,64,128]{3,2,1,0:T(8,128)(2,1)} async-done(((bf16[2,8,64,128]{3,2,1,0:T(8,128)(2,1)}), bf16[16,8,64,128]{3,2,1,0:T(8,128)(2,1)}) %all-gather.2.cloned.1.call-update) | async-done | bytes 2097168 | tf_op jit(solution)/shard_map/all_gather | solution.py:351
  85.6 7.8 %root_attention.1 = (f32[16,136,128]{2,1,0:T(8,128)S(1)}, f32[16,136,128]{2,1,0:T(8,128)S(1)}) custom-call(bf16[16,128,128]{2,1,0:T(8,128)(2,1)S(1)} %all-to-all-done.peer_ref.q_ref, bf16[16,128,128]{2,1,0:T(8,128)(2,1)S(1)} %collective-permute-done.7.q_twin_ref, bf16[16,8,64,128]{3,2,1,0:T(8,128)(2,1)} %all-gather.2.cloned.1.call-done.block_ref), custom_call_target="tpu_custom_call" | custom-call | flops 1073741824 | bytes 6291456 | tf_op jit(solution)/shard_map/root_attention/pallas_call | solution.py:407
  93.4 0.1 convert_element_type.23
  93.5 1.9 %collective-permute-start.8 = (f16[16,136,128]{2,1,0:T(8,128)(2,1)S(1)}, f16[16,136,128]{2,1,0:T(8,128)(2,1)S(1)}, u32[]{:S(2)}, u32[]{:S(2)}) collective-permute-start(f16[16,136,128]{2,1,0:T(8,128)(2,1)S(1)} %convert_element_type.23), channel_id=1, source_target_pairs={{0,1},{1,0},{2,3},{3,2},{4,5},{5,4},{6,7},{7,6},{8,9},{9,8},{10,11... | collective-permute-start | bytes 1671176 | tf_op jit(solution)/shard_map/ppermute | solution.py:417
  95.4 1.9 %collective-permute-done.8 = f16[16,136,128]{2,1,0:T(8,128)(2,1)S(1)} collective-permute-done((f16[16,136,128]{2,1,0:T(8,128)(2,1)S(1)}, f16[16,136,128]{2,1,0:T(8,128)(2,1)S(1)}, u32[]{:S(2)}, u32[]{:S(2)}) %collective-permute-start.8) | collective-permute-done | bytes 557088 | tf_op jit(solution)/shard_map/ppermute | solution.py:417
  97.3 0.1 convert_element_type.24.twin_ref
  97.4 1.8 %all-to-all-done.2 = f16[8,2,136,128]{3,2,1,0:T(8,128)(2,1)S(1)} async-done(((f16[8,2,136,128]{3,2,1,0:T(8,128)(2,1)}), f16[8,2,136,128]{3,2,1,0:T(8,128)(2,1)S(1)}, u32[]{:S(2)}, u32[]{:S(2)}) %all-to-all-start.2) | async-done | bytes 557088 | tf_op jit(solution)/shard_map/all_to_all | solution.py:276
  99.2 0.1 convert_element_type.25.part_ref
  99.3 1.4 %merge_parts.1 = f32[16,136,128]{2,1,0:T(8,128)S(1)} custom-call(s32[2]{0:T(128)S(1)} %fusion.2.idx_ref, f32[8,2,136,128]{3,2,1,0:T(8,128)S(1)} %convert_element_type.25.part_ref, f32[16,136,128]{2,1,0:T(8,128)S(1)} %get-tuple-element.28.own_ref, f32[16,136,128]{2,1,0:T(8,128)S(1)} %convert_element_type.24.twin_ref), custom_call_target="tpu_custom_call" | custom-call | tf_op jit(solution)/shard_map/merge_parts/pallas_call | solution.py:420
  100.7 0.0 copy-start
  100.7 0.0 copy-start.1
  100.7 0.0 copy-start.3
  100.7 0.0 copy-start.4
  100.7 0.9 convert_element_type.26
  101.6 11.5 %all-to-all-start.3 = ((f16[16,136,128]{2,1,0:T(8,128)(2,1)}), f16[16,136,128]{2,1,0:T(8,128)(2,1)S(1)}, u32[]{:S(2)}, u32[]{:S(2)}) async-start(f16[16,136,128]{2,1,0:T(8,128)(2,1)} %convert_element_type.26), calls=%async_computation.3 | async-start | bytes 1114112 | tf_op jit(solution)/shard_map/all_to_all | solution.py:276
  113.8 1.5 %local_attention.1.local_ref = f32[136,128]{1,0:T(8,128)S(1)} custom-call(s32[1]{0:T(128)S(6)} %copy.38.len_ref, bf16[128,128]{1,0:T(8,128)(2,1)S(1)} %get-tuple-element.30.q_ref, bf16[4096,128]{1,0:T(8,128)(2,1)S(1)} %bitcast.19, bf16[4096,128]{1,0:T(8,128)(2,1)S(1)} %bitcast.20, bf16[16,128]{1,0:T(8,128)(2,1)S(1)} %bitcast.22, bf16[16,128]{1,0:T(8,128)(2,1)S(1)} %bitcast.23), custom_call_target="tpu_custom_call" | custom-call | flops 268435456 | bytes 2097152 | tf_op jit(solution)/shard_map/local_attention/pallas_call | solution.py:369
  115.3 12.3 %all-to-all-done.3 = f16[16,136,128]{2,1,0:T(8,128)(2,1)S(1)} async-done(((f16[16,136,128]{2,1,0:T(8,128)(2,1)}), f16[16,136,128]{2,1,0:T(8,128)(2,1)S(1)}, u32[]{:S(2)}, u32[]{:S(2)}) %all-to-all-start.3) | async-done | bytes 557088 | tf_op jit(solution)/shard_map/all_to_all | solution.py:276
  127.6 0.1 convert_element_type.27.part_ref
  127.7 1.2 final_merge.1
  (19 shorter events, 0.1 us)
Async XLA Ops:
  6.5 0.8 copy-start.2
  7.3 10.4 %copy-start.13 = (bf16[32,8,128]{2,1,0:T(8,128)(2,1)S(1)}, bf16[32,8,128]{2,1,0:T(8,128)(2,1)}, u32[]{:S(2)}) copy-start(bf16[32,8,128]{2,1,0:T(8,128)(2,1)} %param.14) | copy-start | bytes 196612
  7.3 14.5 %copy-start.11 = (bf16[1,256,8,128]{3,2,1,0:T(8,128)(2,1)S(1)}, bf16[1,256,8,128]{3,2,1,0:T(8,128)(2,1)}, u32[]{:S(2)}) copy-start(bf16[1,256,8,128]{3,2,1,0:T(8,128)(2,1)} %param.16) | copy-start | bytes 1572868
  7.3 14.5 %copy-start.12 = (bf16[1,256,8,128]{3,2,1,0:T(8,128)(2,1)S(1)}, bf16[1,256,8,128]{3,2,1,0:T(8,128)(2,1)}, u32[]{:S(2)}) copy-start(bf16[1,256,8,128]{3,2,1,0:T(8,128)(2,1)} %param.15) | copy-start | bytes 1572868
  8.2 27.8 %all-to-all-start = ((bf16[16,128,128]{2,1,0:T(8,128)(2,1)}), bf16[16,128,128]{2,1,0:T(8,128)(2,1)S(1)}, u32[]{:S(2)}, u32[]{:S(2)}) async-start(bf16[16,128,128]{2,1,0:T(8,128)(2,1)} %get-tuple-element.18), calls=%async_computation | async-start | bytes 1048576 | tf_op jit(solution)/shard_map/all_to_all | solution.py:276
  16.8 68.8 %all-gather.2.cloned.1.call-start = ((), (), s32[]{:S(2)}) async-start(), calls=%async_computation.4 | async-start | bytes 2359296 | tf_op jit(solution)/shard_map/all_gather | solution.py:351
  17.7 10.3 %copy-start.14 = (s32[512]{0:T(512)S(1)}, s32[512]{0:T(512)}, u32[]{:S(2)}) copy-start(s32[512]{0:T(512)} %param.21) | copy-start | bytes 6148
  17.7 10.3 %copy-start.15 = (s32[16]{0:T(128)S(1)}, s32[16]{0:T(128)}, u32[]{:S(2)}) copy-start(s32[16]{0:T(128)} %param.22) | copy-start | bytes 196
  17.7 9.5 %collective-permute-start = (bf16[8,64,128]{2,1,0:T(8,128)(2,1)S(1)}, bf16[8,64,128]{2,1,0:T(8,128)(2,1)S(1)}, u32[]{:S(2)}, u32[]{:S(2)}) collective-permute-start(bf16[8,64,128]{2,1,0:T(8,128)(2,1)S(1)} %bitcast.30), channel_id=1, source_target_pairs={{0,16},{16,0},{1,17},{17,1},{2,18},{18,2},{3,19},{19,3},{4,20},{20... | collective-permute-start | bytes 393224 | tf_op jit(solution)/shard_map/ppermute | solution.py:349
  22.0 25.9 %copy-start.6 = (bf16[256,8,128]{2,0,1:T(8,128)(2,1)}, bf16[256,8,128]{2,0,1:T(8,128)(2,1)S(1)}, u32[]{:S(2)}) copy-start(bf16[256,8,128]{2,0,1:T(8,128)(2,1)S(1)} %get-tuple-element.21) | copy-start | bytes 1572868
  22.0 27.8 %copy-start.5 = (bf16[256,8,128]{2,0,1:T(8,128)(2,1)}, bf16[256,8,128]{2,0,1:T(8,128)(2,1)S(1)}, u32[]{:S(2)}) copy-start(bf16[256,8,128]{2,0,1:T(8,128)(2,1)S(1)} %get-tuple-element.22) | copy-start | bytes 1572868
  28.7 23.6 %collective-permute-start.3 = (bf16[8,256,128]{2,1,0:T(8,128)(2,1)S(1)}, bf16[8,256,128]{2,1,0:T(8,128)(2,1)S(1)}, u32[]{:S(2)}, u32[]{:S(2)}) collective-permute-start(bf16[8,256,128]{2,1,0:T(8,128)(2,1)S(1)} %bitcast.27), channel_id=1, source_target_pairs={{0,16},{16,0},{1,17},{17,1},{2,18},{18,2},{3,19},{19,3},{4,20},{20... | collective-permute-start | bytes 1572872 | tf_op jit(solution)/shard_map/ppermute | solution.py:355
  32.7 23.3 %collective-permute-start.4 = (bf16[8,256,128]{2,1,0:T(8,128)(2,1)S(1)}, bf16[8,256,128]{2,1,0:T(8,128)(2,1)}, u32[]{:S(2)}, u32[]{:S(2)}) collective-permute-start(bf16[8,256,128]{2,1,0:T(8,128)(2,1)S(1)} %bitcast.24), channel_id=1, source_target_pairs={{0,16},{16,0},{1,17},{17,1},{2,18},{18,2},{3,19},{19,3},{4,20},{20... | collective-permute-start | bytes 1572872 | tf_op jit(solution)/shard_map/ppermute | solution.py:356
  37.4 30.7 %all-to-all-start.1 = ((bf16[8,2,128,128]{3,2,1,0:T(8,128)(2,1)}), bf16[8,2,128,128]{3,2,1,0:T(8,128)(2,1)S(1)}, u32[]{:S(2)}, u32[]{:S(2)}) async-start(bf16[8,2,128,128]{3,2,1,0:T(8,128)(2,1)} %pick_readers.1), calls=%async_computation.1 | async-start | bytes 1048576 | tf_op jit(solution)/shard_map/all_to_all | solution.py:276
  47.9 12.5 %collective-permute-start.1 = (bf16[8,256,128]{2,1,0:T(8,128)(2,1)S(1)}, bf16[8,256,128]{2,1,0:T(8,128)(2,1)S(1)}, u32[]{:S(2)}, u32[]{:S(2)}) collective-permute-start(bf16[8,256,128]{2,1,0:T(8,128)(2,1)S(1)} %bitcast.28), channel_id=1, source_target_pairs={{0,1},{1,0},{2,3},{3,2},{4,5},{5,4},{6,7},{7,6},{8,9},{9,8},{10,11... | collective-permute-start | bytes 1572872 | tf_op jit(solution)/shard_map/ppermute | solution.py:361
  49.8 10.6 %collective-permute-start.2 = (bf16[8,256,128]{2,1,0:T(8,128)(2,1)S(1)}, bf16[8,256,128]{2,1,0:T(8,128)(2,1)S(1)}, u32[]{:S(2)}, u32[]{:S(2)}) collective-permute-start(bf16[8,256,128]{2,1,0:T(8,128)(2,1)S(1)} %bitcast.25), channel_id=1, source_target_pairs={{0,1},{1,0},{2,3},{3,2},{4,5},{5,4},{6,7},{7,6},{8,9},{9,8},{10,11... | collective-permute-start | bytes 1572872 | tf_op jit(solution)/shard_map/ppermute | solution.py:362
  52.3 15.9 %copy-start.7 = (bf16[8,256,128]{2,1,0:T(8,128)(2,1)}, bf16[8,256,128]{2,1,0:T(8,128)(2,1)S(1)}, u32[]{:S(2)}) copy-start(bf16[8,256,128]{2,1,0:T(8,128)(2,1)S(1)} %collective-permute-done.3.refs_4_) | copy-start | bytes 1572868
  52.3 8.1 %collective-permute-start.5 = (bf16[8,256,128]{2,1,0:T(8,128)(2,1)S(1)}, bf16[8,256,128]{2,1,0:T(8,128)(2,1)S(1)}, u32[]{:S(2)}, u32[]{:S(2)}) collective-permute-start(bf16[8,256,128]{2,1,0:T(8,128)(2,1)S(1)} %collective-permute-done.3.refs_4_), channel_id=1, source_target_pairs={{0,1},{1,0},{2,3},{3,2},{4,5},{5,4},{6,7},{7,6},{8,9},{9,8},{10,11... | collective-permute-start | bytes 1572872 | tf_op jit(solution)/shard_map/ppermute | solution.py:365
  56.0 6.1 %collective-permute-start.6 = (bf16[8,256,128]{2,1,0:T(8,128)(2,1)}, bf16[8,256,128]{2,1,0:T(8,128)(2,1)}, u32[]{:S(2)}, u32[]{:S(2)}) collective-permute-start(bf16[8,256,128]{2,1,0:T(8,128)(2,1)} %collective-permute-done.4.refs_5_), channel_id=1, source_target_pairs={{0,1},{1,0},{2,3},{3,2},{4,5},{5,4},{6,7},{7,6},{8,9},{9,8},{10,11... | collective-permute-start | bytes 1572872 | tf_op jit(solution)/shard_map/ppermute | solution.py:366
  57.9 23.0 %collective-permute-start.7 = (bf16[16,128,128]{2,1,0:T(8,128)(2,1)S(1)}, bf16[16,128,128]{2,1,0:T(8,128)(2,1)S(1)}, u32[]{:S(2)}, u32[]{:S(2)}) collective-permute-start(bf16[16,128,128]{2,1,0:T(8,128)(2,1)S(1)} %all-to-all-done.peer_ref.q_ref), channel_id=1, source_target_pairs={{0,1},{1,0},{2,3},{3,2},{4,5},{5,4},{6,7},{7,6},{8,9},{9,8},{10,11... | collective-permute-start | bytes 1572872 | tf_op jit(solution)/shard_map/ppermute | solution.py:402
  60.4 0.8 copy-start.8
  60.4 0.9 copy-start.9
  61.3 0.8 copy-start.10
  77.2 21.9 %all-to-all-start.2 = ((f16[8,2,136,128]{3,2,1,0:T(8,128)(2,1)}), f16[8,2,136,128]{3,2,1,0:T(8,128)(2,1)S(1)}, u32[]{:S(2)}, u32[]{:S(2)}) async-start(f16[8,2,136,128]{3,2,1,0:T(8,128)(2,1)} %bitcast.9), calls=%async_computation.2 | async-start | bytes 1114112 | tf_op jit(solution)/shard_map/all_to_all | solution.py:276
  93.5 3.9 %collective-permute-start.8 = (f16[16,136,128]{2,1,0:T(8,128)(2,1)S(1)}, f16[16,136,128]{2,1,0:T(8,128)(2,1)S(1)}, u32[]{:S(2)}, u32[]{:S(2)}) collective-permute-start(f16[16,136,128]{2,1,0:T(8,128)(2,1)S(1)} %convert_element_type.23), channel_id=1, source_target_pairs={{0,1},{1,0},{2,3},{3,2},{4,5},{5,4},{6,7},{7,6},{8,9},{9,8},{10,11... | collective-permute-start | bytes 1671176 | tf_op jit(solution)/shard_map/ppermute | solution.py:417
  100.7 13.1 %copy-start = (bf16[1,512,8,128]{3,2,1,0:T(8,128)(2,1)S(1)}, bf16[1,512,8,128]{3,2,1,0:T(8,128)(2,1)}, u32[]{:S(2)}) copy-start(bf16[1,512,8,128]{3,2,1,0:T(8,128)(2,1)} %param.17) | copy-start | bytes 3145732
  100.7 13.1 %copy-start.1 = (bf16[1,512,8,128]{3,2,1,0:T(8,128)(2,1)S(1)}, bf16[1,512,8,128]{3,2,1,0:T(8,128)(2,1)}, u32[]{:S(2)}) copy-start(bf16[1,512,8,128]{3,2,1,0:T(8,128)(2,1)} %param.18) | copy-start | bytes 3145732
  100.7 13.1 %copy-start.3 = (bf16[1,2,8,128]{3,2,1,0:T(8,128)(2,1)S(1)}, bf16[1,2,8,128]{3,2,1,0:T(8,128)(2,1)}, u32[]{:S(2)}) copy-start(bf16[1,2,8,128]{3,2,1,0:T(8,128)(2,1)} %param.19) | copy-start | bytes 12292
  100.7 13.1 %copy-start.4 = (bf16[1,2,8,128]{3,2,1,0:T(8,128)(2,1)S(1)}, bf16[1,2,8,128]{3,2,1,0:T(8,128)(2,1)}, u32[]{:S(2)}) copy-start(bf16[1,2,8,128]{3,2,1,0:T(8,128)(2,1)} %param.20) | copy-start | bytes 12292
  101.6 26.0 %all-to-all-start.3 = ((f16[16,136,128]{2,1,0:T(8,128)(2,1)}), f16[16,136,128]{2,1,0:T(8,128)(2,1)S(1)}, u32[]{:S(2)}, u32[]{:S(2)}) async-start(f16[16,136,128]{2,1,0:T(8,128)(2,1)} %convert_element_type.26), calls=%async_computation.3 | async-start | bytes 1114112 | tf_op jit(solution)/shard_map/all_to_all | solution.py:276
Sparse Core Ops, SparseCore 0:
  28.2 57.3 all-gather.1

commit v9 on v7

--- a/solution.py
+++ b/solution.py
@@ -11,7 +11,7 @@
 CAP = 2
 PAD = 8
 LOW = -1e30
-PARTS = 4
+PARTS = 2
 EMPHASIS = 20
 NT = (((1,), (1,)), ((), ()))
 

time: 135 us -> 135 us (level)
  Pallas kernels: 20.2 us -> 18.7 us
  transfers between devices with their start and end apart: 14 -> 14, of which waited for: 6 -> 7; matrix products, arithmetic and copies ran while one was open for 2% -> 2% of each run, Pallas kernels for 13% -> 13%
where the time goes in v9:
time: 135 us; the launch traced here: 134 us
  starting transfers between devices  56.4 us (42%)
  waiting for transfers between devices  36.3 us (27%)
  Pallas kernels  18.7 us (14%)
  between operations  14.4 us (11%)
  local copies, waits for them, and re-layouts  4.47 us (3%)
  other arithmetic  3.33 us (2%)
    all_to_all x4, starting transfers between devices, exchange(): return lax.all_to_all(blocks, axis, split_axis=0, concat_axis=0, tiled=True)  32.6 us
    all_to_all x4, waiting for transfers between devices, exchange(): return lax.all_to_all(blocks, axis, split_axis=0, concat_axis=0, tiled=True)  20.9 us
    pallas_call x1, Pallas kernels, shards(): pl.pallas_call(root_kernel, out_shape=(whole, whole), in_specs=[vmem()] *...  7.13 us
    pallas_call x1, Pallas kernels, shards(): pl.pallas_call(functools.partial(branch_kernel, count), out_shape=jax.Sha...  6.76 us
    all_gather x1, waiting for transfers between devices, shards(): root_own = lax.all_gather(pair, 'z', axis=0, tiled=True)  6.16 us
    ppermute x1, waiting for transfers between devices, shards(): pair = jnp.stack([root_block, lax.ppermute(root_block, 'xhi', swap)])  5.23 us
    ppermute x1, starting transfers between devices, shards(): pair = jnp.stack([root_block, lax.ppermute(root_block, 'xhi', swap)])  4.01 us
    ppermute x1, starting transfers between devices, shards(): values_far = lax.ppermute(values_own, 'xhi', swap)  3.76 us
  transfers between devices with their start and end apart: 14, of which 7 were waited for; matrix products, arithmetic and copies ran while one was open for 2% of the time, Pallas kernels for 13%

profile of v9, /device:TPU:6, one launch (start us, length us, event | category | flops | bytes accessed | tf_op | source)
XLA Modules:
  0.0 133.7 jit_solution(14376757799119301662)
XLA Ops:
  6.5 0.9 copy.37
  7.4 0.9 broadcast_in_dim.46
  8.3 8.6 %all-to-all-start = ((bf16[16,128,128]{2,1,0:T(8,128)(2,1)}), bf16[16,128,128]{2,1,0:T(8,128)(2,1)S(1)}, u32[]{:S(2)}, u32[]{:S(2)}) async-start(bf16[16,128,128]{2,1,0:T(8,128)(2,1)} %broadcast_in_dim.46), calls=%async_computation | async-start | bytes 1048576 | tf_op jit(solution)/shard_map/all_to_all | solution.py:261
  16.9 0.0 all-gather.2.cloned.1.call-start
  16.9 0.0 copy-done.13
  17.0 0.0 copy-start.14
  17.0 0.0 copy-start.15
  17.0 4.0 %collective-permute-start = (bf16[8,64,128]{2,1,0:T(8,128)(2,1)S(1)}, bf16[8,64,128]{2,1,0:T(8,128)(2,1)S(1)}, u32[]{:S(2)}, u32[]{:S(2)}) collective-permute-start(bf16[8,64,128]{2,1,0:T(8,128)(2,1)S(1)} %bitcast.40), channel_id=1, source_target_pairs={{0,16},{16,0},{1,17},{17,1},{2,18},{18,2},{3,19},{19,3},{4,20},{20... | collective-permute-start | bytes 393224 | tf_op jit(solution)/shard_map/ppermute | solution.py:329
  21.0 0.2 copy_bitcast_fusion
  21.2 0.0 copy-start.5
  21.2 0.0 copy-start.4
  21.3 5.2 %collective-permute-done = bf16[8,64,128]{2,1,0:T(8,128)(2,1)S(1)} collective-permute-done((bf16[8,64,128]{2,1,0:T(8,128)(2,1)S(1)}, bf16[8,64,128]{2,1,0:T(8,128)(2,1)S(1)}, u32[]{:S(2)}, u32[]{:S(2)}) %collective-permute-start) | collective-permute-done | bytes 131104 | tf_op jit(solution)/shard_map/ppermute | solution.py:329
  26.5 0.7 pad_maximum_fusion
  27.2 0.0 all-gather.2.cloned.1.call-update
  27.2 0.0 copy-done.14
  27.3 0.1 select_reduce_fusion
  27.3 0.1 reshape.39
  27.4 0.2 fusion
  27.6 0.1 convert_reduce_fusion
  27.7 0.1 fusion.2.idx_ref
  27.9 3.6 %collective-permute-start.3 = (bf16[8,256,128]{2,1,0:T(8,128)(2,1)S(1)}, bf16[8,256,128]{2,1,0:T(8,128)(2,1)S(1)}, u32[]{:S(2)}, u32[]{:S(2)}) collective-permute-start(bf16[8,256,128]{2,1,0:T(8,128)(2,1)S(1)} %bitcast.37), channel_id=1, source_target_pairs={{0,16},{16,0},{1,17},{17,1},{2,18},{18,2},{3,19},{19,3},{4,20},{20... | collective-permute-start | bytes 1572872 | tf_op jit(solution)/shard_map/ppermute | solution.py:335
  31.5 3.8 %collective-permute-start.4 = (bf16[8,256,128]{2,1,0:T(8,128)(2,1)S(1)}, bf16[8,256,128]{2,1,0:T(8,128)(2,1)}, u32[]{:S(2)}, u32[]{:S(2)}) collective-permute-start(bf16[8,256,128]{2,1,0:T(8,128)(2,1)S(1)} %bitcast.34), channel_id=1, source_target_pairs={{0,16},{16,0},{1,17},{17,1},{2,18},{18,2},{3,19},{19,3},{4,20},{20... | collective-permute-start | bytes 1572872 | tf_op jit(solution)/shard_map/ppermute | solution.py:336
  35.2 0.0 all-to-all-done.peer_ref.q_ref
  35.2 1.4 %pick_readers.1 = bf16[8,2,128,128]{3,2,1,0:T(8,128)(2,1)} custom-call(s32[2]{0:T(128)S(1)} %fusion.2.idx_ref, bf16[16,128,128]{2,1,0:T(8,128)(2,1)S(1)} %all-to-all-done.peer_ref.q_ref), custom_call_target="tpu_custom_call" | custom-call | flops 21474836480 | bytes 6291456 | tf_op jit(solution)/shard_map/pick_readers/pallas_call | solution.py:311
  36.6 9.9 %all-to-all-start.1 = ((bf16[8,2,128,128]{3,2,1,0:T(8,128)(2,1)}), bf16[8,2,128,128]{3,2,1,0:T(8,128)(2,1)S(1)}, u32[]{:S(2)}, u32[]{:S(2)}) async-start(bf16[8,2,128,128]{3,2,1,0:T(8,128)(2,1)} %pick_readers.1), calls=%async_computation.1 | async-start | bytes 1048576 | tf_op jit(solution)/shard_map/all_to_all | solution.py:261
  46.6 1.9 %collective-permute-start.1 = (bf16[8,256,128]{2,1,0:T(8,128)(2,1)S(1)}, bf16[8,256,128]{2,1,0:T(8,128)(2,1)S(1)}, u32[]{:S(2)}, u32[]{:S(2)}) collective-permute-start(bf16[8,256,128]{2,1,0:T(8,128)(2,1)S(1)} %bitcast.38), channel_id=1, source_target_pairs={{0,1},{1,0},{2,3},{3,2},{4,5},{5,4},{6,7},{7,6},{8,9},{9,8},{10,11... | collective-permute-start | bytes 1572872 | tf_op jit(solution)/shard_map/ppermute | solution.py:341
  48.5 2.4 %collective-permute-start.2 = (bf16[8,256,128]{2,1,0:T(8,128)(2,1)S(1)}, bf16[8,256,128]{2,1,0:T(8,128)(2,1)S(1)}, u32[]{:S(2)}, u32[]{:S(2)}) collective-permute-start(bf16[8,256,128]{2,1,0:T(8,128)(2,1)S(1)} %bitcast.35), channel_id=1, source_target_pairs={{0,1},{1,0},{2,3},{3,2},{4,5},{5,4},{6,7},{7,6},{8,9},{9,8},{10,11... | collective-permute-start | bytes 1572872 | tf_op jit(solution)/shard_map/ppermute | solution.py:342
  50.9 0.0 collective-permute-done.3.refs_4_
  50.9 1.9 %collective-permute-start.5 = (bf16[8,256,128]{2,1,0:T(8,128)(2,1)S(1)}, bf16[8,256,128]{2,1,0:T(8,128)(2,1)S(1)}, u32[]{:S(2)}, u32[]{:S(2)}) collective-permute-start(bf16[8,256,128]{2,1,0:T(8,128)(2,1)S(1)} %collective-permute-done.3.refs_4_), channel_id=1, source_target_pairs={{0,1},{1,0},{2,3},{3,2},{4,5},{5,4},{6,7},{7,6},{8,9},{9,8},{10,11... | collective-permute-start | bytes 1572872 | tf_op jit(solution)/shard_map/ppermute | solution.py:345
  52.9 2.1 %collective-permute-done.4.refs_5_ = bf16[8,256,128]{2,1,0:T(8,128)(2,1)} collective-permute-done((bf16[8,256,128]{2,1,0:T(8,128)(2,1)S(1)}, bf16[8,256,128]{2,1,0:T(8,128)(2,1)}, u32[]{:S(2)}, u32[]{:S(2)}) %collective-permute-start.4) | collective-permute-done | bytes 524320 | tf_op jit(solution)/shard_map/ppermute | solution.py:336
  54.9 1.9 %collective-permute-start.6 = (bf16[8,256,128]{2,1,0:T(8,128)(2,1)}, bf16[8,256,128]{2,1,0:T(8,128)(2,1)}, u32[]{:S(2)}, u32[]{:S(2)}) collective-permute-start(bf16[8,256,128]{2,1,0:T(8,128)(2,1)} %collective-permute-done.4.refs_5_), channel_id=1, source_target_pairs={{0,1},{1,0},{2,3},{3,2},{4,5},{5,4},{6,7},{7,6},{8,9},{9,8},{10,11... | collective-permute-start | bytes 1572872 | tf_op jit(solution)/shard_map/ppermute | solution.py:346
  56.8 2.4 %collective-permute-start.7 = (bf16[16,128,128]{2,1,0:T(8,128)(2,1)S(1)}, bf16[16,128,128]{2,1,0:T(8,128)(2,1)S(1)}, u32[]{:S(2)}, u32[]{:S(2)}) collective-permute-start(bf16[16,128,128]{2,1,0:T(8,128)(2,1)S(1)} %all-to-all-done.peer_ref.q_ref), channel_id=1, source_target_pairs={{0,1},{1,0},{2,3},{3,2},{4,5},{5,4},{6,7},{7,6},{8,9},{9,8},{10,11... | collective-permute-start | bytes 1572872 | tf_op jit(solution)/shard_map/ppermute | solution.py:382
  59.3 0.0 collective-permute-done.1.refs_2_
  59.3 0.0 collective-permute-done.2.refs_3_
  59.3 0.0 collective-permute-done.5.refs_6_
  59.3 0.7 copy-done.7
  60.1 0.2 copy-done.8
  60.2 0.8 copy-done.9
  61.1 0.0 collective-permute-done.6.refs_7_
  61.1 5.6 %all-to-all-done.1 = bf16[8,2,128,128]{3,2,1,0:T(8,128)(2,1)S(1)} async-done(((bf16[8,2,128,128]{3,2,1,0:T(8,128)(2,1)}), bf16[8,2,128,128]{3,2,1,0:T(8,128)(2,1)S(1)}, u32[]{:S(2)}, u32[]{:S(2)}) %all-to-all-start.1) | async-done | bytes 524320 | tf_op jit(solution)/shard_map/all_to_all | solution.py:261
  66.6 6.8 %branch_attention.1 = f32[16,136,128]{2,1,0:T(8,128)S(1)} custom-call(bf16[16,128,128]{2,1,0:T(8,128)(2,1)S(1)} %bitcast.26, bf16[8,256,128]{2,1,0:T(8,128)(2,1)} %bitcast.39, bf16[8,256,128]{2,1,0:T(8,128)(2,1)} %bitcast.36, bf16[8,256,128]{2,1,0:T(8,128)(2,1)} %copy-done.7, bf16[8,256,128]{2,1,0:T(8,128)(2,1)} %copy-done.8, ...), custom_call_target="tpu_custom_call" | custom-call | flops 1073741824 | bytes 6291456 | tf_op jit(solution)/shard_map/branch_attention/pallas_call | solution.py:371
  73.4 0.9 convert_element_type.22
  74.3 4.2 %all-to-all-start.2 = ((f16[8,2,136,128]{3,2,1,0:T(8,128)(2,1)}), f16[8,2,136,128]{3,2,1,0:T(8,128)(2,1)S(1)}, u32[]{:S(2)}, u32[]{:S(2)}) async-start(f16[8,2,136,128]{3,2,1,0:T(8,128)(2,1)} %bitcast.11), calls=%async_computation.2 | async-start | bytes 1114112 | tf_op jit(solution)/shard_map/all_to_all | solution.py:261
  78.5 0.0 collective-permute-done.7.q_twin_ref
  78.5 6.2 %all-gather.2.cloned.1.call-done.block_ref = bf16[16,8,64,128]{3,2,1,0:T(8,128)(2,1)} async-done(((bf16[2,8,64,128]{3,2,1,0:T(8,128)(2,1)}), bf16[16,8,64,128]{3,2,1,0:T(8,128)(2,1)}) %all-gather.2.cloned.1.call-update) | async-done | bytes 2097168 | tf_op jit(solution)/shard_map/all_gather | solution.py:331
  84.7 7.1 %root_attention.1 = (f32[16,136,128]{2,1,0:T(8,128)S(1)}, f32[16,136,128]{2,1,0:T(8,128)S(1)}) custom-call(bf16[16,128,128]{2,1,0:T(8,128)(2,1)S(1)} %all-to-all-done.peer_ref.q_ref, bf16[16,128,128]{2,1,0:T(8,128)(2,1)S(1)} %collective-permute-done.7.q_twin_ref, bf16[16,8,64,128]{3,2,1,0:T(8,128)(2,1)} %all-gather.2.cloned.1.call-done.block_ref), custom_call_target="tpu_custom_call" | custom-call | flops 1073741824 | bytes 6291456 | tf_op jit(solution)/shard_map/root_attention/pallas_call | solution.py:387
  91.8 0.1 convert_element_type.23
  91.9 1.9 %collective-permute-start.8 = (f16[16,136,128]{2,1,0:T(8,128)(2,1)S(1)}, f16[16,136,128]{2,1,0:T(8,128)(2,1)S(1)}, u32[]{:S(2)}, u32[]{:S(2)}) collective-permute-start(f16[16,136,128]{2,1,0:T(8,128)(2,1)S(1)} %convert_element_type.23), channel_id=1, source_target_pairs={{0,1},{1,0},{2,3},{3,2},{4,5},{5,4},{6,7},{7,6},{8,9},{9,8},{10,11... | collective-permute-start | bytes 1671176 | tf_op jit(solution)/shard_map/ppermute | solution.py:397
  93.8 1.9 %collective-permute-done.8 = f16[16,136,128]{2,1,0:T(8,128)(2,1)S(1)} collective-permute-done((f16[16,136,128]{2,1,0:T(8,128)(2,1)S(1)}, f16[16,136,128]{2,1,0:T(8,128)(2,1)S(1)}, u32[]{:S(2)}, u32[]{:S(2)}) %collective-permute-start.8) | collective-permute-done | bytes 557088 | tf_op jit(solution)/shard_map/ppermute | solution.py:397
  95.8 0.1 convert_element_type.24.twin_ref
  95.8 0.1 all-to-all-done.2
  96.0 0.1 convert_element_type.25.part_ref
  96.1 1.4 %merge_parts.1 = f32[16,136,128]{2,1,0:T(8,128)S(1)} custom-call(s32[2]{0:T(128)S(1)} %fusion.2.idx_ref, f32[8,2,136,128]{3,2,1,0:T(8,128)S(1)} %convert_element_type.25.part_ref, f32[16,136,128]{2,1,0:T(8,128)S(1)} %get-tuple-element.25.own_ref, f32[16,136,128]{2,1,0:T(8,128)S(1)} %convert_element_type.24.twin_ref), custom_call_target="tpu_custom_call" | custom-call | tf_op jit(solution)/shard_map/merge_parts/pallas_call | solution.py:400
  97.5 0.0 copy-start
  97.5 0.0 copy-start.1
  97.5 0.0 copy-start.2
  97.5 0.0 copy-start.3
  97.5 0.9 convert_element_type.26
  98.4 9.9 %all-to-all-start.3 = ((f16[16,136,128]{2,1,0:T(8,128)(2,1)}), f16[16,136,128]{2,1,0:T(8,128)(2,1)S(1)}, u32[]{:S(2)}, u32[]{:S(2)}) async-start(f16[16,136,128]{2,1,0:T(8,128)(2,1)} %convert_element_type.26), calls=%async_computation.3 | async-start | bytes 1114112 | tf_op jit(solution)/shard_map/all_to_all | solution.py:261
  108.9 1.5 %local_attention.1.local_ref = f32[136,128]{1,0:T(8,128)S(1)} custom-call(s32[1]{0:T(128)S(6)} %copy.50.len_ref, bf16[128,128]{1,0:T(8,128)(2,1)S(1)} %bitcast.30, bf16[4096,128]{1,0:T(8,128)(2,1)S(1)} %bitcast.27, bf16[4096,128]{1,0:T(8,128)(2,1)S(1)} %bitcast.28, bf16[16,128]{1,0:T(8,128)(2,1)S(1)} %bitcast.32, bf16[16,128]{1,0:T(8,128)(2,1)S(1)} %bitcast.33), custom_call_target="tpu_custom_call" | custom-call | flops 268435456 | bytes 2097152 | tf_op jit(solution)/shard_map/local_attention/pallas_call | solution.py:349
  110.4 15.2 %all-to-all-done.3 = f16[16,136,128]{2,1,0:T(8,128)(2,1)S(1)} async-done(((f16[16,136,128]{2,1,0:T(8,128)(2,1)}), f16[16,136,128]{2,1,0:T(8,128)(2,1)S(1)}, u32[]{:S(2)}, u32[]{:S(2)}) %all-to-all-start.3) | async-done | bytes 557088 | tf_op jit(solution)/shard_map/all_to_all | solution.py:261
  125.6 0.1 convert_element_type.27.part_ref
  125.7 0.6 final_merge.1
  126.3 0.6 copy.48
  (21 shorter events, 0.1 us)
Async XLA Ops:
  6.5 10.4 %copy-start.12 = (bf16[32,8,128]{2,1,0:T(8,128)(2,1)S(1)}, bf16[32,8,128]{2,1,0:T(8,128)(2,1)}, u32[]{:S(2)}) copy-start(bf16[32,8,128]{2,1,0:T(8,128)(2,1)} %param.13) | copy-start | bytes 196612
  6.5 10.4 %copy-start.13 = (bf16[32,8,128]{2,1,0:T(8,128)(2,1)S(1)}, bf16[32,8,128]{2,1,0:T(8,128)(2,1)}, u32[]{:S(2)}) copy-start(bf16[32,8,128]{2,1,0:T(8,128)(2,1)} %param.14) | copy-start | bytes 196612
  6.5 14.5 %copy-start.11 = (bf16[1,256,8,128]{3,2,1,0:T(8,128)(2,1)S(1)}, bf16[1,256,8,128]{3,2,1,0:T(8,128)(2,1)}, u32[]{:S(2)}) copy-start(bf16[1,256,8,128]{3,2,1,0:T(8,128)(2,1)} %param.15) | copy-start | bytes 1572868
  6.5 14.5 %copy-start.10 = (bf16[1,256,8,128]{3,2,1,0:T(8,128)(2,1)S(1)}, bf16[1,256,8,128]{3,2,1,0:T(8,128)(2,1)}, u32[]{:S(2)}) copy-start(bf16[1,256,8,128]{3,2,1,0:T(8,128)(2,1)} %param.16) | copy-start | bytes 1572868
  8.3 26.9 %all-to-all-start = ((bf16[16,128,128]{2,1,0:T(8,128)(2,1)}), bf16[16,128,128]{2,1,0:T(8,128)(2,1)S(1)}, u32[]{:S(2)}, u32[]{:S(2)}) async-start(bf16[16,128,128]{2,1,0:T(8,128)(2,1)} %broadcast_in_dim.46), calls=%async_computation | async-start | bytes 1048576 | tf_op jit(solution)/shard_map/all_to_all | solution.py:261
  16.9 67.8 %all-gather.2.cloned.1.call-start = ((), (), s32[]{:S(2)}) async-start(), calls=%async_computation.4 | async-start | bytes 2359296 | tf_op jit(solution)/shard_map/all_gather | solution.py:331
  17.0 10.3 %copy-start.14 = (s32[512]{0:T(512)S(1)}, s32[512]{0:T(512)}, u32[]{:S(2)}) copy-start(s32[512]{0:T(512)} %param.21) | copy-start | bytes 6148
  17.0 10.3 %copy-start.15 = (s32[16]{0:T(128)S(1)}, s32[16]{0:T(128)}, u32[]{:S(2)}) copy-start(s32[16]{0:T(128)} %param.22) | copy-start | bytes 196
  17.0 9.5 %collective-permute-start = (bf16[8,64,128]{2,1,0:T(8,128)(2,1)S(1)}, bf16[8,64,128]{2,1,0:T(8,128)(2,1)S(1)}, u32[]{:S(2)}, u32[]{:S(2)}) collective-permute-start(bf16[8,64,128]{2,1,0:T(8,128)(2,1)S(1)} %bitcast.40), channel_id=1, source_target_pairs={{0,16},{16,0},{1,17},{17,1},{2,18},{18,2},{3,19},{19,3},{4,20},{20... | collective-permute-start | bytes 393224 | tf_op jit(solution)/shard_map/ppermute | solution.py:329
  21.2 25.3 %copy-start.5 = (bf16[256,8,128]{2,0,1:T(8,128)(2,1)}, bf16[256,8,128]{2,0,1:T(8,128)(2,1)S(1)}, u32[]{:S(2)}) copy-start(bf16[256,8,128]{2,0,1:T(8,128)(2,1)S(1)} %get-tuple-element.18) | copy-start | bytes 1572868
  21.2 27.3 %copy-start.4 = (bf16[256,8,128]{2,0,1:T(8,128)(2,1)}, bf16[256,8,128]{2,0,1:T(8,128)(2,1)S(1)}, u32[]{:S(2)}) copy-start(bf16[256,8,128]{2,0,1:T(8,128)(2,1)S(1)} %get-tuple-element.19) | copy-start | bytes 1572868
  27.9 23.1 %collective-permute-start.3 = (bf16[8,256,128]{2,1,0:T(8,128)(2,1)S(1)}, bf16[8,256,128]{2,1,0:T(8,128)(2,1)S(1)}, u32[]{:S(2)}, u32[]{:S(2)}) collective-permute-start(bf16[8,256,128]{2,1,0:T(8,128)(2,1)S(1)} %bitcast.37), channel_id=1, source_target_pairs={{0,16},{16,0},{1,17},{17,1},{2,18},{18,2},{3,19},{19,3},{4,20},{20... | collective-permute-start | bytes 1572872 | tf_op jit(solution)/shard_map/ppermute | solution.py:335
  31.5 23.5 %collective-permute-start.4 = (bf16[8,256,128]{2,1,0:T(8,128)(2,1)S(1)}, bf16[8,256,128]{2,1,0:T(8,128)(2,1)}, u32[]{:S(2)}, u32[]{:S(2)}) collective-permute-start(bf16[8,256,128]{2,1,0:T(8,128)(2,1)S(1)} %bitcast.34), channel_id=1, source_target_pairs={{0,16},{16,0},{1,17},{17,1},{2,18},{18,2},{3,19},{19,3},{4,20},{20... | collective-permute-start | bytes 1572872 | tf_op jit(solution)/shard_map/ppermute | solution.py:336
  36.6 30.0 %all-to-all-start.1 = ((bf16[8,2,128,128]{3,2,1,0:T(8,128)(2,1)}), bf16[8,2,128,128]{3,2,1,0:T(8,128)(2,1)S(1)}, u32[]{:S(2)}, u32[]{:S(2)}) async-start(bf16[8,2,128,128]{3,2,1,0:T(8,128)(2,1)} %pick_readers.1), calls=%async_computation.1 | async-start | bytes 1048576 | tf_op jit(solution)/shard_map/all_to_all | solution.py:261
  46.6 12.7 %collective-permute-start.1 = (bf16[8,256,128]{2,1,0:T(8,128)(2,1)S(1)}, bf16[8,256,128]{2,1,0:T(8,128)(2,1)S(1)}, u32[]{:S(2)}, u32[]{:S(2)}) collective-permute-start(bf16[8,256,128]{2,1,0:T(8,128)(2,1)S(1)} %bitcast.38), channel_id=1, source_target_pairs={{0,1},{1,0},{2,3},{3,2},{4,5},{5,4},{6,7},{7,6},{8,9},{9,8},{10,11... | collective-permute-start | bytes 1572872 | tf_op jit(solution)/shard_map/ppermute | solution.py:341
  48.5 10.8 %collective-permute-start.2 = (bf16[8,256,128]{2,1,0:T(8,128)(2,1)S(1)}, bf16[8,256,128]{2,1,0:T(8,128)(2,1)S(1)}, u32[]{:S(2)}, u32[]{:S(2)}) collective-permute-start(bf16[8,256,128]{2,1,0:T(8,128)(2,1)S(1)} %bitcast.35), channel_id=1, source_target_pairs={{0,1},{1,0},{2,3},{3,2},{4,5},{5,4},{6,7},{7,6},{8,9},{9,8},{10,11... | collective-permute-start | bytes 1572872 | tf_op jit(solution)/shard_map/ppermute | solution.py:342
  50.9 15.7 %copy-start.6 = (bf16[8,256,128]{2,1,0:T(8,128)(2,1)}, bf16[8,256,128]{2,1,0:T(8,128)(2,1)S(1)}, u32[]{:S(2)}) copy-start(bf16[8,256,128]{2,1,0:T(8,128)(2,1)S(1)} %collective-permute-done.3.refs_4_) | copy-start | bytes 1572868
  50.9 8.4 %collective-permute-start.5 = (bf16[8,256,128]{2,1,0:T(8,128)(2,1)S(1)}, bf16[8,256,128]{2,1,0:T(8,128)(2,1)S(1)}, u32[]{:S(2)}, u32[]{:S(2)}) collective-permute-start(bf16[8,256,128]{2,1,0:T(8,128)(2,1)S(1)} %collective-permute-done.3.refs_4_), channel_id=1, source_target_pairs={{0,1},{1,0},{2,3},{3,2},{4,5},{5,4},{6,7},{7,6},{8,9},{9,8},{10,11... | collective-permute-start | bytes 1572872 | tf_op jit(solution)/shard_map/ppermute | solution.py:345
  54.9 6.1 %collective-permute-start.6 = (bf16[8,256,128]{2,1,0:T(8,128)(2,1)}, bf16[8,256,128]{2,1,0:T(8,128)(2,1)}, u32[]{:S(2)}, u32[]{:S(2)}) collective-permute-start(bf16[8,256,128]{2,1,0:T(8,128)(2,1)} %collective-permute-done.4.refs_5_), channel_id=1, source_target_pairs={{0,1},{1,0},{2,3},{3,2},{4,5},{5,4},{6,7},{7,6},{8,9},{9,8},{10,11... | collective-permute-start | bytes 1572872 | tf_op jit(solution)/shard_map/ppermute | solution.py:346
  56.8 21.7 %collective-permute-start.7 = (bf16[16,128,128]{2,1,0:T(8,128)(2,1)S(1)}, bf16[16,128,128]{2,1,0:T(8,128)(2,1)S(1)}, u32[]{:S(2)}, u32[]{:S(2)}) collective-permute-start(bf16[16,128,128]{2,1,0:T(8,128)(2,1)S(1)} %all-to-all-done.peer_ref.q_ref), channel_id=1, source_target_pairs={{0,1},{1,0},{2,3},{3,2},{4,5},{5,4},{6,7},{7,6},{8,9},{9,8},{10,11... | collective-permute-start | bytes 1572872 | tf_op jit(solution)/shard_map/ppermute | solution.py:382
  59.3 0.8 copy-start.7
  59.3 1.0 copy-start.8
  60.2 0.8 copy-start.9
  74.3 21.7 %all-to-all-start.2 = ((f16[8,2,136,128]{3,2,1,0:T(8,128)(2,1)}), f16[8,2,136,128]{3,2,1,0:T(8,128)(2,1)S(1)}, u32[]{:S(2)}, u32[]{:S(2)}) async-start(f16[8,2,136,128]{3,2,1,0:T(8,128)(2,1)} %bitcast.11), calls=%async_computation.2 | async-start | bytes 1114112 | tf_op jit(solution)/shard_map/all_to_all | solution.py:261
  91.9 3.9 %collective-permute-start.8 = (f16[16,136,128]{2,1,0:T(8,128)(2,1)S(1)}, f16[16,136,128]{2,1,0:T(8,128)(2,1)S(1)}, u32[]{:S(2)}, u32[]{:S(2)}) collective-permute-start(f16[16,136,128]{2,1,0:T(8,128)(2,1)S(1)} %convert_element_type.23), channel_id=1, source_target_pairs={{0,1},{1,0},{2,3},{3,2},{4,5},{5,4},{6,7},{7,6},{8,9},{9,8},{10,11... | collective-permute-start | bytes 1671176 | tf_op jit(solution)/shard_map/ppermute | solution.py:397
  97.5 11.4 %copy-start = (bf16[1,512,8,128]{3,2,1,0:T(8,128)(2,1)S(1)}, bf16[1,512,8,128]{3,2,1,0:T(8,128)(2,1)}, u32[]{:S(2)}) copy-start(bf16[1,512,8,128]{3,2,1,0:T(8,128)(2,1)} %param.17) | copy-start | bytes 3145732
  97.5 11.4 %copy-start.1 = (bf16[1,512,8,128]{3,2,1,0:T(8,128)(2,1)S(1)}, bf16[1,512,8,128]{3,2,1,0:T(8,128)(2,1)}, u32[]{:S(2)}) copy-start(bf16[1,512,8,128]{3,2,1,0:T(8,128)(2,1)} %param.18) | copy-start | bytes 3145732
  97.5 11.4 %copy-start.2 = (bf16[1,2,8,128]{3,2,1,0:T(8,128)(2,1)S(1)}, bf16[1,2,8,128]{3,2,1,0:T(8,128)(2,1)}, u32[]{:S(2)}) copy-start(bf16[1,2,8,128]{3,2,1,0:T(8,128)(2,1)} %param.19) | copy-start | bytes 12292
  97.5 11.4 %copy-start.3 = (bf16[1,2,8,128]{3,2,1,0:T(8,128)(2,1)S(1)}, bf16[1,2,8,128]{3,2,1,0:T(8,128)(2,1)}, u32[]{:S(2)}) copy-start(bf16[1,2,8,128]{3,2,1,0:T(8,128)(2,1)} %param.20) | copy-start | bytes 12292
  98.4 27.2 %all-to-all-start.3 = ((f16[16,136,128]{2,1,0:T(8,128)(2,1)}), f16[16,136,128]{2,1,0:T(8,128)(2,1)S(1)}, u32[]{:S(2)}, u32[]{:S(2)}) async-start(f16[16,136,128]{2,1,0:T(8,128)(2,1)} %convert_element_type.26), calls=%async_computation.3 | async-start | bytes 1114112 | tf_op jit(solution)/shard_map/all_to_all | solution.py:261
Sparse Core Ops, SparseCore 0:
  27.4 57.2 all-gather.1

commit v10 on v9

--- a/solution.py
+++ b/solution.py
@@ -19,6 +19,13 @@
 def scores_of(rows, keys):
     raw = lax.dot_general(rows, keys, NT, preferred_element_type=jnp.float32)
     return raw * (1.0 / math.sqrt(keys.shape[-1]))
+
+
+def raw_weights(rows, keys):
+    raw = lax.dot_general(rows, keys, NT, preferred_element_type=jnp.float32)
+    top = jnp.max(raw, axis=1, keepdims=True)
+    scale = 1.0 / math.sqrt(keys.shape[-1])
+    return jnp.exp2((raw - top) * (scale * math.log2(math.e))), top * scale
 
 
 def times_values(weights, values):
@@ -114,9 +121,7 @@
         q = q_ref[:, place, :].reshape(slots * per_head, dim)
         found = []
         for block in range(0, count, 2):
-            scores = scores_of(q, held[block, head])
-            high = jnp.max(scores, axis=1, keepdims=True)
-            weights = jnp.exp(scores - high)
+            weights, high = raw_weights(q, held[block, head])
             den = jnp.sum(weights, axis=1, keepdims=True)
             found.append((high, den, times_values(weights, held[block + 1, head])))
         high = functools.reduce(jnp.maximum, [f[0] for f in found])
@@ -159,9 +164,7 @@
         values = held[:, head, half:, :].reshape(span, dim)
         for i, (rows_ref, result_ref) in enumerate(pairs):
             q = rows_ref[:, place, :].reshape(requests * per_head, dim)
-            scores = scores_of(q, keys)
-            high = jnp.max(scores, axis=1, keepdims=True)
-            weights = jnp.exp(scores - high)
+            weights, high = raw_weights(q, keys)
             den = jnp.sum(weights, axis=1, keepdims=True)
             num = times_values(weights, values) / den
             result_ref[:, place, :] = num.reshape(requests, per_head, dim)

time: 135 us -> 136 us (level)
  waiting for transfers between devices: 36.3 us -> 37.7 us
    all_gather x1, waiting for transfers between devices: 6.16 us -> 7.84 us  [shards(): root_own = lax.all_gather(pair, 'z', axis=0, tiled=True)]
  transfers between devices with their start and end apart: 14 -> 14, of which waited for: 7 -> 6; matrix products, arithmetic and copies ran while one was open for 2% -> 2% of each run, Pallas kernels for 13% -> 12%
where the time goes in v10:
time: 136 us; the launch traced here: 134 us
  starting transfers between devices  56 us (41%)
  waiting for transfers between devices  37.7 us (28%)
  Pallas kernels  18.3 us (13%)
  between operations  14.4 us (11%)
  local copies, waits for them, and re-layouts  4.47 us (3%)
  other arithmetic  3.33 us (2%)
    all_to_all x4, starting transfers between devices, exchange(): return lax.all_to_all(blocks, axis, split_axis=0, concat_axis=0, tiled=True)  32 us
    all_to_all x4, waiting for transfers between devices, exchange(): return lax.all_to_all(blocks, axis, split_axis=0, concat_axis=0, tiled=True)  20.8 us
    all_gather x1, waiting for transfers between devices, shards(): root_own = lax.all_gather(pair, 'z', axis=0, tiled=True)  7.84 us
    pallas_call x1, Pallas kernels, shards(): pl.pallas_call(root_kernel, out_shape=(whole, whole), in_specs=[vmem()] *...  6.95 us
    pallas_call x1, Pallas kernels, shards(): pl.pallas_call(functools.partial(branch_kernel, count), out_shape=jax.Sha...  6.49 us
    ppermute x1, waiting for transfers between devices, shards(): pair = jnp.stack([root_block, lax.ppermute(root_block, 'xhi', swap)])  5.23 us
    ppermute x1, starting transfers between devices, shards(): pair = jnp.stack([root_block, lax.ppermute(root_block, 'xhi', swap)])  4.01 us
    ppermute x1, starting transfers between devices, shards(): values_far = lax.ppermute(values_own, 'xhi', swap)  3.76 us
  transfers between devices with their start and end apart: 14, of which 6 were waited for; matrix products, arithmetic and copies ran while one was open for 2% of the time, Pallas kernels for 12%

profile of v10, /device:TPU:6, one launch (start us, length us, event | category | flops | bytes accessed | tf_op | source)
XLA Modules:
  0.0 134.3 jit_solution(289792276002557596)
XLA Ops:
  6.5 0.9 copy.37
  7.4 0.9 broadcast_in_dim.46
  8.3 8.6 %all-to-all-start = ((bf16[16,128,128]{2,1,0:T(8,128)(2,1)}), bf16[16,128,128]{2,1,0:T(8,128)(2,1)S(1)}, u32[]{:S(2)}, u32[]{:S(2)}) async-start(bf16[16,128,128]{2,1,0:T(8,128)(2,1)} %broadcast_in_dim.46), calls=%async_computation | async-start | bytes 1048576 | tf_op jit(solution)/shard_map/all_to_all | solution.py:264
  16.9 0.0 all-gather.2.cloned.1.call-start
  16.9 0.0 copy-done.13
  17.0 0.0 copy-start.14
  17.0 0.0 copy-start.15
  17.0 4.0 %collective-permute-start = (bf16[8,64,128]{2,1,0:T(8,128)(2,1)S(1)}, bf16[8,64,128]{2,1,0:T(8,128)(2,1)S(1)}, u32[]{:S(2)}, u32[]{:S(2)}) collective-permute-start(bf16[8,64,128]{2,1,0:T(8,128)(2,1)S(1)} %bitcast.40), channel_id=1, source_target_pairs={{0,16},{16,0},{1,17},{17,1},{2,18},{18,2},{3,19},{19,3},{4,20},{20... | collective-permute-start | bytes 393224 | tf_op jit(solution)/shard_map/ppermute | solution.py:332
  21.0 0.2 copy_bitcast_fusion
  21.2 0.0 copy-start.5
  21.2 0.0 copy-start.4
  21.3 5.2 %collective-permute-done = bf16[8,64,128]{2,1,0:T(8,128)(2,1)S(1)} collective-permute-done((bf16[8,64,128]{2,1,0:T(8,128)(2,1)S(1)}, bf16[8,64,128]{2,1,0:T(8,128)(2,1)S(1)}, u32[]{:S(2)}, u32[]{:S(2)}) %collective-permute-start) | collective-permute-done | bytes 131104 | tf_op jit(solution)/shard_map/ppermute | solution.py:332
  26.5 0.7 pad_maximum_fusion
  27.2 0.0 all-gather.2.cloned.1.call-update
  27.2 0.0 copy-done.14
  27.3 0.1 select_reduce_fusion
  27.3 0.1 reshape.39
  27.4 0.2 fusion
  27.6 0.1 convert_reduce_fusion
  27.7 0.1 fusion.2.idx_ref
  27.9 3.6 %collective-permute-start.3 = (bf16[8,256,128]{2,1,0:T(8,128)(2,1)S(1)}, bf16[8,256,128]{2,1,0:T(8,128)(2,1)S(1)}, u32[]{:S(2)}, u32[]{:S(2)}) collective-permute-start(bf16[8,256,128]{2,1,0:T(8,128)(2,1)S(1)} %bitcast.37), channel_id=1, source_target_pairs={{0,16},{16,0},{1,17},{17,1},{2,18},{18,2},{3,19},{19,3},{4,20},{20... | collective-permute-start | bytes 1572872 | tf_op jit(solution)/shard_map/ppermute | solution.py:338
  31.5 3.8 %collective-permute-start.4 = (bf16[8,256,128]{2,1,0:T(8,128)(2,1)S(1)}, bf16[8,256,128]{2,1,0:T(8,128)(2,1)}, u32[]{:S(2)}, u32[]{:S(2)}) collective-permute-start(bf16[8,256,128]{2,1,0:T(8,128)(2,1)S(1)} %bitcast.34), channel_id=1, source_target_pairs={{0,16},{16,0},{1,17},{17,1},{2,18},{18,2},{3,19},{19,3},{4,20},{20... | collective-permute-start | bytes 1572872 | tf_op jit(solution)/shard_map/ppermute | solution.py:339
  35.2 0.0 all-to-all-done.peer_ref.q_ref
  35.2 1.4 %pick_readers.1 = bf16[8,2,128,128]{3,2,1,0:T(8,128)(2,1)} custom-call(s32[2]{0:T(128)S(1)} %fusion.2.idx_ref, bf16[16,128,128]{2,1,0:T(8,128)(2,1)S(1)} %all-to-all-done.peer_ref.q_ref), custom_call_target="tpu_custom_call" | custom-call | flops 21474836480 | bytes 6291456 | tf_op jit(solution)/shard_map/pick_readers/pallas_call | solution.py:314
  36.6 9.9 %all-to-all-start.1 = ((bf16[8,2,128,128]{3,2,1,0:T(8,128)(2,1)}), bf16[8,2,128,128]{3,2,1,0:T(8,128)(2,1)S(1)}, u32[]{:S(2)}, u32[]{:S(2)}) async-start(bf16[8,2,128,128]{3,2,1,0:T(8,128)(2,1)} %pick_readers.1), calls=%async_computation.1 | async-start | bytes 1048576 | tf_op jit(solution)/shard_map/all_to_all | solution.py:264
  46.6 1.9 %collective-permute-start.1 = (bf16[8,256,128]{2,1,0:T(8,128)(2,1)S(1)}, bf16[8,256,128]{2,1,0:T(8,128)(2,1)S(1)}, u32[]{:S(2)}, u32[]{:S(2)}) collective-permute-start(bf16[8,256,128]{2,1,0:T(8,128)(2,1)S(1)} %bitcast.38), channel_id=1, source_target_pairs={{0,1},{1,0},{2,3},{3,2},{4,5},{5,4},{6,7},{7,6},{8,9},{9,8},{10,11... | collective-permute-start | bytes 1572872 | tf_op jit(solution)/shard_map/ppermute | solution.py:344
  48.5 2.4 %collective-permute-start.2 = (bf16[8,256,128]{2,1,0:T(8,128)(2,1)S(1)}, bf16[8,256,128]{2,1,0:T(8,128)(2,1)S(1)}, u32[]{:S(2)}, u32[]{:S(2)}) collective-permute-start(bf16[8,256,128]{2,1,0:T(8,128)(2,1)S(1)} %bitcast.35), channel_id=1, source_target_pairs={{0,1},{1,0},{2,3},{3,2},{4,5},{5,4},{6,7},{7,6},{8,9},{9,8},{10,11... | collective-permute-start | bytes 1572872 | tf_op jit(solution)/shard_map/ppermute | solution.py:345
  50.9 0.0 collective-permute-done.3.refs_4_
  50.9 1.9 %collective-permute-start.5 = (bf16[8,256,128]{2,1,0:T(8,128)(2,1)S(1)}, bf16[8,256,128]{2,1,0:T(8,128)(2,1)S(1)}, u32[]{:S(2)}, u32[]{:S(2)}) collective-permute-start(bf16[8,256,128]{2,1,0:T(8,128)(2,1)S(1)} %collective-permute-done.3.refs_4_), channel_id=1, source_target_pairs={{0,1},{1,0},{2,3},{3,2},{4,5},{5,4},{6,7},{7,6},{8,9},{9,8},{10,11... | collective-permute-start | bytes 1572872 | tf_op jit(solution)/shard_map/ppermute | solution.py:348
  52.9 2.1 %collective-permute-done.4.refs_5_ = bf16[8,256,128]{2,1,0:T(8,128)(2,1)} collective-permute-done((bf16[8,256,128]{2,1,0:T(8,128)(2,1)S(1)}, bf16[8,256,128]{2,1,0:T(8,128)(2,1)}, u32[]{:S(2)}, u32[]{:S(2)}) %collective-permute-start.4) | collective-permute-done | bytes 524320 | tf_op jit(solution)/shard_map/ppermute | solution.py:339
  54.9 1.9 %collective-permute-start.6 = (bf16[8,256,128]{2,1,0:T(8,128)(2,1)}, bf16[8,256,128]{2,1,0:T(8,128)(2,1)}, u32[]{:S(2)}, u32[]{:S(2)}) collective-permute-start(bf16[8,256,128]{2,1,0:T(8,128)(2,1)} %collective-permute-done.4.refs_5_), channel_id=1, source_target_pairs={{0,1},{1,0},{2,3},{3,2},{4,5},{5,4},{6,7},{7,6},{8,9},{9,8},{10,11... | collective-permute-start | bytes 1572872 | tf_op jit(solution)/shard_map/ppermute | solution.py:349
  56.8 2.4 %collective-permute-start.7 = (bf16[16,128,128]{2,1,0:T(8,128)(2,1)S(1)}, bf16[16,128,128]{2,1,0:T(8,128)(2,1)S(1)}, u32[]{:S(2)}, u32[]{:S(2)}) collective-permute-start(bf16[16,128,128]{2,1,0:T(8,128)(2,1)S(1)} %all-to-all-done.peer_ref.q_ref), channel_id=1, source_target_pairs={{0,1},{1,0},{2,3},{3,2},{4,5},{5,4},{6,7},{7,6},{8,9},{9,8},{10,11... | collective-permute-start | bytes 1572872 | tf_op jit(solution)/shard_map/ppermute | solution.py:385
  59.3 0.0 collective-permute-done.1.refs_2_
  59.3 0.0 collective-permute-done.2.refs_3_
  59.3 0.0 collective-permute-done.5.refs_6_
  59.3 0.7 copy-done.7
  60.1 0.2 copy-done.8
  60.2 0.8 copy-done.9
  61.1 0.0 collective-permute-done.6.refs_7_
  61.1 5.6 %all-to-all-done.1 = bf16[8,2,128,128]{3,2,1,0:T(8,128)(2,1)S(1)} async-done(((bf16[8,2,128,128]{3,2,1,0:T(8,128)(2,1)}), bf16[8,2,128,128]{3,2,1,0:T(8,128)(2,1)S(1)}, u32[]{:S(2)}, u32[]{:S(2)}) %all-to-all-start.1) | async-done | bytes 524320 | tf_op jit(solution)/shard_map/all_to_all | solution.py:264
  66.6 6.5 %branch_attention.1 = f32[16,136,128]{2,1,0:T(8,128)S(1)} custom-call(bf16[16,128,128]{2,1,0:T(8,128)(2,1)S(1)} %bitcast.26, bf16[8,256,128]{2,1,0:T(8,128)(2,1)} %bitcast.39, bf16[8,256,128]{2,1,0:T(8,128)(2,1)} %bitcast.36, bf16[8,256,128]{2,1,0:T(8,128)(2,1)} %copy-done.7, bf16[8,256,128]{2,1,0:T(8,128)(2,1)} %copy-done.8, ...), custom_call_target="tpu_custom_call" | custom-call | flops 1073741824 | bytes 6291456 | tf_op jit(solution)/shard_map/branch_attention/pallas_call | solution.py:374
  73.1 0.9 convert_element_type.22
  74.0 4.2 %all-to-all-start.2 = ((f16[8,2,136,128]{3,2,1,0:T(8,128)(2,1)}), f16[8,2,136,128]{3,2,1,0:T(8,128)(2,1)S(1)}, u32[]{:S(2)}, u32[]{:S(2)}) async-start(f16[8,2,136,128]{3,2,1,0:T(8,128)(2,1)} %bitcast.11), calls=%async_computation.2 | async-start | bytes 1114112 | tf_op jit(solution)/shard_map/all_to_all | solution.py:264
  78.3 0.0 collective-permute-done.7.q_twin_ref
  78.3 7.8 %all-gather.2.cloned.1.call-done.block_ref = bf16[16,8,64,128]{3,2,1,0:T(8,128)(2,1)} async-done(((bf16[2,8,64,128]{3,2,1,0:T(8,128)(2,1)}), bf16[16,8,64,128]{3,2,1,0:T(8,128)(2,1)}) %all-gather.2.cloned.1.call-update) | async-done | bytes 2097168 | tf_op jit(solution)/shard_map/all_gather | solution.py:334
  86.1 6.9 %root_attention.1 = (f32[16,136,128]{2,1,0:T(8,128)S(1)}, f32[16,136,128]{2,1,0:T(8,128)S(1)}) custom-call(bf16[16,128,128]{2,1,0:T(8,128)(2,1)S(1)} %all-to-all-done.peer_ref.q_ref, bf16[16,128,128]{2,1,0:T(8,128)(2,1)S(1)} %collective-permute-done.7.q_twin_ref, bf16[16,8,64,128]{3,2,1,0:T(8,128)(2,1)} %all-gather.2.cloned.1.call-done.block_ref), custom_call_target="tpu_custom_call" | custom-call | flops 1073741824 | bytes 6291456 | tf_op jit(solution)/shard_map/root_attention/pallas_call | solution.py:390
  93.1 0.1 convert_element_type.23
  93.1 2.1 %collective-permute-start.8 = (f16[16,136,128]{2,1,0:T(8,128)(2,1)S(1)}, f16[16,136,128]{2,1,0:T(8,128)(2,1)S(1)}, u32[]{:S(2)}, u32[]{:S(2)}) collective-permute-start(f16[16,136,128]{2,1,0:T(8,128)(2,1)S(1)} %convert_element_type.23), channel_id=1, source_target_pairs={{0,1},{1,0},{2,3},{3,2},{4,5},{5,4},{6,7},{7,6},{8,9},{9,8},{10,11... | collective-permute-start | bytes 1671176 | tf_op jit(solution)/shard_map/ppermute | solution.py:400
  95.3 1.7 %collective-permute-done.8 = f16[16,136,128]{2,1,0:T(8,128)(2,1)S(1)} collective-permute-done((f16[16,136,128]{2,1,0:T(8,128)(2,1)S(1)}, f16[16,136,128]{2,1,0:T(8,128)(2,1)S(1)}, u32[]{:S(2)}, u32[]{:S(2)}) %collective-permute-start.8) | collective-permute-done | bytes 557088 | tf_op jit(solution)/shard_map/ppermute | solution.py:400
  97.0 0.1 convert_element_type.24.twin_ref
  97.1 0.0 all-to-all-done.2
  97.1 0.1 convert_element_type.25.part_ref
  97.2 1.4 %merge_parts.1 = f32[16,136,128]{2,1,0:T(8,128)S(1)} custom-call(s32[2]{0:T(128)S(1)} %fusion.2.idx_ref, f32[8,2,136,128]{3,2,1,0:T(8,128)S(1)} %convert_element_type.25.part_ref, f32[16,136,128]{2,1,0:T(8,128)S(1)} %get-tuple-element.25.own_ref, f32[16,136,128]{2,1,0:T(8,128)S(1)} %convert_element_type.24.twin_ref), custom_call_target="tpu_custom_call" | custom-call | tf_op jit(solution)/shard_map/merge_parts/pallas_call | solution.py:403
  98.6 0.0 copy-start
  98.6 0.0 copy-start.1
  98.6 0.0 copy-start.2
  98.6 0.0 copy-start.3
  98.6 0.9 convert_element_type.26
  99.5 9.3 %all-to-all-start.3 = ((f16[16,136,128]{2,1,0:T(8,128)(2,1)}), f16[16,136,128]{2,1,0:T(8,128)(2,1)S(1)}, u32[]{:S(2)}, u32[]{:S(2)}) async-start(f16[16,136,128]{2,1,0:T(8,128)(2,1)} %convert_element_type.26), calls=%async_computation.3 | async-start | bytes 1114112 | tf_op jit(solution)/shard_map/all_to_all | solution.py:264
  109.5 1.5 %local_attention.1.local_ref = f32[136,128]{1,0:T(8,128)S(1)} custom-call(s32[1]{0:T(128)S(6)} %copy.50.len_ref, bf16[128,128]{1,0:T(8,128)(2,1)S(1)} %bitcast.30, bf16[4096,128]{1,0:T(8,128)(2,1)S(1)} %bitcast.27, bf16[4096,128]{1,0:T(8,128)(2,1)S(1)} %bitcast.28, bf16[16,128]{1,0:T(8,128)(2,1)S(1)} %bitcast.32, bf16[16,128]{1,0:T(8,128)(2,1)S(1)} %bitcast.33), custom_call_target="tpu_custom_call" | custom-call | flops 268435456 | bytes 2097152 | tf_op jit(solution)/shard_map/local_attention/pallas_call | solution.py:352
  111.0 15.2 %all-to-all-done.3 = f16[16,136,128]{2,1,0:T(8,128)(2,1)S(1)} async-done(((f16[16,136,128]{2,1,0:T(8,128)(2,1)}), f16[16,136,128]{2,1,0:T(8,128)(2,1)S(1)}, u32[]{:S(2)}, u32[]{:S(2)}) %all-to-all-start.3) | async-done | bytes 557088 | tf_op jit(solution)/shard_map/all_to_all | solution.py:264
  126.2 0.1 convert_element_type.27.part_ref
  126.3 0.6 final_merge.1
  126.8 0.6 copy.48
  (21 shorter events, 0.1 us)
Async XLA Ops:
  6.5 10.4 %copy-start.12 = (bf16[32,8,128]{2,1,0:T(8,128)(2,1)S(1)}, bf16[32,8,128]{2,1,0:T(8,128)(2,1)}, u32[]{:S(2)}) copy-start(bf16[32,8,128]{2,1,0:T(8,128)(2,1)} %param.13) | copy-start | bytes 196612
  6.5 10.4 %copy-start.13 = (bf16[32,8,128]{2,1,0:T(8,128)(2,1)S(1)}, bf16[32,8,128]{2,1,0:T(8,128)(2,1)}, u32[]{:S(2)}) copy-start(bf16[32,8,128]{2,1,0:T(8,128)(2,1)} %param.14) | copy-start | bytes 196612
  6.5 14.5 %copy-start.11 = (bf16[1,256,8,128]{3,2,1,0:T(8,128)(2,1)S(1)}, bf16[1,256,8,128]{3,2,1,0:T(8,128)(2,1)}, u32[]{:S(2)}) copy-start(bf16[1,256,8,128]{3,2,1,0:T(8,128)(2,1)} %param.15) | copy-start | bytes 1572868
  6.5 14.5 %copy-start.10 = (bf16[1,256,8,128]{3,2,1,0:T(8,128)(2,1)S(1)}, bf16[1,256,8,128]{3,2,1,0:T(8,128)(2,1)}, u32[]{:S(2)}) copy-start(bf16[1,256,8,128]{3,2,1,0:T(8,128)(2,1)} %param.16) | copy-start | bytes 1572868
  8.3 26.9 %all-to-all-start = ((bf16[16,128,128]{2,1,0:T(8,128)(2,1)}), bf16[16,128,128]{2,1,0:T(8,128)(2,1)S(1)}, u32[]{:S(2)}, u32[]{:S(2)}) async-start(bf16[16,128,128]{2,1,0:T(8,128)(2,1)} %broadcast_in_dim.46), calls=%async_computation | async-start | bytes 1048576 | tf_op jit(solution)/shard_map/all_to_all | solution.py:264
  16.9 69.2 %all-gather.2.cloned.1.call-start = ((), (), s32[]{:S(2)}) async-start(), calls=%async_computation.4 | async-start | bytes 2359296 | tf_op jit(solution)/shard_map/all_gather | solution.py:334
  17.0 10.3 %copy-start.14 = (s32[512]{0:T(512)S(1)}, s32[512]{0:T(512)}, u32[]{:S(2)}) copy-start(s32[512]{0:T(512)} %param.21) | copy-start | bytes 6148
  17.0 10.3 %copy-start.15 = (s32[16]{0:T(128)S(1)}, s32[16]{0:T(128)}, u32[]{:S(2)}) copy-start(s32[16]{0:T(128)} %param.22) | copy-start | bytes 196
  17.0 9.5 %collective-permute-start = (bf16[8,64,128]{2,1,0:T(8,128)(2,1)S(1)}, bf16[8,64,128]{2,1,0:T(8,128)(2,1)S(1)}, u32[]{:S(2)}, u32[]{:S(2)}) collective-permute-start(bf16[8,64,128]{2,1,0:T(8,128)(2,1)S(1)} %bitcast.40), channel_id=1, source_target_pairs={{0,16},{16,0},{1,17},{17,1},{2,18},{18,2},{3,19},{19,3},{4,20},{20... | collective-permute-start | bytes 393224 | tf_op jit(solution)/shard_map/ppermute | solution.py:332
  21.2 25.3 %copy-start.5 = (bf16[256,8,128]{2,0,1:T(8,128)(2,1)}, bf16[256,8,128]{2,0,1:T(8,128)(2,1)S(1)}, u32[]{:S(2)}) copy-start(bf16[256,8,128]{2,0,1:T(8,128)(2,1)S(1)} %get-tuple-element.18) | copy-start | bytes 1572868
  21.2 27.3 %copy-start.4 = (bf16[256,8,128]{2,0,1:T(8,128)(2,1)}, bf16[256,8,128]{2,0,1:T(8,128)(2,1)S(1)}, u32[]{:S(2)}) copy-start(bf16[256,8,128]{2,0,1:T(8,128)(2,1)S(1)} %get-tuple-element.19) | copy-start | bytes 1572868
  27.9 23.1 %collective-permute-start.3 = (bf16[8,256,128]{2,1,0:T(8,128)(2,1)S(1)}, bf16[8,256,128]{2,1,0:T(8,128)(2,1)S(1)}, u32[]{:S(2)}, u32[]{:S(2)}) collective-permute-start(bf16[8,256,128]{2,1,0:T(8,128)(2,1)S(1)} %bitcast.37), channel_id=1, source_target_pairs={{0,16},{16,0},{1,17},{17,1},{2,18},{18,2},{3,19},{19,3},{4,20},{20... | collective-permute-start | bytes 1572872 | tf_op jit(solution)/shard_map/ppermute | solution.py:338
  31.5 23.5 %collective-permute-start.4 = (bf16[8,256,128]{2,1,0:T(8,128)(2,1)S(1)}, bf16[8,256,128]{2,1,0:T(8,128)(2,1)}, u32[]{:S(2)}, u32[]{:S(2)}) collective-permute-start(bf16[8,256,128]{2,1,0:T(8,128)(2,1)S(1)} %bitcast.34), channel_id=1, source_target_pairs={{0,16},{16,0},{1,17},{17,1},{2,18},{18,2},{3,19},{19,3},{4,20},{20... | collective-permute-start | bytes 1572872 | tf_op jit(solution)/shard_map/ppermute | solution.py:339
  36.6 30.0 %all-to-all-start.1 = ((bf16[8,2,128,128]{3,2,1,0:T(8,128)(2,1)}), bf16[8,2,128,128]{3,2,1,0:T(8,128)(2,1)S(1)}, u32[]{:S(2)}, u32[]{:S(2)}) async-start(bf16[8,2,128,128]{3,2,1,0:T(8,128)(2,1)} %pick_readers.1), calls=%async_computation.1 | async-start | bytes 1048576 | tf_op jit(solution)/shard_map/all_to_all | solution.py:264
  46.6 12.7 %collective-permute-start.1 = (bf16[8,256,128]{2,1,0:T(8,128)(2,1)S(1)}, bf16[8,256,128]{2,1,0:T(8,128)(2,1)S(1)}, u32[]{:S(2)}, u32[]{:S(2)}) collective-permute-start(bf16[8,256,128]{2,1,0:T(8,128)(2,1)S(1)} %bitcast.38), channel_id=1, source_target_pairs={{0,1},{1,0},{2,3},{3,2},{4,5},{5,4},{6,7},{7,6},{8,9},{9,8},{10,11... | collective-permute-start | bytes 1572872 | tf_op jit(solution)/shard_map/ppermute | solution.py:344
  48.5 10.8 %collective-permute-start.2 = (bf16[8,256,128]{2,1,0:T(8,128)(2,1)S(1)}, bf16[8,256,128]{2,1,0:T(8,128)(2,1)S(1)}, u32[]{:S(2)}, u32[]{:S(2)}) collective-permute-start(bf16[8,256,128]{2,1,0:T(8,128)(2,1)S(1)} %bitcast.35), channel_id=1, source_target_pairs={{0,1},{1,0},{2,3},{3,2},{4,5},{5,4},{6,7},{7,6},{8,9},{9,8},{10,11... | collective-permute-start | bytes 1572872 | tf_op jit(solution)/shard_map/ppermute | solution.py:345
  50.9 15.7 %copy-start.6 = (bf16[8,256,128]{2,1,0:T(8,128)(2,1)}, bf16[8,256,128]{2,1,0:T(8,128)(2,1)S(1)}, u32[]{:S(2)}) copy-start(bf16[8,256,128]{2,1,0:T(8,128)(2,1)S(1)} %collective-permute-done.3.refs_4_) | copy-start | bytes 1572868
  50.9 8.4 %collective-permute-start.5 = (bf16[8,256,128]{2,1,0:T(8,128)(2,1)S(1)}, bf16[8,256,128]{2,1,0:T(8,128)(2,1)S(1)}, u32[]{:S(2)}, u32[]{:S(2)}) collective-permute-start(bf16[8,256,128]{2,1,0:T(8,128)(2,1)S(1)} %collective-permute-done.3.refs_4_), channel_id=1, source_target_pairs={{0,1},{1,0},{2,3},{3,2},{4,5},{5,4},{6,7},{7,6},{8,9},{9,8},{10,11... | collective-permute-start | bytes 1572872 | tf_op jit(solution)/shard_map/ppermute | solution.py:348
  54.9 6.1 %collective-permute-start.6 = (bf16[8,256,128]{2,1,0:T(8,128)(2,1)}, bf16[8,256,128]{2,1,0:T(8,128)(2,1)}, u32[]{:S(2)}, u32[]{:S(2)}) collective-permute-start(bf16[8,256,128]{2,1,0:T(8,128)(2,1)} %collective-permute-done.4.refs_5_), channel_id=1, source_target_pairs={{0,1},{1,0},{2,3},{3,2},{4,5},{5,4},{6,7},{7,6},{8,9},{9,8},{10,11... | collective-permute-start | bytes 1572872 | tf_op jit(solution)/shard_map/ppermute | solution.py:349
  56.8 21.4 %collective-permute-start.7 = (bf16[16,128,128]{2,1,0:T(8,128)(2,1)S(1)}, bf16[16,128,128]{2,1,0:T(8,128)(2,1)S(1)}, u32[]{:S(2)}, u32[]{:S(2)}) collective-permute-start(bf16[16,128,128]{2,1,0:T(8,128)(2,1)S(1)} %all-to-all-done.peer_ref.q_ref), channel_id=1, source_target_pairs={{0,1},{1,0},{2,3},{3,2},{4,5},{5,4},{6,7},{7,6},{8,9},{9,8},{10,11... | collective-permute-start | bytes 1572872 | tf_op jit(solution)/shard_map/ppermute | solution.py:385
  59.3 0.8 copy-start.7
  59.3 1.0 copy-start.8
  60.2 0.8 copy-start.9
  74.0 23.0 %all-to-all-start.2 = ((f16[8,2,136,128]{3,2,1,0:T(8,128)(2,1)}), f16[8,2,136,128]{3,2,1,0:T(8,128)(2,1)S(1)}, u32[]{:S(2)}, u32[]{:S(2)}) async-start(f16[8,2,136,128]{3,2,1,0:T(8,128)(2,1)} %bitcast.11), calls=%async_computation.2 | async-start | bytes 1114112 | tf_op jit(solution)/shard_map/all_to_all | solution.py:264
  93.1 3.9 %collective-permute-start.8 = (f16[16,136,128]{2,1,0:T(8,128)(2,1)S(1)}, f16[16,136,128]{2,1,0:T(8,128)(2,1)S(1)}, u32[]{:S(2)}, u32[]{:S(2)}) collective-permute-start(f16[16,136,128]{2,1,0:T(8,128)(2,1)S(1)} %convert_element_type.23), channel_id=1, source_target_pairs={{0,1},{1,0},{2,3},{3,2},{4,5},{5,4},{6,7},{7,6},{8,9},{9,8},{10,11... | collective-permute-start | bytes 1671176 | tf_op jit(solution)/shard_map/ppermute | solution.py:400
  98.6 10.9 %copy-start = (bf16[1,512,8,128]{3,2,1,0:T(8,128)(2,1)S(1)}, bf16[1,512,8,128]{3,2,1,0:T(8,128)(2,1)}, u32[]{:S(2)}) copy-start(bf16[1,512,8,128]{3,2,1,0:T(8,128)(2,1)} %param.17) | copy-start | bytes 3145732
  98.6 10.9 %copy-start.1 = (bf16[1,512,8,128]{3,2,1,0:T(8,128)(2,1)S(1)}, bf16[1,512,8,128]{3,2,1,0:T(8,128)(2,1)}, u32[]{:S(2)}) copy-start(bf16[1,512,8,128]{3,2,1,0:T(8,128)(2,1)} %param.18) | copy-start | bytes 3145732
  98.6 10.9 %copy-start.2 = (bf16[1,2,8,128]{3,2,1,0:T(8,128)(2,1)S(1)}, bf16[1,2,8,128]{3,2,1,0:T(8,128)(2,1)}, u32[]{:S(2)}) copy-start(bf16[1,2,8,128]{3,2,1,0:T(8,128)(2,1)} %param.19) | copy-start | bytes 12292
  98.6 10.9 %copy-start.3 = (bf16[1,2,8,128]{3,2,1,0:T(8,128)(2,1)S(1)}, bf16[1,2,8,128]{3,2,1,0:T(8,128)(2,1)}, u32[]{:S(2)}) copy-start(bf16[1,2,8,128]{3,2,1,0:T(8,128)(2,1)} %param.20) | copy-start | bytes 12292
  99.5 26.7 %all-to-all-start.3 = ((f16[16,136,128]{2,1,0:T(8,128)(2,1)}), f16[16,136,128]{2,1,0:T(8,128)(2,1)S(1)}, u32[]{:S(2)}, u32[]{:S(2)}) async-start(f16[16,136,128]{2,1,0:T(8,128)(2,1)} %convert_element_type.26), calls=%async_computation.3 | async-start | bytes 1114112 | tf_op jit(solution)/shard_map/all_to_all | solution.py:264
Sparse Core Ops, SparseCore 0:
  27.4 58.7 all-gather.1
